TPU v7x, 32 devices: a whole 2x2x4 slice. The times are simulated.
32 devices in a mesh: leaf: 2 (over core), row: 4 (over y, x), col: 4 (over z).
Axes of the slice: x: 2, y: 2, z: 4, core: 2. Of those that a mesh axis runs over, the one named last changes fastest.
Arguments:
- rhs: bfloat16 [7680, 512], P(('leaf', 'row'), 'col'), may hold values from -6 to 6
- pivot_inverse: bfloat16 [7680, 2560], P('leaf', 'row'), may hold values from -0.125 to 0.125
- panel: bfloat16 [3072, 2560], P('leaf', 'row'), may hold values from -0.0625 to 0.0625
- live: int32 [3], replicated, may hold values from 10 to 20, as said below
- parent_map: int32 [2, 12], replicated, may hold values from 0 to 19, as said below
Outputs:
- forward_solution: bfloat16 [7680, 512], P(('leaf', 'row'), 'col')
- solution: bfloat16 [7680, 512], P(('leaf', 'row'), 'col')
Inputs may be any that keep to these rules, and one draw needn't show every extreme that they name: `live`: the root front (last index) is full, 20 blocks. `parent_map`: within one front's row the parent blocks are distinct.
All inputs are finite; a program needn't handle non-finite values.
Results may differ from a plain program's by a relative error of at most 0.012.
Values may be sent and summed in bfloat16 or wider, within the bound.
No kernel may reach another device: no remote copies, remote signals or barrier semaphores. Data moves between devices by JAX's collectives and lax.ppermute only.
A program may use at most 64 MiB of HBM per device.

v0:
```python
import jax
import jax.numpy as jnp
from jax import lax
from jax.sharding import PartitionSpec as P

F = 2560
E = 1536


def from_partner(block, axis, apart):
    count = lax.axis_size(axis)
    route = []
    for low in range(count):
        high = low | 1 << apart
        if high != low and high < count:
            route += [(low, high), (high, low)]
    return lax.ppermute(block, axis, route)


def doubling(stacked, bit_count, leaf_pos, swapper):
    for bit_no in range(bit_count):
        partner = swapper(stacked, bit_no)
        upper_half = jnp.right_shift(leaf_pos, bit_no) % 2 == 1
        stacked = jnp.where(
            upper_half,
            jnp.concatenate([partner, stacked], 0),
            jnp.concatenate([stacked, partner], 0),
        )
    return stacked


def halving(partial_value, bit_count, leaf_pos, swapper):
    for bit_no in reversed(range(bit_count)):
        halves = partial_value.reshape((2, partial_value.shape[0] // 2) + partial_value.shape[1:])
        upper_half = jnp.right_shift(leaf_pos, bit_no) % 2 == 1
        kept_half = jnp.where(upper_half, halves[1], halves[0])
        sent_half = jnp.where(upper_half, halves[0], halves[1])
        partial_value = kept_half + swapper(sent_half, bit_no)
    return partial_value[0]


def to_front(group_block, row_count):
    count_g, total_rows, row_width = group_block.shape
    piece_rows = total_rows // row_count
    return (
        group_block.reshape(count_g, row_count, piece_rows, row_width)
        .transpose(1, 0, 2, 3)
        .reshape(count_g * total_rows, row_width)
    )


def block_onehot(mapping):
    return (jnp.arange(F // 128, dtype=jnp.int32)[:, None] == mapping[None, :]).astype(jnp.bfloat16)


def pivot_sum(diag_block, quarter_rows):
    return lax.psum_scatter(
        jnp.dot(diag_block, quarter_rows, preferred_element_type=jnp.float32).astype(jnp.bfloat16),
        "row",
        scatter_dimension=0,
        tiled=True,
    ).astype(jnp.float32)


def quarter_swap(values, bit_no):
    return from_partner(values, "leaf", bit_no)


def update_swap(values, bit_no):
    return from_partner(values, "leaf", bit_no)


def parent_swap(values, bit_no):
    return from_partner(values, "leaf", bit_no)


def reduce_swap(values, bit_no):
    return from_partner(values.astype(jnp.bfloat16), "leaf", bit_no).astype(values.dtype)


def on_device(rhs, pivot_inverse, panel, live, parent_map):
    leaves = lax.axis_size("leaf")
    row_count = lax.axis_size("row")
    tree_depth = leaves.bit_length() - 1
    leaf_pos = lax.axis_index("leaf")
    row_pos = lax.axis_index("row")
    columns = rhs.shape[1]
    quarter = F // row_count
    parent_blocks = F // 128
    child_blocks = E // 128
    layout = []
    vec_off, piv_off, pan_off, front_base = (0, 0, 0, 0)
    for level_no in range(tree_depth + 1):
        groups = 2**level_no
        layout.append((groups, vec_off, piv_off, pan_off, front_base))
        vec_off += F // (row_count * groups)
        piv_off += F // groups
        pan_off += E // groups
        front_base += leaves // groups
    forward_parts = []
    live_masks = []
    incoming = None
    for level_no in range(tree_depth + 1):
        groups, vec_off, piv_off, pan_off, front_base = layout[level_no]
        piece_rows = F // (row_count * groups)
        panel_rows = E // (row_count * groups)
        inner_pos = leaf_pos % groups
        front_no = jnp.right_shift(leaf_pos, level_no)
        live_rows = lax.dynamic_index_in_dim(live, front_base + front_no, 0, keepdims=False) * 128
        first_row = (row_pos * groups + inner_pos) * piece_rows
        live_mask = (first_row + jnp.arange(piece_rows, dtype=jnp.int32) < live_rows)[:, None]
        live_masks.append(live_mask)
        right_side = rhs[vec_off : vec_off + piece_rows]
        if incoming is not None:
            right_side = (right_side.astype(jnp.float32) - incoming).astype(jnp.bfloat16)
        masked = jnp.where(live_mask, right_side, jnp.zeros_like(right_side))
        quarter_rows = doubling(masked[None], level_no, leaf_pos, quarter_swap).reshape(
            quarter, columns
        )
        diag_block = pivot_inverse[piv_off : piv_off + F // groups]
        if level_no < tree_depth:
            off_block = panel[pan_off : pan_off + E // groups]
            forward_value = pivot_sum(diag_block, quarter_rows)
            update_rows = lax.psum(
                jnp.dot(off_block, quarter_rows, preferred_element_type=jnp.float32), "row"
            ).astype(jnp.bfloat16)
        else:
            forward_value = pivot_sum(diag_block, quarter_rows)
        forward_parts.append(jnp.where(live_mask, forward_value, 0.0).astype(jnp.bfloat16))
        if level_no < tree_depth:
            gathered = doubling(update_rows[None], level_no + 1, leaf_pos, update_swap)
            parent_front = jnp.right_shift(leaf_pos, level_no + 1)
            assembled = jnp.zeros((parent_blocks, 128, columns), jnp.float32)
            for side_no in range(2):
                child_update = to_front(
                    gathered[side_no * groups : (side_no + 1) * groups], row_count
                )
                mapping = lax.dynamic_index_in_dim(
                    parent_map, front_base + 2 * parent_front + side_no, 0, keepdims=False
                )
                assembled = assembled + jnp.einsum(
                    "ke,eab->kab",
                    block_onehot(mapping),
                    child_update.reshape(child_blocks, 128, columns),
                    preferred_element_type=jnp.float32,
                )
            parent_groups = 2 * groups
            parent_rows = F // (row_count * parent_groups)
            parent_first = (row_pos * parent_groups + leaf_pos % parent_groups) * parent_rows
            incoming = lax.dynamic_slice_in_dim(
                assembled.reshape(F, columns), parent_first, parent_rows, 0
            )
    backward_parts = [None] * (tree_depth + 1)
    parent_value = None
    for level_no in reversed(range(tree_depth + 1)):
        groups, vec_off, piv_off, pan_off, front_base = layout[level_no]
        piece_rows = F // (row_count * groups)
        panel_rows = E // (row_count * groups)
        inner_pos = leaf_pos % groups
        front_no = jnp.right_shift(leaf_pos, level_no)
        diag_block = pivot_inverse[piv_off : piv_off + F // groups]
        own_piece = forward_parts[level_no]
        if level_no == tree_depth:
            own_rows = lax.all_gather(own_piece, "row", axis=0, tiled=True)
            partial_value = jnp.einsum(
                "ik,ia->ka", diag_block, own_rows, preferred_element_type=jnp.float32
            )
        else:
            own_rows, parent_gathered = (
                lax.all_gather(own_piece, "row", axis=0, tiled=True),
                lax.all_gather(parent_value, "row", axis=0, tiled=True),
            )
            whole_parent = doubling(parent_gathered[None], level_no + 1, leaf_pos, parent_swap)
            parent_full = to_front(whole_parent, row_count)
            mapping = lax.dynamic_index_in_dim(parent_map, front_base + front_no, 0, keepdims=False)
            taken_rows = jnp.einsum(
                "ke,kab->eab",
                block_onehot(mapping),
                parent_full.reshape(parent_blocks, 128, columns),
                preferred_element_type=jnp.float32,
            ).astype(jnp.bfloat16)
            taken_rows = lax.dynamic_index_in_dim(
                taken_rows.reshape(row_count, groups, panel_rows, columns),
                inner_pos,
                1,
                keepdims=False,
            ).reshape(row_count * panel_rows, columns)
            off_block = panel[pan_off : pan_off + E // groups]
            partial_value = jnp.einsum(
                "ik,ia->ka", diag_block, own_rows, preferred_element_type=jnp.float32
            ) - jnp.einsum("ik,ia->ka", off_block, taken_rows, preferred_element_type=jnp.float32)
        if level_no == 0:
            reduced = partial_value
        else:
            reduced = halving(
                partial_value.reshape(groups, piece_rows, columns), level_no, leaf_pos, reduce_swap
            )
        parent_value = jnp.where(live_masks[level_no], reduced, 0.0).astype(jnp.bfloat16)
        backward_parts[level_no] = parent_value
    return (jnp.concatenate(forward_parts, 0), jnp.concatenate(backward_parts, 0))


def solution(mesh):
    in_specs = (P(("leaf", "row"), "col"), P("leaf", "row"), P("leaf", "row"), P(), P())
    out_specs = (P(("leaf", "row"), "col"), P(("leaf", "row"), "col"))
    return jax.shard_map(
        on_device, mesh=mesh, in_specs=in_specs, out_specs=out_specs, check_vma=False
    )
```

profile of v0, /device:TPU:0, one launch (start us, length us, event | category | flops | bytes accessed | tf_op | source)
XLA Modules:
  0.0 132.6 jit_solution(14651014183989970890)
XLA Ops:
  7.2 1.1 slice.30
  8.3 0.2 copy.50
  8.5 1.3 fusion.49
  10.5 0.7 convolution_bitcast_fusion
  11.2 35.4 %all-reduce.1 = bf16[1536,128]{0,1:T(8,128)(2,1)S(1)} all-reduce(f32[1536,128]{0,1:T(8,128)S(1)} %convolution_bitcast_fusion), channel_id=1, replica_groups=mesh['leaf'=2,'row'=4,'col'=4] {'row'}, use_global_device_ids=true, to_apply=%region_1.2 | all-reduce | flops 196608 | bytes 1179648 | tf_op jit(solution)/shard_map/psum | solution.py:124
  47.6 0.8 collective-permute-done
  48.6 0.2 copy.32
  48.9 0.2 copy.34
  49.1 0.5 fusion.26
  49.6 0.5 convolution_add_fusion
  50.1 0.3 copy.36
  50.6 0.2 collective-permute-start.1
  50.8 1.2 collective-permute-done.1
  52.0 0.2 copy.38
  52.2 2.0 %fusion.4 = bf16[1280,128]{0,1:T(8,128)(2,1)S(1)} fusion(bf16[640,128]{1,0:T(8,128)(2,1)S(1)} %bitcast.71, bf16[3840,640]{1,0:T(8,128)(2,1)} %param.6), kind=kOutput, calls=%fused_computation.7 | convolution fusion | flops 209879040 | bytes 2129920 | tf_op jit(solution)/shard_map/dot_general | solution.py:58
  54.2 0.9 copy.48
  55.2 3.1 %fusion = bf16[2560,128]{0,1:T(8,128)(2,1)S(1)} fusion(bf16[3840,640]{1,0:T(8,128)(2,1)} %param.6, bf16[640,128]{0,1:T(8,128)(2,1)S(1)} %copy.50, pred[640]{0:T(1024)(128)(4,1)S(1)} %add_compare_fusion), kind=kOutput, calls=%fused_computation.1 | convolution fusion | flops 419840000 | bytes 4096640 | tf_op jit(solution)/shard_map/dot_general | solution.py:58
  58.3 1.1 copy.46
  59.4 20.2 %reduce-scatter.9.cloned.1.call-done = bf16[320,128]{1,0:T(8,128)(2,1)} async-done(((bf16[1280,128]{1,0:T(8,128)(2,1)}), bf16[320,128]{1,0:T(8,128)(2,1)}) %reduce-scatter.9.cloned.1.call-update) | async-done | bytes 81936
  79.5 1.0 copy.49
  80.7 9.5 %all_gather.10 = bf16[1280,128]{1,0:T(8,128)(2,1)S(1)} all-gather(bf16[320,128]{1,0:T(8,128)(2,1)S(1)} %copy.39), channel_id=1, replica_groups=mesh['leaf'=2,'row'=4,'col'=4] {'row'}, dimensions={0}, use_global_device_ids=true | all-gather | bytes 409600 | tf_op jit(solution)/shard_map/all_gather | solution.py:164
  90.2 1.9 %fusion.11 = f32[640,128]{0,1:T(8,128)S(1)} fusion(bf16[1280,128]{1,0:T(8,128)(2,1)S(1)} %all_gather.10, bf16[3840,640]{1,0:T(8,128)(2,1)} %param.6), kind=kOutput, calls=%fused_computation.14 | convolution fusion | flops 209715200 | bytes 2293760 | tf_op jit(solution)/shard_map/ik,ia->ka/dot_general | solution.py:165
  92.3 1.3 collective-permute-done.2
  93.8 8.0 %all_gather.11 = bf16[1280,128]{1,0:T(8,128)(2,1)S(1)} all-gather(bf16[320,128]{1,0:T(8,128)(2,1)S(1)} %copy.40), channel_id=1, replica_groups=mesh['leaf'=2,'row'=4,'col'=4] {'row'}, dimensions={0}, use_global_device_ids=true | all-gather | bytes 409600 | tf_op jit(solution)/shard_map/all_gather | solution.py:171
  101.8 6.0 %reduce-scatter.7.cloned.1.call-done = bf16[640,128]{1,0:T(8,128)(2,1)} async-done(((bf16[2560,128]{1,0:T(8,128)(2,1)}), bf16[640,128]{1,0:T(8,128)(2,1)}) %reduce-scatter.7.cloned.1.call-update) | async-done | bytes 163856
  107.9 1.1 copy.47
  109.0 0.8 copy.44
  109.8 11.0 %all_gather.9 = bf16[2560,128]{0,1:T(8,128)(2,1)S(1)} all-gather(bf16[640,128]{0,1:T(8,128)(2,1)S(1)} %select_convert_fusion), channel_id=1, replica_groups=mesh['leaf'=2,'row'=4,'col'=4] {'row'}, dimensions={0}, use_global_device_ids=true | all-gather | bytes 819200 | tf_op jit(solution)/shard_map/all_gather | solution.py:170
  121.0 0.6 convolution_convert_fusion.2
  121.8 0.5 fusion.50
  122.3 2.6 %fusion.20 = bf16[640,128]{0,1:T(8,128)(2,1)S(1)} fusion(f32[128,640]{1,0:T(8,128)S(1)} %fusion.50, bf16[2560,128]{0,1:T(8,128)(2,1)S(1)} %all_gather.9, bf16[3840,640]{1,0:T(8,128)(2,1)} %param.6, pred[640]{0:T(1024)(128)(4,1)S(1)} %add_compare_fusion), kind=kOutput, calls=%fused_computation.17 | convolution fusion | flops 419676160 | bytes 4424320 | tf_op jit(solution)/shard_map/ik,ia->ka/dot_general | solution.py:189
  124.9 0.8 copy.45
  (35 shorter events, 1.7 us)
Async XLA Ops:
  7.2 3.3 %copy-start = (bf16[1536,640]{1,0:T(8,128)(2,1)S(1)}, bf16[1536,640]{1,0:T(8,128)(2,1)}, u32[]{:S(2)}) copy-start(bf16[1536,640]{1,0:T(8,128)(2,1)} %param.7) | copy-start | bytes 5898244
  7.2 72.4 %reduce-scatter.9.cloned.1.call-start = ((), (), s32[]{:S(2)}) async-start(), calls=%async_computation.3 | async-start | bytes 409600
  10.5 36.9 %slice-start = ((bf16[960,128]{1,0:T(8,128)(2,1)}), bf16[320,128]{1,0:T(8,128)(2,1)S(1)}, s32[]{:S(2)}) async-start(bf16[960,128]{1,0:T(8,128)(2,1)} %param.5), calls=%async_computation.4 | async-start | bytes 163840 | tf_op jit(solution)/shard_map/slice | solution.py:113
  10.5 37.1 %copy-start.1 = (s32[2,12]{1,0:T(2,128)S(1)}, s32[2,12]{1,0:T(2,128)}, u32[]{:S(2)}) copy-start(s32[2,12]{1,0:T(2,128)} %param.9) | copy-start | bytes 292
  46.7 1.8 %collective-permute-start = (bf16[1,1536,128]{1,2,0:T(8,128)(2,1)S(1)}, bf16[1,1536,128]{1,2,0:T(8,128)(2,1)S(1)}, u32[]{:S(2)}, u32[]{:S(2)}) collective-permute-start(bf16[1,1536,128]{1,2,0:T(8,128)(2,1)S(1)} %bitcast.65), channel_id=1, source_target_pairs={{0,16},{16,0},{1,17},{17,1},{2,18},{18,2},{3,19},{19,3},{4,20},{20... | collective-permute-start | bytes 1179656 | tf_op jit(solution)/shard_map/ppermute | solution.py:17
  50.6 1.4 %collective-permute-start.1 = (bf16[1,320,128]{1,2,0:T(8,128)(2,1)S(1)}, bf16[1,320,128]{1,2,0:T(8,128)(2,1)S(1)}, u32[]{:S(2)}, u32[]{:S(2)}) collective-permute-start(bf16[1,320,128]{1,2,0:T(8,128)(2,1)S(1)} %fusion.30), channel_id=1, source_target_pairs={{0,16},{16,0},{1,17},{17,1},{2,18},{18,2},{3,19},{19,3},{4,20},{20... | collective-permute-start | bytes 245768 | tf_op jit(solution)/shard_map/ppermute | solution.py:17
  55.1 52.7 %reduce-scatter.7.cloned.1.call-start = ((), (), s32[]{:S(2)}) async-start(), calls=%async_computation.2 | async-start | bytes 819200
  92.2 1.4 %collective-permute-start.2 = (bf16[1,320,128]{1,2,0:T(8,128)(2,1)S(1)}, bf16[1,320,128]{1,2,0:T(8,128)(2,1)S(1)}, u32[]{:S(2)}, u32[]{:S(2)}) collective-permute-start(bf16[1,320,128]{1,2,0:T(8,128)(2,1)S(1)} %fusion.31), channel_id=1, source_target_pairs={{0,16},{16,0},{1,17},{17,1},{2,18},{18,2},{3,19},{19,3},{4,20},{20... | collective-permute-start | bytes 245768 | tf_op jit(solution)/shard_map/ppermute | solution.py:17
  101.8 19.0 %collective-permute-start.3 = (bf16[1,1280,128]{2,1,0:T(8,128)(2,1)S(1)}, bf16[1,1280,128]{2,1,0:T(8,128)(2,1)S(1)}, u32[]{:S(2)}, u32[]{:S(2)}) collective-permute-start(bf16[1,1280,128]{2,1,0:T(8,128)(2,1)S(1)} %bitcast.68), channel_id=1, source_target_pairs={{0,16},{16,0},{1,17},{17,1},{2,18},{18,2},{3,19},{19,3},{4,20},{20... | collective-permute-start | bytes 983048 | tf_op jit(solution)/shard_map/ppermute | solution.py:17
Sparse Core Ops, SparseCore 0:
  55.2 24.2 reduce-scatter.8
  82.4 25.3 reduce-scatter.6
where the time goes:
time: 133 us
  blocking collectives  64 us (48%)
  waiting for transfers between devices  29.5 us (22%)
  between operations  15.7 us (12%)
  matrix products  12.5 us (9%)
  local copies, waits for them, and re-layouts  9.9 us (7%)
    psum x1, blocking collectives, on_device(): lax.psum(jnp.dot(off_block, quarter_rows, preferred_element_type=jnp.floa...  35.4 us
    unnamed x4, waiting for transfers between devices  26.2 us
    all_gather x1, blocking collectives, on_device(): lax.all_gather(own_piece, 'row', axis=0, tiled=True)  11 us
    all_gather x1, blocking collectives, on_device(): own_rows = lax.all_gather(own_piece, 'row', axis=0, tiled=True)  9.51 us
    all_gather x1, blocking collectives, on_device(): lax.all_gather(parent_value, 'row', axis=0, tiled=True)  8.02 us
    unnamed x13, local copies, waits for them, and re-layouts  6.16 us
    dot_general x2, matrix products, pivot_sum(): jnp.dot(diag_block, quarter_rows, preferred_element_type=jnp.float32)  5.11 us
    dot_general x2, matrix products, on_device(): jnp.einsum('ik,ia->ka', diag_block, own_rows, preferred_element_type=jnp....  4.5 us
  transfers between devices with their start and end apart: 6, of which 5 were waited for; matrix products, arithmetic and copies ran while one was open for 7% of the time, Pallas kernels for 0%

commit v1 on v0

--- a/solution.py
+++ b/solution.py
@@ -1,6 +1,10 @@
+import functools
+
 import jax
 import jax.numpy as jnp
 from jax import lax
+from jax.experimental import pallas as pl
+from jax.experimental.pallas import tpu as pltpu
 from jax.sharding import PartitionSpec as P
 
 F = 2560
@@ -78,7 +82,7 @@
     return from_partner(values.astype(jnp.bfloat16), "leaf", bit_no).astype(values.dtype)
 
 
-def on_device(rhs, pivot_inverse, panel, live, parent_map):
+def deep_tree(rhs, pivot_inverse, panel, live, parent_map):
     leaves = lax.axis_size("leaf")
     row_count = lax.axis_size("row")
     tree_depth = leaves.bit_length() - 1
@@ -200,6 +204,320 @@
     return (jnp.concatenate(forward_parts, 0), jnp.concatenate(backward_parts, 0))
 
 
+B = 128
+VMEM = pl.BlockSpec(memory_space=pltpu.VMEM)
+SMEM = pl.BlockSpec(memory_space=pltpu.SMEM)
+ANY = pl.BlockSpec(memory_space=pl.ANY)
+BF = jnp.bfloat16
+F32 = jnp.float32
+
+
+def bf16(rows, columns):
+    return jax.ShapeDtypeStruct((rows, columns), BF)
+
+
+def call(body, out_shape, in_specs, scratch, flops, bytes_moved):
+    return pl.pallas_call(
+        body,
+        out_shape=out_shape,
+        in_specs=in_specs,
+        out_specs=jax.tree.map(lambda _: VMEM, out_shape),
+        scratch_shapes=scratch,
+        compiler_params=pltpu.CompilerParams(vmem_limit_bytes=24 * 1024 * 1024),
+        cost_estimate=pl.CostEstimate(flops=flops, bytes_accessed=bytes_moved, transcendentals=0),
+    )
+
+
+def masked_rows(value, first_row, live_blocks):
+    row = first_row + lax.broadcasted_iota(jnp.int32, value.shape, 0)
+    return jnp.where(row < live_blocks * B, value, jnp.zeros_like(value))
+
+
+def rows_at(start, size):
+    return pl.ds(pl.multiple_of(start, 16), size)
+
+
+def mm(left, right):
+    return jnp.dot(left, right, preferred_element_type=F32)
+
+
+def panel_kernel(sizes, live, pmap, rhs, panel, send, keep, b_v, w_v, c_v, sems):
+    quarter, half, parts, update_rows = sizes
+    leaf_pos = lax.axis_index("leaf")
+    row_pos = lax.axis_index("row")
+    get_b = pltpu.make_async_copy(rhs.at[pl.ds(0, quarter)], b_v, sems.at[0])
+    get_b.start()
+    step = update_rows // parts
+    copies = []
+    for i in range(parts):
+        rows = pl.ds(i * step, step)
+        copies.append(pltpu.make_async_copy(panel.at[rows], w_v.at[rows], sems.at[1 + i]))
+        copies[-1].start()
+    c_v[...] = jnp.zeros_like(c_v)
+    get_b.wait()
+    masked = masked_rows(b_v[...], row_pos * quarter, live[leaf_pos])
+    for i in range(parts):
+        copies[i].wait()
+        product = mm(w_v[pl.ds(i * step, step)], masked).astype(BF)
+        for e in range(step // B):
+            block = pmap[leaf_pos, i * (step // B) + e]
+            c_v[pl.ds(pl.multiple_of(block * B, B), B)] = product[e * B : (e + 1) * B]
+    for k in range(4):
+        base = (row_pos ^ k) * quarter
+        keep[pl.ds(k * half, half)] = c_v[rows_at(base + leaf_pos * half, half)]
+        send[pl.ds(k * half, half)] = c_v[rows_at(base + (1 - leaf_pos) * half, half)]
+
+
+def leaf_pivot_kernel(
+    sizes, live, rhs, pivot, send_x, send_y, keep_x, keep_y, b_v, d_v, sems
+):
+    quarter, half = sizes
+    leaf_pos = lax.axis_index("leaf")
+    row_pos = lax.axis_index("row")
+    get_b = pltpu.make_async_copy(rhs.at[pl.ds(0, quarter)], b_v, sems.at[4])
+    get_b.start()
+    order = (3, 1, 2, 0)
+    copies = {}
+    for k in order:
+        rows = rows_at((row_pos ^ k) * quarter, quarter)
+        copies[k] = pltpu.make_async_copy(pivot.at[rows], d_v.at[k], sems.at[k])
+        copies[k].start()
+    get_b.wait()
+    masked = masked_rows(b_v[...], row_pos * quarter, live[leaf_pos])
+    first, second = pl.ds(0, half), pl.ds(half, half)
+    low = {1: (send_x, first), 3: (send_x, second), 0: (keep_x, first), 2: (keep_x, second)}
+    high = {2: (send_y, first), 3: (send_y, second), 0: (keep_y, first), 1: (keep_y, second)}
+    for k in order:
+        copies[k].wait()
+        product = mm(d_v[k], masked).astype(BF)
+        ref, rows = low[k]
+        ref[rows] = product[:half]
+        ref, rows = high[k]
+        ref[rows] = product[half:]
+
+
+def root_pivot_kernel(sizes, own, other, pivot, out0, out1, out2, out3, q_v, d_v, sems):
+    quarter, half, base = sizes
+    leaf_pos = lax.axis_index("leaf")
+    row_pos = lax.axis_index("row")
+    outs = (out0, out1, out2, out3)
+    order = (3, 1, 2, 0)
+    copies = {}
+    for k in order:
+        rows = rows_at(base + (row_pos ^ k) * half, half)
+        copies[k] = pltpu.make_async_copy(pivot.at[rows], d_v.at[k], sems.at[k])
+        copies[k].start()
+    q_v[rows_at(leaf_pos * half, half)] = own[...]
+    q_v[rows_at((1 - leaf_pos) * half, half)] = other[...]
+    right = q_v[...]
+    for k in order:
+        copies[k].wait()
+        outs[k][...] = mm(d_v[k], right).astype(BF)
+
+
+def root_transposed_kernel(sizes, y0, y1, y2, y3, pivot, keep, send, y_v, d_v, s_v, sem):
+    quarter, half, base = sizes
+    leaf_pos = lax.axis_index("leaf")
+    row_pos = lax.axis_index("row")
+    get_d = pltpu.make_async_copy(pivot.at[pl.ds(base, 4 * half)], d_v, sem)
+    get_d.start()
+    for k, piece in enumerate((y0, y1, y2, y3)):
+        y_v[rows_at((row_pos ^ k) * half, half)] = piece[...]
+    turned = y_v[...].T
+    get_d.wait()
+    s_v[...] = mm(turned, d_v[...]).T
+    keep[...] = s_v[rows_at(leaf_pos * half, half)]
+    send[...] = s_v[rows_at((1 - leaf_pos) * half, half)].astype(BF)
+
+
+def leaf_transposed_kernel(
+    sizes, f0, f1, f2, f3a, f3b, root_piece, pivot, total, forward, y_v, d_v, sem
+):
+    quarter, half = sizes
+    row_pos = lax.axis_index("row")
+    get_d = pltpu.make_async_copy(pivot.at[pl.ds(0, 4 * quarter)], d_v, sem)
+    get_d.start()
+    for k, piece in enumerate((f0, f1, f2)):
+        y_v[rows_at((row_pos ^ k) * quarter, quarter)] = piece[...]
+    y_v[rows_at((row_pos ^ 3) * quarter, half)] = f3a[...]
+    y_v[rows_at((row_pos ^ 3) * quarter + half, half)] = f3b[...]
+    forward[pl.ds(0, quarter)] = f0[...]
+    forward[pl.ds(quarter, half)] = root_piece[...]
+    turned = y_v[...].T
+    get_d.wait()
+    total[...] = mm(turned, d_v[...])
+
+
+def last_kernel(
+    sizes, live, pmap, s0, s1, s2, s3, t0, t1, t2, t3, total, panel, out, s_v, w_v, p_v, sem
+):
+    quarter, half, update_rows = sizes
+    leaf_pos = lax.axis_index("leaf")
+    row_pos = lax.axis_index("row")
+    get_p = pltpu.make_async_copy(panel.at[pl.ds(0, update_rows)], p_v, sem)
+    get_p.start()
+    for k, (mine, theirs) in enumerate(((s0, t0), (s1, t1), (s2, t2), (s3, t3))):
+        base = (row_pos ^ k) * quarter
+        s_v[rows_at(base + leaf_pos * half, half)] = mine[...]
+        s_v[rows_at(base + (1 - leaf_pos) * half, half)] = theirs[...]
+    for e in range(update_rows // B):
+        block = pmap[leaf_pos, e]
+        w_v[pl.ds(e * B, B)] = s_v[pl.ds(pl.multiple_of(block * B, B), B)]
+    turned = w_v[...].T
+    get_p.wait()
+    value = (total[...] - mm(turned, p_v[...])).T
+    out[pl.ds(0, quarter)] = masked_rows(value, row_pos * quarter, live[leaf_pos]).astype(BF)
+    out[pl.ds(quarter, half)] = s0[...]
+
+
+def row_swap(value, apart):
+    count = lax.axis_size("row")
+    return lax.ppermute(value, "row", [(r, r ^ apart) for r in range(count)])
+
+
+def leaf_swap(value):
+    return lax.ppermute(value, "leaf", [(0, 1), (1, 0)])
+
+
+def two_levels(rhs, pivot_inverse, panel, live, parent_map):
+    columns = rhs.shape[1]
+    quarter = pivot_inverse.shape[1]
+    half = quarter // 2
+    front = 4 * quarter
+    updates = parent_map.shape[1] * B
+    leaf_pos = lax.axis_index("leaf")
+    row_pos = lax.axis_index("row")
+
+    def live_rows(value, first_row, front_no):
+        row = first_row + lax.broadcasted_iota(jnp.int32, value.shape, 0)
+        count = lax.dynamic_index_in_dim(live, front_no, 0, keepdims=False) * B
+        return jnp.where(row < count, value, 0.0)
+
+    root_first = (2 * row_pos + leaf_pos) * half
+
+    parts = 4 if updates % (4 * B) == 0 else 1
+    sent, kept = call(
+        functools.partial(panel_kernel, (quarter, half, parts, updates)),
+        (bf16(4 * half, columns), bf16(4 * half, columns)),
+        [SMEM, SMEM, ANY, ANY],
+        [
+            pltpu.VMEM((quarter, columns), BF),
+            pltpu.VMEM((updates, quarter), BF),
+            pltpu.VMEM((front, columns), BF),
+            pltpu.SemaphoreType.DMA((1 + parts,)),
+        ],
+        2 * updates * quarter * columns,
+        2 * updates * quarter,
+    )(live, parent_map, rhs, panel)
+    partner = leaf_swap(sent)
+
+    def summed(k):
+        rows = slice(k * half, (k + 1) * half)
+        return kept[rows].astype(F32) + partner[rows].astype(F32)
+
+    arrived = [row_swap(summed(k).astype(BF), k) for k in (3, 1, 2)]
+    incoming = summed(0)
+    for value in arrived:
+        incoming = incoming + value.astype(F32)
+    right_side = (rhs[quarter:].astype(F32) - incoming).astype(BF)
+    right_side = live_rows(right_side, root_first, 2).astype(BF)
+    right_other = leaf_swap(right_side)
+
+    send_x, send_y, keep_x, keep_y = call(
+        functools.partial(leaf_pivot_kernel, (quarter, half)),
+        (bf16(quarter, columns),) * 4,
+        [SMEM, ANY, ANY],
+        [
+            pltpu.VMEM((quarter, columns), BF),
+            pltpu.VMEM((4, quarter, quarter), BF),
+            pltpu.SemaphoreType.DMA((5,)),
+        ],
+        2 * front * quarter * columns,
+        2 * front * quarter,
+    )(live, rhs, pivot_inverse)
+    sum_x = keep_x.astype(F32) + row_swap(send_x, 1).astype(F32)
+    sum_y = keep_y.astype(F32) + row_swap(send_y, 2).astype(F32)
+    low = sum_x[:half] + row_swap(sum_x[half:].astype(BF), 2).astype(F32)
+    high = sum_y[:half] + row_swap(sum_y[half:].astype(BF), 1).astype(F32)
+    leaf_forward = live_rows(
+        jnp.concatenate([low, high], 0), row_pos * quarter, leaf_pos
+    ).astype(BF)
+
+    outs = call(
+        functools.partial(root_pivot_kernel, (quarter, half, front)),
+        (bf16(half, columns),) * 4,
+        [VMEM, VMEM, ANY],
+        [
+            pltpu.VMEM((quarter, columns), BF),
+            pltpu.VMEM((4, half, quarter), BF),
+            pltpu.SemaphoreType.DMA((4,)),
+        ],
+        front * quarter * columns,
+        front * quarter,
+    )(right_side, right_other, pivot_inverse)
+    root_forward = outs[0].astype(F32)
+    for k in (3, 1, 2):
+        root_forward = root_forward + row_swap(outs[k], k).astype(F32)
+    root_forward = live_rows(root_forward, root_first, 2).astype(BF)
+
+    root_rows = [root_forward] + [row_swap(root_forward, k) for k in (1, 2, 3)]
+    root_keep, root_send = call(
+        functools.partial(root_transposed_kernel, (quarter, half, front)),
+        (jax.ShapeDtypeStruct((half, columns), F32), bf16(half, columns)),
+        [VMEM, VMEM, VMEM, VMEM, ANY],
+        [
+            pltpu.VMEM((4 * half, columns), BF),
+            pltpu.VMEM((4 * half, quarter), BF),
+            pltpu.VMEM((quarter, columns), F32),
+            pltpu.SemaphoreType.DMA,
+        ],
+        front * quarter * columns,
+        front * quarter,
+    )(*root_rows, pivot_inverse)
+    root_value = root_keep + leaf_swap(root_send).astype(F32)
+    root_value = live_rows(root_value, root_first, 2).astype(BF)
+    mine = [root_value] + [row_swap(root_value, k) for k in (1, 2, 3)]
+    theirs = [leaf_swap(value) for value in mine]
+
+    from_x = row_swap(leaf_forward, 1)
+    from_y = row_swap(leaf_forward, 2)
+    third_low = row_swap(from_x[:half], 2)
+    third_high = row_swap(from_y[half:], 1)
+    total, forward = call(
+        functools.partial(leaf_transposed_kernel, (quarter, half)),
+        (jax.ShapeDtypeStruct((columns, quarter), F32), bf16(quarter + half, columns)),
+        [VMEM] * 6 + [ANY],
+        [
+            pltpu.VMEM((front, columns), BF),
+            pltpu.VMEM((front, quarter), BF),
+            pltpu.SemaphoreType.DMA,
+        ],
+        2 * front * quarter * columns,
+        2 * front * quarter,
+    )(leaf_forward, from_x, from_y, third_low, third_high, root_forward, pivot_inverse)
+
+    backward = call(
+        functools.partial(last_kernel, (quarter, half, updates)),
+        bf16(quarter + half, columns),
+        [SMEM, SMEM] + [VMEM] * 9 + [ANY],
+        [
+            pltpu.VMEM((front, columns), BF),
+            pltpu.VMEM((updates, columns), BF),
+            pltpu.VMEM((updates, quarter), BF),
+            pltpu.SemaphoreType.DMA,
+        ],
+        2 * updates * quarter * columns,
+        2 * updates * quarter,
+    )(live, parent_map, *mine, *theirs, total, panel)
+    return forward, backward
+
+
+def on_device(rhs, pivot_inverse, panel, live, parent_map):
+    if lax.axis_size("leaf") == 2 and lax.axis_size("row") == 4:
+        return two_levels(rhs, pivot_inverse, panel, live, parent_map)
+    return deep_tree(rhs, pivot_inverse, panel, live, parent_map)
+
+
 def solution(mesh):
     in_specs = (P(("leaf", "row"), "col"), P("leaf", "row"), P("leaf", "row"), P(), P())
     out_specs = (P(("leaf", "row"), "col"), P(("leaf", "row"), "col"))

time: 133 us -> 67.6 us (0.51)
  blocking collectives: 64 us -> 0 us
  starting transfers between devices: 0.43 us -> 23.4 us
  Pallas kernels: 0 us -> 13.7 us
  between operations: 15.7 us -> 2.17 us
  matrix products: 12.5 us -> 0 us
  waiting for transfers between devices: 29.5 us -> 17.5 us
  local copies, waits for them, and re-layouts: 9.9 us -> 7.02 us
  other arithmetic: 0.68 us -> 3.48 us
    psum x1 -> x0, blocking collectives: 35.4 us -> none  [on_device(): lax.psum(jnp.dot(off_block, quarter_rows, preferred_element_type=jnp.floa...]
    all_gather x3 -> x0, blocking collectives: 28.5 us -> none  [the longest x1 11 us: on_device(): lax.all_gather(own_piece, 'row', axis=0, tiled=True)]
    unnamed x4 -> x0, waiting for transfers between devices: 26.2 us -> none
    ppermute x4 -> x27, starting transfers between devices: 0.35 us -> 23.4 us  [the longest x20 22.7 us: row_swap(): return lax.ppermute(value, 'row', [(r, r ^ apart) for r in range(count)])]
    ppermute x4 -> x27, waiting for transfers between devices: 3.3 us -> 17.5 us  [the longest x20 16.3 us: row_swap(): return lax.ppermute(value, 'row', [(r, r ^ apart) for r in range(count)])]
    pallas_call x0 -> x6, Pallas kernels: none -> 13.7 us  [the longest x1 3.67 us: two_levels(): call(functools.partial(panel_kernel, (quarter, half, parts, updates)), (b...]
    dot_general x9 -> x0, matrix products: 12.5 us -> none  [the longest x2 5.11 us: pivot_sum(): jnp.dot(diag_block, quarter_rows, preferred_element_type=jnp.float32)]
    slice x6 -> x4, local copies, waits for them, and re-layouts: 1.56 us -> 0.03 us  [the longest x1 0.01 us: two_levels(): low = sum_x[:half] + row_swap(sum_x[half:].astype(BF), 2).astype(F32)]
  transfers between devices with their start and end apart: 6 -> 27, of which waited for: 5 -> 15; matrix products, arithmetic and copies ran while one was open for 7% -> 6% of each run, Pallas kernels for 0% -> 12%
where the time goes in v1:
time: 67.6 us; the launch traced here: 67.3 us
  starting transfers between devices  23.4 us (35%)
  waiting for transfers between devices  17.5 us (26%)
  Pallas kernels  13.7 us (20%)
  local copies, waits for them, and re-layouts  7.02 us (10%)
  other arithmetic  3.48 us (5%)
  between operations  2.17 us (3%)
    ppermute x20, starting transfers between devices, row_swap(): return lax.ppermute(value, 'row', [(r, r ^ apart) for r in range(count)])  22.7 us
    ppermute x20, waiting for transfers between devices, row_swap(): return lax.ppermute(value, 'row', [(r, r ^ apart) for r in range(count)])  16.3 us
    unnamed x14, local copies, waits for them, and re-layouts  6.39 us
    pallas_call x1, Pallas kernels, two_levels(): call(functools.partial(panel_kernel, (quarter, half, parts, updates)), (b...  3.67 us
    pallas_call x1, Pallas kernels, two_levels(): call(functools.partial(leaf_pivot_kernel, (quarter, half)), (bf16(quarter...  3.22 us
    pallas_call x1, Pallas kernels, two_levels(): call(functools.partial(last_kernel, (quarter, half, updates)), bf16(quart...  2.34 us
    pallas_call x1, Pallas kernels, two_levels(): call(functools.partial(root_pivot_kernel, (quarter, half, front)), (bf16(...  2.18 us
    pallas_call x1, Pallas kernels, two_levels(): call(functools.partial(leaf_transposed_kernel, (quarter, half)), (jax.Sha...  1.37 us
  transfers between devices with their start and end apart: 27, of which 15 were waited for; matrix products, arithmetic and copies ran while one was open for 6% of the time, Pallas kernels for 12%

profile of v1, /device:TPU:0, one launch (start us, length us, event | category | flops | bytes accessed | tf_op | source)
XLA Modules:
  0.0 67.3 jit_solution(2788960841275565205)
XLA Ops:
  0.6 2.4 %copy-done = bf16[3840,640]{1,0:T(8,128)(2,1)S(1)} copy-done((bf16[3840,640]{1,0:T(8,128)(2,1)S(1)}, bf16[3840,640]{1,0:T(8,128)(2,1)}, u32[]{:S(2)}) %copy-start) | copy-done | bytes 4915224
  3.0 0.9 %copy-done.3 = bf16[960,128]{1,0:T(8,128)(2,1)S(1)} copy-done((bf16[960,128]{1,0:T(8,128)(2,1)S(1)}, bf16[960,128]{1,0:T(8,128)(2,1)}, u32[]{:S(2)}) %copy-start.3) | copy-done | bytes 245784
  4.6 3.2 %shard_map.68 = (bf16[640,128]{1,0:T(8,128)(2,1)S(1)}, bf16[640,128]{1,0:T(8,128)(2,1)S(1)}, bf16[640,128]{1,0:T(8,128)(2,1)S(1)}, bf16[640,128]{1,0:T(8,128)(2,1)S(1)}) custom-call(s32[3]{0:T(128)S(1)} %copy-done.4, bf16[960,128]{1,0:T(8,128)(2,1)S(1)} %copy-done.3, bf16[3840,640]{1,0:T(8,128)(2,1)S(1)} %copy-done), custom_call_target="tpu_custom_call" | custom-call | flops 419430400 | bytes 3276800 | tf_op jit(solution)/shard_map/pallas_call | solution.py:426
  7.9 3.0 %collective-permute-start = (bf16[640,128]{1,0:T(8,128)(2,1)S(1)}, bf16[640,128]{1,0:T(8,128)(2,1)}, u32[]{:S(2)}, u32[]{:S(2)}) collective-permute-start(bf16[640,128]{1,0:T(8,128)(2,1)S(1)} %get-tuple-element.17), channel_id=1, source_target_pairs={{0,4},{4,0},{8,12},{12,8},{1,5},{5,1},{9,13},{13,9},{2,6},{6,2},{1... | collective-permute-start | bytes 491528 | tf_op jit(solution)/shard_map/ppermute | solution.py:375
  10.9 1.5 %collective-permute-start.2 = (bf16[640,128]{1,0:T(8,128)(2,1)S(1)}, bf16[640,128]{1,0:T(8,128)(2,1)S(1)}, u32[]{:S(2)}, u32[]{:S(2)}) collective-permute-start(bf16[640,128]{1,0:T(8,128)(2,1)S(1)} %get-tuple-element.19), channel_id=1, source_target_pairs={{0,8},{4,12},{8,0},{12,4},{1,9},{5,13},{9,1},{13,5},{2,10},{6,14},... | collective-permute-start | bytes 491528 | tf_op jit(solution)/shard_map/ppermute | solution.py:375
  12.4 3.7 %shard_map.69 = (bf16[1280,128]{1,0:T(8,128)(2,1)S(1)}, bf16[1280,128]{1,0:T(8,128)(2,1)S(1)}) custom-call(s32[3]{0:T(128)S(1)} %copy-done.4, s32[2,12]{1,0:T(2,128)S(1)} %copy-done.6, bf16[960,128]{1,0:T(8,128)(2,1)S(1)} %copy-done.3, bf16[1536,640]{1,0:T(8,128)(2,1)S(1)} %copy-done.2), custom_call_target="tpu_custom_call" | custom-call | flops 251658240 | bytes 1966080 | tf_op jit(solution)/shard_map/pallas_call | solution.py:399
  18.1 1.0 %convert_add_fusion.1 = f32[640,128]{1,0:T(8,128)S(1)} fusion(bf16[640,128]{1,0:T(8,128)(2,1)} %collective-permute-done, bf16[640,128]{1,0:T(8,128)(2,1)S(1)} %get-tuple-element.16), kind=kLoop, calls=%fused_computation.3 | loop fusion | flops 245760 | bytes 655360 | tf_op jit(solution)/shard_map/add | solution.py:438
  19.6 1.0 %add_convert_fusion.2 = (bf16[320,128]{1,0:T(8,128)(2,1)S(1)}, bf16[320,128]{1,0:T(8,128)(2,1)S(1)}, bf16[320,128]{1,0:T(8,128)(2,1)S(1)}) fusion(bf16[1280,128]{1,0:T(8,128)(2,1)} %collective-permute-done.8, bf16[1280,128]{1,0:T(8,128)(2,1)S(1)} %get-tuple-element.20), kind=kLoop, calls=%fused_computation.13 | loop fusion | flops 491520 | bytes 737280 | tf_op jit(solution)/shard_map/convert_element_type | solution.py:418
  20.7 1.6 %collective-permute-start.9 = (bf16[320,128]{1,0:T(8,128)(2,1)S(1)}, bf16[320,128]{1,0:T(8,128)(2,1)S(1)}, u32[]{:S(2)}, u32[]{:S(2)}) collective-permute-start(bf16[320,128]{1,0:T(8,128)(2,1)S(1)} %get-tuple-element.30), channel_id=1, source_target_pairs={{0,12},{4,8},{8,4},{12,0},{1,13},{5,9},{9,5},{13,1},{2,14},{6,10},... | collective-permute-start | bytes 245768 | tf_op jit(solution)/shard_map/ppermute | solution.py:375
  22.3 1.9 %collective-permute-start.10 = (bf16[320,128]{1,0:T(8,128)(2,1)S(1)}, bf16[320,128]{1,0:T(8,128)(2,1)S(1)}, u32[]{:S(2)}, u32[]{:S(2)}) collective-permute-start(bf16[320,128]{1,0:T(8,128)(2,1)S(1)} %get-tuple-element.32), channel_id=1, source_target_pairs={{0,4},{4,0},{8,12},{12,8},{1,5},{5,1},{9,13},{13,9},{2,6},{6,2},{1... | collective-permute-start | bytes 245768 | tf_op jit(solution)/shard_map/ppermute | solution.py:375
  24.5 2.0 %collective-permute-done.9 = bf16[320,128]{1,0:T(8,128)(2,1)S(1)} collective-permute-done((bf16[320,128]{1,0:T(8,128)(2,1)S(1)}, bf16[320,128]{1,0:T(8,128)(2,1)S(1)}, u32[]{:S(2)}, u32[]{:S(2)}) %collective-permute-start.9) | collective-permute-done | bytes 81952 | tf_op jit(solution)/shard_map/ppermute | solution.py:375
  26.5 1.5 %collective-permute-done.11 = bf16[320,128]{1,0:T(8,128)(2,1)S(1)} collective-permute-done((bf16[320,128]{1,0:T(8,128)(2,1)S(1)}, bf16[320,128]{1,0:T(8,128)(2,1)S(1)}, u32[]{:S(2)}, u32[]{:S(2)}) %collective-permute-start.11) | collective-permute-done | bytes 81952 | tf_op jit(solution)/shard_map/ppermute | solution.py:375
  28.8 1.0 %fusion.1.own = bf16[320,128]{1,0:T(8,128)(2,1)S(1)} fusion(bf16[320,128]{1,0:T(8,128)(2,1)S(1)} %collective-permute-done.11, bf16[320,128]{1,0:T(8,128)(2,1)S(1)} %collective-permute-done.10, bf16[320,128]{1,0:T(8,128)(2,1)S(1)} %collective-permute-done.9, bf16[1280,128]{1,0:T(8,128)(2,1)} %collective-permute-done.8, ...), kind=kLoop, calls=%fused_computation.14 | loop fusion | flops 532480 | bytes 573760 | tf_op jit(solution)/shard_map/jit(_where)/select_n | solution.py:394
  29.9 1.2 %collective-permute-done.12.other = bf16[320,128]{1,0:T(8,128)(2,1)S(1)} collective-permute-done((bf16[320,128]{1,0:T(8,128)(2,1)S(1)}, bf16[320,128]{1,0:T(8,128)(2,1)S(1)}, u32[]{:S(2)}, u32[]{:S(2)}) %collective-permute-start.12) | collective-permute-done | bytes 81952 | tf_op jit(solution)/shard_map/ppermute | solution.py:379
  31.2 2.4 %copy-done.1 = bf16[3840,640]{1,0:T(8,128)(2,1)S(1)} copy-done((bf16[3840,640]{1,0:T(8,128)(2,1)S(1)}, bf16[3840,640]{1,0:T(8,128)(2,1)}, u32[]{:S(2)}) %copy-start.1) | copy-done | bytes 4915224
  33.6 2.2 %shard_map.70 = (bf16[320,128]{1,0:T(8,128)(2,1)S(1)}, bf16[320,128]{1,0:T(8,128)(2,1)S(1)}, bf16[320,128]{1,0:T(8,128)(2,1)S(1)}, bf16[320,128]{1,0:T(8,128)(2,1)S(1)}) custom-call(bf16[320,128]{1,0:T(8,128)(2,1)S(1)} %fusion.1.own, bf16[320,128]{1,0:T(8,128)(2,1)S(1)} %collective-permute-done.12.other, bf16[3840,640]{1,0:T(8,128)(2,1)S(1)} %copy-done.1), custom_call_target="tpu_custom_call" | custom-call | flops 209715200 | bytes 1638400 | tf_op jit(solution)/shard_map/pallas_call | solution.py:446
  35.8 1.3 %collective-permute-start.13 = (bf16[320,128]{1,0:T(8,128)(2,1)S(1)}, bf16[320,128]{1,0:T(8,128)(2,1)S(1)}, u32[]{:S(2)}, u32[]{:S(2)}) collective-permute-start(bf16[320,128]{1,0:T(8,128)(2,1)S(1)} %get-tuple-element.23), channel_id=1, source_target_pairs={{0,12},{4,8},{8,4},{12,0},{1,13},{5,9},{9,5},{13,1},{2,14},{6,10},... | collective-permute-start | bytes 245768 | tf_op jit(solution)/shard_map/ppermute | solution.py:375
  37.1 1.0 %collective-permute-start.14 = (bf16[320,128]{1,0:T(8,128)(2,1)S(1)}, bf16[320,128]{1,0:T(8,128)(2,1)S(1)}, u32[]{:S(2)}, u32[]{:S(2)}) collective-permute-start(bf16[320,128]{1,0:T(8,128)(2,1)S(1)} %get-tuple-element.24), channel_id=1, source_target_pairs={{0,4},{4,0},{8,12},{12,8},{1,5},{5,1},{9,13},{13,9},{2,6},{6,2},{1... | collective-permute-start | bytes 245768 | tf_op jit(solution)/shard_map/ppermute | solution.py:375
  38.1 1.2 %collective-permute-start.15 = (bf16[320,128]{1,0:T(8,128)(2,1)S(1)}, bf16[320,128]{1,0:T(8,128)(2,1)S(1)}, u32[]{:S(2)}, u32[]{:S(2)}) collective-permute-start(bf16[320,128]{1,0:T(8,128)(2,1)S(1)} %get-tuple-element.25), channel_id=1, source_target_pairs={{0,8},{4,12},{8,0},{12,4},{1,9},{5,13},{9,1},{13,5},{2,10},{6,14},... | collective-permute-start | bytes 245768 | tf_op jit(solution)/shard_map/ppermute | solution.py:375
  39.3 2.7 %collective-permute-done.13 = bf16[320,128]{1,0:T(8,128)(2,1)S(1)} collective-permute-done((bf16[320,128]{1,0:T(8,128)(2,1)S(1)}, bf16[320,128]{1,0:T(8,128)(2,1)S(1)}, u32[]{:S(2)}, u32[]{:S(2)}) %collective-permute-start.13) | collective-permute-done | bytes 81952 | tf_op jit(solution)/shard_map/ppermute | solution.py:375
  43.1 1.3 %collective-permute-start.18 = (bf16[320,128]{1,0:T(8,128)(2,1)S(1)}, bf16[320,128]{1,0:T(8,128)(2,1)S(1)}, u32[]{:S(2)}, u32[]{:S(2)}) collective-permute-start(bf16[320,128]{1,0:T(8,128)(2,1)S(1)} %select_convert_fusion.1.root_piece.y0), channel_id=1, source_target_pairs={{0,12},{4,8},{8,4},{12,0},{1,13},{5,9},{9,5},{13,1},{2,14},{6,10},... | collective-permute-start | bytes 245768 | tf_op jit(solution)/shard_map/ppermute | solution.py:375
  45.3 1.4 %collective-permute-start.16 = (bf16[320,128]{1,0:T(8,128)(2,1)S(1)}, bf16[320,128]{1,0:T(8,128)(2,1)S(1)}, u32[]{:S(2)}, u32[]{:S(2)}) collective-permute-start(bf16[320,128]{1,0:T(8,128)(2,1)S(1)} %select_convert_fusion.1.root_piece.y0), channel_id=1, source_target_pairs={{0,4},{4,0},{8,12},{12,8},{1,5},{5,1},{9,13},{13,9},{2,6},{6,2},{1... | collective-permute-start | bytes 245768 | tf_op jit(solution)/shard_map/ppermute | solution.py:375
  46.8 1.0 %collective-permute-start.5 = (bf16[640,128]{1,0:T(8,128)(2,1)S(1)}, bf16[640,128]{1,0:T(8,128)(2,1)S(1)}, u32[]{:S(2)}, u32[]{:S(2)}) collective-permute-start(bf16[640,128]{1,0:T(8,128)(2,1)S(1)} %fusion.f0), channel_id=1, source_target_pairs={{0,8},{4,12},{8,0},{12,4},{1,9},{5,13},{9,1},{13,5},{2,10},{6,14},... | collective-permute-start | bytes 491528 | tf_op jit(solution)/shard_map/ppermute | solution.py:375
  47.8 1.4 %collective-permute-done.18.y3 = bf16[320,128]{1,0:T(8,128)(2,1)S(1)} collective-permute-done((bf16[320,128]{1,0:T(8,128)(2,1)S(1)}, bf16[320,128]{1,0:T(8,128)(2,1)S(1)}, u32[]{:S(2)}, u32[]{:S(2)}) %collective-permute-start.18) | collective-permute-done | bytes 81952 | tf_op jit(solution)/shard_map/ppermute | solution.py:375
  49.2 1.3 %collective-permute-done.17.y2 = bf16[320,128]{1,0:T(8,128)(2,1)S(1)} collective-permute-done((bf16[320,128]{1,0:T(8,128)(2,1)S(1)}, bf16[320,128]{1,0:T(8,128)(2,1)S(1)}, u32[]{:S(2)}, u32[]{:S(2)}) %collective-permute-start.17) | collective-permute-done | bytes 81952 | tf_op jit(solution)/shard_map/ppermute | solution.py:375
  53.8 1.7 %collective-permute-start.22 = (bf16[320,128]{1,0:T(8,128)(2,1)S(1)}, bf16[320,128]{1,0:T(8,128)(2,1)S(1)}, u32[]{:S(2)}, u32[]{:S(2)}) collective-permute-start(bf16[320,128]{1,0:T(8,128)(2,1)S(1)} %select_convert_fusion.s0), channel_id=1, source_target_pairs={{0,12},{4,8},{8,4},{12,0},{1,13},{5,9},{9,5},{13,1},{2,14},{6,10},... | collective-permute-start | bytes 245768 | tf_op jit(solution)/shard_map/ppermute | solution.py:375
  55.6 1.2 %collective-permute-start.21 = (bf16[320,128]{1,0:T(8,128)(2,1)S(1)}, bf16[320,128]{1,0:T(8,128)(2,1)S(1)}, u32[]{:S(2)}, u32[]{:S(2)}) collective-permute-start(bf16[320,128]{1,0:T(8,128)(2,1)S(1)} %select_convert_fusion.s0), channel_id=1, source_target_pairs={{0,8},{4,12},{8,0},{12,4},{1,9},{5,13},{9,1},{13,5},{2,10},{6,14},... | collective-permute-start | bytes 245768 | tf_op jit(solution)/shard_map/ppermute | solution.py:375
  57.4 1.2 %collective-permute-done.4.f1 = bf16[640,128]{1,0:T(8,128)(2,1)S(1)} collective-permute-done((bf16[640,128]{1,0:T(8,128)(2,1)S(1)}, bf16[640,128]{1,0:T(8,128)(2,1)S(1)}, u32[]{:S(2)}, u32[]{:S(2)}) %collective-permute-start.4) | collective-permute-done | bytes 163872 | tf_op jit(solution)/shard_map/ppermute | solution.py:375
  59.4 1.0 %collective-permute-done.7.f3b = bf16[320,128]{1,0:T(8,128)(2,1)S(1)} collective-permute-done((bf16[320,128]{1,0:T(8,128)(2,1)S(1)}, bf16[320,128]{1,0:T(8,128)(2,1)S(1)}, u32[]{:S(2)}, u32[]{:S(2)}) %collective-permute-start.7) | collective-permute-done | bytes 81952 | tf_op jit(solution)/shard_map/ppermute | solution.py:375
  60.3 2.0 %collective-permute-done.22.s3 = bf16[320,128]{1,0:T(8,128)(2,1)S(1)} collective-permute-done((bf16[320,128]{1,0:T(8,128)(2,1)S(1)}, bf16[320,128]{1,0:T(8,128)(2,1)S(1)}, u32[]{:S(2)}, u32[]{:S(2)}) %collective-permute-start.22) | collective-permute-done | bytes 81952 | tf_op jit(solution)/shard_map/ppermute | solution.py:375
  63.5 1.4 %shard_map.71 = (f32[128,640]{1,0:T(8,128)S(1)}, bf16[960,128]{1,0:T(8,128)(2,1)}) custom-call(bf16[640,128]{1,0:T(8,128)(2,1)S(1)} %fusion.f0, bf16[640,128]{1,0:T(8,128)(2,1)S(1)} %collective-permute-done.4.f1, bf16[640,128]{1,0:T(8,128)(2,1)S(1)} %collective-permute-done.5.f2, bf16[320,128]{1,0:T(8,128)(2,1)S(1)} %collective-permute-done.6.f3a, ...), custom_call_target="tpu_custom_call" | custom-call | flops 419430400 | bytes 3276800 | tf_op jit(solution)/shard_map/pallas_call | solution.py:486
  65.0 2.3 %shard_map.73 = bf16[960,128]{1,0:T(8,128)(2,1)} custom-call(s32[3]{0:T(128)S(1)} %copy-done.5, s32[2,12]{1,0:T(2,128)S(1)} %copy-done.6, bf16[320,128]{1,0:T(8,128)(2,1)S(1)} %select_convert_fusion.s0, bf16[320,128]{1,0:T(8,128)(2,1)S(1)} %collective-permute-done.20.s1, bf16[320,128]{1,0:T(8,128)(2,1)S(1)} %collective-permute-done.21.s2, ...), custom_call_target="tpu_custom_call" | custom-call | flops 251658240 | bytes 1966080 | tf_op jit(solution)/shard_map/pallas_call | solution.py:499
  (58 shorter events, 11.3 us)
Async XLA Ops:
  0.6 2.4 %copy-start = (bf16[3840,640]{1,0:T(8,128)(2,1)S(1)}, bf16[3840,640]{1,0:T(8,128)(2,1)}, u32[]{:S(2)}) copy-start(bf16[3840,640]{1,0:T(8,128)(2,1)} %pivot.7) | copy-start | bytes 14745604
  4.6 7.8 %copy-start.2 = (bf16[1536,640]{1,0:T(8,128)(2,1)S(1)}, bf16[1536,640]{1,0:T(8,128)(2,1)}, u32[]{:S(2)}) copy-start(bf16[1536,640]{1,0:T(8,128)(2,1)} %panel.3) | copy-start | bytes 5898244
  4.6 7.8 %copy-start.6 = (s32[2,12]{1,0:T(2,128)S(1)}, s32[2,12]{1,0:T(2,128)}, u32[]{:S(2)}) copy-start(s32[2,12]{1,0:T(2,128)} %pmap.3) | copy-start | bytes 292
  4.6 11.5 %copy-start.5 = (s32[3]{0:T(128)S(1)}, s32[3]{0:T(128)}, u32[]{:S(2)}) copy-start(s32[3]{0:T(128)} %live.5) | copy-start | bytes 40
  7.9 10.2 %collective-permute-start = (bf16[640,128]{1,0:T(8,128)(2,1)S(1)}, bf16[640,128]{1,0:T(8,128)(2,1)}, u32[]{:S(2)}, u32[]{:S(2)}) collective-permute-start(bf16[640,128]{1,0:T(8,128)(2,1)S(1)} %get-tuple-element.17), channel_id=1, source_target_pairs={{0,4},{4,0},{8,12},{12,8},{1,5},{5,1},{9,13},{13,9},{2,6},{6,2},{1... | collective-permute-start | bytes 491528 | tf_op jit(solution)/shard_map/ppermute | solution.py:375
  10.9 13.4 %collective-permute-start.2 = (bf16[640,128]{1,0:T(8,128)(2,1)S(1)}, bf16[640,128]{1,0:T(8,128)(2,1)S(1)}, u32[]{:S(2)}, u32[]{:S(2)}) collective-permute-start(bf16[640,128]{1,0:T(8,128)(2,1)S(1)} %get-tuple-element.19), channel_id=1, source_target_pairs={{0,8},{4,12},{8,0},{12,4},{1,9},{5,13},{9,1},{13,5},{2,10},{6,14},... | collective-permute-start | bytes 491528 | tf_op jit(solution)/shard_map/ppermute | solution.py:375
  16.1 3.6 %collective-permute-start.8 = (bf16[1280,128]{1,0:T(8,128)(2,1)S(1)}, bf16[1280,128]{1,0:T(8,128)(2,1)}, u32[]{:S(2)}, u32[]{:S(2)}) collective-permute-start(bf16[1280,128]{1,0:T(8,128)(2,1)S(1)} %get-tuple-element.21), channel_id=1, source_target_pairs={{0,16},{16,0},{1,17},{17,1},{2,18},{18,2},{3,19},{19,3},{4,20},{20... | collective-permute-start | bytes 983048 | tf_op jit(solution)/shard_map/ppermute | solution.py:379
  19.1 10.8 %collective-permute-start.1 = (bf16[320,128]{1,0:T(8,128)(2,1)S(1)}, bf16[320,128]{1,0:T(8,128)(2,1)S(1)}, u32[]{:S(2)}, u32[]{:S(2)}) collective-permute-start(bf16[320,128]{1,0:T(8,128)(2,1)S(1)} %slice.87), channel_id=1, source_target_pairs={{0,8},{4,12},{8,0},{12,4},{1,9},{5,13},{9,1},{13,5},{2,10},{6,14},... | collective-permute-start | bytes 245768 | tf_op jit(solution)/shard_map/ppermute | solution.py:375
  20.7 5.8 %collective-permute-start.9 = (bf16[320,128]{1,0:T(8,128)(2,1)S(1)}, bf16[320,128]{1,0:T(8,128)(2,1)S(1)}, u32[]{:S(2)}, u32[]{:S(2)}) collective-permute-start(bf16[320,128]{1,0:T(8,128)(2,1)S(1)} %get-tuple-element.30), channel_id=1, source_target_pairs={{0,12},{4,8},{8,4},{12,0},{1,13},{5,9},{9,5},{13,1},{2,14},{6,10},... | collective-permute-start | bytes 245768 | tf_op jit(solution)/shard_map/ppermute | solution.py:375
  22.2 5.7 %collective-permute-start.11 = (bf16[320,128]{1,0:T(8,128)(2,1)S(1)}, bf16[320,128]{1,0:T(8,128)(2,1)S(1)}, u32[]{:S(2)}, u32[]{:S(2)}) collective-permute-start(bf16[320,128]{1,0:T(8,128)(2,1)S(1)} %get-tuple-element.31), channel_id=1, source_target_pairs={{0,8},{4,12},{8,0},{12,4},{1,9},{5,13},{9,1},{13,5},{2,10},{6,14},... | collective-permute-start | bytes 245768 | tf_op jit(solution)/shard_map/ppermute | solution.py:375
  22.3 6.4 %collective-permute-start.10 = (bf16[320,128]{1,0:T(8,128)(2,1)S(1)}, bf16[320,128]{1,0:T(8,128)(2,1)S(1)}, u32[]{:S(2)}, u32[]{:S(2)}) collective-permute-start(bf16[320,128]{1,0:T(8,128)(2,1)S(1)} %get-tuple-element.32), channel_id=1, source_target_pairs={{0,4},{4,0},{8,12},{12,8},{1,5},{5,1},{9,13},{13,9},{2,6},{6,2},{1... | collective-permute-start | bytes 245768 | tf_op jit(solution)/shard_map/ppermute | solution.py:375
  24.3 15.0 %collective-permute-start.3 = (bf16[320,128]{1,0:T(8,128)(2,1)S(1)}, bf16[320,128]{1,0:T(8,128)(2,1)S(1)}, u32[]{:S(2)}, u32[]{:S(2)}) collective-permute-start(bf16[320,128]{1,0:T(8,128)(2,1)S(1)} %slice.86), channel_id=1, source_target_pairs={{0,4},{4,0},{8,12},{12,8},{1,5},{5,1},{9,13},{13,9},{2,6},{6,2},{1... | collective-permute-start | bytes 245768 | tf_op jit(solution)/shard_map/ppermute | solution.py:375
  29.8 1.3 %collective-permute-start.12 = (bf16[320,128]{1,0:T(8,128)(2,1)S(1)}, bf16[320,128]{1,0:T(8,128)(2,1)S(1)}, u32[]{:S(2)}, u32[]{:S(2)}) collective-permute-start(bf16[320,128]{1,0:T(8,128)(2,1)S(1)} %fusion.1.own), channel_id=1, source_target_pairs={{0,16},{16,0},{1,17},{17,1},{2,18},{18,2},{3,19},{19,3},{4,20},{20... | collective-permute-start | bytes 245768 | tf_op jit(solution)/shard_map/ppermute | solution.py:379
  31.2 2.4 %copy-start.1 = (bf16[3840,640]{1,0:T(8,128)(2,1)S(1)}, bf16[3840,640]{1,0:T(8,128)(2,1)}, u32[]{:S(2)}) copy-start(bf16[3840,640]{1,0:T(8,128)(2,1)} %pivot.7) | copy-start | bytes 14745604
  35.8 6.3 %collective-permute-start.13 = (bf16[320,128]{1,0:T(8,128)(2,1)S(1)}, bf16[320,128]{1,0:T(8,128)(2,1)S(1)}, u32[]{:S(2)}, u32[]{:S(2)}) collective-permute-start(bf16[320,128]{1,0:T(8,128)(2,1)S(1)} %get-tuple-element.23), channel_id=1, source_target_pairs={{0,12},{4,8},{8,4},{12,0},{1,13},{5,9},{9,5},{13,1},{2,14},{6,10},... | collective-permute-start | bytes 245768 | tf_op jit(solution)/shard_map/ppermute | solution.py:375
  37.1 5.2 %collective-permute-start.14 = (bf16[320,128]{1,0:T(8,128)(2,1)S(1)}, bf16[320,128]{1,0:T(8,128)(2,1)S(1)}, u32[]{:S(2)}, u32[]{:S(2)}) collective-permute-start(bf16[320,128]{1,0:T(8,128)(2,1)S(1)} %get-tuple-element.24), channel_id=1, source_target_pairs={{0,4},{4,0},{8,12},{12,8},{1,5},{5,1},{9,13},{13,9},{2,6},{6,2},{1... | collective-permute-start | bytes 245768 | tf_op jit(solution)/shard_map/ppermute | solution.py:375
  38.1 4.9 %collective-permute-start.15 = (bf16[320,128]{1,0:T(8,128)(2,1)S(1)}, bf16[320,128]{1,0:T(8,128)(2,1)S(1)}, u32[]{:S(2)}, u32[]{:S(2)}) collective-permute-start(bf16[320,128]{1,0:T(8,128)(2,1)S(1)} %get-tuple-element.25), channel_id=1, source_target_pairs={{0,8},{4,12},{8,0},{12,4},{1,9},{5,13},{9,1},{13,5},{2,10},{6,14},... | collective-permute-start | bytes 245768 | tf_op jit(solution)/shard_map/ppermute | solution.py:375
  43.1 6.1 %collective-permute-start.18 = (bf16[320,128]{1,0:T(8,128)(2,1)S(1)}, bf16[320,128]{1,0:T(8,128)(2,1)S(1)}, u32[]{:S(2)}, u32[]{:S(2)}) collective-permute-start(bf16[320,128]{1,0:T(8,128)(2,1)S(1)} %select_convert_fusion.1.root_piece.y0), channel_id=1, source_target_pairs={{0,12},{4,8},{8,4},{12,0},{1,13},{5,9},{9,5},{13,1},{2,14},{6,10},... | collective-permute-start | bytes 245768 | tf_op jit(solution)/shard_map/ppermute | solution.py:375
  44.4 6.1 %collective-permute-start.17 = (bf16[320,128]{1,0:T(8,128)(2,1)S(1)}, bf16[320,128]{1,0:T(8,128)(2,1)S(1)}, u32[]{:S(2)}, u32[]{:S(2)}) collective-permute-start(bf16[320,128]{1,0:T(8,128)(2,1)S(1)} %select_convert_fusion.1.root_piece.y0), channel_id=1, source_target_pairs={{0,8},{4,12},{8,0},{12,4},{1,9},{5,13},{9,1},{13,5},{2,10},{6,14},... | collective-permute-start | bytes 245768 | tf_op jit(solution)/shard_map/ppermute | solution.py:375
  45.3 5.2 %collective-permute-start.16 = (bf16[320,128]{1,0:T(8,128)(2,1)S(1)}, bf16[320,128]{1,0:T(8,128)(2,1)S(1)}, u32[]{:S(2)}, u32[]{:S(2)}) collective-permute-start(bf16[320,128]{1,0:T(8,128)(2,1)S(1)} %select_convert_fusion.1.root_piece.y0), channel_id=1, source_target_pairs={{0,4},{4,0},{8,12},{12,8},{1,5},{5,1},{9,13},{13,9},{2,6},{6,2},{1... | collective-permute-start | bytes 245768 | tf_op jit(solution)/shard_map/ppermute | solution.py:375
  46.8 6.3 %collective-permute-start.5 = (bf16[640,128]{1,0:T(8,128)(2,1)S(1)}, bf16[640,128]{1,0:T(8,128)(2,1)S(1)}, u32[]{:S(2)}, u32[]{:S(2)}) collective-permute-start(bf16[640,128]{1,0:T(8,128)(2,1)S(1)} %fusion.f0), channel_id=1, source_target_pairs={{0,8},{4,12},{8,0},{12,4},{1,9},{5,13},{9,1},{13,5},{2,10},{6,14},... | collective-permute-start | bytes 491528 | tf_op jit(solution)/shard_map/ppermute | solution.py:375
  51.4 2.3 %collective-permute-start.19 = (bf16[320,128]{1,0:T(8,128)(2,1)S(1)}, bf16[320,128]{1,0:T(8,128)(2,1)S(1)}, u32[]{:S(2)}, u32[]{:S(2)}) collective-permute-start(bf16[320,128]{1,0:T(8,128)(2,1)S(1)} %get-tuple-element.28), channel_id=1, source_target_pairs={{0,16},{16,0},{1,17},{17,1},{2,18},{18,2},{3,19},{19,3},{4,20},{20... | collective-permute-start | bytes 245768 | tf_op jit(solution)/shard_map/ppermute | solution.py:379
  51.5 7.1 %collective-permute-start.4 = (bf16[640,128]{1,0:T(8,128)(2,1)S(1)}, bf16[640,128]{1,0:T(8,128)(2,1)S(1)}, u32[]{:S(2)}, u32[]{:S(2)}) collective-permute-start(bf16[640,128]{1,0:T(8,128)(2,1)S(1)} %fusion.f0), channel_id=1, source_target_pairs={{0,4},{4,0},{8,12},{12,8},{1,5},{5,1},{9,13},{13,9},{2,6},{6,2},{1... | collective-permute-start | bytes 491528 | tf_op jit(solution)/shard_map/ppermute | solution.py:375
  53.2 7.2 %collective-permute-start.7 = (bf16[320,128]{1,0:T(8,128)(2,1)S(1)}, bf16[320,128]{1,0:T(8,128)(2,1)S(1)}, u32[]{:S(2)}, u32[]{:S(2)}) collective-permute-start(bf16[320,128]{1,0:T(8,128)(2,1)S(1)} %slice.68), channel_id=1, source_target_pairs={{0,4},{4,0},{8,12},{12,8},{1,5},{5,1},{9,13},{13,9},{2,6},{6,2},{1... | collective-permute-start | bytes 245768 | tf_op jit(solution)/shard_map/ppermute | solution.py:375
  53.8 8.5 %collective-permute-start.22 = (bf16[320,128]{1,0:T(8,128)(2,1)S(1)}, bf16[320,128]{1,0:T(8,128)(2,1)S(1)}, u32[]{:S(2)}, u32[]{:S(2)}) collective-permute-start(bf16[320,128]{1,0:T(8,128)(2,1)S(1)} %select_convert_fusion.s0), channel_id=1, source_target_pairs={{0,12},{4,8},{8,4},{12,0},{1,13},{5,9},{9,5},{13,1},{2,14},{6,10},... | collective-permute-start | bytes 245768 | tf_op jit(solution)/shard_map/ppermute | solution.py:375
  55.6 6.7 %collective-permute-start.21 = (bf16[320,128]{1,0:T(8,128)(2,1)S(1)}, bf16[320,128]{1,0:T(8,128)(2,1)S(1)}, u32[]{:S(2)}, u32[]{:S(2)}) collective-permute-start(bf16[320,128]{1,0:T(8,128)(2,1)S(1)} %select_convert_fusion.s0), channel_id=1, source_target_pairs={{0,8},{4,12},{8,0},{12,4},{1,9},{5,13},{9,1},{13,5},{2,10},{6,14},... | collective-permute-start | bytes 245768 | tf_op jit(solution)/shard_map/ppermute | solution.py:375
  56.8 6.6 %collective-permute-start.20 = (bf16[320,128]{1,0:T(8,128)(2,1)S(1)}, bf16[320,128]{1,0:T(8,128)(2,1)S(1)}, u32[]{:S(2)}, u32[]{:S(2)}) collective-permute-start(bf16[320,128]{1,0:T(8,128)(2,1)S(1)} %select_convert_fusion.s0), channel_id=1, source_target_pairs={{0,4},{4,0},{8,12},{12,8},{1,5},{5,1},{9,13},{13,9},{2,6},{6,2},{1... | collective-permute-start | bytes 245768 | tf_op jit(solution)/shard_map/ppermute | solution.py:375
  58.6 4.9 %collective-permute-start.6 = (bf16[320,128]{1,0:T(8,128)(2,1)S(1)}, bf16[320,128]{1,0:T(8,128)(2,1)S(1)}, u32[]{:S(2)}, u32[]{:S(2)}) collective-permute-start(bf16[320,128]{1,0:T(8,128)(2,1)S(1)} %slice.67), channel_id=1, source_target_pairs={{0,8},{4,12},{8,0},{12,4},{1,9},{5,13},{9,1},{13,5},{2,10},{6,14},... | collective-permute-start | bytes 245768 | tf_op jit(solution)/shard_map/ppermute | solution.py:375
  60.3 4.6 %collective-permute-start.23 = (bf16[320,128]{1,0:T(8,128)(2,1)S(1)}, bf16[320,128]{1,0:T(8,128)(2,1)S(1)}, u32[]{:S(2)}, u32[]{:S(2)}) collective-permute-start(bf16[320,128]{1,0:T(8,128)(2,1)S(1)} %select_convert_fusion.s0), channel_id=1, source_target_pairs={{0,16},{16,0},{1,17},{17,1},{2,18},{18,2},{3,19},{19,3},{4,20},{20... | collective-permute-start | bytes 245768 | tf_op jit(solution)/shard_map/ppermute | solution.py:379
  62.3 2.6 %collective-permute-start.26 = (bf16[320,128]{1,0:T(8,128)(2,1)S(1)}, bf16[320,128]{1,0:T(8,128)(2,1)S(1)}, u32[]{:S(2)}, u32[]{:S(2)}) collective-permute-start(bf16[320,128]{1,0:T(8,128)(2,1)S(1)} %collective-permute-done.22.s3), channel_id=1, source_target_pairs={{0,16},{16,0},{1,17},{17,1},{2,18},{18,2},{3,19},{19,3},{4,20},{20... | collective-permute-start | bytes 245768 | tf_op jit(solution)/shard_map/ppermute | solution.py:379
  62.3 2.6 %collective-permute-start.25 = (bf16[320,128]{1,0:T(8,128)(2,1)S(1)}, bf16[320,128]{1,0:T(8,128)(2,1)S(1)}, u32[]{:S(2)}, u32[]{:S(2)}) collective-permute-start(bf16[320,128]{1,0:T(8,128)(2,1)S(1)} %collective-permute-done.21.s2), channel_id=1, source_target_pairs={{0,16},{16,0},{1,17},{17,1},{2,18},{18,2},{3,19},{19,3},{4,20},{20... | collective-permute-start | bytes 245768 | tf_op jit(solution)/shard_map/ppermute | solution.py:379
  63.4 1.5 %collective-permute-start.24 = (bf16[320,128]{1,0:T(8,128)(2,1)S(1)}, bf16[320,128]{1,0:T(8,128)(2,1)S(1)}, u32[]{:S(2)}, u32[]{:S(2)}) collective-permute-start(bf16[320,128]{1,0:T(8,128)(2,1)S(1)} %collective-permute-done.20.s1), channel_id=1, source_target_pairs={{0,16},{16,0},{1,17},{17,1},{2,18},{18,2},{3,19},{19,3},{4,20},{20... | collective-permute-start | bytes 245768 | tf_op jit(solution)/shard_map/ppermute | solution.py:379
  (2 other events, 1.6 us)

commit v2 on v0

--- a/solution.py
+++ b/solution.py
@@ -1,6 +1,10 @@
+import functools
+
 import jax
 import jax.numpy as jnp
 from jax import lax
+from jax.experimental import pallas as pl
+from jax.experimental.pallas import tpu as pltpu
 from jax.sharding import PartitionSpec as P
 
 F = 2560
@@ -78,7 +82,7 @@
     return from_partner(values.astype(jnp.bfloat16), "leaf", bit_no).astype(values.dtype)
 
 
-def on_device(rhs, pivot_inverse, panel, live, parent_map):
+def deep_tree(rhs, pivot_inverse, panel, live, parent_map):
     leaves = lax.axis_size("leaf")
     row_count = lax.axis_size("row")
     tree_depth = leaves.bit_length() - 1
@@ -200,6 +204,253 @@
     return (jnp.concatenate(forward_parts, 0), jnp.concatenate(backward_parts, 0))
 
 
+B = 128
+VMEM = pl.BlockSpec(memory_space=pltpu.VMEM)
+SMEM = pl.BlockSpec(memory_space=pltpu.SMEM)
+ANY = pl.BlockSpec(memory_space=pl.ANY)
+BF = jnp.bfloat16
+F32 = jnp.float32
+MIB = 1024 * 1024
+
+
+def shaped(rows, columns, dtype=BF):
+    return jax.ShapeDtypeStruct((rows, columns), dtype)
+
+
+def kept(rows, columns, dtype=BF):
+    return pltpu.VMEM((rows, columns), dtype)
+
+
+def call(body, out_shape, in_specs, scratch, limit, flops, bytes_moved):
+    return pl.pallas_call(
+        body,
+        out_shape=out_shape,
+        in_specs=in_specs,
+        out_specs=jax.tree.map(lambda _: VMEM, out_shape, is_leaf=lambda s: hasattr(s, "shape")),
+        scratch_shapes=scratch,
+        compiler_params=pltpu.CompilerParams(vmem_limit_bytes=limit * MIB),
+        cost_estimate=pl.CostEstimate(flops=flops, bytes_accessed=bytes_moved, transcendentals=0),
+    )
+
+
+def masked_rows(value, first_row, live_blocks):
+    row = first_row + lax.broadcasted_iota(jnp.int32, value.shape, 0)
+    return jnp.where(row < live_blocks * B, value, jnp.zeros_like(value))
+
+
+def rows_at(start, size):
+    return pl.ds(pl.multiple_of(start, 16), size)
+
+
+def mm(left, right):
+    return jnp.dot(left, right, preferred_element_type=F32)
+
+
+def panel_kernel(sizes, live, pmap, rhs, panel, send, keep, w_v, b_v, c_v, sems):
+    quarter, half, parts, update_rows = sizes
+    leaf_pos = lax.axis_index("leaf")
+    row_pos = lax.axis_index("row")
+    get_b = pltpu.make_async_copy(rhs.at[pl.ds(0, quarter)], b_v, sems.at[0])
+    get_b.start()
+    step = update_rows // parts
+    copies = []
+    for i in range(parts):
+        rows = pl.ds(i * step, step)
+        copies.append(pltpu.make_async_copy(panel.at[rows], w_v.at[rows], sems.at[1 + i]))
+        copies[-1].start()
+    c_v[...] = jnp.zeros_like(c_v)
+    get_b.wait()
+    masked = masked_rows(b_v[...], row_pos * quarter, live[leaf_pos])
+    for i in range(parts):
+        copies[i].wait()
+        product = mm(w_v[pl.ds(i * step, step)], masked).astype(BF)
+        for e in range(step // B):
+            block = pmap[leaf_pos, i * (step // B) + e]
+            c_v[pl.ds(pl.multiple_of(block * B, B), B)] = product[e * B : (e + 1) * B]
+    for r in range(4):
+        base = r * quarter
+        keep[pl.ds(r * half, half)] = c_v[rows_at(base + leaf_pos * half, half)]
+        send[pl.ds(r * half, half)] = c_v[rows_at(base + (1 - leaf_pos) * half, half)]
+
+
+def leaf_pivot_kernel(sizes, live, rhs, pivot, after, partial, d_v, b_v, sems):
+    quarter, half = sizes
+    leaf_pos = lax.axis_index("leaf")
+    row_pos = lax.axis_index("row")
+    get_b = pltpu.make_async_copy(rhs.at[pl.ds(0, quarter)], b_v, sems.at[6])
+    get_b.start()
+    copies = []
+    for k in range(6):
+        rows = pl.ds(k * quarter, quarter)
+        copies.append(pltpu.make_async_copy(pivot.at[rows], d_v.at[rows], sems.at[k]))
+        copies[-1].start()
+    get_b.wait()
+    masked = masked_rows(b_v[...], row_pos * quarter, live[leaf_pos])
+    for k in range(4):
+        copies[k].wait()
+        rows = pl.ds(k * quarter, quarter)
+        partial[rows] = mm(d_v[rows], masked).astype(BF)
+    copies[4].wait()
+    copies[5].wait()
+
+
+def root_pivot_kernel(sizes, own, other, pivot, partial, q_v):
+    quarter, half, base = sizes
+    leaf_pos = lax.axis_index("leaf")
+    q_v[rows_at(leaf_pos * half, half)] = own[...]
+    q_v[rows_at((1 - leaf_pos) * half, half)] = other[...]
+    partial[...] = mm(pivot[pl.ds(base, 4 * half)], q_v[...]).astype(BF)
+
+
+def root_transposed_kernel(sizes, y, pivot, keep, send, s_v):
+    quarter, half, base = sizes
+    leaf_pos = lax.axis_index("leaf")
+    s_v[...] = mm(y[...].T, pivot[pl.ds(base, 4 * half)]).T
+    keep[...] = s_v[rows_at(leaf_pos * half, half)]
+    send[...] = s_v[rows_at((1 - leaf_pos) * half, half)].astype(BF)
+
+
+def leaf_transposed_kernel(sizes, y, own, root_piece, pivot, total, forward):
+    quarter, half = sizes
+    forward[pl.ds(0, quarter)] = own[...]
+    forward[pl.ds(quarter, half)] = root_piece[...]
+    total[...] = mm(y[...].T, pivot[pl.ds(0, 4 * quarter)])
+
+
+def last_kernel(sizes, live, pmap, mine, theirs, own, total, w_v, out, s_v, p_v):
+    quarter, half, update_rows = sizes
+    leaf_pos = lax.axis_index("leaf")
+    row_pos = lax.axis_index("row")
+    for r in range(4):
+        rows = pl.ds(r * half, half)
+        s_v[rows_at(r * quarter + leaf_pos * half, half)] = mine[rows]
+        s_v[rows_at(r * quarter + (1 - leaf_pos) * half, half)] = theirs[rows]
+    for e in range(update_rows // B):
+        block = pmap[leaf_pos, e]
+        p_v[pl.ds(e * B, B)] = s_v[pl.ds(pl.multiple_of(block * B, B), B)]
+    value = (total[...] - mm(p_v[...].T, w_v[...])).T
+    out[pl.ds(0, quarter)] = masked_rows(value, row_pos * quarter, live[leaf_pos]).astype(BF)
+    out[pl.ds(quarter, half)] = own[...]
+
+
+def leaf_swap(value):
+    return lax.ppermute(value, "leaf", [(0, 1), (1, 0)])
+
+
+def row_trade(value):
+    return lax.all_to_all(value, "row", 0, 0, tiled=True)
+
+
+def row_sum(value):
+    parts = row_trade(value).reshape(4, value.shape[0] // 4, value.shape[1])
+    return parts.astype(F32).sum(0)
+
+
+def row_gather(value):
+    return row_trade(jnp.concatenate([value] * 4, 0))
+
+
+def two_levels(rhs, pivot_inverse, panel, live, parent_map):
+    columns = rhs.shape[1]
+    quarter = pivot_inverse.shape[1]
+    half = quarter // 2
+    front = 4 * quarter
+    updates = parent_map.shape[1] * B
+    leaf_pos = lax.axis_index("leaf")
+    row_pos = lax.axis_index("row")
+
+    def live_rows(value, first_row, front_no):
+        row = first_row + lax.broadcasted_iota(jnp.int32, value.shape, 0)
+        count = lax.dynamic_index_in_dim(live, front_no, 0, keepdims=False) * B
+        return jnp.where(row < count, value, 0.0).astype(BF)
+
+    root_first = (2 * row_pos + leaf_pos) * half
+    root = live.shape[0] - 1
+
+    parts = 4 if updates % (4 * B) == 0 else 1
+    sent, keep, w_v = call(
+        functools.partial(panel_kernel, (quarter, half, parts, updates)),
+        (shaped(4 * half, columns), shaped(4 * half, columns), kept(updates, quarter)),
+        [SMEM, SMEM, ANY, ANY],
+        [
+            pltpu.VMEM((quarter, columns), BF),
+            pltpu.VMEM((front, columns), BF),
+            pltpu.SemaphoreType.DMA((1 + parts,)),
+        ],
+        56,
+        2 * updates * quarter * columns,
+        2 * updates * quarter,
+    )(live, parent_map, rhs, panel)
+    update = keep.astype(F32) + leaf_swap(sent).astype(F32)
+    incoming = row_sum(update.astype(BF))
+    right_side = (rhs[quarter:].astype(F32) - incoming).astype(BF)
+    right_side = live_rows(right_side, root_first, root)
+    partial, d_v = call(
+        functools.partial(leaf_pivot_kernel, (quarter, half)),
+        (shaped(front, columns), kept(6 * quarter, quarter)),
+        [SMEM, ANY, ANY, ANY],
+        [pltpu.VMEM((quarter, columns), BF), pltpu.SemaphoreType.DMA((7,))],
+        50,
+        2 * front * quarter * columns,
+        2 * front * quarter,
+    )(live, rhs, pivot_inverse, sent)
+    right_other = leaf_swap(right_side)
+    partial, right_other = lax.optimization_barrier((partial, right_other))
+    leaf_forward = live_rows(row_sum(partial), row_pos * quarter, leaf_pos)
+
+    root_partial = call(
+        functools.partial(root_pivot_kernel, (quarter, half, front)),
+        shaped(4 * half, columns),
+        [VMEM, VMEM, VMEM],
+        [pltpu.VMEM((quarter, columns), BF)],
+        16,
+        front * quarter * columns,
+        front * quarter,
+    )(right_side, right_other, d_v)
+    root_forward = live_rows(row_sum(root_partial), root_first, root)
+
+    root_keep, root_send = call(
+        functools.partial(root_transposed_kernel, (quarter, half, front)),
+        (shaped(half, columns, F32), shaped(half, columns)),
+        [VMEM, VMEM],
+        [pltpu.VMEM((quarter, columns), F32)],
+        16,
+        front * quarter * columns,
+        front * quarter,
+    )(row_gather(root_forward), d_v)
+    root_value = root_keep + leaf_swap(root_send).astype(F32)
+    root_value = live_rows(root_value, root_first, root)
+    mine = row_gather(root_value)
+    theirs = leaf_swap(mine)
+
+    total, forward = call(
+        functools.partial(leaf_transposed_kernel, (quarter, half)),
+        (shaped(columns, quarter, F32), shaped(quarter + half, columns)),
+        [VMEM] * 4,
+        [],
+        16,
+        2 * front * quarter * columns,
+        2 * front * quarter,
+    )(row_gather(leaf_forward), leaf_forward, root_forward, d_v)
+
+    backward = call(
+        functools.partial(last_kernel, (quarter, half, updates)),
+        shaped(quarter + half, columns),
+        [SMEM, SMEM] + [VMEM] * 5,
+        [pltpu.VMEM((front, columns), BF), pltpu.VMEM((updates, columns), BF)],
+        16,
+        2 * updates * quarter * columns,
+        2 * updates * quarter,
+    )(live, parent_map, mine, theirs, root_value, total, w_v)
+    return forward, backward
+
+
+def on_device(rhs, pivot_inverse, panel, live, parent_map):
+    if lax.axis_size("leaf") == 2 and lax.axis_size("row") == 4:
+        return two_levels(rhs, pivot_inverse, panel, live, parent_map)
+    return deep_tree(rhs, pivot_inverse, panel, live, parent_map)
+
+
 def solution(mesh):
     in_specs = (P(("leaf", "row"), "col"), P("leaf", "row"), P("leaf", "row"), P(), P())
     out_specs = (P(("leaf", "row"), "col"), P(("leaf", "row"), "col"))

time: 133 us -> 87.9 us (0.66)
  blocking collectives: 64 us -> 18.7 us
  starting transfers between devices: 0.43 us -> 16.9 us
  Pallas kernels: 0 us -> 13.8 us
  between operations: 15.7 us -> 2.13 us
  matrix products: 12.5 us -> 0 us
  waiting for transfers between devices: 29.5 us -> 22.5 us
  other arithmetic: 0.68 us -> 6.1 us
  local copies, waits for them, and re-layouts: 9.9 us -> 6.94 us
    psum x1 -> x0, blocking collectives: 35.4 us -> none  [on_device(): lax.psum(jnp.dot(off_block, quarter_rows, preferred_element_type=jnp.floa...]
    all_gather x3 -> x0, blocking collectives: 28.5 us -> none  [the longest x1 11 us: on_device(): lax.all_gather(own_piece, 'row', axis=0, tiled=True)]
    unnamed x4 -> x0, waiting for transfers between devices: 26.2 us -> none
    all_to_all x0 -> x4, waiting for transfers between devices: none -> 21.1 us  [row_trade(): return lax.all_to_all(value, 'row', 0, 0, tiled=True)]
    all_to_all x0 -> x2, blocking collectives: none -> 18.7 us  [row_trade(): return lax.all_to_all(value, 'row', 0, 0, tiled=True)]
    all_to_all x0 -> x4, starting transfers between devices: none -> 16.2 us  [row_trade(): return lax.all_to_all(value, 'row', 0, 0, tiled=True)]
    pallas_call x0 -> x6, Pallas kernels: none -> 13.8 us  [the longest x1 4.8 us: two_levels(): call(functools.partial(leaf_pivot_kernel, (quarter, half)), (shaped(front...]
    dot_general x9 -> x0, matrix products: 12.5 us -> none  [the longest x2 5.11 us: pivot_sum(): jnp.dot(diag_block, quarter_rows, preferred_element_type=jnp.float32)]
  transfers between devices with their start and end apart: 6 -> 8, of which waited for: 5 -> 5; matrix products, arithmetic and copies ran while one was open for 7% -> 3% of each run, Pallas kernels for 0% -> 8%
where the time goes in v2:
time: 87.9 us; the launch traced here: 87.2 us
  waiting for transfers between devices  22.5 us (26%)
  blocking collectives  18.7 us (21%)
  starting transfers between devices  16.9 us (19%)
  Pallas kernels  13.8 us (16%)
  local copies, waits for them, and re-layouts  6.94 us (8%)
  other arithmetic  6.1 us (7%)
  between operations  2.13 us (2%)
    all_to_all x4, waiting for transfers between devices, row_trade(): return lax.all_to_all(value, 'row', 0, 0, tiled=True)  21.1 us
    all_to_all x2, blocking collectives, row_trade(): return lax.all_to_all(value, 'row', 0, 0, tiled=True)  18.7 us
    all_to_all x4, starting transfers between devices, row_trade(): return lax.all_to_all(value, 'row', 0, 0, tiled=True)  16.2 us
    unnamed x12, local copies, waits for them, and re-layouts  6.35 us
    pallas_call x1, Pallas kernels, two_levels(): call(functools.partial(leaf_pivot_kernel, (quarter, half)), (shaped(front...  4.8 us
    pallas_call x1, Pallas kernels, two_levels(): call(functools.partial(panel_kernel, (quarter, half, parts, updates)), (s...  4.15 us
    pallas_call x1, Pallas kernels, two_levels(): call(functools.partial(last_kernel, (quarter, half, updates)), shaped(qua...  2.34 us
    convert_element_type x1, other arithmetic, two_levels(): incoming = row_sum(update.astype(BF))  1.78 us
  transfers between devices with their start and end apart: 8, of which 5 were waited for; matrix products, arithmetic and copies ran while one was open for 3% of the time, Pallas kernels for 8%

profile of v2, /device:TPU:0, one launch (start us, length us, event | category | flops | bytes accessed | tf_op | source)
XLA Modules:
  0.0 87.2 jit_solution(37140293388104946)
XLA Ops:
  0.6 4.1 %shard_map.68 = (bf16[1280,128]{1,0:T(8,128)(2,1)}, bf16[1280,128]{1,0:T(8,128)(2,1)}, bf16[1536,640]{1,0:T(8,128)(2,1)S(1)}) custom-call(s32[3]{0:T(128)} %live.5, s32[2,12]{1,0:T(2,128)} %pmap.3, bf16[960,128]{1,0:T(8,128)(2,1)} %rhs.3, bf16[1536,640]{1,0:T(8,128)(2,1)} %panel.1), custom_call_target="tpu_custom_call" | custom-call | flops 251658240 | bytes 1966080 | tf_op jit(solution)/shard_map/pallas_call | solution.py:371
  4.8 0.5 collective-permute-start
  5.3 1.5 %collective-permute-done = bf16[1280,128]{1,0:T(8,128)(2,1)S(1)} collective-permute-done((bf16[1280,128]{1,0:T(8,128)(2,1)}, bf16[1280,128]{1,0:T(8,128)(2,1)S(1)}, u32[]{:S(2)}, u32[]{:S(2)}) %collective-permute-start) | collective-permute-done | bytes 327712 | tf_op jit(solution)/shard_map/ppermute | solution.py:337
  6.8 1.8 %add_convert_fusion = bf16[1280,128]{1,0:T(8,128)(2,1)} fusion(bf16[1280,128]{1,0:T(8,128)(2,1)S(1)} %collective-permute-done, bf16[1280,128]{1,0:T(8,128)(2,1)} %get-tuple-element.15), kind=kLoop, calls=%fused_computation.4 | loop fusion | flops 655360 | bytes 983040 | tf_op jit(solution)/shard_map/convert_element_type | solution.py:385
  8.6 5.1 %all-to-all-start = ((bf16[4,320,128]{2,1,0:T(8,128)(2,1)}), bf16[4,320,128]{2,1,0:T(8,128)(2,1)S(1)}, u32[]{:S(2)}, u32[]{:S(2)}) async-start(bf16[4,320,128]{2,1,0:T(8,128)(2,1)} %bitcast.2), calls=%async_computation | async-start | bytes 655360 | tf_op jit(solution)/shard_map/all_to_all | solution.py:341
  13.6 0.6 fusion.1
  14.9 4.9 %all-to-all-done = bf16[4,320,128]{2,1,0:T(8,128)(2,1)S(1)} async-done(((bf16[4,320,128]{2,1,0:T(8,128)(2,1)}), bf16[4,320,128]{2,1,0:T(8,128)(2,1)S(1)}, u32[]{:S(2)}, u32[]{:S(2)}) %all-to-all-start) | async-done | bytes 327712 | tf_op jit(solution)/shard_map/all_to_all | solution.py:341
  19.9 1.0 %fusion.own = bf16[320,128]{1,0:T(8,128)(2,1)S(1)} fusion(f32[320,128]{1,0:T(8,128)S(1)} %convert_reduce_fusion.2, bf16[960,128]{1,0:T(8,128)(2,1)} %rhs.3, pred[320]{0:T(512)(128)(4,1)S(1)} %add_compare_fusion.1), kind=kLoop, calls=%fused_computation.11 | loop fusion | flops 163840 | bytes 328000 | tf_op jit(solution)/shard_map/jit(_where)/select_n | solution.py:365
  20.9 0.1 collective-permute-start.1
  21.0 4.8 %shard_map.69 = (bf16[2560,128]{1,0:T(8,128)(2,1)}, bf16[3840,640]{1,0:T(8,128)(2,1)S(1)}) custom-call(s32[3]{0:T(128)} %live.5, bf16[960,128]{1,0:T(8,128)(2,1)} %rhs.3, bf16[3840,640]{1,0:T(8,128)(2,1)} %pivot.1, bf16[1280,128]{1,0:T(8,128)(2,1)} %get-tuple-element.13.after), custom_call_target="tpu_custom_call" | custom-call | flops 419430400 | bytes 3276800 | tf_op jit(solution)/shard_map/pallas_call | solution.py:388
  25.8 0.6 shard_map.70
  26.4 1.6 %copy-done = bf16[3840,640]{1,0:T(8,128)(2,1)} copy-done((bf16[3840,640]{1,0:T(8,128)(2,1)}, bf16[3840,640]{1,0:T(8,128)(2,1)S(1)}, u32[]{:S(2)}) %copy-start) | copy-done | bytes 4915224
  28.0 9.9 %all_to_all.60 = bf16[4,320,128]{2,1,0:T(8,128)(2,1)S(1)} all-to-all(bf16[4,320,128]{2,1,0:T(8,128)(2,1)S(1)} %bitcast.15), channel_id=1, replica_groups=mesh['leaf'=2,'row'=4,'col'=4] {'row'}, dimensions={0} | all-to-all | bytes 655360 | tf_op jit(solution)/shard_map/all_to_all | solution.py:341
  37.9 0.1 select_convert_fusion.2.root_piece
  38.1 8.8 %all_to_all.61 = bf16[4,320,128]{2,1,0:T(8,128)(2,1)S(1)} all-to-all(bf16[4,320,128]{2,1,0:T(8,128)(2,1)S(1)} %bitcast.17), channel_id=1, replica_groups=mesh['leaf'=2,'row'=4,'col'=4] {'row'}, dimensions={0} | all-to-all | bytes 655360 | tf_op jit(solution)/shard_map/all_to_all | solution.py:341
  46.8 4.2 %all-to-all-start.1 = ((bf16[4,640,128]{2,1,0:T(8,128)(2,1)}), bf16[4,640,128]{2,1,0:T(8,128)(2,1)}, u32[]{:S(2)}, u32[]{:S(2)}) async-start(bf16[4,640,128]{2,1,0:T(8,128)(2,1)} %bitcast.3), calls=%async_computation.1 | async-start | bytes 1310720 | tf_op jit(solution)/shard_map/all_to_all | solution.py:341
  51.7 2.4 %copy-done.1 = bf16[3840,640]{1,0:T(8,128)(2,1)S(1)} copy-done((bf16[3840,640]{1,0:T(8,128)(2,1)S(1)}, bf16[3840,640]{1,0:T(8,128)(2,1)}, u32[]{:S(2)}) %copy-start.1) | copy-done | bytes 4915224
  54.1 0.6 shard_map.72
  54.8 4.3 %all-to-all-done.1 = bf16[4,640,128]{2,1,0:T(8,128)(2,1)} async-done(((bf16[4,640,128]{2,1,0:T(8,128)(2,1)}), bf16[4,640,128]{2,1,0:T(8,128)(2,1)}, u32[]{:S(2)}, u32[]{:S(2)}) %all-to-all-start.1) | async-done | bytes 655392 | tf_op jit(solution)/shard_map/all_to_all | solution.py:341
  59.1 1.2 %convert_reduce_fusion = bf16[640,128]{1,0:T(8,128)(2,1)S(1)} fusion(bf16[4,640,128]{2,1,0:T(8,128)(2,1)} %all-to-all-done.1), kind=kLoop, calls=%fused_computation | loop fusion | flops 573440 | bytes 819200 | tf_op jit(solution)/shard_map/reduce_sum | solution.py:346
  60.3 0.2 select_convert_fusion.own
  60.4 0.1 select_convert_fusion.1.own
  60.6 0.7 pad_maximum_fusion.2
  61.3 3.5 %all-to-all-start.5 = ((bf16[4,320,128]{2,1,0:T(8,128)(2,1)}), bf16[4,320,128]{2,1,0:T(8,128)(2,1)S(1)}, u32[]{:S(2)}, u32[]{:S(2)}) async-start(bf16[4,320,128]{2,1,0:T(8,128)(2,1)} %bitcast.9), calls=%async_computation.5 | async-start | bytes 655360 | tf_op jit(solution)/shard_map/all_to_all | solution.py:341
  64.8 0.9 %pad_maximum_fusion = bf16[2560,128]{1,0:T(8,128)(2,1)} fusion(bf16[640,128]{1,0:T(8,128)(2,1)S(1)} %select_convert_fusion.own), kind=kLoop, calls=%fused_computation.1 | loop fusion | flops 2621440 | bytes 819200 | tf_op jit(solution)/shard_map/concatenate | solution.py:350
  65.7 4.6 %all-to-all-done.5 = bf16[4,320,128]{2,1,0:T(8,128)(2,1)S(1)} async-done(((bf16[4,320,128]{2,1,0:T(8,128)(2,1)}), bf16[4,320,128]{2,1,0:T(8,128)(2,1)S(1)}, u32[]{:S(2)}, u32[]{:S(2)}) %all-to-all-start.5) | async-done | bytes 327712 | tf_op jit(solution)/shard_map/all_to_all | solution.py:341
  70.3 3.5 %all-to-all-start.2 = ((bf16[4,640,128]{2,1,0:T(8,128)(2,1)}), bf16[4,640,128]{2,1,0:T(8,128)(2,1)S(1)}, u32[]{:S(2)}, u32[]{:S(2)}) async-start(bf16[4,640,128]{2,1,0:T(8,128)(2,1)} %bitcast.16), calls=%async_computation.2 | async-start | bytes 1310720 | tf_op jit(solution)/shard_map/all_to_all | solution.py:341
  73.8 0.1 collective-permute-start.3
  73.8 7.2 %all-to-all-done.2 = bf16[4,640,128]{2,1,0:T(8,128)(2,1)S(1)} async-done(((bf16[4,640,128]{2,1,0:T(8,128)(2,1)}), bf16[4,640,128]{2,1,0:T(8,128)(2,1)S(1)}, u32[]{:S(2)}, u32[]{:S(2)}) %all-to-all-start.2) | async-done | bytes 655392 | tf_op jit(solution)/shard_map/all_to_all | solution.py:341
  81.1 2.4 %copy-done.2 = bf16[3840,640]{1,0:T(8,128)(2,1)S(1)} copy-done((bf16[3840,640]{1,0:T(8,128)(2,1)S(1)}, bf16[3840,640]{1,0:T(8,128)(2,1)}, u32[]{:S(2)}) %copy-start.2) | copy-done | bytes 4915224
  83.5 1.4 %shard_map.71 = (f32[128,640]{1,0:T(8,128)S(1)}, bf16[960,128]{1,0:T(8,128)(2,1)}) custom-call(bf16[2560,128]{1,0:T(8,128)(2,1)S(1)} %bitcast.11, bf16[640,128]{1,0:T(8,128)(2,1)S(1)} %select_convert_fusion.own, bf16[320,128]{1,0:T(8,128)(2,1)S(1)} %select_convert_fusion.2.root_piece, bf16[3840,640]{1,0:T(8,128)(2,1)S(1)} %copy-done.2), custom_call_target="tpu_custom_call" | custom-call | flops 419430400 | bytes 3276800 | tf_op jit(solution)/shard_map/pallas_call | solution.py:426
  84.8 2.3 %shard_map.73 = bf16[960,128]{1,0:T(8,128)(2,1)} custom-call(s32[3]{0:T(128)S(1)} %copy-done.4, s32[2,12]{1,0:T(2,128)S(1)} %copy-done.5, bf16[1280,128]{1,0:T(8,128)(2,1)S(1)} %bitcast.14, bf16[1280,128]{1,0:T(8,128)(2,1)} %collective-permute-done.3.theirs, bf16[320,128]{1,0:T(8,128)(2,1)S(1)} %select_convert_fusion.1.own, ...), custom_call_target="tpu_custom_call" | custom-call | flops 251658240 | bytes 1966080 | tf_op jit(solution)/shard_map/pallas_call | solution.py:436
  (18 shorter events, 0.2 us)
Async XLA Ops:
  4.8 8.9 %copy-start.3 = (s32[3]{0:T(128)S(1)}, s32[3]{0:T(128)}, u32[]{:S(2)}) copy-start(s32[3]{0:T(128)} %live.5) | copy-start | bytes 40
  4.8 2.0 %collective-permute-start = (bf16[1280,128]{1,0:T(8,128)(2,1)}, bf16[1280,128]{1,0:T(8,128)(2,1)S(1)}, u32[]{:S(2)}, u32[]{:S(2)}) collective-permute-start(bf16[1280,128]{1,0:T(8,128)(2,1)} %get-tuple-element.13.after), channel_id=1, source_target_pairs={{0,16},{16,0},{1,17},{17,1},{2,18},{18,2},{3,19},{19,3},{4,20},{20... | collective-permute-start | bytes 983048 | tf_op jit(solution)/shard_map/ppermute | solution.py:337
  8.6 11.3 %all-to-all-start = ((bf16[4,320,128]{2,1,0:T(8,128)(2,1)}), bf16[4,320,128]{2,1,0:T(8,128)(2,1)S(1)}, u32[]{:S(2)}, u32[]{:S(2)}) async-start(bf16[4,320,128]{2,1,0:T(8,128)(2,1)} %bitcast.2), calls=%async_computation | async-start | bytes 655360 | tf_op jit(solution)/shard_map/all_to_all | solution.py:341
  20.9 4.9 %collective-permute-start.1 = (bf16[320,128]{1,0:T(8,128)(2,1)S(1)}, bf16[320,128]{1,0:T(8,128)(2,1)S(1)}, u32[]{:S(2)}, u32[]{:S(2)}) collective-permute-start(bf16[320,128]{1,0:T(8,128)(2,1)S(1)} %fusion.own), channel_id=1, source_target_pairs={{0,16},{16,0},{1,17},{17,1},{2,18},{18,2},{3,19},{19,3},{4,20},{20... | collective-permute-start | bytes 245768 | tf_op jit(solution)/shard_map/ppermute | solution.py:337
  25.8 2.2 %copy-start = (bf16[3840,640]{1,0:T(8,128)(2,1)}, bf16[3840,640]{1,0:T(8,128)(2,1)S(1)}, u32[]{:S(2)}) copy-start(bf16[3840,640]{1,0:T(8,128)(2,1)S(1)} %get-tuple-element.18.pivot) | copy-start | bytes 14745604
  46.8 12.3 %all-to-all-start.1 = ((bf16[4,640,128]{2,1,0:T(8,128)(2,1)}), bf16[4,640,128]{2,1,0:T(8,128)(2,1)}, u32[]{:S(2)}, u32[]{:S(2)}) async-start(bf16[4,640,128]{2,1,0:T(8,128)(2,1)} %bitcast.3), calls=%async_computation.1 | async-start | bytes 1310720 | tf_op jit(solution)/shard_map/all_to_all | solution.py:341
  51.7 2.4 %copy-start.1 = (bf16[3840,640]{1,0:T(8,128)(2,1)S(1)}, bf16[3840,640]{1,0:T(8,128)(2,1)}, u32[]{:S(2)}) copy-start(bf16[3840,640]{1,0:T(8,128)(2,1)} %copy-done) | copy-start | bytes 14745604
  54.7 5.8 %collective-permute-start.2 = (bf16[320,128]{1,0:T(8,128)(2,1)S(1)}, bf16[320,128]{1,0:T(8,128)(2,1)S(1)}, u32[]{:S(2)}, u32[]{:S(2)}) collective-permute-start(bf16[320,128]{1,0:T(8,128)(2,1)S(1)} %get-tuple-element.21), channel_id=1, source_target_pairs={{0,16},{16,0},{1,17},{17,1},{2,18},{18,2},{3,19},{19,3},{4,20},{20... | collective-permute-start | bytes 245768 | tf_op jit(solution)/shard_map/ppermute | solution.py:337
  61.3 9.0 %all-to-all-start.5 = ((bf16[4,320,128]{2,1,0:T(8,128)(2,1)}), bf16[4,320,128]{2,1,0:T(8,128)(2,1)S(1)}, u32[]{:S(2)}, u32[]{:S(2)}) async-start(bf16[4,320,128]{2,1,0:T(8,128)(2,1)} %bitcast.9), calls=%async_computation.5 | async-start | bytes 655360 | tf_op jit(solution)/shard_map/all_to_all | solution.py:341
  70.3 10.8 %all-to-all-start.2 = ((bf16[4,640,128]{2,1,0:T(8,128)(2,1)}), bf16[4,640,128]{2,1,0:T(8,128)(2,1)S(1)}, u32[]{:S(2)}, u32[]{:S(2)}) async-start(bf16[4,640,128]{2,1,0:T(8,128)(2,1)} %bitcast.16), calls=%async_computation.2 | async-start | bytes 1310720 | tf_op jit(solution)/shard_map/all_to_all | solution.py:341
  73.8 11.1 %collective-permute-start.3 = (bf16[1280,128]{1,0:T(8,128)(2,1)S(1)}, bf16[1280,128]{1,0:T(8,128)(2,1)}, u32[]{:S(2)}, u32[]{:S(2)}) collective-permute-start(bf16[1280,128]{1,0:T(8,128)(2,1)S(1)} %bitcast.13), channel_id=1, source_target_pairs={{0,16},{16,0},{1,17},{17,1},{2,18},{18,2},{3,19},{19,3},{4,20},{20... | collective-permute-start | bytes 983048 | tf_op jit(solution)/shard_map/ppermute | solution.py:337
  81.1 2.4 %copy-start.2 = (bf16[3840,640]{1,0:T(8,128)(2,1)S(1)}, bf16[3840,640]{1,0:T(8,128)(2,1)}, u32[]{:S(2)}) copy-start(bf16[3840,640]{1,0:T(8,128)(2,1)} %copy-done) | copy-start | bytes 14745604
  83.4 1.4 %copy-start.4 = (s32[3]{0:T(128)S(1)}, s32[3]{0:T(128)}, u32[]{:S(2)}) copy-start(s32[3]{0:T(128)} %live.5) | copy-start | bytes 40
  83.4 1.4 %copy-start.5 = (s32[2,12]{1,0:T(2,128)S(1)}, s32[2,12]{1,0:T(2,128)}, u32[]{:S(2)}) copy-start(s32[2,12]{1,0:T(2,128)} %pmap.3) | copy-start | bytes 292

commit v3 on v0

--- a/solution.py
+++ b/solution.py
@@ -1,6 +1,10 @@
+import functools
+
 import jax
 import jax.numpy as jnp
 from jax import lax
+from jax.experimental import pallas as pl
+from jax.experimental.pallas import tpu as pltpu
 from jax.sharding import PartitionSpec as P
 
 F = 2560
@@ -78,7 +82,7 @@
     return from_partner(values.astype(jnp.bfloat16), "leaf", bit_no).astype(values.dtype)
 
 
-def on_device(rhs, pivot_inverse, panel, live, parent_map):
+def deep_tree(rhs, pivot_inverse, panel, live, parent_map):
     leaves = lax.axis_size("leaf")
     row_count = lax.axis_size("row")
     tree_depth = leaves.bit_length() - 1
@@ -200,6 +204,336 @@
     return (jnp.concatenate(forward_parts, 0), jnp.concatenate(backward_parts, 0))
 
 
+B = 128
+VMEM = pl.BlockSpec(memory_space=pltpu.VMEM)
+ANY = pl.BlockSpec(memory_space=pl.ANY)
+BF = jnp.bfloat16
+F32 = jnp.float32
+MIB = 1024 * 1024
+
+
+def stored(rows, columns, dtype=BF):
+    return jax.ShapeDtypeStruct((rows, columns), dtype)
+
+
+def kept(rows, columns, dtype=BF):
+    return pltpu.VMEM((rows, columns), dtype)
+
+
+def call(body, out_shape, in_specs, scratch, limit, flops, bytes_moved):
+    return pl.pallas_call(
+        body,
+        out_shape=out_shape,
+        in_specs=in_specs,
+        out_specs=jax.tree.map(lambda _: VMEM, out_shape, is_leaf=lambda s: hasattr(s, "shape")),
+        scratch_shapes=scratch,
+        compiler_params=pltpu.CompilerParams(vmem_limit_bytes=limit),
+        cost_estimate=pl.CostEstimate(flops=flops, bytes_accessed=bytes_moved, transcendentals=0),
+    )
+
+
+def rows_at(start, size):
+    return pl.ds(pl.multiple_of(start, 16), size)
+
+
+def mm(left, right):
+    return jnp.dot(left, right, preferred_element_type=F32)
+
+
+def row_order(row_pos, leaf_pos):
+    first = 1 + leaf_pos
+    return (row_pos, row_pos ^ (3 - first), row_pos ^ first, row_pos ^ 3)
+
+
+def panel_kernel(
+    sizes, live, pmap, rhs, panel, send, keep, b_v, masked, mask, w_v, c_v, live_s, pmap_s, sems
+):
+    quarter, half, parts, update_rows = sizes
+    leaf_pos = lax.axis_index("leaf")
+    row_pos = lax.axis_index("row")
+    gets = [
+        pltpu.make_async_copy(live, live_s, sems.at[0]),
+        pltpu.make_async_copy(rhs, b_v, sems.at[1]),
+        pltpu.make_async_copy(pmap, pmap_s, sems.at[2]),
+    ]
+    step = update_rows // parts
+    for i in range(parts):
+        rows = pl.ds(i * step, step)
+        gets.append(pltpu.make_async_copy(panel.at[rows], w_v.at[rows], sems.at[3 + i]))
+    for get in gets:
+        get.start()
+    c_v[...] = jnp.zeros_like(c_v)
+    gets[0].wait()
+    gets[1].wait()
+    value = b_v[pl.ds(0, quarter)]
+    row = row_pos * quarter + lax.broadcasted_iota(jnp.int32, value.shape, 0)
+    alive = row < live_s[leaf_pos] * B
+    mask[...] = jnp.where(alive, 1.0, 0.0).astype(BF)
+    masked[...] = jnp.where(alive, value, jnp.zeros_like(value))
+    right = masked[...]
+    gets[2].wait()
+    for i in range(parts):
+        gets[3 + i].wait()
+        product = mm(w_v[pl.ds(i * step, step)], right).astype(BF)
+        for e in range(step // B):
+            block = pmap_s[leaf_pos, i * (step // B) + e]
+            c_v[pl.ds(pl.multiple_of(block * B, B), B)] = product[e * B : (e + 1) * B]
+    for k, r in enumerate(row_order(row_pos, leaf_pos)):
+        keep[pl.ds(k * half, half)] = c_v[rows_at(r * quarter + leaf_pos * half, half)]
+    for k, r in enumerate(row_order(row_pos, 1 - leaf_pos)):
+        send[pl.ds(k * half, half)] = c_v[rows_at(r * quarter + (1 - leaf_pos) * half, half)]
+
+
+def leaf_pivot_kernel(sizes, masked, pivot, after, send, keep, d_v, sems):
+    quarter, half = sizes
+    order = row_order(lax.axis_index("row"), lax.axis_index("leaf"))
+    gets = []
+    for k in (2, 3, 0, 1):
+        rows = rows_at(order[k] * quarter, quarter)
+        gets.append(pltpu.make_async_copy(pivot.at[rows], d_v.at[rows], sems.at[k]))
+    rows = pl.ds(4 * quarter, 4 * half)
+    gets.append(pltpu.make_async_copy(pivot.at[rows], d_v.at[rows], sems.at[4]))
+    for get in gets:
+        get.start()
+    right = masked[...]
+    for get, k in zip(gets, (2, 3, 0, 1)):
+        get.wait()
+        out = keep if k < 2 else send
+        product = mm(d_v[rows_at(order[k] * quarter, quarter)], right)
+        out[pl.ds((k % 2) * quarter, quarter)] = product.astype(BF)
+    gets[-1].wait()
+
+
+def scatter_kernel(sizes, live, pmap, w_v, after, out, live_s, pmap_s, sems):
+    quarter, update_rows = sizes
+    leaf_pos = lax.axis_index("leaf")
+    row_pos = lax.axis_index("row")
+    gets = [
+        pltpu.make_async_copy(live, live_s, sems.at[0]),
+        pltpu.make_async_copy(pmap, pmap_s, sems.at[1]),
+    ]
+    for get in gets:
+        get.start()
+    out[...] = jnp.zeros_like(out)
+    for get in gets:
+        get.wait()
+    column = row_pos * quarter + lax.broadcasted_iota(jnp.int32, (B, quarter), 1)
+    alive = column < live_s[leaf_pos] * B
+    for e in range(update_rows // B):
+        value = w_v[pl.ds(e * B, B)]
+        block = pmap_s[leaf_pos, e]
+        out[pl.ds(pl.multiple_of(block * B, B), B)] = jnp.where(alive, value, jnp.zeros_like(value))
+
+
+def root_pivot_kernel(sizes, own, other, d_v, send, keep, q_v):
+    quarter, half, base = sizes
+    leaf_pos = lax.axis_index("leaf")
+    order = row_order(lax.axis_index("row"), leaf_pos)
+    q_v[rows_at(leaf_pos * half, half)] = own[...]
+    q_v[rows_at((1 - leaf_pos) * half, half)] = other[...]
+    right = q_v[...]
+    for k in range(4):
+        out = keep if k < 2 else send
+        product = mm(d_v[rows_at(base + order[k] * half, half)], right)
+        out[pl.ds((k % 2) * half, half)] = product.astype(BF)
+
+
+def root_transposed_kernel(sizes, near, far, d_v, keep, send, y_v, s_v):
+    quarter, half, base = sizes
+    leaf_pos = lax.axis_index("leaf")
+    order = row_order(lax.axis_index("row"), leaf_pos)
+    for k in range(4):
+        part = (near if k < 2 else far)[pl.ds((k % 2) * half, half)]
+        y_v[rows_at(order[k] * half, half)] = part
+    s_v[...] = mm(y_v[...].T, d_v[pl.ds(base, 4 * half)]).T
+    keep[...] = s_v[rows_at(leaf_pos * half, half)]
+    send[...] = s_v[rows_at((1 - leaf_pos) * half, half)].astype(BF)
+
+
+def leaf_transposed_kernel(sizes, near, far, d_v, mask, total, y_v):
+    quarter, half = sizes
+    order = row_order(lax.axis_index("row"), lax.axis_index("leaf"))
+    for k in range(4):
+        part = (near if k < 2 else far)[pl.ds((k % 2) * quarter, quarter)]
+        y_v[rows_at(order[k] * quarter, quarter)] = part
+    value = mm(y_v[...].T, d_v[pl.ds(0, 4 * quarter)])
+    total[...] = jnp.where(mask[...].astype(F32).T > 0.0, value, 0.0)
+
+
+def place(sizes, which, mine, theirs, s_v, w_v, panel_rows):
+    quarter, half = sizes
+    leaf_pos = lax.axis_index("leaf")
+    row_pos = lax.axis_index("row")
+    at = 0
+    for source, side in ((mine, leaf_pos), (theirs, 1 - leaf_pos)):
+        order = row_order(row_pos, side)
+        for k in range(2):
+            rows = pl.ds(at, half)
+            s_v[rows] = source[pl.ds(k * half, half)]
+            w_v[rows] = panel_rows[rows_at(order[which + k] * quarter + side * half, half)]
+            at += half
+
+
+def early_kernel(sizes, mine, theirs, total, panel_rows, out, s_v, w_v):
+    place(sizes, 0, mine, theirs, s_v, w_v, panel_rows)
+    out[...] = total[...] - mm(s_v[...].T, w_v[...])
+
+
+def last_kernel(sizes, mine, theirs, total, panel_rows, near, out, s_v, w_v):
+    quarter, half = sizes
+    place(sizes, 2, mine, theirs, s_v, w_v, panel_rows)
+    value = total[...] - mm(s_v[...].T, w_v[...])
+    out[pl.ds(0, quarter)] = value.T.astype(BF)
+    out[pl.ds(quarter, half)] = near[pl.ds(0, half)]
+
+
+def leaf_swap(value):
+    return lax.ppermute(value, "leaf", [(0, 1), (1, 0)])
+
+
+def row_swap(value, phase):
+    route = []
+    for leaf in range(2):
+        apart = (1 + leaf) if phase == 0 else (2 - leaf)
+        route += [(4 * leaf + r, 4 * leaf + (r ^ apart)) for r in range(4)]
+    return lax.ppermute(value, ("leaf", "row"), route)
+
+
+def added(left, right):
+    return left.astype(F32) + right.astype(F32)
+
+
+def two_levels(rhs, pivot_inverse, panel, live, parent_map):
+    columns = rhs.shape[1]
+    quarter = pivot_inverse.shape[1]
+    half = quarter // 2
+    front = 4 * quarter
+    updates = parent_map.shape[1] * B
+    barrier = lax.optimization_barrier
+    smem = [pltpu.SMEM(live.shape, jnp.int32), pltpu.SMEM(parent_map.shape, jnp.int32)]
+
+    parts = 4 if updates % (4 * B) == 0 else 1
+    sent, keep, b_v, masked, mask, w_v = call(
+        functools.partial(panel_kernel, (quarter, half, parts, updates)),
+        (
+            kept(4 * half, columns),
+            kept(4 * half, columns),
+            kept(quarter + half, columns),
+            kept(quarter, columns),
+            kept(quarter, columns),
+            kept(updates, quarter),
+        ),
+        [ANY] * 4,
+        [pltpu.VMEM((front, columns), BF), *smem, pltpu.SemaphoreType.DMA((3 + parts,))],
+        62_100_000,
+        2 * updates * quarter * columns,
+        2 * updates * quarter,
+    )(live, parent_map, rhs, panel)
+    got = leaf_swap(sent)
+    away = added(keep[quarter:], got[quarter:]).astype(BF)
+    home = added(keep[:quarter], got[:quarter])
+    home = home + row_swap(away, 0).astype(F32)
+    incoming = home[:half] + row_swap(home[half:].astype(BF), 1).astype(F32)
+    right_side = (b_v[quarter:].astype(F32) - incoming).astype(BF)
+    right_other = leaf_swap(right_side)
+
+    send_e, keep_e, d_v = call(
+        functools.partial(leaf_pivot_kernel, (quarter, half)),
+        (kept(2 * quarter, columns), kept(2 * quarter, columns), kept(front + 4 * half, quarter)),
+        [VMEM, ANY, ANY],
+        [pltpu.SemaphoreType.DMA((5,))],
+        48 * MIB,
+        2 * front * quarter * columns,
+        2 * front * quarter,
+    )(masked, pivot_inverse, away)
+
+    send_e, home = barrier((send_e, home))
+    send_e = barrier((send_e, incoming))[0]
+    home_e = keep_e.astype(F32) + row_swap(send_e, 0).astype(F32)
+
+    send, keep = call(
+        functools.partial(root_pivot_kernel, (quarter, half, front)),
+        (kept(quarter, columns), kept(quarter, columns)),
+        [VMEM, VMEM, VMEM],
+        [pltpu.VMEM((quarter, columns), BF)],
+        16 * MIB,
+        front * quarter * columns,
+        front * quarter,
+    )(right_side, right_other, d_v)
+    home = keep.astype(F32) + row_swap(send, 0).astype(F32)
+    root_forward = (home[:half] + row_swap(home[half:].astype(BF), 1).astype(F32)).astype(BF)
+
+    away_e = barrier((home_e[quarter:].astype(BF), home))[0]
+    leaf_forward = home_e[:quarter] + row_swap(away_e, 1).astype(F32)
+    leaf_forward = jnp.where(mask > 0, leaf_forward, 0.0).astype(BF)
+
+    near = jnp.concatenate([root_forward, row_swap(root_forward, 1)], 0)
+    far = row_swap(near, 0)
+    root_keep, root_send = call(
+        functools.partial(root_transposed_kernel, (quarter, half, front)),
+        (kept(half, columns, F32), kept(half, columns)),
+        [VMEM, VMEM, VMEM],
+        [pltpu.VMEM((4 * half, columns), BF), pltpu.VMEM((quarter, columns), F32)],
+        16 * MIB,
+        front * quarter * columns,
+        front * quarter,
+    )(near, far, d_v)
+    root_value = (root_keep + leaf_swap(root_send).astype(F32)).astype(BF)
+
+    near_e = jnp.concatenate([leaf_forward, row_swap(leaf_forward, 1)], 0)
+    far_e = row_swap(near_e, 0)
+    panel_rows = call(
+        functools.partial(scatter_kernel, (quarter, updates)),
+        kept(front, quarter),
+        [ANY, ANY, VMEM, ANY],
+        [*smem, pltpu.SemaphoreType.DMA((2,))],
+        16 * MIB,
+        0,
+        4 * front * quarter,
+    )(live, parent_map, w_v, right_side)
+    total = call(
+        functools.partial(leaf_transposed_kernel, (quarter, half)),
+        kept(columns, quarter, F32),
+        [VMEM] * 4,
+        [pltpu.VMEM((front, columns), BF)],
+        16 * MIB,
+        2 * front * quarter * columns,
+        2 * front * quarter,
+    )(near_e, far_e, d_v, mask)
+    forward = jnp.concatenate([leaf_forward, root_forward], 0)
+
+    near = jnp.concatenate([root_value, row_swap(root_value, 1)], 0)
+    far = row_swap(near, 0)
+    near_other = leaf_swap(near)
+    scratch = [pltpu.VMEM((4 * half, columns), BF), pltpu.VMEM((4 * half, quarter), BF)]
+    total = call(
+        functools.partial(early_kernel, (quarter, half)),
+        kept(columns, quarter, F32),
+        [VMEM] * 4,
+        scratch,
+        16 * MIB,
+        front * quarter * columns,
+        front * quarter,
+    )(near, near_other, total, panel_rows)
+    far_other = leaf_swap(far)
+    backward = call(
+        functools.partial(last_kernel, (quarter, half)),
+        stored(quarter + half, columns),
+        [VMEM] * 5,
+        scratch,
+        16 * MIB,
+        front * quarter * columns,
+        front * quarter,
+    )(far, far_other, total, panel_rows, near)
+    return forward, backward
+
+
+def on_device(rhs, pivot_inverse, panel, live, parent_map):
+    if lax.axis_size("leaf") == 2 and lax.axis_size("row") == 4:
+        return two_levels(rhs, pivot_inverse, panel, live, parent_map)
+    return deep_tree(rhs, pivot_inverse, panel, live, parent_map)
+
+
 def solution(mesh):
     in_specs = (P(("leaf", "row"), "col"), P("leaf", "row"), P("leaf", "row"), P(), P())
     out_specs = (P(("leaf", "row"), "col"), P(("leaf", "row"), "col"))

time: 133 us -> 60.7 us (0.46)
  blocking collectives: 64 us -> 0 us
  starting transfers between devices: 0.43 us -> 21.4 us
  between operations: 15.7 us -> 0.81 us
  matrix products: 12.5 us -> 0 us
  Pallas kernels: 0 us -> 10.3 us
  local copies, waits for them, and re-layouts: 9.9 us -> 0.05 us
  waiting for transfers between devices: 29.5 us -> 26.8 us
    psum x1 -> x0, blocking collectives: 35.4 us -> none  [on_device(): lax.psum(jnp.dot(off_block, quarter_rows, preferred_element_type=jnp.floa...]
    all_gather x3 -> x0, blocking collectives: 28.5 us -> none  [the longest x1 11 us: on_device(): lax.all_gather(own_piece, 'row', axis=0, tiled=True)]
    unnamed x4 -> x0, waiting for transfers between devices: 26.2 us -> none
    ppermute x4 -> x17, waiting for transfers between devices: 3.3 us -> 26.8 us  [the longest x12 25.5 us: row_swap(): return lax.ppermute(value, ('leaf', 'row'), route)]
    ppermute x4 -> x17, starting transfers between devices: 0.35 us -> 21.4 us  [the longest x12 20.7 us: row_swap(): return lax.ppermute(value, ('leaf', 'row'), route)]
    dot_general x9 -> x0, matrix products: 12.5 us -> none  [the longest x2 5.11 us: pivot_sum(): jnp.dot(diag_block, quarter_rows, preferred_element_type=jnp.float32)]
    pallas_call x0 -> x8, Pallas kernels: none -> 10.3 us  [the longest x1 3.17 us: two_levels(): call(functools.partial(leaf_pivot_kernel, (quarter, half)), (kept(2 * qua...]
    unnamed x13 -> x4, local copies, waits for them, and re-layouts: 6.16 us -> 0.01 us
  transfers between devices with their start and end apart: 6 -> 17, of which waited for: 5 -> 11; matrix products, arithmetic and copies ran while one was open for 7% -> 2% of each run, Pallas kernels for 0% -> 10%
where the time goes in v3:
time: 60.7 us; the launch traced here: 60.5 us
  waiting for transfers between devices  26.8 us (44%)
  starting transfers between devices  21.4 us (35%)
  Pallas kernels  10.3 us (17%)
  other arithmetic  1.12 us (2%)
  between operations  0.81 us (1%)
    ppermute x12, waiting for transfers between devices, row_swap(): return lax.ppermute(value, ('leaf', 'row'), route)  25.5 us
    ppermute x12, starting transfers between devices, row_swap(): return lax.ppermute(value, ('leaf', 'row'), route)  20.7 us
    pallas_call x1, Pallas kernels, two_levels(): call(functools.partial(leaf_pivot_kernel, (quarter, half)), (kept(2 * qua...  3.17 us
    pallas_call x1, Pallas kernels, two_levels(): call(functools.partial(panel_kernel, (quarter, half, parts, updates)), (k...  2.71 us
    ppermute x5, waiting for transfers between devices, leaf_swap(): return lax.ppermute(value, 'leaf', [(0, 1), (1, 0)])  1.27 us
    pallas_call x1, Pallas kernels, two_levels(): call(functools.partial(last_kernel, (quarter, half)), stored(quarter + ha...  1.24 us
  transfers between devices with their start and end apart: 17, of which 11 were waited for; matrix products, arithmetic and copies ran while one was open for 2% of the time, Pallas kernels for 10%

profile of v3, /device:TPU:0, one launch (start us, length us, event | category | flops | bytes accessed | tf_op | source)
XLA Modules:
  0.0 60.5 jit_solution(12093280871149006198)
XLA Ops:
  0.6 2.7 %shard_map.68 = (bf16[1280,128]{1,0:T(8,128)(2,1)S(1)}, bf16[1280,128]{1,0:T(8,128)(2,1)S(1)}, bf16[960,128]{1,0:T(8,128)(2,1)S(1)}, bf16[640,128]{1,0:T(8,128)(...) custom-call(s32[3]{0:T(128)} %live.3, s32[2,12]{1,0:T(2,128)} %pmap.3, bf16[960,128]{1,0:T(8,128)(2,1)} %rhs.1, ...), custom_call_target="tpu_custom_call" | custom-call | flops 251658240 | bytes 1966080 | tf_op jit(solution)/shard_map/pallas_call | solution.py:416
  3.3 0.5 collective-permute-start
  3.9 1.3 %collective-permute-done = bf16[1280,128]{1,0:T(8,128)(2,1)S(1)} collective-permute-done((bf16[1280,128]{1,0:T(8,128)(2,1)S(1)}, bf16[1280,128]{1,0:T(8,128)(2,1)S(1)}, u32[]{:S(2)}, u32[]{:S(2)}) %collective-permute-start) | collective-permute-done | bytes 327712 | tf_op jit(solution)/shard_map/ppermute | solution.py:391
  5.2 2.9 %collective-permute-start.1 = (bf16[640,128]{1,0:T(8,128)(2,1)S(1)}, bf16[640,128]{1,0:T(8,128)(2,1)S(1)}, u32[]{:S(2)}, u32[]{:S(2)}) collective-permute-start(bf16[640,128]{1,0:T(8,128)(2,1)S(1)} %add_convert_fusion.after), channel_id=1, source_target_pairs={{0,4},{4,0},{8,12},{12,8},{16,24},{20,28},{24,16},{28,20},{1,5},{5... | collective-permute-start | bytes 491528 | tf_op jit(solution)/shard_map/ppermute | solution.py:399
  8.1 3.3 %collective-permute-done.1 = bf16[640,128]{1,0:T(8,128)(2,1)S(1)} collective-permute-done((bf16[640,128]{1,0:T(8,128)(2,1)S(1)}, bf16[640,128]{1,0:T(8,128)(2,1)S(1)}, u32[]{:S(2)}, u32[]{:S(2)}) %collective-permute-start.1) | collective-permute-done | bytes 163872 | tf_op jit(solution)/shard_map/ppermute | solution.py:399
  11.5 2.1 %collective-permute-start.2 = (bf16[320,128]{1,0:T(8,128)(2,1)S(1)}, bf16[320,128]{1,0:T(8,128)(2,1)S(1)}, u32[]{:S(2)}, u32[]{:S(2)}) collective-permute-start(bf16[320,128]{1,0:T(8,128)(2,1)S(1)} %slice.74), channel_id=1, source_target_pairs={{0,8},{4,12},{8,0},{12,4},{16,20},{20,16},{24,28},{28,24},{1,9},{5... | collective-permute-start | bytes 245768 | tf_op jit(solution)/shard_map/ppermute | solution.py:399
  13.6 2.4 %collective-permute-done.2 = bf16[320,128]{1,0:T(8,128)(2,1)S(1)} collective-permute-done((bf16[320,128]{1,0:T(8,128)(2,1)S(1)}, bf16[320,128]{1,0:T(8,128)(2,1)S(1)}, u32[]{:S(2)}, u32[]{:S(2)}) %collective-permute-start.2) | collective-permute-done | bytes 81952 | tf_op jit(solution)/shard_map/ppermute | solution.py:399
  16.1 3.2 %shard_map.69 = (bf16[1280,128]{1,0:T(8,128)(2,1)S(1)}, bf16[1280,128]{1,0:T(8,128)(2,1)S(1)}, bf16[3840,640]{1,0:T(8,128)(2,1)S(1)}) custom-call(bf16[640,128]{1,0:T(8,128)(2,1)S(1)} %get-tuple-element.19.masked, bf16[3840,640]{1,0:T(8,128)(2,1)} %pivot.1, bf16[640,128]{1,0:T(8,128)(2,1)S(1)} %add_convert_fusion.after), custom_call_target="tpu_custom_call" | custom-call | flops 419430400 | bytes 3276800 | tf_op jit(solution)/shard_map/pallas_call | solution.py:440
  19.3 0.6 %shard_map.70 = (bf16[640,128]{1,0:T(8,128)(2,1)S(1)}, bf16[640,128]{1,0:T(8,128)(2,1)S(1)}) custom-call(bf16[320,128]{1,0:T(8,128)(2,1)S(1)} %subtract_convert_fusion, bf16[320,128]{1,0:T(8,128)(2,1)S(1)} %collective-permute-done.4.other, bf16[3840,640]{1,0:T(8,128)(2,1)S(1)} %get-tuple-element.27.d_v), custom_call_target="tpu_custom_call" | custom-call | flops 209715200 | bytes 1638400 | tf_op jit(solution)/shard_map/pallas_call | solution.py:454
  19.9 2.1 %collective-permute-start.5 = (bf16[640,128]{1,0:T(8,128)(2,1)S(1)}, bf16[640,128]{1,0:T(8,128)(2,1)S(1)}, u32[]{:S(2)}, u32[]{:S(2)}) collective-permute-start(bf16[640,128]{1,0:T(8,128)(2,1)S(1)} %get-tuple-element.29), channel_id=1, source_target_pairs={{0,4},{4,0},{8,12},{12,8},{16,24},{20,28},{24,16},{28,20},{1,5},{5... | collective-permute-start | bytes 491528 | tf_op jit(solution)/shard_map/ppermute | solution.py:399
  22.0 3.3 %collective-permute-done.5 = bf16[640,128]{1,0:T(8,128)(2,1)S(1)} collective-permute-done((bf16[640,128]{1,0:T(8,128)(2,1)S(1)}, bf16[640,128]{1,0:T(8,128)(2,1)S(1)}, u32[]{:S(2)}, u32[]{:S(2)}) %collective-permute-start.5) | collective-permute-done | bytes 163872 | tf_op jit(solution)/shard_map/ppermute | solution.py:399
  25.4 2.1 %collective-permute-start.7 = (bf16[320,128]{1,0:T(8,128)(2,1)S(1)}, bf16[320,128]{1,0:T(8,128)(2,1)S(1)}, u32[]{:S(2)}, u32[]{:S(2)}) collective-permute-start(bf16[320,128]{1,0:T(8,128)(2,1)S(1)} %slice.73), channel_id=1, source_target_pairs={{0,8},{4,12},{8,0},{12,4},{16,20},{20,16},{24,28},{28,24},{1,9},{5... | collective-permute-start | bytes 245768 | tf_op jit(solution)/shard_map/ppermute | solution.py:399
  27.5 1.5 %collective-permute-start.3 = (bf16[1280,128]{1,0:T(8,128)(2,1)S(1)}, bf16[1280,128]{1,0:T(8,128)(2,1)S(1)}, u32[]{:S(2)}, u32[]{:S(2)}) collective-permute-start(bf16[1280,128]{1,0:T(8,128)(2,1)S(1)} %get-tuple-element.25), channel_id=1, source_target_pairs={{0,4},{4,0},{8,12},{12,8},{16,24},{20,28},{24,16},{28,20},{1,5},{5... | collective-permute-start | bytes 983048 | tf_op jit(solution)/shard_map/ppermute | solution.py:399
  29.0 1.5 %collective-permute-done.7 = bf16[320,128]{1,0:T(8,128)(2,1)S(1)} collective-permute-done((bf16[320,128]{1,0:T(8,128)(2,1)S(1)}, bf16[320,128]{1,0:T(8,128)(2,1)S(1)}, u32[]{:S(2)}, u32[]{:S(2)}) %collective-permute-start.7) | collective-permute-done | bytes 81952 | tf_op jit(solution)/shard_map/ppermute | solution.py:399
  30.5 2.4 %collective-permute-start.8 = (bf16[320,128]{1,0:T(8,128)(2,1)S(1)}, bf16[320,128]{1,0:T(8,128)(2,1)S(1)}, u32[]{:S(2)}, u32[]{:S(2)}) collective-permute-start(bf16[320,128]{1,0:T(8,128)(2,1)S(1)} %fusion.2), channel_id=1, source_target_pairs={{0,8},{4,12},{8,0},{12,4},{16,20},{20,16},{24,28},{28,24},{1,9},{5... | collective-permute-start | bytes 245768 | tf_op jit(solution)/shard_map/ppermute | solution.py:399
  32.9 2.4 %collective-permute-done.8 = bf16[320,128]{1,0:T(8,128)(2,1)S(1)} collective-permute-done((bf16[320,128]{1,0:T(8,128)(2,1)S(1)}, bf16[320,128]{1,0:T(8,128)(2,1)S(1)}, u32[]{:S(2)}, u32[]{:S(2)}) %collective-permute-start.8) | collective-permute-done | bytes 81952 | tf_op jit(solution)/shard_map/ppermute | solution.py:399
  35.3 2.1 %collective-permute-start.9 = (bf16[640,128]{1,0:T(8,128)(2,1)S(1)}, bf16[640,128]{1,0:T(8,128)(2,1)S(1)}, u32[]{:S(2)}, u32[]{:S(2)}) collective-permute-start(bf16[640,128]{1,0:T(8,128)(2,1)S(1)} %pad_maximum_fusion.2.near), channel_id=1, source_target_pairs={{0,4},{4,0},{8,12},{12,8},{16,24},{20,28},{24,16},{28,20},{1,5},{5... | collective-permute-start | bytes 491528 | tf_op jit(solution)/shard_map/ppermute | solution.py:399
  37.5 1.6 %collective-permute-start.6 = (bf16[640,128]{1,0:T(8,128)(2,1)S(1)}, bf16[640,128]{1,0:T(8,128)(2,1)S(1)}, u32[]{:S(2)}, u32[]{:S(2)}) collective-permute-start(bf16[640,128]{1,0:T(8,128)(2,1)S(1)} %slice.72), channel_id=1, source_target_pairs={{0,8},{4,12},{8,0},{12,4},{16,20},{20,16},{24,28},{28,24},{1,9},{5... | collective-permute-start | bytes 491528 | tf_op jit(solution)/shard_map/ppermute | solution.py:399
  39.1 2.0 %collective-permute-done.9.far = bf16[640,128]{1,0:T(8,128)(2,1)S(1)} collective-permute-done((bf16[640,128]{1,0:T(8,128)(2,1)S(1)}, bf16[640,128]{1,0:T(8,128)(2,1)S(1)}, u32[]{:S(2)}, u32[]{:S(2)}) %collective-permute-start.9) | collective-permute-done | bytes 163872 | tf_op jit(solution)/shard_map/ppermute | solution.py:399
  41.1 0.6 %shard_map.71 = (f32[320,128]{1,0:T(8,128)S(1)}, bf16[320,128]{1,0:T(8,128)(2,1)S(1)}) custom-call(bf16[640,128]{1,0:T(8,128)(2,1)S(1)} %pad_maximum_fusion.2.near, bf16[640,128]{1,0:T(8,128)(2,1)S(1)} %collective-permute-done.9.far, bf16[3840,640]{1,0:T(8,128)(2,1)S(1)} %get-tuple-element.27.d_v), custom_call_target="tpu_custom_call" | custom-call | flops 209715200 | bytes 1638400 | tf_op jit(solution)/shard_map/pallas_call | solution.py:472
  41.8 1.1 %collective-permute-done.6 = bf16[640,128]{1,0:T(8,128)(2,1)S(1)} collective-permute-done((bf16[640,128]{1,0:T(8,128)(2,1)S(1)}, bf16[640,128]{1,0:T(8,128)(2,1)S(1)}, u32[]{:S(2)}, u32[]{:S(2)}) %collective-permute-start.6) | collective-permute-done | bytes 163872 | tf_op jit(solution)/shard_map/ppermute | solution.py:399
  43.0 1.6 %collective-permute-start.15 = (bf16[640,128]{1,0:T(8,128)(2,1)S(1)}, bf16[640,128]{1,0:T(8,128)(2,1)S(1)}, u32[]{:S(2)}, u32[]{:S(2)}) collective-permute-start(bf16[640,128]{1,0:T(8,128)(2,1)S(1)} %fusion.1), channel_id=1, source_target_pairs={{0,8},{4,12},{8,0},{12,4},{16,20},{20,16},{24,28},{28,24},{1,9},{5... | collective-permute-start | bytes 491528 | tf_op jit(solution)/shard_map/ppermute | solution.py:399
  44.6 0.6 collective-permute-start.11
  45.2 3.2 %collective-permute-done.15 = bf16[640,128]{1,0:T(8,128)(2,1)S(1)} collective-permute-done((bf16[640,128]{1,0:T(8,128)(2,1)S(1)}, bf16[640,128]{1,0:T(8,128)(2,1)S(1)}, u32[]{:S(2)}, u32[]{:S(2)}) %collective-permute-start.15) | collective-permute-done | bytes 163872 | tf_op jit(solution)/shard_map/ppermute | solution.py:399
  48.4 0.6 collective-permute-start.16
  49.3 1.3 %collective-permute-start.12 = (bf16[640,128]{1,0:T(8,128)(2,1)S(1)}, bf16[640,128]{1,0:T(8,128)(2,1)S(1)}, u32[]{:S(2)}, u32[]{:S(2)}) collective-permute-start(bf16[640,128]{1,0:T(8,128)(2,1)S(1)} %pad_maximum_fusion.3.mine.near), channel_id=1, source_target_pairs={{0,4},{4,0},{8,12},{12,8},{16,24},{20,28},{24,16},{28,20},{1,5},{5... | collective-permute-start | bytes 491528 | tf_op jit(solution)/shard_map/ppermute | solution.py:399
  50.6 0.8 %shard_map.73.panel_rows = bf16[2560,640]{1,0:T(8,128)(2,1)S(1)} custom-call(s32[3]{0:T(128)S(1)} %copy-done.1, s32[2,12]{1,0:T(2,128)S(1)} %copy-done, bf16[1536,640]{1,0:T(8,128)(2,1)S(1)} %get-tuple-element.33.w_v, bf16[320,128]{1,0:T(8,128)(2,1)S(1)} %subtract_convert_fusion), custom_call_target="tpu_custom_call" | custom-call | bytes 6553600 | tf_op jit(solution)/shard_map/pallas_call | solution.py:485
  51.4 5.9 %collective-permute-done.12.mine = bf16[640,128]{1,0:T(8,128)(2,1)S(1)} collective-permute-done((bf16[640,128]{1,0:T(8,128)(2,1)S(1)}, bf16[640,128]{1,0:T(8,128)(2,1)S(1)}, u32[]{:S(2)}, u32[]{:S(2)}) %collective-permute-start.12) | collective-permute-done | bytes 163872 | tf_op jit(solution)/shard_map/ppermute | solution.py:399
  57.3 0.7 %pad_maximum_fusion.1 = bf16[960,128]{1,0:T(8,128)(2,1)} fusion(bf16[320,128]{1,0:T(8,128)(2,1)S(1)} %fusion.2, bf16[640,128]{1,0:T(8,128)(2,1)S(1)} %fusion.1), kind=kLoop, calls=%fused_computation.9 | loop fusion | flops 491520 | bytes 491520 | tf_op jit(solution)/shard_map/concatenate | solution.py:503
  58.0 0.8 %shard_map.72.total = f32[128,640]{1,0:T(8,128)S(1)} custom-call(bf16[1280,128]{1,0:T(8,128)(2,1)S(1)} %pad_maximum_fusion.near, bf16[1280,128]{1,0:T(8,128)(2,1)S(1)} %collective-permute-done.16.far, bf16[3840,640]{1,0:T(8,128)(2,1)S(1)} %get-tuple-element.27.d_v, bf16[640,128]{1,0:T(8,128)(2,1)S(1)} %get-tuple-element.18.mask), custom_call_target="tpu_custom_call" | custom-call | flops 419430400 | bytes 3276800 | tf_op jit(solution)/shard_map/pallas_call | solution.py:494
  58.8 0.5 shard_map.74.total
  59.3 1.2 %shard_map.75 = bf16[960,128]{1,0:T(8,128)(2,1)} custom-call(bf16[640,128]{1,0:T(8,128)(2,1)S(1)} %collective-permute-done.12.mine, bf16[640,128]{1,0:T(8,128)(2,1)S(1)} %collective-permute-done.13.theirs, f32[128,640]{1,0:T(8,128)S(1)} %shard_map.74.total, bf16[2560,640]{1,0:T(8,128)(2,1)S(1)} %shard_map.73.panel_rows, ...), custom_call_target="tpu_custom_call" | custom-call | flops 209715200 | bytes 1638400 | tf_op jit(solution)/shard_map/pallas_call | solution.py:519
  (29 shorter events, 0.9 us)
Async XLA Ops:
  3.3 1.8 %collective-permute-start = (bf16[1280,128]{1,0:T(8,128)(2,1)S(1)}, bf16[1280,128]{1,0:T(8,128)(2,1)S(1)}, u32[]{:S(2)}, u32[]{:S(2)}) collective-permute-start(bf16[1280,128]{1,0:T(8,128)(2,1)S(1)} %get-tuple-element.21), channel_id=1, source_target_pairs={{0,16},{16,0},{1,17},{17,1},{2,18},{18,2},{3,19},{19,3},{4,20},{20... | collective-permute-start | bytes 983048 | tf_op jit(solution)/shard_map/ppermute | solution.py:391
  5.2 6.2 %collective-permute-start.1 = (bf16[640,128]{1,0:T(8,128)(2,1)S(1)}, bf16[640,128]{1,0:T(8,128)(2,1)S(1)}, u32[]{:S(2)}, u32[]{:S(2)}) collective-permute-start(bf16[640,128]{1,0:T(8,128)(2,1)S(1)} %add_convert_fusion.after), channel_id=1, source_target_pairs={{0,4},{4,0},{8,12},{12,8},{16,24},{20,28},{24,16},{28,20},{1,5},{5... | collective-permute-start | bytes 491528 | tf_op jit(solution)/shard_map/ppermute | solution.py:399
  11.5 4.5 %collective-permute-start.2 = (bf16[320,128]{1,0:T(8,128)(2,1)S(1)}, bf16[320,128]{1,0:T(8,128)(2,1)S(1)}, u32[]{:S(2)}, u32[]{:S(2)}) collective-permute-start(bf16[320,128]{1,0:T(8,128)(2,1)S(1)} %slice.74), channel_id=1, source_target_pairs={{0,8},{4,12},{8,0},{12,4},{16,20},{20,16},{24,28},{28,24},{1,9},{5... | collective-permute-start | bytes 245768 | tf_op jit(solution)/shard_map/ppermute | solution.py:399
  16.0 3.3 %collective-permute-start.4 = (bf16[320,128]{1,0:T(8,128)(2,1)S(1)}, bf16[320,128]{1,0:T(8,128)(2,1)S(1)}, u32[]{:S(2)}, u32[]{:S(2)}) collective-permute-start(bf16[320,128]{1,0:T(8,128)(2,1)S(1)} %subtract_convert_fusion), channel_id=1, source_target_pairs={{0,16},{16,0},{1,17},{17,1},{2,18},{18,2},{3,19},{19,3},{4,20},{20... | collective-permute-start | bytes 245768 | tf_op jit(solution)/shard_map/ppermute | solution.py:391
  19.9 5.4 %collective-permute-start.5 = (bf16[640,128]{1,0:T(8,128)(2,1)S(1)}, bf16[640,128]{1,0:T(8,128)(2,1)S(1)}, u32[]{:S(2)}, u32[]{:S(2)}) collective-permute-start(bf16[640,128]{1,0:T(8,128)(2,1)S(1)} %get-tuple-element.29), channel_id=1, source_target_pairs={{0,4},{4,0},{8,12},{12,8},{16,24},{20,28},{24,16},{28,20},{1,5},{5... | collective-permute-start | bytes 491528 | tf_op jit(solution)/shard_map/ppermute | solution.py:399
  25.4 5.1 %collective-permute-start.7 = (bf16[320,128]{1,0:T(8,128)(2,1)S(1)}, bf16[320,128]{1,0:T(8,128)(2,1)S(1)}, u32[]{:S(2)}, u32[]{:S(2)}) collective-permute-start(bf16[320,128]{1,0:T(8,128)(2,1)S(1)} %slice.73), channel_id=1, source_target_pairs={{0,8},{4,12},{8,0},{12,4},{16,20},{20,16},{24,28},{28,24},{1,9},{5... | collective-permute-start | bytes 245768 | tf_op jit(solution)/shard_map/ppermute | solution.py:399
  27.5 9.9 %collective-permute-start.3 = (bf16[1280,128]{1,0:T(8,128)(2,1)S(1)}, bf16[1280,128]{1,0:T(8,128)(2,1)S(1)}, u32[]{:S(2)}, u32[]{:S(2)}) collective-permute-start(bf16[1280,128]{1,0:T(8,128)(2,1)S(1)} %get-tuple-element.25), channel_id=1, source_target_pairs={{0,4},{4,0},{8,12},{12,8},{16,24},{20,28},{24,16},{28,20},{1,5},{5... | collective-permute-start | bytes 983048 | tf_op jit(solution)/shard_map/ppermute | solution.py:399
  30.5 4.8 %collective-permute-start.8 = (bf16[320,128]{1,0:T(8,128)(2,1)S(1)}, bf16[320,128]{1,0:T(8,128)(2,1)S(1)}, u32[]{:S(2)}, u32[]{:S(2)}) collective-permute-start(bf16[320,128]{1,0:T(8,128)(2,1)S(1)} %fusion.2), channel_id=1, source_target_pairs={{0,8},{4,12},{8,0},{12,4},{16,20},{20,16},{24,28},{28,24},{1,9},{5... | collective-permute-start | bytes 245768 | tf_op jit(solution)/shard_map/ppermute | solution.py:399
  35.3 5.8 %collective-permute-start.9 = (bf16[640,128]{1,0:T(8,128)(2,1)S(1)}, bf16[640,128]{1,0:T(8,128)(2,1)S(1)}, u32[]{:S(2)}, u32[]{:S(2)}) collective-permute-start(bf16[640,128]{1,0:T(8,128)(2,1)S(1)} %pad_maximum_fusion.2.near), channel_id=1, source_target_pairs={{0,4},{4,0},{8,12},{12,8},{16,24},{20,28},{24,16},{28,20},{1,5},{5... | collective-permute-start | bytes 491528 | tf_op jit(solution)/shard_map/ppermute | solution.py:399
  37.5 13.1 %copy-start = (s32[2,12]{1,0:T(2,128)S(1)}, s32[2,12]{1,0:T(2,128)}, u32[]{:S(2)}) copy-start(s32[2,12]{1,0:T(2,128)} %pmap.3) | copy-start | bytes 292
  37.5 13.1 %copy-start.1 = (s32[3]{0:T(128)S(1)}, s32[3]{0:T(128)}, u32[]{:S(2)}) copy-start(s32[3]{0:T(128)} %live.3) | copy-start | bytes 40
  37.5 5.4 %collective-permute-start.6 = (bf16[640,128]{1,0:T(8,128)(2,1)S(1)}, bf16[640,128]{1,0:T(8,128)(2,1)S(1)}, u32[]{:S(2)}, u32[]{:S(2)}) collective-permute-start(bf16[640,128]{1,0:T(8,128)(2,1)S(1)} %slice.72), channel_id=1, source_target_pairs={{0,8},{4,12},{8,0},{12,4},{16,20},{20,16},{24,28},{28,24},{1,9},{5... | collective-permute-start | bytes 491528 | tf_op jit(solution)/shard_map/ppermute | solution.py:399
  41.7 2.8 %collective-permute-start.10 = (bf16[320,128]{1,0:T(8,128)(2,1)S(1)}, bf16[320,128]{1,0:T(8,128)(2,1)S(1)}, u32[]{:S(2)}, u32[]{:S(2)}) collective-permute-start(bf16[320,128]{1,0:T(8,128)(2,1)S(1)} %get-tuple-element.32), channel_id=1, source_target_pairs={{0,16},{16,0},{1,17},{17,1},{2,18},{18,2},{3,19},{19,3},{4,20},{20... | collective-permute-start | bytes 245768 | tf_op jit(solution)/shard_map/ppermute | solution.py:391
  43.0 5.4 %collective-permute-start.15 = (bf16[640,128]{1,0:T(8,128)(2,1)S(1)}, bf16[640,128]{1,0:T(8,128)(2,1)S(1)}, u32[]{:S(2)}, u32[]{:S(2)}) collective-permute-start(bf16[640,128]{1,0:T(8,128)(2,1)S(1)} %fusion.1), channel_id=1, source_target_pairs={{0,8},{4,12},{8,0},{12,4},{16,20},{20,16},{24,28},{28,24},{1,9},{5... | collective-permute-start | bytes 491528 | tf_op jit(solution)/shard_map/ppermute | solution.py:399
  44.6 4.7 %collective-permute-start.11 = (bf16[320,128]{1,0:T(8,128)(2,1)S(1)}, bf16[320,128]{1,0:T(8,128)(2,1)S(1)}, u32[]{:S(2)}, u32[]{:S(2)}) collective-permute-start(bf16[320,128]{1,0:T(8,128)(2,1)S(1)} %add_convert_fusion.1), channel_id=1, source_target_pairs={{0,8},{4,12},{8,0},{12,4},{16,20},{20,16},{24,28},{28,24},{1,9},{5... | collective-permute-start | bytes 245768 | tf_op jit(solution)/shard_map/ppermute | solution.py:399
  48.4 9.6 %collective-permute-start.16 = (bf16[1280,128]{1,0:T(8,128)(2,1)S(1)}, bf16[1280,128]{1,0:T(8,128)(2,1)S(1)}, u32[]{:S(2)}, u32[]{:S(2)}) collective-permute-start(bf16[1280,128]{1,0:T(8,128)(2,1)S(1)} %pad_maximum_fusion.near), channel_id=1, source_target_pairs={{0,4},{4,0},{8,12},{12,8},{16,24},{20,28},{24,16},{28,20},{1,5},{5... | collective-permute-start | bytes 983048 | tf_op jit(solution)/shard_map/ppermute | solution.py:399
  49.3 8.0 %collective-permute-start.12 = (bf16[640,128]{1,0:T(8,128)(2,1)S(1)}, bf16[640,128]{1,0:T(8,128)(2,1)S(1)}, u32[]{:S(2)}, u32[]{:S(2)}) collective-permute-start(bf16[640,128]{1,0:T(8,128)(2,1)S(1)} %pad_maximum_fusion.3.mine.near), channel_id=1, source_target_pairs={{0,4},{4,0},{8,12},{12,8},{16,24},{20,28},{24,16},{28,20},{1,5},{5... | collective-permute-start | bytes 491528 | tf_op jit(solution)/shard_map/ppermute | solution.py:399
  50.6 8.2 %collective-permute-start.14 = (bf16[640,128]{1,0:T(8,128)(2,1)S(1)}, bf16[640,128]{1,0:T(8,128)(2,1)S(1)}, u32[]{:S(2)}, u32[]{:S(2)}) collective-permute-start(bf16[640,128]{1,0:T(8,128)(2,1)S(1)} %pad_maximum_fusion.3.mine.near), channel_id=1, source_target_pairs={{0,16},{16,0},{1,17},{17,1},{2,18},{18,2},{3,19},{19,3},{4,20},{20... | collective-permute-start | bytes 491528 | tf_op jit(solution)/shard_map/ppermute | solution.py:391
  57.3 2.0 %collective-permute-start.13 = (bf16[640,128]{1,0:T(8,128)(2,1)S(1)}, bf16[640,128]{1,0:T(8,128)(2,1)S(1)}, u32[]{:S(2)}, u32[]{:S(2)}) collective-permute-start(bf16[640,128]{1,0:T(8,128)(2,1)S(1)} %collective-permute-done.12.mine), channel_id=1, source_target_pairs={{0,16},{16,0},{1,17},{17,1},{2,18},{18,2},{3,19},{19,3},{4,20},{20... | collective-permute-start | bytes 491528 | tf_op jit(solution)/shard_map/ppermute | solution.py:391

commit v4 on v3

--- a/solution.py
+++ b/solution.py
@@ -246,7 +246,23 @@
 
 
 def panel_kernel(
-    sizes, live, pmap, rhs, panel, send, keep, b_v, masked, mask, w_v, c_v, live_s, pmap_s, sems
+    sizes,
+    live,
+    pmap,
+    rhs,
+    panel,
+    pivot,
+    send,
+    keep,
+    b_v,
+    masked,
+    mask,
+    w_v,
+    d_v,
+    c_v,
+    live_s,
+    pmap_s,
+    sems,
 ):
     quarter, half, parts, update_rows = sizes
     leaf_pos = lax.axis_index("leaf")
@@ -260,6 +276,7 @@
     for i in range(parts):
         rows = pl.ds(i * step, step)
         gets.append(pltpu.make_async_copy(panel.at[rows], w_v.at[rows], sems.at[3 + i]))
+    gets.append(pltpu.make_async_copy(pivot, d_v, sems.at[3 + parts]))
     for get in gets:
         get.start()
     c_v[...] = jnp.zeros_like(c_v)
@@ -278,30 +295,23 @@
         for e in range(step // B):
             block = pmap_s[leaf_pos, i * (step // B) + e]
             c_v[pl.ds(pl.multiple_of(block * B, B), B)] = product[e * B : (e + 1) * B]
-    for k, r in enumerate(row_order(row_pos, leaf_pos)):
-        keep[pl.ds(k * half, half)] = c_v[rows_at(r * quarter + leaf_pos * half, half)]
-    for k, r in enumerate(row_order(row_pos, 1 - leaf_pos)):
-        send[pl.ds(k * half, half)] = c_v[rows_at(r * quarter + (1 - leaf_pos) * half, half)]
-
-
-def leaf_pivot_kernel(sizes, masked, pivot, after, send, keep, d_v, sems):
+    for out, side in ((keep, leaf_pos), (send, 1 - leaf_pos)):
+        near = (row_pos ^ (1 + side)) * quarter
+        out[pl.ds(0, quarter)] = c_v[rows_at(near, quarter)]
+        at = side * half
+        out[pl.ds(quarter, half)] = c_v[rows_at((row_pos ^ 3) * quarter + at, half)]
+        out[pl.ds(quarter + half, half)] = c_v[rows_at(row_pos * quarter + at, half)]
+    gets[3 + parts].wait()
+
+
+def leaf_pivot_kernel(sizes, masked, d_v, after, send, keep):
     quarter, half = sizes
     order = row_order(lax.axis_index("row"), lax.axis_index("leaf"))
-    gets = []
+    right = masked[...]
     for k in (2, 3, 0, 1):
-        rows = rows_at(order[k] * quarter, quarter)
-        gets.append(pltpu.make_async_copy(pivot.at[rows], d_v.at[rows], sems.at[k]))
-    rows = pl.ds(4 * quarter, 4 * half)
-    gets.append(pltpu.make_async_copy(pivot.at[rows], d_v.at[rows], sems.at[4]))
-    for get in gets:
-        get.start()
-    right = masked[...]
-    for get, k in zip(gets, (2, 3, 0, 1)):
-        get.wait()
         out = keep if k < 2 else send
         product = mm(d_v[rows_at(order[k] * quarter, quarter)], right)
         out[pl.ds((k % 2) * quarter, quarter)] = product.astype(BF)
-    gets[-1].wait()
 
 
 def scatter_kernel(sizes, live, pmap, w_v, after, out, live_s, pmap_s, sems):
@@ -325,66 +335,42 @@
         out[pl.ds(pl.multiple_of(block * B, B), B)] = jnp.where(alive, value, jnp.zeros_like(value))
 
 
-def root_pivot_kernel(sizes, own, other, d_v, send, keep, q_v):
-    quarter, half, base = sizes
-    leaf_pos = lax.axis_index("leaf")
-    order = row_order(lax.axis_index("row"), leaf_pos)
-    q_v[rows_at(leaf_pos * half, half)] = own[...]
-    q_v[rows_at((1 - leaf_pos) * half, half)] = other[...]
-    right = q_v[...]
-    for k in range(4):
-        out = keep if k < 2 else send
-        product = mm(d_v[rows_at(base + order[k] * half, half)], right)
-        out[pl.ds((k % 2) * half, half)] = product.astype(BF)
-
-
-def root_transposed_kernel(sizes, near, far, d_v, keep, send, y_v, s_v):
-    quarter, half, base = sizes
-    leaf_pos = lax.axis_index("leaf")
-    order = row_order(lax.axis_index("row"), leaf_pos)
-    for k in range(4):
-        part = (near if k < 2 else far)[pl.ds((k % 2) * half, half)]
-        y_v[rows_at(order[k] * half, half)] = part
-    s_v[...] = mm(y_v[...].T, d_v[pl.ds(base, 4 * half)]).T
-    keep[...] = s_v[rows_at(leaf_pos * half, half)]
-    send[...] = s_v[rows_at((1 - leaf_pos) * half, half)].astype(BF)
-
-
-def leaf_transposed_kernel(sizes, near, far, d_v, mask, total, y_v):
+def root_pivot_kernel(sizes, own, other, d_v, out):
+    base, rows = sizes
+    right = -(own[...].astype(F32) + other[...].astype(F32))
+    out[...] = mm(d_v[pl.ds(base, rows)], right.astype(BF)).astype(BF)
+
+
+def root_transposed_kernel(sizes, y, d_v, out):
+    base, rows = sizes
+    out[...] = mm(y[...].T, d_v[pl.ds(base, rows)]).T.astype(BF)
+
+
+def leaf_transposed_kernel(sizes, near, far, d_v, mask, root_rows, panel_rows, total, y_v):
     quarter, half = sizes
-    order = row_order(lax.axis_index("row"), lax.axis_index("leaf"))
+    row_pos = lax.axis_index("row")
+    order = row_order(row_pos, lax.axis_index("leaf"))
     for k in range(4):
         part = (near if k < 2 else far)[pl.ds((k % 2) * quarter, quarter)]
         y_v[rows_at(order[k] * quarter, quarter)] = part
     value = mm(y_v[...].T, d_v[pl.ds(0, 4 * quarter)])
-    total[...] = jnp.where(mask[...].astype(F32).T > 0.0, value, 0.0)
-
-
-def place(sizes, which, mine, theirs, s_v, w_v, panel_rows):
+    value = jnp.where(mask[...].astype(F32).T > 0.0, value, 0.0)
+    own = panel_rows[rows_at(row_pos * quarter, quarter)]
+    total[...] = value - mm(root_rows[...].T, own)
+
+
+def last_kernel(sizes, mine, theirs, mine_far, theirs_far, total, panel_rows, root_rows, out):
     quarter, half = sizes
     leaf_pos = lax.axis_index("leaf")
     row_pos = lax.axis_index("row")
-    at = 0
-    for source, side in ((mine, leaf_pos), (theirs, 1 - leaf_pos)):
-        order = row_order(row_pos, side)
-        for k in range(2):
-            rows = pl.ds(at, half)
-            s_v[rows] = source[pl.ds(k * half, half)]
-            w_v[rows] = panel_rows[rows_at(order[which + k] * quarter + side * half, half)]
-            at += half
-
-
-def early_kernel(sizes, mine, theirs, total, panel_rows, out, s_v, w_v):
-    place(sizes, 0, mine, theirs, s_v, w_v, panel_rows)
-    out[...] = total[...] - mm(s_v[...].T, w_v[...])
-
-
-def last_kernel(sizes, mine, theirs, total, panel_rows, near, out, s_v, w_v):
-    quarter, half = sizes
-    place(sizes, 2, mine, theirs, s_v, w_v, panel_rows)
-    value = total[...] - mm(s_v[...].T, w_v[...])
+    value = total[...]
+    for near, far, side in ((mine, mine_far, leaf_pos), (theirs, theirs_far, 1 - leaf_pos)):
+        rows = rows_at((row_pos ^ (1 + side)) * quarter, quarter)
+        value = value - mm(near[...].T, panel_rows[rows])
+        rows = rows_at((row_pos ^ 3) * quarter + side * half, half)
+        value = value - mm(far[...].T, panel_rows[rows])
     out[pl.ds(0, quarter)] = value.T.astype(BF)
-    out[pl.ds(quarter, half)] = near[pl.ds(0, half)]
+    out[pl.ds(quarter, half)] = root_rows[rows_at(leaf_pos * half, half)]
 
 
 def leaf_swap(value):
@@ -394,7 +380,7 @@
 def row_swap(value, phase):
     route = []
     for leaf in range(2):
-        apart = (1 + leaf) if phase == 0 else (2 - leaf)
+        apart = (1 + leaf, 2 - leaf, 3)[phase]
         route += [(4 * leaf + r, 4 * leaf + (r ^ apart)) for r in range(4)]
     return lax.ppermute(value, ("leaf", "row"), route)
 
@@ -409,11 +395,13 @@
     half = quarter // 2
     front = 4 * quarter
     updates = parent_map.shape[1] * B
-    barrier = lax.optimization_barrier
+    leaf_pos = lax.axis_index("leaf")
+    row_pos = lax.axis_index("row")
+    after = lambda value, other: lax.optimization_barrier((value, other))[0]
     smem = [pltpu.SMEM(live.shape, jnp.int32), pltpu.SMEM(parent_map.shape, jnp.int32)]
 
     parts = 4 if updates % (4 * B) == 0 else 1
-    sent, keep, b_v, masked, mask, w_v = call(
+    sent, keep, b_v, masked, mask, w_v, d_v = call(
         functools.partial(panel_kernel, (quarter, half, parts, updates)),
         (
             kept(4 * half, columns),
@@ -422,66 +410,51 @@
             kept(quarter, columns),
             kept(quarter, columns),
             kept(updates, quarter),
+            kept(front + 4 * half, quarter),
         ),
-        [ANY] * 4,
-        [pltpu.VMEM((front, columns), BF), *smem, pltpu.SemaphoreType.DMA((3 + parts,))],
-        62_100_000,
+        [ANY] * 5,
+        [pltpu.VMEM((front, columns), BF), *smem, pltpu.SemaphoreType.DMA((4 + parts,))],
+        57_100_000,
         2 * updates * quarter * columns,
         2 * updates * quarter,
-    )(live, parent_map, rhs, panel)
+    )(live, parent_map, rhs, panel, pivot_inverse)
     got = leaf_swap(sent)
-    away = added(keep[quarter:], got[quarter:]).astype(BF)
-    home = added(keep[:quarter], got[:quarter])
-    home = home + row_swap(away, 0).astype(F32)
-    incoming = home[:half] + row_swap(home[half:].astype(BF), 1).astype(F32)
-    right_side = (b_v[quarter:].astype(F32) - incoming).astype(BF)
-    right_other = leaf_swap(right_side)
-
-    send_e, keep_e, d_v = call(
+    update = added(keep, got)
+    away_far = update[quarter : quarter + half].astype(BF)
+    away_near = update[:quarter].astype(BF)
+    from_far = row_swap(away_far, 2)
+    from_near = row_swap(away_near, 0)
+
+    send_e, keep_e = call(
         functools.partial(leaf_pivot_kernel, (quarter, half)),
-        (kept(2 * quarter, columns), kept(2 * quarter, columns), kept(front + 4 * half, quarter)),
-        [VMEM, ANY, ANY],
-        [pltpu.SemaphoreType.DMA((5,))],
-        48 * MIB,
+        (kept(2 * quarter, columns), kept(2 * quarter, columns)),
+        [VMEM, VMEM, ANY],
+        [],
+        16 * MIB,
         2 * front * quarter * columns,
         2 * front * quarter,
-    )(masked, pivot_inverse, away)
-
-    send_e, home = barrier((send_e, home))
-    send_e = barrier((send_e, incoming))[0]
-    home_e = keep_e.astype(F32) + row_swap(send_e, 0).astype(F32)
-
-    send, keep = call(
-        functools.partial(root_pivot_kernel, (quarter, half, front)),
-        (kept(quarter, columns), kept(quarter, columns)),
+    )(masked, d_v, away_near)
+    got_e = row_swap(send_e, 0)
+    from_near = after(from_near, send_e)
+
+    term = update[quarter + half :] + from_far.astype(F32) - b_v[quarter:].astype(F32)
+    lower = jnp.where(leaf_pos == 0, term, 0.0)
+    upper = jnp.where(leaf_pos == 0, 0.0, term)
+    negated = (from_near.astype(F32) + jnp.concatenate([lower, upper], 0)).astype(BF)
+    negated_other = leaf_swap(negated)
+
+    partial = call(
+        functools.partial(root_pivot_kernel, (front, 4 * half)),
+        kept(4 * half, columns),
         [VMEM, VMEM, VMEM],
-        [pltpu.VMEM((quarter, columns), BF)],
+        [],
         16 * MIB,
         front * quarter * columns,
         front * quarter,
-    )(right_side, right_other, d_v)
-    home = keep.astype(F32) + row_swap(send, 0).astype(F32)
-    root_forward = (home[:half] + row_swap(home[half:].astype(BF), 1).astype(F32)).astype(BF)
-
-    away_e = barrier((home_e[quarter:].astype(BF), home))[0]
-    leaf_forward = home_e[:quarter] + row_swap(away_e, 1).astype(F32)
-    leaf_forward = jnp.where(mask > 0, leaf_forward, 0.0).astype(BF)
-
-    near = jnp.concatenate([root_forward, row_swap(root_forward, 1)], 0)
-    far = row_swap(near, 0)
-    root_keep, root_send = call(
-        functools.partial(root_transposed_kernel, (quarter, half, front)),
-        (kept(half, columns, F32), kept(half, columns)),
-        [VMEM, VMEM, VMEM],
-        [pltpu.VMEM((4 * half, columns), BF), pltpu.VMEM((quarter, columns), F32)],
-        16 * MIB,
-        front * quarter * columns,
-        front * quarter,
-    )(near, far, d_v)
-    root_value = (root_keep + leaf_swap(root_send).astype(F32)).astype(BF)
-
-    near_e = jnp.concatenate([leaf_forward, row_swap(leaf_forward, 1)], 0)
-    far_e = row_swap(near_e, 0)
+    )(negated, negated_other, d_v)
+    home_e = added(keep_e, got_e)
+    away_e = home_e[quarter:].astype(BF)
+    got_e = row_swap(away_e, 1)
     panel_rows = call(
         functools.partial(scatter_kernel, (quarter, updates)),
         kept(front, quarter),
@@ -490,41 +463,50 @@
         16 * MIB,
         0,
         4 * front * quarter,
-    )(live, parent_map, w_v, right_side)
+    )(live, parent_map, w_v, away_e)
+    partial = added(partial, after(row_swap(partial, 0), panel_rows))
+    root_forward = (partial + row_swap(partial.astype(BF), 1).astype(F32)).astype(BF)
+    leaf_forward = home_e[:quarter] + got_e.astype(F32)
+    leaf_forward = jnp.where(mask > 0, leaf_forward, 0.0).astype(BF)
+
+    part = call(
+        functools.partial(root_transposed_kernel, (front, 4 * half)),
+        kept(quarter, columns),
+        [VMEM, VMEM],
+        [],
+        16 * MIB,
+        front * quarter * columns,
+        front * quarter,
+    )(root_forward, d_v)
+    root_rows = added(part, leaf_swap(part)).astype(BF)
+
+    near_e = jnp.concatenate([leaf_forward, row_swap(leaf_forward, 1)], 0)
+    far_e = row_swap(near_e, 0)
+    root_piece = lax.dynamic_slice_in_dim(root_forward, row_pos * half, half, 0)
+    forward = jnp.concatenate([leaf_forward, root_piece], 0)
+
+    near = row_swap(root_rows, 0)
+    far = row_swap(lax.dynamic_slice_in_dim(root_rows, leaf_pos * half, half, 0), 2)
     total = call(
         functools.partial(leaf_transposed_kernel, (quarter, half)),
         kept(columns, quarter, F32),
-        [VMEM] * 4,
+        [VMEM] * 6,
         [pltpu.VMEM((front, columns), BF)],
         16 * MIB,
         2 * front * quarter * columns,
         2 * front * quarter,
-    )(near_e, far_e, d_v, mask)
-    forward = jnp.concatenate([leaf_forward, root_forward], 0)
-
-    near = jnp.concatenate([root_value, row_swap(root_value, 1)], 0)
-    far = row_swap(near, 0)
+    )(near_e, far_e, d_v, mask, root_rows, panel_rows)
     near_other = leaf_swap(near)
-    scratch = [pltpu.VMEM((4 * half, columns), BF), pltpu.VMEM((4 * half, quarter), BF)]
-    total = call(
-        functools.partial(early_kernel, (quarter, half)),
-        kept(columns, quarter, F32),
-        [VMEM] * 4,
-        scratch,
-        16 * MIB,
-        front * quarter * columns,
-        front * quarter,
-    )(near, near_other, total, panel_rows)
     far_other = leaf_swap(far)
     backward = call(
         functools.partial(last_kernel, (quarter, half)),
         stored(quarter + half, columns),
-        [VMEM] * 5,
-        scratch,
+        [VMEM] * 7,
+        [],
         16 * MIB,
         front * quarter * columns,
         front * quarter,
-    )(far, far_other, total, panel_rows, near)
+    )(near, near_other, far, far_other, total, panel_rows, root_rows)
     return forward, backward
 
 

time: 60.7 us -> 56.5 us (0.931)
  local copies, waits for them, and re-layouts: 0.05 us -> 10.1 us
  starting transfers between devices: 21.4 us -> 13.4 us
  waiting for transfers between devices: 26.8 us -> 22.1 us
  Pallas kernels: 10.3 us -> 8.5 us
    unnamed x4 -> x24, local copies, waits for them, and re-layouts: 0.01 us -> 10 us
    ppermute x12 -> x10, starting transfers between devices: 20.7 us -> 12.8 us  [row_swap(): return lax.ppermute(value, ('leaf', 'row'), route)]
    ppermute x12 -> x10, waiting for transfers between devices: 25.5 us -> 18.7 us  [row_swap(): return lax.ppermute(value, ('leaf', 'row'), route)]
    pallas_call x1, Pallas kernels: 3.17 us -> 1.01 us  [two_levels(): call(functools.partial(leaf_pivot_kernel, (quarter, half)), (kept(2 * qua...]
    ppermute x5, waiting for transfers between devices: 1.27 us -> 3.37 us  [leaf_swap(): return lax.ppermute(value, 'leaf', [(0, 1), (1, 0)])]
    pallas_call x3 -> x2, Pallas kernels: 1.68 us -> 1.12 us  [the longest x1 0.6 us: two_levels(): call(functools.partial(root_pivot_kernel, (front, 4 * half)), kept(4 * ha...]
  transfers between devices with their start and end apart: 17 -> 15, of which waited for: 11 -> 8; matrix products, arithmetic and copies ran while one was open for 2% -> 2% of each run, Pallas kernels for 10% -> 7%
where the time goes in v4:
time: 56.5 us; the launch traced here: 56.2 us
  waiting for transfers between devices  22.1 us (39%)
  starting transfers between devices  13.4 us (24%)
  local copies, waits for them, and re-layouts  10.1 us (18%)
  Pallas kernels  8.5 us (15%)
  other arithmetic  1.3 us (2%)
  between operations  0.88 us (2%)
    ppermute x10, waiting for transfers between devices, row_swap(): return lax.ppermute(value, ('leaf', 'row'), route)  18.7 us
    ppermute x10, starting transfers between devices, row_swap(): return lax.ppermute(value, ('leaf', 'row'), route)  12.8 us
    unnamed x24, local copies, waits for them, and re-layouts  10 us
    ppermute x5, waiting for transfers between devices, leaf_swap(): return lax.ppermute(value, 'leaf', [(0, 1), (1, 0)])  3.37 us
    pallas_call x1, Pallas kernels, two_levels(): call(functools.partial(panel_kernel, (quarter, half, parts, updates)), (k...  3.21 us
    pallas_call x1, Pallas kernels, two_levels(): call(functools.partial(last_kernel, (quarter, half)), stored(quarter + ha...  1.48 us
  transfers between devices with their start and end apart: 15, of which 8 were waited for; matrix products, arithmetic and copies ran while one was open for 2% of the time, Pallas kernels for 7%

profile of v4, /device:TPU:0, one launch (start us, length us, event | category | flops | bytes accessed | tf_op | source)
XLA Modules:
  0.0 56.2 jit_solution(5615176036102418360)
XLA Ops:
  0.6 3.2 %shard_map.68 = (bf16[1280,128]{1,0:T(8,128)(2,1)S(1)}, bf16[1280,128]{1,0:T(8,128)(2,1)S(1)}, bf16[960,128]{1,0:T(8,128)(2,1)S(1)}, bf16[640,128]{1,0:T(8,128)(...) custom-call(s32[3]{0:T(128)} %live.3, s32[2,12]{1,0:T(2,128)} %pmap.3, ...), custom_call_target="tpu_custom_call" | custom-call | flops 251658240 | bytes 1966080 | tf_op jit(solution)/shard_map/pallas_call | solution.py:404
  3.9 2.2 %copy-done = bf16[3840,640]{1,0:T(8,128)(2,1)} copy-done((bf16[3840,640]{1,0:T(8,128)(2,1)}, bf16[3840,640]{1,0:T(8,128)(2,1)S(1)}, u32[]{:S(2)}) %copy-start) | copy-done | bytes 4915224
  6.1 1.3 %copy-done.6 = bf16[1536,640]{1,0:T(8,128)(2,1)} copy-done((bf16[1536,640]{1,0:T(8,128)(2,1)}, bf16[1536,640]{1,0:T(8,128)(2,1)S(1)}, u32[]{:S(2)}) %copy-start.6) | copy-done | bytes 1966104
  7.4 0.5 collective-permute-start
  7.8 1.3 %collective-permute-done = bf16[1280,128]{1,0:T(8,128)(2,1)S(1)} collective-permute-done((bf16[1280,128]{1,0:T(8,128)(2,1)S(1)}, bf16[1280,128]{1,0:T(8,128)(2,1)S(1)}, u32[]{:S(2)}, u32[]{:S(2)}) %collective-permute-start) | collective-permute-done | bytes 327712 | tf_op jit(solution)/shard_map/ppermute | solution.py:377
  9.2 3.9 %collective-permute-start.4 = (bf16[320,128]{1,0:T(8,128)(2,1)S(1)}, bf16[320,128]{1,0:T(8,128)(2,1)S(1)}, u32[]{:S(2)}, u32[]{:S(2)}) collective-permute-start(bf16[320,128]{1,0:T(8,128)(2,1)S(1)} %slice.31), channel_id=1, source_target_pairs={{0,12},{4,8},{8,4},{12,0},{16,28},{20,24},{24,20},{28,16},{1,13},{... | collective-permute-start | bytes 245768 | tf_op jit(solution)/shard_map/ppermute | solution.py:385
  13.1 0.6 %collective-permute-start.3 = (bf16[640,128]{1,0:T(8,128)(2,1)S(1)}, bf16[640,128]{1,0:T(8,128)(2,1)S(1)}, u32[]{:S(2)}, u32[]{:S(2)}) collective-permute-start(bf16[640,128]{1,0:T(8,128)(2,1)S(1)} %slice.27.after), channel_id=1, source_target_pairs={{0,4},{4,0},{8,12},{12,8},{16,24},{20,28},{24,16},{28,20},{1,5},{5... | collective-permute-start | bytes 491528 | tf_op jit(solution)/shard_map/ppermute | solution.py:385
  13.7 2.4 %copy-done.1 = bf16[3840,640]{1,0:T(8,128)(2,1)S(1)} copy-done((bf16[3840,640]{1,0:T(8,128)(2,1)S(1)}, bf16[3840,640]{1,0:T(8,128)(2,1)}, u32[]{:S(2)}) %copy-start.1) | copy-done | bytes 4915224
  16.1 1.0 %shard_map.69 = (bf16[1280,128]{1,0:T(8,128)(2,1)S(1)}, bf16[1280,128]{1,0:T(8,128)(2,1)S(1)}) custom-call(bf16[640,128]{1,0:T(8,128)(2,1)S(1)} %get-tuple-element.14.masked, bf16[3840,640]{1,0:T(8,128)(2,1)S(1)} %copy-done.1, bf16[640,128]{1,0:T(8,128)(2,1)S(1)} %slice.27.after), custom_call_target="tpu_custom_call" | custom-call | flops 419430400 | bytes 3276800 | tf_op jit(solution)/shard_map/pallas_call | solution.py:428
  17.1 1.6 %collective-permute-start.1 = (bf16[1280,128]{1,0:T(8,128)(2,1)S(1)}, bf16[1280,128]{1,0:T(8,128)(2,1)S(1)}, u32[]{:S(2)}, u32[]{:S(2)}) collective-permute-start(bf16[1280,128]{1,0:T(8,128)(2,1)S(1)} %get-tuple-element.19), channel_id=1, source_target_pairs={{0,4},{4,0},{8,12},{12,8},{16,24},{20,28},{24,16},{28,20},{1,5},{5... | collective-permute-start | bytes 983048 | tf_op jit(solution)/shard_map/ppermute | solution.py:385
  18.9 1.4 %collective-permute-done.5.other = bf16[640,128]{1,0:T(8,128)(2,1)S(1)} collective-permute-done((bf16[640,128]{1,0:T(8,128)(2,1)S(1)}, bf16[640,128]{1,0:T(8,128)(2,1)S(1)}, u32[]{:S(2)}, u32[]{:S(2)}) %collective-permute-start.5) | collective-permute-done | bytes 163872 | tf_op jit(solution)/shard_map/ppermute | solution.py:377
  20.3 0.6 %shard_map.70 = bf16[1280,128]{1,0:T(8,128)(2,1)S(1)} custom-call(bf16[640,128]{1,0:T(8,128)(2,1)S(1)} %fusion.3.own, bf16[640,128]{1,0:T(8,128)(2,1)S(1)} %collective-permute-done.5.other, bf16[3840,640]{1,0:T(8,128)(2,1)S(1)} %copy-done.2), custom_call_target="tpu_custom_call" | custom-call | flops 209715200 | bytes 1638400 | tf_op jit(solution)/shard_map/pallas_call | solution.py:446
  20.9 0.7 %collective-permute-start.6 = (bf16[1280,128]{1,0:T(8,128)(2,1)S(1)}, bf16[1280,128]{1,0:T(8,128)(2,1)S(1)}, u32[]{:S(2)}, u32[]{:S(2)}) collective-permute-start(bf16[1280,128]{1,0:T(8,128)(2,1)S(1)} %shard_map.70), channel_id=1, source_target_pairs={{0,4},{4,0},{8,12},{12,8},{16,24},{20,28},{24,16},{28,20},{1,5},{5... | collective-permute-start | bytes 983048 | tf_op jit(solution)/shard_map/ppermute | solution.py:385
  21.6 2.7 %collective-permute-done.1 = bf16[1280,128]{1,0:T(8,128)(2,1)S(1)} collective-permute-done((bf16[1280,128]{1,0:T(8,128)(2,1)S(1)}, bf16[1280,128]{1,0:T(8,128)(2,1)S(1)}, u32[]{:S(2)}, u32[]{:S(2)}) %collective-permute-start.1) | collective-permute-done | bytes 327712 | tf_op jit(solution)/shard_map/ppermute | solution.py:385
  24.4 0.8 %shard_map.71.panel_rows = bf16[2560,640]{1,0:T(8,128)(2,1)S(1)} custom-call(s32[3]{0:T(128)S(1)} %copy-done.9, s32[2,12]{1,0:T(2,128)S(1)} %copy-done.8, bf16[1536,640]{1,0:T(8,128)(2,1)S(1)} %copy-done.7, bf16[640,128]{1,0:T(8,128)(2,1)S(1)} %slice.50.after), custom_call_target="tpu_custom_call" | custom-call | bytes 6553600 | tf_op jit(solution)/shard_map/pallas_call | solution.py:458
  25.1 1.7 %copy-done.4 = bf16[2560,640]{1,0:T(8,128)(2,1)} copy-done((bf16[2560,640]{1,0:T(8,128)(2,1)}, bf16[2560,640]{1,0:T(8,128)(2,1)S(1)}, u32[]{:S(2)}) %copy-start.4) | copy-done | bytes 3276824
  26.8 1.2 %collective-permute-done.6 = bf16[1280,128]{1,0:T(8,128)(2,1)S(1)} collective-permute-done((bf16[1280,128]{1,0:T(8,128)(2,1)S(1)}, bf16[1280,128]{1,0:T(8,128)(2,1)S(1)}, u32[]{:S(2)}, u32[]{:S(2)}) %collective-permute-start.6) | collective-permute-done | bytes 327712 | tf_op jit(solution)/shard_map/ppermute | solution.py:385
  28.1 0.6 %collective-permute-start.7 = (bf16[1280,128]{1,0:T(8,128)(2,1)S(1)}, bf16[1280,128]{1,0:T(8,128)(2,1)S(1)}, u32[]{:S(2)}, u32[]{:S(2)}) collective-permute-start(bf16[1280,128]{1,0:T(8,128)(2,1)S(1)} %fusion), channel_id=1, source_target_pairs={{0,8},{4,12},{8,0},{12,4},{16,20},{20,16},{24,28},{28,24},{1,9},{5... | collective-permute-start | bytes 983048 | tf_op jit(solution)/shard_map/ppermute | solution.py:385
  28.7 1.5 %collective-permute-start.2 = (bf16[640,128]{1,0:T(8,128)(2,1)S(1)}, bf16[640,128]{1,0:T(8,128)(2,1)S(1)}, u32[]{:S(2)}, u32[]{:S(2)}) collective-permute-start(bf16[640,128]{1,0:T(8,128)(2,1)S(1)} %slice.50.after), channel_id=1, source_target_pairs={{0,8},{4,12},{8,0},{12,4},{16,20},{20,16},{24,28},{28,24},{1,9},{5... | collective-permute-start | bytes 491528 | tf_op jit(solution)/shard_map/ppermute | solution.py:385
  30.2 5.0 %collective-permute-done.7 = bf16[1280,128]{1,0:T(8,128)(2,1)S(1)} collective-permute-done((bf16[1280,128]{1,0:T(8,128)(2,1)S(1)}, bf16[1280,128]{1,0:T(8,128)(2,1)S(1)}, u32[]{:S(2)}, u32[]{:S(2)}) %collective-permute-start.7) | collective-permute-done | bytes 327712 | tf_op jit(solution)/shard_map/ppermute | solution.py:385
  35.4 2.4 %copy-done.3 = bf16[3840,640]{1,0:T(8,128)(2,1)S(1)} copy-done((bf16[3840,640]{1,0:T(8,128)(2,1)S(1)}, bf16[3840,640]{1,0:T(8,128)(2,1)}, u32[]{:S(2)}) %copy-start.3) | copy-done | bytes 4915224
  37.8 0.5 shard_map.72
  38.5 0.6 %collective-permute-start.13 = (bf16[640,128]{1,0:T(8,128)(2,1)S(1)}, bf16[640,128]{1,0:T(8,128)(2,1)S(1)}, u32[]{:S(2)}, u32[]{:S(2)}) collective-permute-start(bf16[640,128]{1,0:T(8,128)(2,1)S(1)} %fusion.2), channel_id=1, source_target_pairs={{0,8},{4,12},{8,0},{12,4},{16,20},{20,16},{24,28},{28,24},{1,9},{5... | collective-permute-start | bytes 491528 | tf_op jit(solution)/shard_map/ppermute | solution.py:385
  39.0 0.7 %collective-permute-done.8 = bf16[640,128]{1,0:T(8,128)(2,1)S(1)} collective-permute-done((bf16[640,128]{1,0:T(8,128)(2,1)S(1)}, bf16[640,128]{1,0:T(8,128)(2,1)S(1)}, u32[]{:S(2)}, u32[]{:S(2)}) %collective-permute-start.8) | collective-permute-done | bytes 163872 | tf_op jit(solution)/shard_map/ppermute | solution.py:377
  39.8 1.3 %collective-permute-start.9 = (bf16[640,128]{1,0:T(8,128)(2,1)S(1)}, bf16[640,128]{1,0:T(8,128)(2,1)S(1)}, u32[]{:S(2)}, u32[]{:S(2)}) collective-permute-start(bf16[640,128]{1,0:T(8,128)(2,1)S(1)} %add_convert_fusion.1.root_rows), channel_id=1, source_target_pairs={{0,4},{4,0},{8,12},{12,8},{16,24},{20,28},{24,16},{28,20},{1,5},{5... | collective-permute-start | bytes 491528 | tf_op jit(solution)/shard_map/ppermute | solution.py:385
  41.1 3.9 %collective-permute-done.13 = bf16[640,128]{1,0:T(8,128)(2,1)S(1)} collective-permute-done((bf16[640,128]{1,0:T(8,128)(2,1)S(1)}, bf16[640,128]{1,0:T(8,128)(2,1)S(1)}, u32[]{:S(2)}, u32[]{:S(2)}) %collective-permute-start.13) | collective-permute-done | bytes 163872 | tf_op jit(solution)/shard_map/ppermute | solution.py:385
  45.1 1.4 %collective-permute-start.14 = (bf16[1280,128]{1,0:T(8,128)(2,1)S(1)}, bf16[1280,128]{1,0:T(8,128)(2,1)S(1)}, u32[]{:S(2)}, u32[]{:S(2)}) collective-permute-start(bf16[1280,128]{1,0:T(8,128)(2,1)S(1)} %pad_maximum_fusion.near), channel_id=1, source_target_pairs={{0,4},{4,0},{8,12},{12,8},{16,24},{20,28},{24,16},{28,20},{1,5},{5... | collective-permute-start | bytes 983048 | tf_op jit(solution)/shard_map/ppermute | solution.py:385
  46.5 0.6 %collective-permute-start.11 = (bf16[320,128]{1,0:T(8,128)(2,1)S(1)}, bf16[320,128]{1,0:T(8,128)(2,1)S(1)}, u32[]{:S(2)}, u32[]{:S(2)}) collective-permute-start(bf16[320,128]{1,0:T(8,128)(2,1)S(1)} %constant_dynamic-slice_fusion), channel_id=1, source_target_pairs={{0,12},{4,8},{8,4},{12,0},{16,28},{20,24},{24,20},{28,16},{1,13},{... | collective-permute-start | bytes 245768 | tf_op jit(solution)/shard_map/ppermute | solution.py:385
  47.1 5.9 %collective-permute-done.11.mine_far = bf16[320,128]{1,0:T(8,128)(2,1)S(1)} collective-permute-done((bf16[320,128]{1,0:T(8,128)(2,1)S(1)}, bf16[320,128]{1,0:T(8,128)(2,1)S(1)}, u32[]{:S(2)}, u32[]{:S(2)}) %collective-permute-start.11) | collective-permute-done | bytes 81952 | tf_op jit(solution)/shard_map/ppermute | solution.py:385
  53.0 0.7 %pad_maximum_fusion.1 = bf16[960,128]{1,0:T(8,128)(2,1)} fusion(bf16[320,128]{1,0:T(8,128)(2,1)S(1)} %constant_dynamic-slice_fusion.1, bf16[640,128]{1,0:T(8,128)(2,1)S(1)} %fusion.2), kind=kLoop, calls=%fused_computation.13 | loop fusion | flops 491520 | bytes 491520 | tf_op jit(solution)/shard_map/concatenate | solution.py:486
  53.8 0.9 %shard_map.73.total = f32[128,640]{1,0:T(8,128)S(1)} custom-call(bf16[1280,128]{1,0:T(8,128)(2,1)S(1)} %pad_maximum_fusion.near, bf16[1280,128]{1,0:T(8,128)(2,1)S(1)} %collective-permute-done.14.far, bf16[3840,640]{1,0:T(8,128)(2,1)S(1)} %bitcast.1, bf16[640,128]{1,0:T(8,128)(2,1)S(1)} %get-tuple-element.13.mask, ...), custom_call_target="tpu_custom_call" | custom-call | flops 419430400 | bytes 3276800 | tf_op jit(solution)/shard_map/pallas_call | solution.py:490
  54.7 1.5 %shard_map.74 = bf16[960,128]{1,0:T(8,128)(2,1)} custom-call(bf16[640,128]{1,0:T(8,128)(2,1)S(1)} %collective-permute-done.9.mine, bf16[640,128]{1,0:T(8,128)(2,1)S(1)} %collective-permute-done.10.theirs, bf16[320,128]{1,0:T(8,128)(2,1)S(1)} %collective-permute-done.11.mine_far, bf16[320,128]{1,0:T(8,128)(2,1)S(1)} %collective-permute-done.12.theirs_far, ...), custom_call_target="tpu_custom_call" | custom-call | flops 209715200 | bytes 1638400 | tf_op jit(solution)/shard_map/pallas_call | solution.py:501
  (45 shorter events, 0.9 us)
Async XLA Ops:
  3.8 2.2 %copy-start = (bf16[3840,640]{1,0:T(8,128)(2,1)}, bf16[3840,640]{1,0:T(8,128)(2,1)S(1)}, u32[]{:S(2)}) copy-start(bf16[3840,640]{1,0:T(8,128)(2,1)S(1)} %get-tuple-element.15.d_v) | copy-start | bytes 14745604
  6.0 1.3 %copy-start.6 = (bf16[1536,640]{1,0:T(8,128)(2,1)}, bf16[1536,640]{1,0:T(8,128)(2,1)S(1)}, u32[]{:S(2)}) copy-start(bf16[1536,640]{1,0:T(8,128)(2,1)S(1)} %get-tuple-element.22.w_v) | copy-start | bytes 5898244
  7.4 1.7 %collective-permute-start = (bf16[1280,128]{1,0:T(8,128)(2,1)S(1)}, bf16[1280,128]{1,0:T(8,128)(2,1)S(1)}, u32[]{:S(2)}, u32[]{:S(2)}) collective-permute-start(bf16[1280,128]{1,0:T(8,128)(2,1)S(1)} %get-tuple-element.17), channel_id=1, source_target_pairs={{0,16},{16,0},{1,17},{17,1},{2,18},{18,2},{3,19},{19,3},{4,20},{20... | collective-permute-start | bytes 983048 | tf_op jit(solution)/shard_map/ppermute | solution.py:377
  9.2 9.5 %collective-permute-start.4 = (bf16[320,128]{1,0:T(8,128)(2,1)S(1)}, bf16[320,128]{1,0:T(8,128)(2,1)S(1)}, u32[]{:S(2)}, u32[]{:S(2)}) collective-permute-start(bf16[320,128]{1,0:T(8,128)(2,1)S(1)} %slice.31), channel_id=1, source_target_pairs={{0,12},{4,8},{8,4},{12,0},{16,28},{20,24},{24,20},{28,16},{1,13},{... | collective-permute-start | bytes 245768 | tf_op jit(solution)/shard_map/ppermute | solution.py:385
  13.1 5.6 %collective-permute-start.3 = (bf16[640,128]{1,0:T(8,128)(2,1)S(1)}, bf16[640,128]{1,0:T(8,128)(2,1)S(1)}, u32[]{:S(2)}, u32[]{:S(2)}) collective-permute-start(bf16[640,128]{1,0:T(8,128)(2,1)S(1)} %slice.27.after), channel_id=1, source_target_pairs={{0,4},{4,0},{8,12},{12,8},{16,24},{20,28},{24,16},{28,20},{1,5},{5... | collective-permute-start | bytes 491528 | tf_op jit(solution)/shard_map/ppermute | solution.py:385
  13.7 2.4 %copy-start.1 = (bf16[3840,640]{1,0:T(8,128)(2,1)S(1)}, bf16[3840,640]{1,0:T(8,128)(2,1)}, u32[]{:S(2)}) copy-start(bf16[3840,640]{1,0:T(8,128)(2,1)} %copy-done) | copy-start | bytes 14745604
  16.1 4.2 %copy-start.2 = (bf16[3840,640]{1,0:T(8,128)(2,1)S(1)}, bf16[3840,640]{1,0:T(8,128)(2,1)}, u32[]{:S(2)}) copy-start(bf16[3840,640]{1,0:T(8,128)(2,1)} %copy-done) | copy-start | bytes 14745604
  17.1 7.1 %collective-permute-start.1 = (bf16[1280,128]{1,0:T(8,128)(2,1)S(1)}, bf16[1280,128]{1,0:T(8,128)(2,1)S(1)}, u32[]{:S(2)}, u32[]{:S(2)}) collective-permute-start(bf16[1280,128]{1,0:T(8,128)(2,1)S(1)} %get-tuple-element.19), channel_id=1, source_target_pairs={{0,4},{4,0},{8,12},{12,8},{16,24},{20,28},{24,16},{28,20},{1,5},{5... | collective-permute-start | bytes 983048 | tf_op jit(solution)/shard_map/ppermute | solution.py:385
  18.8 5.6 %copy-start.7 = (bf16[1536,640]{1,0:T(8,128)(2,1)S(1)}, bf16[1536,640]{1,0:T(8,128)(2,1)}, u32[]{:S(2)}) copy-start(bf16[1536,640]{1,0:T(8,128)(2,1)} %copy-done.6) | copy-start | bytes 5898244
  18.8 5.6 %copy-start.8 = (s32[2,12]{1,0:T(2,128)S(1)}, s32[2,12]{1,0:T(2,128)}, u32[]{:S(2)}) copy-start(s32[2,12]{1,0:T(2,128)} %pmap.3) | copy-start | bytes 292
  18.8 5.6 %copy-start.9 = (s32[3]{0:T(128)S(1)}, s32[3]{0:T(128)}, u32[]{:S(2)}) copy-start(s32[3]{0:T(128)} %live.3) | copy-start | bytes 40
  18.8 1.5 %collective-permute-start.5 = (bf16[640,128]{1,0:T(8,128)(2,1)S(1)}, bf16[640,128]{1,0:T(8,128)(2,1)S(1)}, u32[]{:S(2)}, u32[]{:S(2)}) collective-permute-start(bf16[640,128]{1,0:T(8,128)(2,1)S(1)} %fusion.3.own), channel_id=1, source_target_pairs={{0,16},{16,0},{1,17},{17,1},{2,18},{18,2},{3,19},{19,3},{4,20},{20... | collective-permute-start | bytes 491528 | tf_op jit(solution)/shard_map/ppermute | solution.py:377
  20.9 7.1 %collective-permute-start.6 = (bf16[1280,128]{1,0:T(8,128)(2,1)S(1)}, bf16[1280,128]{1,0:T(8,128)(2,1)S(1)}, u32[]{:S(2)}, u32[]{:S(2)}) collective-permute-start(bf16[1280,128]{1,0:T(8,128)(2,1)S(1)} %shard_map.70), channel_id=1, source_target_pairs={{0,4},{4,0},{8,12},{12,8},{16,24},{20,28},{24,16},{28,20},{1,5},{5... | collective-permute-start | bytes 983048 | tf_op jit(solution)/shard_map/ppermute | solution.py:385
  25.1 1.7 %copy-start.4 = (bf16[2560,640]{1,0:T(8,128)(2,1)}, bf16[2560,640]{1,0:T(8,128)(2,1)S(1)}, u32[]{:S(2)}) copy-start(bf16[2560,640]{1,0:T(8,128)(2,1)S(1)} %shard_map.71.panel_rows) | copy-start | bytes 9830404
  28.1 7.1 %collective-permute-start.7 = (bf16[1280,128]{1,0:T(8,128)(2,1)S(1)}, bf16[1280,128]{1,0:T(8,128)(2,1)S(1)}, u32[]{:S(2)}, u32[]{:S(2)}) collective-permute-start(bf16[1280,128]{1,0:T(8,128)(2,1)S(1)} %fusion), channel_id=1, source_target_pairs={{0,8},{4,12},{8,0},{12,4},{16,20},{20,16},{24,28},{28,24},{1,9},{5... | collective-permute-start | bytes 983048 | tf_op jit(solution)/shard_map/ppermute | solution.py:385
  28.7 25.1 %slice-start = ((s8[4915200]{0:T(1024)(128)(4,1)}), s8[720896]{0:T(1024)(128)(4,1)S(1)}, s32[]{:S(2)}) async-start(s8[4915200]{0:T(1024)(128)(4,1)} %bitcast), calls=%async_computation | async-start | bytes 1441792
  28.7 9.7 %collective-permute-start.2 = (bf16[640,128]{1,0:T(8,128)(2,1)S(1)}, bf16[640,128]{1,0:T(8,128)(2,1)S(1)}, u32[]{:S(2)}, u32[]{:S(2)}) collective-permute-start(bf16[640,128]{1,0:T(8,128)(2,1)S(1)} %slice.50.after), channel_id=1, source_target_pairs={{0,8},{4,12},{8,0},{12,4},{16,20},{20,16},{24,28},{28,24},{1,9},{5... | collective-permute-start | bytes 491528 | tf_op jit(solution)/shard_map/ppermute | solution.py:385
  35.4 2.4 %copy-start.3 = (bf16[3840,640]{1,0:T(8,128)(2,1)S(1)}, bf16[3840,640]{1,0:T(8,128)(2,1)}, u32[]{:S(2)}) copy-start(bf16[3840,640]{1,0:T(8,128)(2,1)} %copy-done) | copy-start | bytes 14745604
  37.8 16.0 %slice-start.1 = ((s8[4915200]{0:T(1024)(128)(4,1)}), s8[4194304]{0:T(1024)(128)(4,1)S(1)}, s32[]{:S(2)}) async-start(s8[4915200]{0:T(1024)(128)(4,1)} %bitcast), calls=%async_computation.1 | async-start | bytes 8388608
  37.8 16.0 %copy-start.5 = (bf16[2560,640]{1,0:T(8,128)(2,1)S(1)}, bf16[2560,640]{1,0:T(8,128)(2,1)}, u32[]{:S(2)}) copy-start(bf16[2560,640]{1,0:T(8,128)(2,1)} %copy-done.4) | copy-start | bytes 9830404
  38.3 1.5 %collective-permute-start.8 = (bf16[640,128]{1,0:T(8,128)(2,1)S(1)}, bf16[640,128]{1,0:T(8,128)(2,1)S(1)}, u32[]{:S(2)}, u32[]{:S(2)}) collective-permute-start(bf16[640,128]{1,0:T(8,128)(2,1)S(1)} %shard_map.72), channel_id=1, source_target_pairs={{0,16},{16,0},{1,17},{17,1},{2,18},{18,2},{3,19},{19,3},{4,20},{20... | collective-permute-start | bytes 491528 | tf_op jit(solution)/shard_map/ppermute | solution.py:377
  38.5 6.6 %collective-permute-start.13 = (bf16[640,128]{1,0:T(8,128)(2,1)S(1)}, bf16[640,128]{1,0:T(8,128)(2,1)S(1)}, u32[]{:S(2)}, u32[]{:S(2)}) collective-permute-start(bf16[640,128]{1,0:T(8,128)(2,1)S(1)} %fusion.2), channel_id=1, source_target_pairs={{0,8},{4,12},{8,0},{12,4},{16,20},{20,16},{24,28},{28,24},{1,9},{5... | collective-permute-start | bytes 491528 | tf_op jit(solution)/shard_map/ppermute | solution.py:385
  39.8 7.3 %collective-permute-start.9 = (bf16[640,128]{1,0:T(8,128)(2,1)S(1)}, bf16[640,128]{1,0:T(8,128)(2,1)S(1)}, u32[]{:S(2)}, u32[]{:S(2)}) collective-permute-start(bf16[640,128]{1,0:T(8,128)(2,1)S(1)} %add_convert_fusion.1.root_rows), channel_id=1, source_target_pairs={{0,4},{4,0},{8,12},{12,8},{16,24},{20,28},{24,16},{28,20},{1,5},{5... | collective-permute-start | bytes 491528 | tf_op jit(solution)/shard_map/ppermute | solution.py:385
  45.1 8.7 %collective-permute-start.14 = (bf16[1280,128]{1,0:T(8,128)(2,1)S(1)}, bf16[1280,128]{1,0:T(8,128)(2,1)S(1)}, u32[]{:S(2)}, u32[]{:S(2)}) collective-permute-start(bf16[1280,128]{1,0:T(8,128)(2,1)S(1)} %pad_maximum_fusion.near), channel_id=1, source_target_pairs={{0,4},{4,0},{8,12},{12,8},{16,24},{20,28},{24,16},{28,20},{1,5},{5... | collective-permute-start | bytes 983048 | tf_op jit(solution)/shard_map/ppermute | solution.py:385
  46.5 6.5 %collective-permute-start.11 = (bf16[320,128]{1,0:T(8,128)(2,1)S(1)}, bf16[320,128]{1,0:T(8,128)(2,1)S(1)}, u32[]{:S(2)}, u32[]{:S(2)}) collective-permute-start(bf16[320,128]{1,0:T(8,128)(2,1)S(1)} %constant_dynamic-slice_fusion), channel_id=1, source_target_pairs={{0,12},{4,8},{8,4},{12,0},{16,28},{20,24},{24,20},{28,16},{1,13},{... | collective-permute-start | bytes 245768 | tf_op jit(solution)/shard_map/ppermute | solution.py:385
  47.1 7.6 %collective-permute-start.10 = (bf16[640,128]{1,0:T(8,128)(2,1)S(1)}, bf16[640,128]{1,0:T(8,128)(2,1)S(1)}, u32[]{:S(2)}, u32[]{:S(2)}) collective-permute-start(bf16[640,128]{1,0:T(8,128)(2,1)S(1)} %collective-permute-done.9.mine), channel_id=1, source_target_pairs={{0,16},{16,0},{1,17},{17,1},{2,18},{18,2},{3,19},{19,3},{4,20},{20... | collective-permute-start | bytes 491528 | tf_op jit(solution)/shard_map/ppermute | solution.py:377
  53.0 1.7 %collective-permute-start.12 = (bf16[320,128]{1,0:T(8,128)(2,1)S(1)}, bf16[320,128]{1,0:T(8,128)(2,1)S(1)}, u32[]{:S(2)}, u32[]{:S(2)}) collective-permute-start(bf16[320,128]{1,0:T(8,128)(2,1)S(1)} %collective-permute-done.11.mine_far), channel_id=1, source_target_pairs={{0,16},{16,0},{1,17},{17,1},{2,18},{18,2},{3,19},{19,3},{4,20},{20... | collective-permute-start | bytes 245768 | tf_op jit(solution)/shard_map/ppermute | solution.py:377

commit v5 on v4

--- a/solution.py
+++ b/solution.py
@@ -297,10 +297,11 @@
             c_v[pl.ds(pl.multiple_of(block * B, B), B)] = product[e * B : (e + 1) * B]
     for out, side in ((keep, leaf_pos), (send, 1 - leaf_pos)):
         near = (row_pos ^ (1 + side)) * quarter
-        out[pl.ds(0, quarter)] = c_v[rows_at(near, quarter)]
-        at = side * half
-        out[pl.ds(quarter, half)] = c_v[rows_at((row_pos ^ 3) * quarter + at, half)]
-        out[pl.ds(quarter + half, half)] = c_v[rows_at(row_pos * quarter + at, half)]
+        mine, other = side * half, (1 - side) * half
+        out[pl.ds(0, half)] = c_v[rows_at(near + mine, half)]
+        out[pl.ds(half, half)] = c_v[rows_at(near + other, half)]
+        out[pl.ds(quarter, half)] = c_v[rows_at((row_pos ^ 3) * quarter + mine, half)]
+        out[pl.ds(quarter + half, half)] = c_v[rows_at(row_pos * quarter + mine, half)]
     gets[3 + parts].wait()
 
 
@@ -335,28 +336,45 @@
         out[pl.ds(pl.multiple_of(block * B, B), B)] = jnp.where(alive, value, jnp.zeros_like(value))
 
 
-def root_pivot_kernel(sizes, own, other, d_v, out):
-    base, rows = sizes
-    right = -(own[...].astype(F32) + other[...].astype(F32))
-    out[...] = mm(d_v[pl.ds(base, rows)], right.astype(BF)).astype(BF)
-
-
-def root_transposed_kernel(sizes, y, d_v, out):
-    base, rows = sizes
-    out[...] = mm(y[...].T, d_v[pl.ds(base, rows)]).T.astype(BF)
+def root_pivot_kernel(sizes, own, other, d_v, out, q_v):
+    half, base = sizes
+    leaf_pos = lax.axis_index("leaf")
+    first, second = pl.ds(0, half), pl.ds(half, half)
+    for mine, theirs, at in ((first, second, leaf_pos), (second, first, 1 - leaf_pos)):
+        value = own[mine].astype(F32) + other[theirs].astype(F32)
+        q_v[rows_at(at * half, half)] = (-value).astype(BF)
+    out[...] = mm(d_v[pl.ds(base, 4 * half)], q_v[...]).astype(BF)
+
+
+def root_transposed_kernel(sizes, y, d_v, out, piece, s_v):
+    half, base = sizes
+    leaf_pos = lax.axis_index("leaf")
+    row_pos = lax.axis_index("row")
+    piece[...] = y[rows_at(row_pos * half, half)]
+    s_v[...] = mm(y[...].T, d_v[pl.ds(base, 4 * half)]).T
+    out[pl.ds(0, half)] = s_v[rows_at(leaf_pos * half, half)].astype(BF)
+    out[pl.ds(half, half)] = s_v[rows_at((1 - leaf_pos) * half, half)].astype(BF)
+
+
+def near_product(rows, row, side, panel_rows, half):
+    value = 0.0
+    for k, at in enumerate((side, 1 - side)):
+        part = rows[pl.ds(k * half, half)].T
+        value = value + mm(part, panel_rows[rows_at((2 * row + at) * half, half)])
+    return value
 
 
 def leaf_transposed_kernel(sizes, near, far, d_v, mask, root_rows, panel_rows, total, y_v):
     quarter, half = sizes
     row_pos = lax.axis_index("row")
-    order = row_order(row_pos, lax.axis_index("leaf"))
+    leaf_pos = lax.axis_index("leaf")
+    order = row_order(row_pos, leaf_pos)
     for k in range(4):
         part = (near if k < 2 else far)[pl.ds((k % 2) * quarter, quarter)]
         y_v[rows_at(order[k] * quarter, quarter)] = part
     value = mm(y_v[...].T, d_v[pl.ds(0, 4 * quarter)])
     value = jnp.where(mask[...].astype(F32).T > 0.0, value, 0.0)
-    own = panel_rows[rows_at(row_pos * quarter, quarter)]
-    total[...] = value - mm(root_rows[...].T, own)
+    total[...] = value - near_product(root_rows, row_pos, leaf_pos, panel_rows, half)
 
 
 def last_kernel(sizes, mine, theirs, mine_far, theirs_far, total, panel_rows, root_rows, out):
@@ -365,12 +383,11 @@
     row_pos = lax.axis_index("row")
     value = total[...]
     for near, far, side in ((mine, mine_far, leaf_pos), (theirs, theirs_far, 1 - leaf_pos)):
-        rows = rows_at((row_pos ^ (1 + side)) * quarter, quarter)
-        value = value - mm(near[...].T, panel_rows[rows])
+        value = value - near_product(near, row_pos ^ (1 + side), side, panel_rows, half)
         rows = rows_at((row_pos ^ 3) * quarter + side * half, half)
         value = value - mm(far[...].T, panel_rows[rows])
     out[pl.ds(0, quarter)] = value.T.astype(BF)
-    out[pl.ds(quarter, half)] = root_rows[rows_at(leaf_pos * half, half)]
+    out[pl.ds(quarter, half)] = root_rows[pl.ds(0, half)]
 
 
 def leaf_swap(value):
@@ -395,8 +412,6 @@
     half = quarter // 2
     front = 4 * quarter
     updates = parent_map.shape[1] * B
-    leaf_pos = lax.axis_index("leaf")
-    row_pos = lax.axis_index("row")
     after = lambda value, other: lax.optimization_barrier((value, other))[0]
     smem = [pltpu.SMEM(live.shape, jnp.int32), pltpu.SMEM(parent_map.shape, jnp.int32)]
 
@@ -438,16 +453,15 @@
     from_near = after(from_near, send_e)
 
     term = update[quarter + half :] + from_far.astype(F32) - b_v[quarter:].astype(F32)
-    lower = jnp.where(leaf_pos == 0, term, 0.0)
-    upper = jnp.where(leaf_pos == 0, 0.0, term)
-    negated = (from_near.astype(F32) + jnp.concatenate([lower, upper], 0)).astype(BF)
+    from_near = from_near.astype(F32)
+    negated = jnp.concatenate([from_near[:half] + term, from_near[half:]], 0).astype(BF)
     negated_other = leaf_swap(negated)
 
     partial = call(
-        functools.partial(root_pivot_kernel, (front, 4 * half)),
+        functools.partial(root_pivot_kernel, (half, front)),
         kept(4 * half, columns),
         [VMEM, VMEM, VMEM],
-        [],
+        [pltpu.VMEM((quarter, columns), BF)],
         16 * MIB,
         front * quarter * columns,
         front * quarter,
@@ -469,24 +483,26 @@
     leaf_forward = home_e[:quarter] + got_e.astype(F32)
     leaf_forward = jnp.where(mask > 0, leaf_forward, 0.0).astype(BF)
 
-    part = call(
-        functools.partial(root_transposed_kernel, (front, 4 * half)),
-        kept(quarter, columns),
+    part, root_piece = call(
+        functools.partial(root_transposed_kernel, (half, front)),
+        (kept(quarter, columns), kept(half, columns)),
         [VMEM, VMEM],
-        [],
+        [pltpu.VMEM((quarter, columns), F32)],
         16 * MIB,
         front * quarter * columns,
         front * quarter,
     )(root_forward, d_v)
-    root_rows = added(part, leaf_swap(part)).astype(BF)
+    got = leaf_swap(part)
+    root_mine = added(part[:half], got[half:]).astype(BF)
+    root_other = added(part[half:], got[:half]).astype(BF)
+    root_rows = jnp.concatenate([root_mine, root_other], 0)
 
     near_e = jnp.concatenate([leaf_forward, row_swap(leaf_forward, 1)], 0)
     far_e = row_swap(near_e, 0)
-    root_piece = lax.dynamic_slice_in_dim(root_forward, row_pos * half, half, 0)
     forward = jnp.concatenate([leaf_forward, root_piece], 0)
 
     near = row_swap(root_rows, 0)
-    far = row_swap(lax.dynamic_slice_in_dim(root_rows, leaf_pos * half, half, 0), 2)
+    far = row_swap(root_mine, 2)
     total = call(
         functools.partial(leaf_transposed_kernel, (quarter, half)),
         kept(columns, quarter, F32),

time: 56.5 us -> 49.4 us (0.87)
  local copies, waits for them, and re-layouts: 10.1 us -> 0.06 us
  starting transfers between devices: 13.4 us -> 14.9 us
  waiting for transfers between devices: 22.1 us -> 23.3 us
    unnamed x24 -> x4, local copies, waits for them, and re-layouts: 10 us -> 0.01 us
    ppermute x10, waiting for transfers between devices: 18.7 us -> 20.7 us  [row_swap(): return lax.ppermute(value, ('leaf', 'row'), route)]
    ppermute x10, starting transfers between devices: 12.8 us -> 14.2 us  [row_swap(): return lax.ppermute(value, ('leaf', 'row'), route)]
    ppermute x5, waiting for transfers between devices: 3.37 us -> 2.65 us  [leaf_swap(): return lax.ppermute(value, 'leaf', [(0, 1), (1, 0)])]
  transfers between devices with their start and end apart: 15 -> 15, of which waited for: 8 -> 9; matrix products, arithmetic and copies ran while one was open for 2% -> 3% of each run, Pallas kernels for 7% -> 8%
where the time goes in v5:
time: 49.4 us; the launch traced here: 49.2 us
  waiting for transfers between devices  23.3 us (47%)
  starting transfers between devices  14.9 us (30%)
  Pallas kernels  8.82 us (18%)
  other arithmetic  1.3 us (3%)
  between operations  0.8 us (2%)
    ppermute x10, waiting for transfers between devices, row_swap(): return lax.ppermute(value, ('leaf', 'row'), route)  20.7 us
    ppermute x10, starting transfers between devices, row_swap(): return lax.ppermute(value, ('leaf', 'row'), route)  14.2 us
    pallas_call x1, Pallas kernels, two_levels(): call(functools.partial(panel_kernel, (quarter, half, parts, updates)), (k...  3.21 us
    ppermute x5, waiting for transfers between devices, leaf_swap(): return lax.ppermute(value, 'leaf', [(0, 1), (1, 0)])  2.65 us
    pallas_call x1, Pallas kernels, two_levels(): call(functools.partial(last_kernel, (quarter, half)), stored(quarter + ha...  1.62 us
    pallas_call x1, Pallas kernels, two_levels(): call(functools.partial(leaf_pivot_kernel, (quarter, half)), (kept(2 * qua...  1.01 us
  transfers between devices with their start and end apart: 15, of which 9 were waited for; matrix products, arithmetic and copies ran while one was open for 3% of the time, Pallas kernels for 8%

profile of v5, /device:TPU:0, one launch (start us, length us, event | category | flops | bytes accessed | tf_op | source)
XLA Modules:
  0.0 49.2 jit_solution(11697844435317531554)
XLA Ops:
  0.6 3.2 %shard_map.68 = (bf16[1280,128]{1,0:T(8,128)(2,1)S(1)}, bf16[1280,128]{1,0:T(8,128)(2,1)S(1)}, bf16[960,128]{1,0:T(8,128)(2,1)S(1)}, bf16[640,128]{1,0:T(8,128)(...) custom-call(s32[3]{0:T(128)} %live.3, s32[2,12]{1,0:T(2,128)} %pmap.3, ...), custom_call_target="tpu_custom_call" | custom-call | flops 251658240 | bytes 1966080 | tf_op jit(solution)/shard_map/pallas_call | solution.py:419
  3.8 0.5 %collective-permute-start = (bf16[1280,128]{1,0:T(8,128)(2,1)S(1)}, bf16[1280,128]{1,0:T(8,128)(2,1)S(1)}, u32[]{:S(2)}, u32[]{:S(2)}) collective-permute-start(bf16[1280,128]{1,0:T(8,128)(2,1)S(1)} %get-tuple-element.19), channel_id=1, source_target_pairs={{0,16},{16,0},{1,17},{17,1},{2,18},{18,2},{3,19},{19,3},{4,20},{20... | collective-permute-start | bytes 983048 | tf_op jit(solution)/shard_map/ppermute | solution.py:394
  4.4 1.3 %collective-permute-done = bf16[1280,128]{1,0:T(8,128)(2,1)S(1)} collective-permute-done((bf16[1280,128]{1,0:T(8,128)(2,1)S(1)}, bf16[1280,128]{1,0:T(8,128)(2,1)S(1)}, u32[]{:S(2)}, u32[]{:S(2)}) %collective-permute-start) | collective-permute-done | bytes 327712 | tf_op jit(solution)/shard_map/ppermute | solution.py:394
  5.6 0.1 convert_add_fusion.2
  5.7 2.9 %collective-permute-start.3 = (bf16[640,128]{1,0:T(8,128)(2,1)S(1)}, bf16[640,128]{1,0:T(8,128)(2,1)S(1)}, u32[]{:S(2)}, u32[]{:S(2)}) collective-permute-start(bf16[640,128]{1,0:T(8,128)(2,1)S(1)} %slice.56.after), channel_id=1, source_target_pairs={{0,4},{4,0},{8,12},{12,8},{16,24},{20,28},{24,16},{28,20},{1,5},{5... | collective-permute-start | bytes 491528 | tf_op jit(solution)/shard_map/ppermute | solution.py:402
  8.7 1.5 %collective-permute-start.4 = (bf16[320,128]{1,0:T(8,128)(2,1)S(1)}, bf16[320,128]{1,0:T(8,128)(2,1)S(1)}, u32[]{:S(2)}, u32[]{:S(2)}) collective-permute-start(bf16[320,128]{1,0:T(8,128)(2,1)S(1)} %slice.60), channel_id=1, source_target_pairs={{0,12},{4,8},{8,4},{12,0},{16,28},{20,24},{24,20},{28,16},{1,13},{... | collective-permute-start | bytes 245768 | tf_op jit(solution)/shard_map/ppermute | solution.py:402
  10.2 1.0 %shard_map.69 = (bf16[1280,128]{1,0:T(8,128)(2,1)S(1)}, bf16[1280,128]{1,0:T(8,128)(2,1)S(1)}) custom-call(bf16[640,128]{1,0:T(8,128)(2,1)S(1)} %get-tuple-element.16.masked, bf16[3840,640]{1,0:T(8,128)(2,1)S(1)} %get-tuple-element.17.d_v, bf16[640,128]{1,0:T(8,128)(2,1)S(1)} %slice.56.after), custom_call_target="tpu_custom_call" | custom-call | flops 419430400 | bytes 3276800 | tf_op jit(solution)/shard_map/pallas_call | solution.py:443
  11.2 1.6 %collective-permute-start.1 = (bf16[1280,128]{1,0:T(8,128)(2,1)S(1)}, bf16[1280,128]{1,0:T(8,128)(2,1)S(1)}, u32[]{:S(2)}, u32[]{:S(2)}) collective-permute-start(bf16[1280,128]{1,0:T(8,128)(2,1)S(1)} %get-tuple-element.21), channel_id=1, source_target_pairs={{0,4},{4,0},{8,12},{12,8},{16,24},{20,28},{24,16},{28,20},{1,5},{5... | collective-permute-start | bytes 983048 | tf_op jit(solution)/shard_map/ppermute | solution.py:402
  12.7 0.1 collective-permute-done.3
  12.8 2.5 %collective-permute-done.4 = bf16[320,128]{1,0:T(8,128)(2,1)S(1)} collective-permute-done((bf16[320,128]{1,0:T(8,128)(2,1)S(1)}, bf16[320,128]{1,0:T(8,128)(2,1)S(1)}, u32[]{:S(2)}, u32[]{:S(2)}) %collective-permute-start.4) | collective-permute-done | bytes 81952 | tf_op jit(solution)/shard_map/ppermute | solution.py:402
  15.4 0.1 collective-permute-start.5
  15.5 1.4 %collective-permute-done.5.other = bf16[640,128]{1,0:T(8,128)(2,1)S(1)} collective-permute-done((bf16[640,128]{1,0:T(8,128)(2,1)S(1)}, bf16[640,128]{1,0:T(8,128)(2,1)S(1)}, u32[]{:S(2)}, u32[]{:S(2)}) %collective-permute-start.5) | collective-permute-done | bytes 163872 | tf_op jit(solution)/shard_map/ppermute | solution.py:394
  16.9 0.6 %shard_map.70 = bf16[1280,128]{1,0:T(8,128)(2,1)S(1)} custom-call(bf16[640,128]{1,0:T(8,128)(2,1)S(1)} %pad_maximum_fusion.2.own, bf16[640,128]{1,0:T(8,128)(2,1)S(1)} %collective-permute-done.5.other, bf16[3840,640]{1,0:T(8,128)(2,1)S(1)} %get-tuple-element.17.d_v), custom_call_target="tpu_custom_call" | custom-call | flops 209715200 | bytes 1638400 | tf_op jit(solution)/shard_map/pallas_call | solution.py:460
  17.5 1.6 %collective-permute-start.6 = (bf16[1280,128]{1,0:T(8,128)(2,1)S(1)}, bf16[1280,128]{1,0:T(8,128)(2,1)S(1)}, u32[]{:S(2)}, u32[]{:S(2)}) collective-permute-start(bf16[1280,128]{1,0:T(8,128)(2,1)S(1)} %shard_map.70), channel_id=1, source_target_pairs={{0,4},{4,0},{8,12},{12,8},{16,24},{20,28},{24,16},{28,20},{1,5},{5... | collective-permute-start | bytes 983048 | tf_op jit(solution)/shard_map/ppermute | solution.py:402
  19.2 0.6 %collective-permute-start.2 = (bf16[640,128]{1,0:T(8,128)(2,1)S(1)}, bf16[640,128]{1,0:T(8,128)(2,1)S(1)}, u32[]{:S(2)}, u32[]{:S(2)}) collective-permute-start(bf16[640,128]{1,0:T(8,128)(2,1)S(1)} %slice.83.after), channel_id=1, source_target_pairs={{0,8},{4,12},{8,0},{12,4},{16,20},{20,16},{24,28},{28,24},{1,9},{5... | collective-permute-start | bytes 491528 | tf_op jit(solution)/shard_map/ppermute | solution.py:402
  19.8 0.8 %shard_map.71.panel_rows = bf16[2560,640]{1,0:T(8,128)(2,1)S(1)} custom-call(s32[3]{0:T(128)S(1)} %copy-done.1, s32[2,12]{1,0:T(2,128)S(1)} %copy-done, bf16[1536,640]{1,0:T(8,128)(2,1)S(1)} %get-tuple-element.24.w_v, bf16[640,128]{1,0:T(8,128)(2,1)S(1)} %slice.83.after), custom_call_target="tpu_custom_call" | custom-call | bytes 6553600 | tf_op jit(solution)/shard_map/pallas_call | solution.py:472
  20.5 5.5 %collective-permute-done.6 = bf16[1280,128]{1,0:T(8,128)(2,1)S(1)} collective-permute-done((bf16[1280,128]{1,0:T(8,128)(2,1)S(1)}, bf16[1280,128]{1,0:T(8,128)(2,1)S(1)}, u32[]{:S(2)}, u32[]{:S(2)}) %collective-permute-start.6) | collective-permute-done | bytes 327712 | tf_op jit(solution)/shard_map/ppermute | solution.py:402
  26.1 0.1 fusion
  26.2 0.7 %collective-permute-start.7 = (bf16[1280,128]{1,0:T(8,128)(2,1)S(1)}, bf16[1280,128]{1,0:T(8,128)(2,1)S(1)}, u32[]{:S(2)}, u32[]{:S(2)}) collective-permute-start(bf16[1280,128]{1,0:T(8,128)(2,1)S(1)} %fusion), channel_id=1, source_target_pairs={{0,8},{4,12},{8,0},{12,4},{16,20},{20,16},{24,28},{28,24},{1,9},{5... | collective-permute-start | bytes 983048 | tf_op jit(solution)/shard_map/ppermute | solution.py:402
  26.9 1.4 %collective-permute-start.13 = (bf16[640,128]{1,0:T(8,128)(2,1)S(1)}, bf16[640,128]{1,0:T(8,128)(2,1)S(1)}, u32[]{:S(2)}, u32[]{:S(2)}) collective-permute-start(bf16[640,128]{1,0:T(8,128)(2,1)S(1)} %fusion.2), channel_id=1, source_target_pairs={{0,8},{4,12},{8,0},{12,4},{16,20},{20,16},{24,28},{28,24},{1,9},{5... | collective-permute-start | bytes 491528 | tf_op jit(solution)/shard_map/ppermute | solution.py:402
  28.4 4.9 %collective-permute-done.7 = bf16[1280,128]{1,0:T(8,128)(2,1)S(1)} collective-permute-done((bf16[1280,128]{1,0:T(8,128)(2,1)S(1)}, bf16[1280,128]{1,0:T(8,128)(2,1)S(1)}, u32[]{:S(2)}, u32[]{:S(2)}) %collective-permute-start.7) | collective-permute-done | bytes 327712 | tf_op jit(solution)/shard_map/ppermute | solution.py:402
  33.3 0.1 add_convert_fusion.y
  33.4 0.6 %shard_map.72 = (bf16[640,128]{1,0:T(8,128)(2,1)S(1)}, bf16[320,128]{1,0:T(8,128)(2,1)S(1)}) custom-call(bf16[1280,128]{1,0:T(8,128)(2,1)S(1)} %add_convert_fusion.y, bf16[3840,640]{1,0:T(8,128)(2,1)S(1)} %get-tuple-element.17.d_v), custom_call_target="tpu_custom_call" | custom-call | flops 209715200 | bytes 1638400 | tf_op jit(solution)/shard_map/pallas_call | solution.py:486
  34.1 0.9 %collective-permute-done.13 = bf16[640,128]{1,0:T(8,128)(2,1)S(1)} collective-permute-done((bf16[640,128]{1,0:T(8,128)(2,1)S(1)}, bf16[640,128]{1,0:T(8,128)(2,1)S(1)}, u32[]{:S(2)}, u32[]{:S(2)}) %collective-permute-start.13) | collective-permute-done | bytes 163872 | tf_op jit(solution)/shard_map/ppermute | solution.py:402
  35.1 1.5 %collective-permute-start.14 = (bf16[1280,128]{1,0:T(8,128)(2,1)S(1)}, bf16[1280,128]{1,0:T(8,128)(2,1)S(1)}, u32[]{:S(2)}, u32[]{:S(2)}) collective-permute-start(bf16[1280,128]{1,0:T(8,128)(2,1)S(1)} %pad_maximum_fusion.near), channel_id=1, source_target_pairs={{0,4},{4,0},{8,12},{12,8},{16,24},{20,28},{24,16},{28,20},{1,5},{5... | collective-permute-start | bytes 983048 | tf_op jit(solution)/shard_map/ppermute | solution.py:402
  36.6 0.7 %collective-permute-start.9 = (bf16[640,128]{1,0:T(8,128)(2,1)S(1)}, bf16[640,128]{1,0:T(8,128)(2,1)S(1)}, u32[]{:S(2)}, u32[]{:S(2)}) collective-permute-start(bf16[640,128]{1,0:T(8,128)(2,1)S(1)} %pad_maximum_fusion.3.root_rows), channel_id=1, source_target_pairs={{0,4},{4,0},{8,12},{12,8},{16,24},{20,28},{24,16},{28,20},{1,5},{5... | collective-permute-start | bytes 491528 | tf_op jit(solution)/shard_map/ppermute | solution.py:402
  37.3 1.8 %collective-permute-start.11 = (bf16[320,128]{1,0:T(8,128)(2,1)S(1)}, bf16[320,128]{1,0:T(8,128)(2,1)S(1)}, u32[]{:S(2)}, u32[]{:S(2)}) collective-permute-start(bf16[320,128]{1,0:T(8,128)(2,1)S(1)} %get-tuple-element.30), channel_id=1, source_target_pairs={{0,12},{4,8},{8,4},{12,0},{16,28},{20,24},{24,20},{28,16},{1,13},{... | collective-permute-start | bytes 245768 | tf_op jit(solution)/shard_map/ppermute | solution.py:402
  39.1 5.7 %collective-permute-done.9.mine = bf16[640,128]{1,0:T(8,128)(2,1)S(1)} collective-permute-done((bf16[640,128]{1,0:T(8,128)(2,1)S(1)}, bf16[640,128]{1,0:T(8,128)(2,1)S(1)}, u32[]{:S(2)}, u32[]{:S(2)}) %collective-permute-start.9) | collective-permute-done | bytes 163872 | tf_op jit(solution)/shard_map/ppermute | solution.py:402
  44.9 1.0 %collective-permute-done.11.mine_far = bf16[320,128]{1,0:T(8,128)(2,1)S(1)} collective-permute-done((bf16[320,128]{1,0:T(8,128)(2,1)S(1)}, bf16[320,128]{1,0:T(8,128)(2,1)S(1)}, u32[]{:S(2)}, u32[]{:S(2)}) %collective-permute-start.11) | collective-permute-done | bytes 81952 | tf_op jit(solution)/shard_map/ppermute | solution.py:402
  45.8 0.7 %pad_maximum_fusion.1 = bf16[960,128]{1,0:T(8,128)(2,1)} fusion(bf16[320,128]{1,0:T(8,128)(2,1)S(1)} %get-tuple-element.26, bf16[640,128]{1,0:T(8,128)(2,1)S(1)} %fusion.2), kind=kLoop, calls=%fused_computation.10 | loop fusion | flops 491520 | bytes 491520 | tf_op jit(solution)/shard_map/concatenate | solution.py:502
  46.5 1.0 %shard_map.73.total = f32[128,640]{1,0:T(8,128)S(1)} custom-call(bf16[1280,128]{1,0:T(8,128)(2,1)S(1)} %pad_maximum_fusion.near, bf16[1280,128]{1,0:T(8,128)(2,1)S(1)} %collective-permute-done.14.far, bf16[3840,640]{1,0:T(8,128)(2,1)S(1)} %get-tuple-element.17.d_v, bf16[640,128]{1,0:T(8,128)(2,1)S(1)} %get-tuple-element.15.mask, ...), custom_call_target="tpu_custom_call" | custom-call | flops 419430400 | bytes 3276800 | tf_op jit(solution)/shard_map/pallas_call | solution.py:506
  47.5 1.6 %shard_map.74 = bf16[960,128]{1,0:T(8,128)(2,1)} custom-call(bf16[640,128]{1,0:T(8,128)(2,1)S(1)} %collective-permute-done.9.mine, bf16[640,128]{1,0:T(8,128)(2,1)S(1)} %collective-permute-done.10.theirs, bf16[320,128]{1,0:T(8,128)(2,1)S(1)} %collective-permute-done.11.mine_far, bf16[320,128]{1,0:T(8,128)(2,1)S(1)} %collective-permute-done.12.theirs_far, ...), custom_call_target="tpu_custom_call" | custom-call | flops 209715200 | bytes 1638400 | tf_op jit(solution)/shard_map/pallas_call | solution.py:517
  (24 shorter events, 0.4 us)
Async XLA Ops:
  3.8 1.8 %collective-permute-start = (bf16[1280,128]{1,0:T(8,128)(2,1)S(1)}, bf16[1280,128]{1,0:T(8,128)(2,1)S(1)}, u32[]{:S(2)}, u32[]{:S(2)}) collective-permute-start(bf16[1280,128]{1,0:T(8,128)(2,1)S(1)} %get-tuple-element.19), channel_id=1, source_target_pairs={{0,16},{16,0},{1,17},{17,1},{2,18},{18,2},{3,19},{19,3},{4,20},{20... | collective-permute-start | bytes 983048 | tf_op jit(solution)/shard_map/ppermute | solution.py:394
  5.7 7.1 %collective-permute-start.3 = (bf16[640,128]{1,0:T(8,128)(2,1)S(1)}, bf16[640,128]{1,0:T(8,128)(2,1)S(1)}, u32[]{:S(2)}, u32[]{:S(2)}) collective-permute-start(bf16[640,128]{1,0:T(8,128)(2,1)S(1)} %slice.56.after), channel_id=1, source_target_pairs={{0,4},{4,0},{8,12},{12,8},{16,24},{20,28},{24,16},{28,20},{1,5},{5... | collective-permute-start | bytes 491528 | tf_op jit(solution)/shard_map/ppermute | solution.py:402
  8.7 6.6 %collective-permute-start.4 = (bf16[320,128]{1,0:T(8,128)(2,1)S(1)}, bf16[320,128]{1,0:T(8,128)(2,1)S(1)}, u32[]{:S(2)}, u32[]{:S(2)}) collective-permute-start(bf16[320,128]{1,0:T(8,128)(2,1)S(1)} %slice.60), channel_id=1, source_target_pairs={{0,12},{4,8},{8,4},{12,0},{16,28},{20,24},{24,20},{28,16},{1,13},{... | collective-permute-start | bytes 245768 | tf_op jit(solution)/shard_map/ppermute | solution.py:402
  11.2 7.9 %collective-permute-start.1 = (bf16[1280,128]{1,0:T(8,128)(2,1)S(1)}, bf16[1280,128]{1,0:T(8,128)(2,1)S(1)}, u32[]{:S(2)}, u32[]{:S(2)}) collective-permute-start(bf16[1280,128]{1,0:T(8,128)(2,1)S(1)} %get-tuple-element.21), channel_id=1, source_target_pairs={{0,4},{4,0},{8,12},{12,8},{16,24},{20,28},{24,16},{28,20},{1,5},{5... | collective-permute-start | bytes 983048 | tf_op jit(solution)/shard_map/ppermute | solution.py:402
  15.4 4.4 %copy-start = (s32[2,12]{1,0:T(2,128)S(1)}, s32[2,12]{1,0:T(2,128)}, u32[]{:S(2)}) copy-start(s32[2,12]{1,0:T(2,128)} %pmap.3) | copy-start | bytes 292
  15.4 4.4 %copy-start.1 = (s32[3]{0:T(128)S(1)}, s32[3]{0:T(128)}, u32[]{:S(2)}) copy-start(s32[3]{0:T(128)} %live.3) | copy-start | bytes 40
  15.4 1.5 %collective-permute-start.5 = (bf16[640,128]{1,0:T(8,128)(2,1)S(1)}, bf16[640,128]{1,0:T(8,128)(2,1)S(1)}, u32[]{:S(2)}, u32[]{:S(2)}) collective-permute-start(bf16[640,128]{1,0:T(8,128)(2,1)S(1)} %pad_maximum_fusion.2.own), channel_id=1, source_target_pairs={{0,16},{16,0},{1,17},{17,1},{2,18},{18,2},{3,19},{19,3},{4,20},{20... | collective-permute-start | bytes 491528 | tf_op jit(solution)/shard_map/ppermute | solution.py:394
  17.5 8.5 %collective-permute-start.6 = (bf16[1280,128]{1,0:T(8,128)(2,1)S(1)}, bf16[1280,128]{1,0:T(8,128)(2,1)S(1)}, u32[]{:S(2)}, u32[]{:S(2)}) collective-permute-start(bf16[1280,128]{1,0:T(8,128)(2,1)S(1)} %shard_map.70), channel_id=1, source_target_pairs={{0,4},{4,0},{8,12},{12,8},{16,24},{20,28},{24,16},{28,20},{1,5},{5... | collective-permute-start | bytes 983048 | tf_op jit(solution)/shard_map/ppermute | solution.py:402
  19.2 7.7 %collective-permute-start.2 = (bf16[640,128]{1,0:T(8,128)(2,1)S(1)}, bf16[640,128]{1,0:T(8,128)(2,1)S(1)}, u32[]{:S(2)}, u32[]{:S(2)}) collective-permute-start(bf16[640,128]{1,0:T(8,128)(2,1)S(1)} %slice.83.after), channel_id=1, source_target_pairs={{0,8},{4,12},{8,0},{12,4},{16,20},{20,16},{24,28},{28,24},{1,9},{5... | collective-permute-start | bytes 491528 | tf_op jit(solution)/shard_map/ppermute | solution.py:402
  26.2 7.1 %collective-permute-start.7 = (bf16[1280,128]{1,0:T(8,128)(2,1)S(1)}, bf16[1280,128]{1,0:T(8,128)(2,1)S(1)}, u32[]{:S(2)}, u32[]{:S(2)}) collective-permute-start(bf16[1280,128]{1,0:T(8,128)(2,1)S(1)} %fusion), channel_id=1, source_target_pairs={{0,8},{4,12},{8,0},{12,4},{16,20},{20,16},{24,28},{28,24},{1,9},{5... | collective-permute-start | bytes 983048 | tf_op jit(solution)/shard_map/ppermute | solution.py:402
  26.9 8.1 %collective-permute-start.13 = (bf16[640,128]{1,0:T(8,128)(2,1)S(1)}, bf16[640,128]{1,0:T(8,128)(2,1)S(1)}, u32[]{:S(2)}, u32[]{:S(2)}) collective-permute-start(bf16[640,128]{1,0:T(8,128)(2,1)S(1)} %fusion.2), channel_id=1, source_target_pairs={{0,8},{4,12},{8,0},{12,4},{16,20},{20,16},{24,28},{28,24},{1,9},{5... | collective-permute-start | bytes 491528 | tf_op jit(solution)/shard_map/ppermute | solution.py:402
  34.0 2.5 %collective-permute-start.8 = (bf16[640,128]{1,0:T(8,128)(2,1)S(1)}, bf16[640,128]{1,0:T(8,128)(2,1)S(1)}, u32[]{:S(2)}, u32[]{:S(2)}) collective-permute-start(bf16[640,128]{1,0:T(8,128)(2,1)S(1)} %get-tuple-element.27), channel_id=1, source_target_pairs={{0,16},{16,0},{1,17},{17,1},{2,18},{18,2},{3,19},{19,3},{4,20},{20... | collective-permute-start | bytes 491528 | tf_op jit(solution)/shard_map/ppermute | solution.py:394
  35.1 11.4 %collective-permute-start.14 = (bf16[1280,128]{1,0:T(8,128)(2,1)S(1)}, bf16[1280,128]{1,0:T(8,128)(2,1)S(1)}, u32[]{:S(2)}, u32[]{:S(2)}) collective-permute-start(bf16[1280,128]{1,0:T(8,128)(2,1)S(1)} %pad_maximum_fusion.near), channel_id=1, source_target_pairs={{0,4},{4,0},{8,12},{12,8},{16,24},{20,28},{24,16},{28,20},{1,5},{5... | collective-permute-start | bytes 983048 | tf_op jit(solution)/shard_map/ppermute | solution.py:402
  36.6 8.2 %collective-permute-start.9 = (bf16[640,128]{1,0:T(8,128)(2,1)S(1)}, bf16[640,128]{1,0:T(8,128)(2,1)S(1)}, u32[]{:S(2)}, u32[]{:S(2)}) collective-permute-start(bf16[640,128]{1,0:T(8,128)(2,1)S(1)} %pad_maximum_fusion.3.root_rows), channel_id=1, source_target_pairs={{0,4},{4,0},{8,12},{12,8},{16,24},{20,28},{24,16},{28,20},{1,5},{5... | collective-permute-start | bytes 491528 | tf_op jit(solution)/shard_map/ppermute | solution.py:402
  37.3 8.5 %collective-permute-start.11 = (bf16[320,128]{1,0:T(8,128)(2,1)S(1)}, bf16[320,128]{1,0:T(8,128)(2,1)S(1)}, u32[]{:S(2)}, u32[]{:S(2)}) collective-permute-start(bf16[320,128]{1,0:T(8,128)(2,1)S(1)} %get-tuple-element.30), channel_id=1, source_target_pairs={{0,12},{4,8},{8,4},{12,0},{16,28},{20,24},{24,20},{28,16},{1,13},{... | collective-permute-start | bytes 245768 | tf_op jit(solution)/shard_map/ppermute | solution.py:402
  44.9 2.7 %collective-permute-start.10 = (bf16[640,128]{1,0:T(8,128)(2,1)S(1)}, bf16[640,128]{1,0:T(8,128)(2,1)S(1)}, u32[]{:S(2)}, u32[]{:S(2)}) collective-permute-start(bf16[640,128]{1,0:T(8,128)(2,1)S(1)} %collective-permute-done.9.mine), channel_id=1, source_target_pairs={{0,16},{16,0},{1,17},{17,1},{2,18},{18,2},{3,19},{19,3},{4,20},{20... | collective-permute-start | bytes 491528 | tf_op jit(solution)/shard_map/ppermute | solution.py:394
  45.8 1.7 %collective-permute-start.12 = (bf16[320,128]{1,0:T(8,128)(2,1)S(1)}, bf16[320,128]{1,0:T(8,128)(2,1)S(1)}, u32[]{:S(2)}, u32[]{:S(2)}) collective-permute-start(bf16[320,128]{1,0:T(8,128)(2,1)S(1)} %collective-permute-done.11.mine_far), channel_id=1, source_target_pairs={{0,16},{16,0},{1,17},{17,1},{2,18},{18,2},{3,19},{19,3},{4,20},{20... | collective-permute-start | bytes 245768 | tf_op jit(solution)/shard_map/ppermute | solution.py:394

commit v6 on v5

--- a/solution.py
+++ b/solution.py
@@ -241,8 +241,7 @@
 
 
 def row_order(row_pos, leaf_pos):
-    first = 1 + leaf_pos
-    return (row_pos, row_pos ^ (3 - first), row_pos ^ first, row_pos ^ 3)
+    return (row_pos, row_pos ^ (1 + leaf_pos), row_pos ^ (2 - leaf_pos), row_pos ^ 3)
 
 
 def panel_kernel(
@@ -305,14 +304,13 @@
     gets[3 + parts].wait()
 
 
-def leaf_pivot_kernel(sizes, masked, d_v, after, send, keep):
-    quarter, half = sizes
+def leaf_pivot_kernel(sizes, masked, d_v, after, *outs):
+    quarter = sizes
     order = row_order(lax.axis_index("row"), lax.axis_index("leaf"))
     right = masked[...]
-    for k in (2, 3, 0, 1):
-        out = keep if k < 2 else send
+    for k in (3, 1, 2, 0):
         product = mm(d_v[rows_at(order[k] * quarter, quarter)], right)
-        out[pl.ds((k % 2) * quarter, quarter)] = product.astype(BF)
+        outs[k][...] = product.astype(BF)
 
 
 def scatter_kernel(sizes, live, pmap, w_v, after, out, live_s, pmap_s, sems):
@@ -325,6 +323,7 @@
     ]
     for get in gets:
         get.start()
+    per_row = quarter // B
     out[...] = jnp.zeros_like(out)
     for get in gets:
         get.wait()
@@ -333,15 +332,17 @@
     for e in range(update_rows // B):
         value = w_v[pl.ds(e * B, B)]
         block = pmap_s[leaf_pos, e]
-        out[pl.ds(pl.multiple_of(block * B, B), B)] = jnp.where(alive, value, jnp.zeros_like(value))
-
-
-def root_pivot_kernel(sizes, own, other, d_v, out, q_v):
+        away = (block // per_row) ^ row_pos
+        slot = jnp.where(away == 1 + leaf_pos, 1, jnp.where(away == 2 - leaf_pos, 2, away))
+        at = (slot * per_row + block % per_row) * B
+        out[pl.ds(pl.multiple_of(at, B), B)] = jnp.where(alive, value, jnp.zeros_like(value))
+
+
+def root_pivot_kernel(sizes, mine, yours, other_mine, other_yours, d_v, out, q_v):
     half, base = sizes
     leaf_pos = lax.axis_index("leaf")
-    first, second = pl.ds(0, half), pl.ds(half, half)
-    for mine, theirs, at in ((first, second, leaf_pos), (second, first, 1 - leaf_pos)):
-        value = own[mine].astype(F32) + other[theirs].astype(F32)
+    for own, other, at in ((mine, other_yours, leaf_pos), (yours, other_mine, 1 - leaf_pos)):
+        value = own[...].astype(F32) + other[...].astype(F32)
         q_v[rows_at(at * half, half)] = (-value).astype(BF)
     out[...] = mm(d_v[pl.ds(base, 4 * half)], q_v[...]).astype(BF)
 
@@ -356,36 +357,40 @@
     out[pl.ds(half, half)] = s_v[rows_at((1 - leaf_pos) * half, half)].astype(BF)
 
 
-def near_product(rows, row, side, panel_rows, half):
-    value = 0.0
-    for k, at in enumerate((side, 1 - side)):
-        part = rows[pl.ds(k * half, half)].T
-        value = value + mm(part, panel_rows[rows_at((2 * row + at) * half, half)])
-    return value
-
-
-def leaf_transposed_kernel(sizes, near, far, d_v, mask, root_rows, panel_rows, total, y_v):
+def put(target, slot, half, source, order):
+    for k, side in enumerate(order):
+        at = 2 * slot * half + side * half
+        target[rows_at(at, half)] = source[pl.ds(k * half, half)]
+
+
+def leaf_transposed_kernel(
+    sizes, near, far, d_v, mask, root_rows, panel_rows, root_piece, total, forward, y_v, s_v
+):
     quarter, half = sizes
     row_pos = lax.axis_index("row")
     leaf_pos = lax.axis_index("leaf")
     order = row_order(row_pos, leaf_pos)
-    for k in range(4):
-        part = (near if k < 2 else far)[pl.ds((k % 2) * quarter, quarter)]
-        y_v[rows_at(order[k] * quarter, quarter)] = part
+    own = near[pl.ds(0, quarter)]
+    forward[pl.ds(0, quarter)] = own
+    forward[pl.ds(quarter, half)] = root_piece[...]
+    for k, part in enumerate(
+        (own, near[pl.ds(quarter, quarter)], far[pl.ds(0, quarter)], far[pl.ds(quarter, quarter)])
+    ):
+        y_v[rows_at(order[(0, 2, 1, 3)[k]] * quarter, quarter)] = part
     value = mm(y_v[...].T, d_v[pl.ds(0, 4 * quarter)])
     value = jnp.where(mask[...].astype(F32).T > 0.0, value, 0.0)
-    total[...] = value - near_product(root_rows, row_pos, leaf_pos, panel_rows, half)
-
-
-def last_kernel(sizes, mine, theirs, mine_far, theirs_far, total, panel_rows, root_rows, out):
+    put(s_v, 0, half, root_rows, (leaf_pos, 1 - leaf_pos))
+    total[...] = value - mm(s_v[...].T, panel_rows[pl.ds(0, quarter)])
+
+
+def last_kernel(sizes, mine, theirs, mine_far, theirs_far, total, panel_rows, root_rows, out, s_v):
     quarter, half = sizes
     leaf_pos = lax.axis_index("leaf")
-    row_pos = lax.axis_index("row")
-    value = total[...]
-    for near, far, side in ((mine, mine_far, leaf_pos), (theirs, theirs_far, 1 - leaf_pos)):
-        value = value - near_product(near, row_pos ^ (1 + side), side, panel_rows, half)
-        rows = rows_at((row_pos ^ 3) * quarter + side * half, half)
-        value = value - mm(far[...].T, panel_rows[rows])
+    put(s_v, 1, half, mine, (leaf_pos, 1 - leaf_pos))
+    put(s_v, 0, half, theirs, (1 - leaf_pos, leaf_pos))
+    put(s_v, 2, half, mine_far, (leaf_pos,))
+    put(s_v, 2, half, theirs_far, (1 - leaf_pos,))
+    value = total[...] - mm(s_v[...].T, panel_rows[pl.ds(quarter, 3 * quarter)])
     out[pl.ds(0, quarter)] = value.T.astype(BF)
     out[pl.ds(quarter, half)] = root_rows[pl.ds(0, half)]
 
@@ -440,35 +445,39 @@
     from_far = row_swap(away_far, 2)
     from_near = row_swap(away_near, 0)
 
-    send_e, keep_e = call(
-        functools.partial(leaf_pivot_kernel, (quarter, half)),
-        (kept(2 * quarter, columns), kept(2 * quarter, columns)),
+    pieces = call(
+        functools.partial(leaf_pivot_kernel, quarter),
+        (kept(quarter, columns),) * 4,
         [VMEM, VMEM, ANY],
         [],
         16 * MIB,
         2 * front * quarter * columns,
         2 * front * quarter,
     )(masked, d_v, away_near)
-    got_e = row_swap(send_e, 0)
-    from_near = after(from_near, send_e)
+    from_near = after(from_near, pieces[0])
+    leaf_forward = pieces[0].astype(F32)
+    for phase in (2, 0, 1):
+        leaf_forward = leaf_forward + row_swap(pieces[1 + phase], phase).astype(F32)
+    leaf_forward = jnp.where(mask > 0, leaf_forward, 0.0).astype(BF)
+    near_e = jnp.concatenate([leaf_forward, row_swap(leaf_forward, 1)], 0)
+    far_e = row_swap(near_e, 0)
 
     term = update[quarter + half :] + from_far.astype(F32) - b_v[quarter:].astype(F32)
     from_near = from_near.astype(F32)
-    negated = jnp.concatenate([from_near[:half] + term, from_near[half:]], 0).astype(BF)
-    negated_other = leaf_swap(negated)
+    negated_mine = (from_near[:half] + term).astype(BF)
+    negated_yours = from_near[half:].astype(BF)
+    other_yours = leaf_swap(negated_yours)
+    other_mine = leaf_swap(negated_mine)
 
     partial = call(
         functools.partial(root_pivot_kernel, (half, front)),
         kept(4 * half, columns),
-        [VMEM, VMEM, VMEM],
+        [VMEM] * 5,
         [pltpu.VMEM((quarter, columns), BF)],
         16 * MIB,
-        front * quarter * columns,
-        front * quarter,
-    )(negated, negated_other, d_v)
-    home_e = added(keep_e, got_e)
-    away_e = home_e[quarter:].astype(BF)
-    got_e = row_swap(away_e, 1)
+        0,
+        0,
+    )(negated_mine, negated_yours, other_mine, other_yours, d_v)
     panel_rows = call(
         functools.partial(scatter_kernel, (quarter, updates)),
         kept(front, quarter),
@@ -476,12 +485,11 @@
         [*smem, pltpu.SemaphoreType.DMA((2,))],
         16 * MIB,
         0,
-        4 * front * quarter,
-    )(live, parent_map, w_v, away_e)
-    partial = added(partial, after(row_swap(partial, 0), panel_rows))
-    root_forward = (partial + row_swap(partial.astype(BF), 1).astype(F32)).astype(BF)
-    leaf_forward = home_e[:quarter] + got_e.astype(F32)
-    leaf_forward = jnp.where(mask > 0, leaf_forward, 0.0).astype(BF)
+        0,
+    )(live, parent_map, w_v, leaf_forward)
+    partial = added(partial, after(row_swap(partial, 1), panel_rows))
+    got = after(row_swap(partial.astype(BF), 0), near_e)
+    root_forward = (partial + got.astype(F32)).astype(BF)
 
     part, root_piece = call(
         functools.partial(root_transposed_kernel, (half, front)),
@@ -489,36 +497,33 @@
         [VMEM, VMEM],
         [pltpu.VMEM((quarter, columns), F32)],
         16 * MIB,
-        front * quarter * columns,
-        front * quarter,
+        0,
+        0,
     )(root_forward, d_v)
     got = leaf_swap(part)
     root_mine = added(part[:half], got[half:]).astype(BF)
     root_other = added(part[half:], got[:half]).astype(BF)
     root_rows = jnp.concatenate([root_mine, root_other], 0)
 
-    near_e = jnp.concatenate([leaf_forward, row_swap(leaf_forward, 1)], 0)
-    far_e = row_swap(near_e, 0)
-    forward = jnp.concatenate([leaf_forward, root_piece], 0)
-
-    near = row_swap(root_rows, 0)
+    near = row_swap(root_rows, 1)
     far = row_swap(root_mine, 2)
-    total = call(
+    total, forward = call(
         functools.partial(leaf_transposed_kernel, (quarter, half)),
-        kept(columns, quarter, F32),
-        [VMEM] * 6,
-        [pltpu.VMEM((front, columns), BF)],
+        (kept(columns, quarter, F32), stored(quarter + half, columns)),
+        [VMEM] * 7,
+        [pltpu.VMEM((front, columns), BF), pltpu.VMEM((quarter, columns), BF)],
         16 * MIB,
         2 * front * quarter * columns,
         2 * front * quarter,
-    )(near_e, far_e, d_v, mask, root_rows, panel_rows)
+    )(near_e, far_e, d_v, mask, root_rows, panel_rows, root_piece)
+    near = after(near, total)
     near_other = leaf_swap(near)
     far_other = leaf_swap(far)
     backward = call(
         functools.partial(last_kernel, (quarter, half)),
         stored(quarter + half, columns),
         [VMEM] * 7,
-        [],
+        [pltpu.VMEM((3 * quarter, columns), BF)],
         16 * MIB,
         front * quarter * columns,
         front * quarter,

time: 49.4 us -> 48.2 us (0.976)
  waiting for transfers between devices: 23.3 us -> 20 us
  starting transfers between devices: 14.9 us -> 17.5 us
  other arithmetic: 1.3 us -> 0.56 us
    ppermute x10 -> x11, waiting for transfers between devices: 20.7 us -> 16.4 us  [row_swap(): return lax.ppermute(value, ('leaf', 'row'), route)]
    ppermute x10 -> x11, starting transfers between devices: 14.2 us -> 16.2 us  [row_swap(): return lax.ppermute(value, ('leaf', 'row'), route)]
    ppermute x5 -> x6, waiting for transfers between devices: 2.65 us -> 3.51 us  [leaf_swap(): return lax.ppermute(value, 'leaf', [(0, 1), (1, 0)])]
    concatenate x2 -> x0, other arithmetic: 0.72 us -> none  [the longest x1 0.71 us: two_levels(): forward = jnp.concatenate([leaf_forward, root_piece], 0)]
    pallas_call x2, Pallas kernels: 1.99 us -> 2.63 us  [the longest x1 1.62 us: two_levels(): call(functools.partial(leaf_transposed_kernel, (quarter, half)), (kept(co...]
    ppermute x5 -> x6, starting transfers between devices: 0.67 us -> 1.24 us  [leaf_swap(): return lax.ppermute(value, 'leaf', [(0, 1), (1, 0)])]
  transfers between devices with their start and end apart: 15 -> 17, of which waited for: 9 -> 11; matrix products, arithmetic and copies ran while one was open for 3% -> 1% of each run, Pallas kernels for 8% -> 9%
where the time goes in v6:
time: 48.2 us; the launch traced here: 48.1 us
  waiting for transfers between devices  20 us (41%)
  starting transfers between devices  17.5 us (36%)
  Pallas kernels  9.31 us (19%)
  between operations  0.77 us (2%)
  other arithmetic  0.56 us (1%)
    ppermute x11, waiting for transfers between devices, row_swap(): return lax.ppermute(value, ('leaf', 'row'), route)  16.4 us
    ppermute x11, starting transfers between devices, row_swap(): return lax.ppermute(value, ('leaf', 'row'), route)  16.2 us
    ppermute x6, waiting for transfers between devices, leaf_swap(): return lax.ppermute(value, 'leaf', [(0, 1), (1, 0)])  3.51 us
    pallas_call x1, Pallas kernels, two_levels(): call(functools.partial(panel_kernel, (quarter, half, parts, updates)), (k...  3.21 us
    pallas_call x1, Pallas kernels, two_levels(): call(functools.partial(leaf_transposed_kernel, (quarter, half)), (kept(co...  1.62 us
    pallas_call x1, Pallas kernels, two_levels(): call(functools.partial(last_kernel, (quarter, half)), stored(quarter + ha...  1.4 us
    ppermute x6, starting transfers between devices, leaf_swap(): return lax.ppermute(value, 'leaf', [(0, 1), (1, 0)])  1.24 us
    pallas_call x1, Pallas kernels, two_levels(): call(functools.partial(leaf_pivot_kernel, quarter), (kept(quarter, column...  1.01 us
  transfers between devices with their start and end apart: 17, of which 11 were waited for; matrix products, arithmetic and copies ran while one was open for 1% of the time, Pallas kernels for 9%

profile of v6, /device:TPU:0, one launch (start us, length us, event | category | flops | bytes accessed | tf_op | source)
XLA Modules:
  0.0 48.1 jit_solution(17000678548242664767)
XLA Ops:
  0.6 3.2 %shard_map.68 = (bf16[1280,128]{1,0:T(8,128)(2,1)S(1)}, bf16[1280,128]{1,0:T(8,128)(2,1)S(1)}, bf16[960,128]{1,0:T(8,128)(2,1)S(1)}, bf16[640,128]{1,0:T(8,128)(...) custom-call(s32[3]{0:T(128)} %live.3, s32[2,12]{1,0:T(2,128)} %pmap.3, ...), custom_call_target="tpu_custom_call" | custom-call | flops 251658240 | bytes 1966080 | tf_op jit(solution)/shard_map/pallas_call | solution.py:424
  3.8 0.5 %collective-permute-start = (bf16[1280,128]{1,0:T(8,128)(2,1)S(1)}, bf16[1280,128]{1,0:T(8,128)(2,1)S(1)}, u32[]{:S(2)}, u32[]{:S(2)}) collective-permute-start(bf16[1280,128]{1,0:T(8,128)(2,1)S(1)} %get-tuple-element.25), channel_id=1, source_target_pairs={{0,16},{16,0},{1,17},{17,1},{2,18},{18,2},{3,19},{19,3},{4,20},{20... | collective-permute-start | bytes 983048 | tf_op jit(solution)/shard_map/ppermute | solution.py:399
  4.4 1.3 %collective-permute-done = bf16[1280,128]{1,0:T(8,128)(2,1)S(1)} collective-permute-done((bf16[1280,128]{1,0:T(8,128)(2,1)S(1)}, bf16[1280,128]{1,0:T(8,128)(2,1)S(1)}, u32[]{:S(2)}, u32[]{:S(2)}) %collective-permute-start) | collective-permute-done | bytes 327712 | tf_op jit(solution)/shard_map/ppermute | solution.py:399
  5.7 2.9 %collective-permute-start.6 = (bf16[640,128]{1,0:T(8,128)(2,1)S(1)}, bf16[640,128]{1,0:T(8,128)(2,1)S(1)}, u32[]{:S(2)}, u32[]{:S(2)}) collective-permute-start(bf16[640,128]{1,0:T(8,128)(2,1)S(1)} %slice.47.after), channel_id=1, source_target_pairs={{0,4},{4,0},{8,12},{12,8},{16,24},{20,28},{24,16},{28,20},{1,5},{5... | collective-permute-start | bytes 491528 | tf_op jit(solution)/shard_map/ppermute | solution.py:407
  8.7 1.5 %collective-permute-start.7 = (bf16[320,128]{1,0:T(8,128)(2,1)S(1)}, bf16[320,128]{1,0:T(8,128)(2,1)S(1)}, u32[]{:S(2)}, u32[]{:S(2)}) collective-permute-start(bf16[320,128]{1,0:T(8,128)(2,1)S(1)} %slice.49), channel_id=1, source_target_pairs={{0,12},{4,8},{8,4},{12,0},{16,28},{20,24},{24,20},{28,16},{1,13},{... | collective-permute-start | bytes 245768 | tf_op jit(solution)/shard_map/ppermute | solution.py:407
  10.2 1.0 %shard_map.69 = (bf16[640,128]{1,0:T(8,128)(2,1)S(1)}, bf16[640,128]{1,0:T(8,128)(2,1)S(1)}, bf16[640,128]{1,0:T(8,128)(2,1)S(1)}, bf16[640,128]{1,0:T(8,128)(2,1)S(1)}) custom-call(bf16[640,128]{1,0:T(8,128)(2,1)S(1)} %get-tuple-element.22.masked, bf16[3840,640]{1,0:T(8,128)(2,1)S(1)} %get-tuple-element.23.d_v, bf16[640,128]{1,0:T(8,128)(2,1)S(1)} %slice.47.after), custom_call_target="tpu_custom_call" | custom-call | flops 419430400 | bytes 3276800 | tf_op jit(solution)/shard_map/pallas_call | solution.py:448
  11.2 1.5 %collective-permute-start.1 = (bf16[640,128]{1,0:T(8,128)(2,1)S(1)}, bf16[640,128]{1,0:T(8,128)(2,1)S(1)}, u32[]{:S(2)}, u32[]{:S(2)}) collective-permute-start(bf16[640,128]{1,0:T(8,128)(2,1)S(1)} %get-tuple-element.27), channel_id=1, source_target_pairs={{0,12},{4,8},{8,4},{12,0},{16,28},{20,24},{24,20},{28,16},{1,13},{... | collective-permute-start | bytes 491528 | tf_op jit(solution)/shard_map/ppermute | solution.py:407
  12.7 0.1 collective-permute-start.2
  12.8 1.9 %collective-permute-start.3 = (bf16[640,128]{1,0:T(8,128)(2,1)S(1)}, bf16[640,128]{1,0:T(8,128)(2,1)S(1)}, u32[]{:S(2)}, u32[]{:S(2)}) collective-permute-start(bf16[640,128]{1,0:T(8,128)(2,1)S(1)} %get-tuple-element.29), channel_id=1, source_target_pairs={{0,8},{4,12},{8,0},{12,4},{16,20},{20,16},{24,28},{28,24},{1,9},{5... | collective-permute-start | bytes 491528 | tf_op jit(solution)/shard_map/ppermute | solution.py:407
  14.8 1.3 %collective-permute-done.7 = bf16[320,128]{1,0:T(8,128)(2,1)S(1)} collective-permute-done((bf16[320,128]{1,0:T(8,128)(2,1)S(1)}, bf16[320,128]{1,0:T(8,128)(2,1)S(1)}, u32[]{:S(2)}, u32[]{:S(2)}) %collective-permute-start.7) | collective-permute-done | bytes 81952 | tf_op jit(solution)/shard_map/ppermute | solution.py:407
  16.3 1.3 %collective-permute-done.8.other_mine = bf16[320,128]{1,0:T(8,128)(2,1)S(1)} collective-permute-done((bf16[320,128]{1,0:T(8,128)(2,1)S(1)}, bf16[320,128]{1,0:T(8,128)(2,1)S(1)}, u32[]{:S(2)}, u32[]{:S(2)}) %collective-permute-start.8) | collective-permute-done | bytes 81952 | tf_op jit(solution)/shard_map/ppermute | solution.py:399
  17.6 0.6 %shard_map.70 = bf16[1280,128]{1,0:T(8,128)(2,1)S(1)} custom-call(bf16[320,128]{1,0:T(8,128)(2,1)S(1)} %fusion.3.mine, bf16[320,128]{1,0:T(8,128)(2,1)S(1)} %slice.42.yours, bf16[320,128]{1,0:T(8,128)(2,1)S(1)} %collective-permute-done.8.other_mine, bf16[320,128]{1,0:T(8,128)(2,1)S(1)} %collective-permute-done.9.other_yours, ...), custom_call_target="tpu_custom_call" | custom-call | tf_op jit(solution)/shard_map/pallas_call | solution.py:472
  18.2 0.2 collective-permute-start.10
  18.4 1.2 %collective-permute-done.1 = bf16[640,128]{1,0:T(8,128)(2,1)S(1)} collective-permute-done((bf16[640,128]{1,0:T(8,128)(2,1)S(1)}, bf16[640,128]{1,0:T(8,128)(2,1)S(1)}, u32[]{:S(2)}, u32[]{:S(2)}) %collective-permute-start.1) | collective-permute-done | bytes 163872 | tf_op jit(solution)/shard_map/ppermute | solution.py:407
  19.6 1.7 %collective-permute-done.2 = bf16[640,128]{1,0:T(8,128)(2,1)S(1)} collective-permute-done((bf16[640,128]{1,0:T(8,128)(2,1)S(1)}, bf16[640,128]{1,0:T(8,128)(2,1)S(1)}, u32[]{:S(2)}, u32[]{:S(2)}) %collective-permute-start.2) | collective-permute-done | bytes 163872 | tf_op jit(solution)/shard_map/ppermute | solution.py:407
  21.3 0.9 %collective-permute-done.3 = bf16[640,128]{1,0:T(8,128)(2,1)S(1)} collective-permute-done((bf16[640,128]{1,0:T(8,128)(2,1)S(1)}, bf16[640,128]{1,0:T(8,128)(2,1)S(1)}, u32[]{:S(2)}, u32[]{:S(2)}) %collective-permute-start.3) | collective-permute-done | bytes 163872 | tf_op jit(solution)/shard_map/ppermute | solution.py:407
  22.2 0.1 select_convert_fusion.after
  22.3 1.5 %collective-permute-start.4 = (bf16[640,128]{1,0:T(8,128)(2,1)S(1)}, bf16[640,128]{1,0:T(8,128)(2,1)S(1)}, u32[]{:S(2)}, u32[]{:S(2)}) collective-permute-start(bf16[640,128]{1,0:T(8,128)(2,1)S(1)} %select_convert_fusion.after), channel_id=1, source_target_pairs={{0,8},{4,12},{8,0},{12,4},{16,20},{20,16},{24,28},{28,24},{1,9},{5... | collective-permute-start | bytes 491528 | tf_op jit(solution)/shard_map/ppermute | solution.py:407
  23.9 0.8 %shard_map.71.panel_rows = bf16[2560,640]{1,0:T(8,128)(2,1)S(1)} custom-call(s32[3]{0:T(128)S(1)} %copy-done.1, s32[2,12]{1,0:T(2,128)S(1)} %copy-done, bf16[1536,640]{1,0:T(8,128)(2,1)S(1)} %get-tuple-element.32.w_v, bf16[640,128]{1,0:T(8,128)(2,1)S(1)} %select_convert_fusion.after), custom_call_target="tpu_custom_call" | custom-call | tf_op jit(solution)/shard_map/pallas_call | solution.py:481
  24.7 1.0 %collective-permute-done.10 = bf16[1280,128]{1,0:T(8,128)(2,1)S(1)} collective-permute-done((bf16[1280,128]{1,0:T(8,128)(2,1)S(1)}, bf16[1280,128]{1,0:T(8,128)(2,1)S(1)}, u32[]{:S(2)}, u32[]{:S(2)}) %collective-permute-start.10) | collective-permute-done | bytes 327712 | tf_op jit(solution)/shard_map/ppermute | solution.py:407
  25.8 1.8 %collective-permute-start.11 = (bf16[1280,128]{1,0:T(8,128)(2,1)S(1)}, bf16[1280,128]{1,0:T(8,128)(2,1)S(1)}, u32[]{:S(2)}, u32[]{:S(2)}) collective-permute-start(bf16[1280,128]{1,0:T(8,128)(2,1)S(1)} %fusion), channel_id=1, source_target_pairs={{0,4},{4,0},{8,12},{12,8},{16,24},{20,28},{24,16},{28,20},{1,5},{5... | collective-permute-start | bytes 983048 | tf_op jit(solution)/shard_map/ppermute | solution.py:407
  27.8 5.2 %collective-permute-done.11 = bf16[1280,128]{1,0:T(8,128)(2,1)S(1)} collective-permute-done((bf16[1280,128]{1,0:T(8,128)(2,1)S(1)}, bf16[1280,128]{1,0:T(8,128)(2,1)S(1)}, u32[]{:S(2)}, u32[]{:S(2)}) %collective-permute-start.11) | collective-permute-done | bytes 327712 | tf_op jit(solution)/shard_map/ppermute | solution.py:407
  33.0 0.1 add_convert_fusion.y
  33.1 0.6 %shard_map.72 = (bf16[640,128]{1,0:T(8,128)(2,1)S(1)}, bf16[320,128]{1,0:T(8,128)(2,1)S(1)}) custom-call(bf16[1280,128]{1,0:T(8,128)(2,1)S(1)} %add_convert_fusion.y, bf16[3840,640]{1,0:T(8,128)(2,1)S(1)} %get-tuple-element.23.d_v), custom_call_target="tpu_custom_call" | custom-call | tf_op jit(solution)/shard_map/pallas_call | solution.py:494
  33.8 1.8 %collective-permute-start.5 = (bf16[1280,128]{1,0:T(8,128)(2,1)S(1)}, bf16[1280,128]{1,0:T(8,128)(2,1)S(1)}, u32[]{:S(2)}, u32[]{:S(2)}) collective-permute-start(bf16[1280,128]{1,0:T(8,128)(2,1)S(1)} %pad_maximum_fusion.near), channel_id=1, source_target_pairs={{0,4},{4,0},{8,12},{12,8},{16,24},{20,28},{24,16},{28,20},{1,5},{5... | collective-permute-start | bytes 983048 | tf_op jit(solution)/shard_map/ppermute | solution.py:407
  35.7 0.3 collective-permute-start.13
  36.0 2.5 %collective-permute-start.15 = (bf16[320,128]{1,0:T(8,128)(2,1)S(1)}, bf16[320,128]{1,0:T(8,128)(2,1)S(1)}, u32[]{:S(2)}, u32[]{:S(2)}) collective-permute-start(bf16[320,128]{1,0:T(8,128)(2,1)S(1)} %get-tuple-element.42), channel_id=1, source_target_pairs={{0,12},{4,8},{8,4},{12,0},{16,28},{20,24},{24,20},{28,16},{1,13},{... | collective-permute-start | bytes 245768 | tf_op jit(solution)/shard_map/ppermute | solution.py:407
  38.5 5.0 %collective-permute-done.5.far = bf16[1280,128]{1,0:T(8,128)(2,1)S(1)} collective-permute-done((bf16[1280,128]{1,0:T(8,128)(2,1)S(1)}, bf16[1280,128]{1,0:T(8,128)(2,1)S(1)}, u32[]{:S(2)}, u32[]{:S(2)}) %collective-permute-start.5) | collective-permute-done | bytes 327712 | tf_op jit(solution)/shard_map/ppermute | solution.py:407
  43.5 1.6 %shard_map.73 = (f32[128,640]{1,0:T(8,128)S(1)}, bf16[960,128]{1,0:T(8,128)(2,1)}) custom-call(bf16[1280,128]{1,0:T(8,128)(2,1)S(1)} %pad_maximum_fusion.near, bf16[1280,128]{1,0:T(8,128)(2,1)S(1)} %collective-permute-done.5.far, bf16[3840,640]{1,0:T(8,128)(2,1)S(1)} %get-tuple-element.23.d_v, bf16[640,128]{1,0:T(8,128)(2,1)S(1)} %get-tuple-element.21.mask, ...), custom_call_target="tpu_custom_call" | custom-call | flops 419430400 | bytes 3276800 | tf_op jit(solution)/shard_map/pallas_call | solution.py:510
  45.2 0.5 %collective-permute-start.16 = (bf16[320,128]{1,0:T(8,128)(2,1)S(1)}, bf16[320,128]{1,0:T(8,128)(2,1)S(1)}, u32[]{:S(2)}, u32[]{:S(2)}) collective-permute-start(bf16[320,128]{1,0:T(8,128)(2,1)S(1)} %collective-permute-done.15.mine_far), channel_id=1, source_target_pairs={{0,16},{16,0},{1,17},{17,1},{2,18},{18,2},{3,19},{19,3},{4,20},{20... | collective-permute-start | bytes 245768 | tf_op jit(solution)/shard_map/ppermute | solution.py:399
  45.7 1.0 %collective-permute-done.16.theirs_far = bf16[320,128]{1,0:T(8,128)(2,1)S(1)} collective-permute-done((bf16[320,128]{1,0:T(8,128)(2,1)S(1)}, bf16[320,128]{1,0:T(8,128)(2,1)S(1)}, u32[]{:S(2)}, u32[]{:S(2)}) %collective-permute-start.16) | collective-permute-done | bytes 81952 | tf_op jit(solution)/shard_map/ppermute | solution.py:399
  46.7 1.4 %shard_map.74 = bf16[960,128]{1,0:T(8,128)(2,1)} custom-call(bf16[640,128]{1,0:T(8,128)(2,1)S(1)} %collective-permute-done.13.mine, bf16[640,128]{1,0:T(8,128)(2,1)S(1)} %collective-permute-done.14.theirs, bf16[320,128]{1,0:T(8,128)(2,1)S(1)} %collective-permute-done.15.mine_far, bf16[320,128]{1,0:T(8,128)(2,1)S(1)} %collective-permute-done.16.theirs_far, ...), custom_call_target="tpu_custom_call" | custom-call | flops 209715200 | bytes 1638400 | tf_op jit(solution)/shard_map/pallas_call | solution.py:522
  (24 shorter events, 0.7 us)
Async XLA Ops:
  3.8 1.8 %collective-permute-start = (bf16[1280,128]{1,0:T(8,128)(2,1)S(1)}, bf16[1280,128]{1,0:T(8,128)(2,1)S(1)}, u32[]{:S(2)}, u32[]{:S(2)}) collective-permute-start(bf16[1280,128]{1,0:T(8,128)(2,1)S(1)} %get-tuple-element.25), channel_id=1, source_target_pairs={{0,16},{16,0},{1,17},{17,1},{2,18},{18,2},{3,19},{19,3},{4,20},{20... | collective-permute-start | bytes 983048 | tf_op jit(solution)/shard_map/ppermute | solution.py:399
  5.7 9.0 %collective-permute-start.6 = (bf16[640,128]{1,0:T(8,128)(2,1)S(1)}, bf16[640,128]{1,0:T(8,128)(2,1)S(1)}, u32[]{:S(2)}, u32[]{:S(2)}) collective-permute-start(bf16[640,128]{1,0:T(8,128)(2,1)S(1)} %slice.47.after), channel_id=1, source_target_pairs={{0,4},{4,0},{8,12},{12,8},{16,24},{20,28},{24,16},{28,20},{1,5},{5... | collective-permute-start | bytes 491528 | tf_op jit(solution)/shard_map/ppermute | solution.py:407
  8.7 7.5 %collective-permute-start.7 = (bf16[320,128]{1,0:T(8,128)(2,1)S(1)}, bf16[320,128]{1,0:T(8,128)(2,1)S(1)}, u32[]{:S(2)}, u32[]{:S(2)}) collective-permute-start(bf16[320,128]{1,0:T(8,128)(2,1)S(1)} %slice.49), channel_id=1, source_target_pairs={{0,12},{4,8},{8,4},{12,0},{16,28},{20,24},{24,20},{28,16},{1,13},{... | collective-permute-start | bytes 245768 | tf_op jit(solution)/shard_map/ppermute | solution.py:407
  11.2 8.4 %collective-permute-start.1 = (bf16[640,128]{1,0:T(8,128)(2,1)S(1)}, bf16[640,128]{1,0:T(8,128)(2,1)S(1)}, u32[]{:S(2)}, u32[]{:S(2)}) collective-permute-start(bf16[640,128]{1,0:T(8,128)(2,1)S(1)} %get-tuple-element.27), channel_id=1, source_target_pairs={{0,12},{4,8},{8,4},{12,0},{16,28},{20,24},{24,20},{28,16},{1,13},{... | collective-permute-start | bytes 491528 | tf_op jit(solution)/shard_map/ppermute | solution.py:407
  12.7 8.6 %collective-permute-start.2 = (bf16[640,128]{1,0:T(8,128)(2,1)S(1)}, bf16[640,128]{1,0:T(8,128)(2,1)S(1)}, u32[]{:S(2)}, u32[]{:S(2)}) collective-permute-start(bf16[640,128]{1,0:T(8,128)(2,1)S(1)} %get-tuple-element.28), channel_id=1, source_target_pairs={{0,4},{4,0},{8,12},{12,8},{16,24},{20,28},{24,16},{28,20},{1,5},{5... | collective-permute-start | bytes 491528 | tf_op jit(solution)/shard_map/ppermute | solution.py:407
  12.8 9.4 %collective-permute-start.3 = (bf16[640,128]{1,0:T(8,128)(2,1)S(1)}, bf16[640,128]{1,0:T(8,128)(2,1)S(1)}, u32[]{:S(2)}, u32[]{:S(2)}) collective-permute-start(bf16[640,128]{1,0:T(8,128)(2,1)S(1)} %get-tuple-element.29), channel_id=1, source_target_pairs={{0,8},{4,12},{8,0},{12,4},{16,20},{20,16},{24,28},{28,24},{1,9},{5... | collective-permute-start | bytes 491528 | tf_op jit(solution)/shard_map/ppermute | solution.py:407
  14.7 1.6 %collective-permute-start.9 = (bf16[320,128]{1,0:T(8,128)(2,1)S(1)}, bf16[320,128]{1,0:T(8,128)(2,1)S(1)}, u32[]{:S(2)}, u32[]{:S(2)}) collective-permute-start(bf16[320,128]{1,0:T(8,128)(2,1)S(1)} %slice.42.yours), channel_id=1, source_target_pairs={{0,16},{16,0},{1,17},{17,1},{2,18},{18,2},{3,19},{19,3},{4,20},{20... | collective-permute-start | bytes 245768 | tf_op jit(solution)/shard_map/ppermute | solution.py:399
  16.2 7.7 %copy-start = (s32[2,12]{1,0:T(2,128)S(1)}, s32[2,12]{1,0:T(2,128)}, u32[]{:S(2)}) copy-start(s32[2,12]{1,0:T(2,128)} %pmap.3) | copy-start | bytes 292
  16.2 7.7 %copy-start.1 = (s32[3]{0:T(128)S(1)}, s32[3]{0:T(128)}, u32[]{:S(2)}) copy-start(s32[3]{0:T(128)} %live.3) | copy-start | bytes 40
  16.2 1.3 %collective-permute-start.8 = (bf16[320,128]{1,0:T(8,128)(2,1)S(1)}, bf16[320,128]{1,0:T(8,128)(2,1)S(1)}, u32[]{:S(2)}, u32[]{:S(2)}) collective-permute-start(bf16[320,128]{1,0:T(8,128)(2,1)S(1)} %fusion.3.mine), channel_id=1, source_target_pairs={{0,16},{16,0},{1,17},{17,1},{2,18},{18,2},{3,19},{19,3},{4,20},{20... | collective-permute-start | bytes 245768 | tf_op jit(solution)/shard_map/ppermute | solution.py:399
  18.2 7.5 %collective-permute-start.10 = (bf16[1280,128]{1,0:T(8,128)(2,1)S(1)}, bf16[1280,128]{1,0:T(8,128)(2,1)S(1)}, u32[]{:S(2)}, u32[]{:S(2)}) collective-permute-start(bf16[1280,128]{1,0:T(8,128)(2,1)S(1)} %shard_map.70), channel_id=1, source_target_pairs={{0,8},{4,12},{8,0},{12,4},{16,20},{20,16},{24,28},{28,24},{1,9},{5... | collective-permute-start | bytes 983048 | tf_op jit(solution)/shard_map/ppermute | solution.py:407
  22.3 5.4 %collective-permute-start.4 = (bf16[640,128]{1,0:T(8,128)(2,1)S(1)}, bf16[640,128]{1,0:T(8,128)(2,1)S(1)}, u32[]{:S(2)}, u32[]{:S(2)}) collective-permute-start(bf16[640,128]{1,0:T(8,128)(2,1)S(1)} %select_convert_fusion.after), channel_id=1, source_target_pairs={{0,8},{4,12},{8,0},{12,4},{16,20},{20,16},{24,28},{28,24},{1,9},{5... | collective-permute-start | bytes 491528 | tf_op jit(solution)/shard_map/ppermute | solution.py:407
  25.8 7.1 %collective-permute-start.11 = (bf16[1280,128]{1,0:T(8,128)(2,1)S(1)}, bf16[1280,128]{1,0:T(8,128)(2,1)S(1)}, u32[]{:S(2)}, u32[]{:S(2)}) collective-permute-start(bf16[1280,128]{1,0:T(8,128)(2,1)S(1)} %fusion), channel_id=1, source_target_pairs={{0,4},{4,0},{8,12},{12,8},{16,24},{20,28},{24,16},{28,20},{1,5},{5... | collective-permute-start | bytes 983048 | tf_op jit(solution)/shard_map/ppermute | solution.py:407
  33.7 1.9 %collective-permute-start.12 = (bf16[640,128]{1,0:T(8,128)(2,1)S(1)}, bf16[640,128]{1,0:T(8,128)(2,1)S(1)}, u32[]{:S(2)}, u32[]{:S(2)}) collective-permute-start(bf16[640,128]{1,0:T(8,128)(2,1)S(1)} %get-tuple-element.35), channel_id=1, source_target_pairs={{0,16},{16,0},{1,17},{17,1},{2,18},{18,2},{3,19},{19,3},{4,20},{20... | collective-permute-start | bytes 491528 | tf_op jit(solution)/shard_map/ppermute | solution.py:399
  33.8 9.8 %collective-permute-start.5 = (bf16[1280,128]{1,0:T(8,128)(2,1)S(1)}, bf16[1280,128]{1,0:T(8,128)(2,1)S(1)}, u32[]{:S(2)}, u32[]{:S(2)}) collective-permute-start(bf16[1280,128]{1,0:T(8,128)(2,1)S(1)} %pad_maximum_fusion.near), channel_id=1, source_target_pairs={{0,4},{4,0},{8,12},{12,8},{16,24},{20,28},{24,16},{28,20},{1,5},{5... | collective-permute-start | bytes 983048 | tf_op jit(solution)/shard_map/ppermute | solution.py:407
  35.7 9.5 %collective-permute-start.13 = (bf16[640,128]{1,0:T(8,128)(2,1)S(1)}, bf16[640,128]{1,0:T(8,128)(2,1)S(1)}, u32[]{:S(2)}, u32[]{:S(2)}) collective-permute-start(bf16[640,128]{1,0:T(8,128)(2,1)S(1)} %pad_maximum_fusion.1.root_rows), channel_id=1, source_target_pairs={{0,8},{4,12},{8,0},{12,4},{16,20},{20,16},{24,28},{28,24},{1,9},{5... | collective-permute-start | bytes 491528 | tf_op jit(solution)/shard_map/ppermute | solution.py:407
  36.0 9.2 %collective-permute-start.15 = (bf16[320,128]{1,0:T(8,128)(2,1)S(1)}, bf16[320,128]{1,0:T(8,128)(2,1)S(1)}, u32[]{:S(2)}, u32[]{:S(2)}) collective-permute-start(bf16[320,128]{1,0:T(8,128)(2,1)S(1)} %get-tuple-element.42), channel_id=1, source_target_pairs={{0,12},{4,8},{8,4},{12,0},{16,28},{20,24},{24,20},{28,16},{1,13},{... | collective-permute-start | bytes 245768 | tf_op jit(solution)/shard_map/ppermute | solution.py:407
  45.2 1.5 %collective-permute-start.14 = (bf16[640,128]{1,0:T(8,128)(2,1)S(1)}, bf16[640,128]{1,0:T(8,128)(2,1)S(1)}, u32[]{:S(2)}, u32[]{:S(2)}) collective-permute-start(bf16[640,128]{1,0:T(8,128)(2,1)S(1)} %collective-permute-done.13.mine), channel_id=1, source_target_pairs={{0,16},{16,0},{1,17},{17,1},{2,18},{18,2},{3,19},{19,3},{4,20},{20... | collective-permute-start | bytes 491528 | tf_op jit(solution)/shard_map/ppermute | solution.py:399
  45.2 1.5 %collective-permute-start.16 = (bf16[320,128]{1,0:T(8,128)(2,1)S(1)}, bf16[320,128]{1,0:T(8,128)(2,1)S(1)}, u32[]{:S(2)}, u32[]{:S(2)}) collective-permute-start(bf16[320,128]{1,0:T(8,128)(2,1)S(1)} %collective-permute-done.15.mine_far), channel_id=1, source_target_pairs={{0,16},{16,0},{1,17},{17,1},{2,18},{18,2},{3,19},{19,3},{4,20},{20... | collective-permute-start | bytes 245768 | tf_op jit(solution)/shard_map/ppermute | solution.py:399

commit v7 on v6

--- a/solution.py
+++ b/solution.py
@@ -364,19 +364,29 @@
 
 
 def leaf_transposed_kernel(
-    sizes, near, far, d_v, mask, root_rows, panel_rows, root_piece, total, forward, y_v, s_v
+    sizes,
+    own,
+    rows_x,
+    rows_y,
+    rows_d,
+    d_v,
+    mask,
+    root_rows,
+    panel_rows,
+    root_piece,
+    total,
+    forward,
+    y_v,
+    s_v,
 ):
     quarter, half = sizes
     row_pos = lax.axis_index("row")
     leaf_pos = lax.axis_index("leaf")
     order = row_order(row_pos, leaf_pos)
-    own = near[pl.ds(0, quarter)]
-    forward[pl.ds(0, quarter)] = own
+    forward[pl.ds(0, quarter)] = own[...]
     forward[pl.ds(quarter, half)] = root_piece[...]
-    for k, part in enumerate(
-        (own, near[pl.ds(quarter, quarter)], far[pl.ds(0, quarter)], far[pl.ds(quarter, quarter)])
-    ):
-        y_v[rows_at(order[(0, 2, 1, 3)[k]] * quarter, quarter)] = part
+    for k, part in enumerate((own, rows_x, rows_y, rows_d)):
+        y_v[rows_at(order[k] * quarter, quarter)] = part[...]
     value = mm(y_v[...].T, d_v[pl.ds(0, 4 * quarter)])
     value = jnp.where(mask[...].astype(F32).T > 0.0, value, 0.0)
     put(s_v, 0, half, root_rows, (leaf_pos, 1 - leaf_pos))
@@ -459,8 +469,9 @@
     for phase in (2, 0, 1):
         leaf_forward = leaf_forward + row_swap(pieces[1 + phase], phase).astype(F32)
     leaf_forward = jnp.where(mask > 0, leaf_forward, 0.0).astype(BF)
-    near_e = jnp.concatenate([leaf_forward, row_swap(leaf_forward, 1)], 0)
-    far_e = row_swap(near_e, 0)
+    rows_y = row_swap(leaf_forward, 1)
+    rows_x = row_swap(leaf_forward, 0)
+    rows_d = row_swap(rows_y, 0)
 
     term = update[quarter + half :] + from_far.astype(F32) - b_v[quarter:].astype(F32)
     from_near = from_near.astype(F32)
@@ -484,11 +495,11 @@
         [ANY, ANY, VMEM, ANY],
         [*smem, pltpu.SemaphoreType.DMA((2,))],
         16 * MIB,
-        0,
-        0,
-    )(live, parent_map, w_v, leaf_forward)
-    partial = added(partial, after(row_swap(partial, 1), panel_rows))
-    got = after(row_swap(partial.astype(BF), 0), near_e)
+        2000000000,
+        4 * front * quarter,
+    )(live, parent_map, w_v, after(rows_y, rows_x))
+    partial = added(partial, row_swap(partial, 1))
+    got = after(row_swap(partial.astype(BF), 0), panel_rows)
     root_forward = (partial + got.astype(F32)).astype(BF)
 
     part, root_piece = call(
@@ -500,7 +511,7 @@
         0,
         0,
     )(root_forward, d_v)
-    got = leaf_swap(part)
+    got = after(leaf_swap(part), rows_d)
     root_mine = added(part[:half], got[half:]).astype(BF)
     root_other = added(part[half:], got[:half]).astype(BF)
     root_rows = jnp.concatenate([root_mine, root_other], 0)
@@ -510,12 +521,12 @@
     total, forward = call(
         functools.partial(leaf_transposed_kernel, (quarter, half)),
         (kept(columns, quarter, F32), stored(quarter + half, columns)),
-        [VMEM] * 7,
+        [VMEM] * 9,
         [pltpu.VMEM((front, columns), BF), pltpu.VMEM((quarter, columns), BF)],
         16 * MIB,
         2 * front * quarter * columns,
         2 * front * quarter,
-    )(near_e, far_e, d_v, mask, root_rows, panel_rows, root_piece)
+    )(leaf_forward, rows_x, rows_y, rows_d, d_v, mask, root_rows, panel_rows, root_piece)
     near = after(near, total)
     near_other = leaf_swap(near)
     far_other = leaf_swap(far)

time: 48.2 us -> 45.9 us (0.952)
  waiting for transfers between devices: 20 us -> 14 us
  starting transfers between devices: 17.5 us -> 21 us
    ppermute x11 -> x12, waiting for transfers between devices: 16.4 us -> 10 us  [row_swap(): return lax.ppermute(value, ('leaf', 'row'), route)]
    ppermute x11 -> x12, starting transfers between devices: 16.2 us -> 19.8 us  [row_swap(): return lax.ppermute(value, ('leaf', 'row'), route)]
  transfers between devices with their start and end apart: 17 -> 18, of which waited for: 11 -> 12; matrix products, arithmetic and copies ran while one was open for 1% -> 1% of each run, Pallas kernels for 9% -> 10%
where the time goes in v7:
time: 45.9 us; the launch traced here: 45.7 us
  starting transfers between devices  21 us (46%)
  waiting for transfers between devices  14 us (31%)
  Pallas kernels  9.31 us (20%)
  between operations  0.79 us (2%)
  other arithmetic  0.53 us (1%)
    ppermute x12, starting transfers between devices, row_swap(): return lax.ppermute(value, ('leaf', 'row'), route)  19.8 us
    ppermute x12, waiting for transfers between devices, row_swap(): return lax.ppermute(value, ('leaf', 'row'), route)  10 us
    ppermute x6, waiting for transfers between devices, leaf_swap(): return lax.ppermute(value, 'leaf', [(0, 1), (1, 0)])  3.94 us
    pallas_call x1, Pallas kernels, two_levels(): call(functools.partial(panel_kernel, (quarter, half, parts, updates)), (k...  3.21 us
    pallas_call x1, Pallas kernels, two_levels(): call(functools.partial(leaf_transposed_kernel, (quarter, half)), (kept(co...  1.61 us
    pallas_call x1, Pallas kernels, two_levels(): call(functools.partial(last_kernel, (quarter, half)), stored(quarter + ha...  1.42 us
    ppermute x6, starting transfers between devices, leaf_swap(): return lax.ppermute(value, 'leaf', [(0, 1), (1, 0)])  1.24 us
    pallas_call x1, Pallas kernels, two_levels(): call(functools.partial(leaf_pivot_kernel, quarter), (kept(quarter, column...  1.01 us
  transfers between devices with their start and end apart: 18, of which 12 were waited for; matrix products, arithmetic and copies ran while one was open for 1% of the time, Pallas kernels for 10%

profile of v7, /device:TPU:0, one launch (start us, length us, event | category | flops | bytes accessed | tf_op | source)
XLA Modules:
  0.0 45.7 jit_solution(18268072237561487273)
XLA Ops:
  0.6 3.2 %shard_map.68 = (bf16[1280,128]{1,0:T(8,128)(2,1)S(1)}, bf16[1280,128]{1,0:T(8,128)(2,1)S(1)}, bf16[960,128]{1,0:T(8,128)(2,1)S(1)}, bf16[640,128]{1,0:T(8,128)(...) custom-call(s32[3]{0:T(128)} %live.3, s32[2,12]{1,0:T(2,128)} %pmap.3, ...), custom_call_target="tpu_custom_call" | custom-call | flops 251658240 | bytes 1966080 | tf_op jit(solution)/shard_map/pallas_call | solution.py:434
  3.9 0.5 %collective-permute-start = (bf16[1280,128]{1,0:T(8,128)(2,1)S(1)}, bf16[1280,128]{1,0:T(8,128)(2,1)S(1)}, u32[]{:S(2)}, u32[]{:S(2)}) collective-permute-start(bf16[1280,128]{1,0:T(8,128)(2,1)S(1)} %get-tuple-element.26), channel_id=1, source_target_pairs={{0,16},{16,0},{1,17},{17,1},{2,18},{18,2},{3,19},{19,3},{4,20},{20... | collective-permute-start | bytes 983048 | tf_op jit(solution)/shard_map/ppermute | solution.py:409
  4.4 1.3 %collective-permute-done = bf16[1280,128]{1,0:T(8,128)(2,1)S(1)} collective-permute-done((bf16[1280,128]{1,0:T(8,128)(2,1)S(1)}, bf16[1280,128]{1,0:T(8,128)(2,1)S(1)}, u32[]{:S(2)}, u32[]{:S(2)}) %collective-permute-start) | collective-permute-done | bytes 327712 | tf_op jit(solution)/shard_map/ppermute | solution.py:409
  5.7 2.9 %collective-permute-start.7 = (bf16[640,128]{1,0:T(8,128)(2,1)S(1)}, bf16[640,128]{1,0:T(8,128)(2,1)S(1)}, u32[]{:S(2)}, u32[]{:S(2)}) collective-permute-start(bf16[640,128]{1,0:T(8,128)(2,1)S(1)} %slice.47.after), channel_id=1, source_target_pairs={{0,4},{4,0},{8,12},{12,8},{16,24},{20,28},{24,16},{28,20},{1,5},{5... | collective-permute-start | bytes 491528 | tf_op jit(solution)/shard_map/ppermute | solution.py:417
  8.7 1.5 %collective-permute-start.8 = (bf16[320,128]{1,0:T(8,128)(2,1)S(1)}, bf16[320,128]{1,0:T(8,128)(2,1)S(1)}, u32[]{:S(2)}, u32[]{:S(2)}) collective-permute-start(bf16[320,128]{1,0:T(8,128)(2,1)S(1)} %slice.49), channel_id=1, source_target_pairs={{0,12},{4,8},{8,4},{12,0},{16,28},{20,24},{24,20},{28,16},{1,13},{... | collective-permute-start | bytes 245768 | tf_op jit(solution)/shard_map/ppermute | solution.py:417
  10.2 1.0 %shard_map.69 = (bf16[640,128]{1,0:T(8,128)(2,1)S(1)}, bf16[640,128]{1,0:T(8,128)(2,1)S(1)}, bf16[640,128]{1,0:T(8,128)(2,1)S(1)}, bf16[640,128]{1,0:T(8,128)(2,1)S(1)}) custom-call(bf16[640,128]{1,0:T(8,128)(2,1)S(1)} %get-tuple-element.23.masked, bf16[3840,640]{1,0:T(8,128)(2,1)S(1)} %get-tuple-element.24.d_v, bf16[640,128]{1,0:T(8,128)(2,1)S(1)} %slice.47.after), custom_call_target="tpu_custom_call" | custom-call | flops 419430400 | bytes 3276800 | tf_op jit(solution)/shard_map/pallas_call | solution.py:458
  11.2 1.5 %collective-permute-start.1 = (bf16[640,128]{1,0:T(8,128)(2,1)S(1)}, bf16[640,128]{1,0:T(8,128)(2,1)S(1)}, u32[]{:S(2)}, u32[]{:S(2)}) collective-permute-start(bf16[640,128]{1,0:T(8,128)(2,1)S(1)} %get-tuple-element.28), channel_id=1, source_target_pairs={{0,12},{4,8},{8,4},{12,0},{16,28},{20,24},{24,20},{28,16},{1,13},{... | collective-permute-start | bytes 491528 | tf_op jit(solution)/shard_map/ppermute | solution.py:417
  12.8 1.9 %collective-permute-start.3 = (bf16[640,128]{1,0:T(8,128)(2,1)S(1)}, bf16[640,128]{1,0:T(8,128)(2,1)S(1)}, u32[]{:S(2)}, u32[]{:S(2)}) collective-permute-start(bf16[640,128]{1,0:T(8,128)(2,1)S(1)} %get-tuple-element.30), channel_id=1, source_target_pairs={{0,8},{4,12},{8,0},{12,4},{16,20},{20,16},{24,28},{28,24},{1,9},{5... | collective-permute-start | bytes 491528 | tf_op jit(solution)/shard_map/ppermute | solution.py:417
  14.8 1.3 %collective-permute-done.8 = bf16[320,128]{1,0:T(8,128)(2,1)S(1)} collective-permute-done((bf16[320,128]{1,0:T(8,128)(2,1)S(1)}, bf16[320,128]{1,0:T(8,128)(2,1)S(1)}, u32[]{:S(2)}, u32[]{:S(2)}) %collective-permute-start.8) | collective-permute-done | bytes 81952 | tf_op jit(solution)/shard_map/ppermute | solution.py:417
  16.3 1.3 %collective-permute-done.9.other_mine = bf16[320,128]{1,0:T(8,128)(2,1)S(1)} collective-permute-done((bf16[320,128]{1,0:T(8,128)(2,1)S(1)}, bf16[320,128]{1,0:T(8,128)(2,1)S(1)}, u32[]{:S(2)}, u32[]{:S(2)}) %collective-permute-start.9) | collective-permute-done | bytes 81952 | tf_op jit(solution)/shard_map/ppermute | solution.py:409
  17.6 0.6 %shard_map.70 = bf16[1280,128]{1,0:T(8,128)(2,1)S(1)} custom-call(bf16[320,128]{1,0:T(8,128)(2,1)S(1)} %fusion.3.mine, bf16[320,128]{1,0:T(8,128)(2,1)S(1)} %slice.42.yours, bf16[320,128]{1,0:T(8,128)(2,1)S(1)} %collective-permute-done.9.other_mine, bf16[320,128]{1,0:T(8,128)(2,1)S(1)} %collective-permute-done.10.other_yours, ...), custom_call_target="tpu_custom_call" | custom-call | tf_op jit(solution)/shard_map/pallas_call | solution.py:483
  18.2 0.2 collective-permute-start.11
  18.5 1.1 %collective-permute-done.1 = bf16[640,128]{1,0:T(8,128)(2,1)S(1)} collective-permute-done((bf16[640,128]{1,0:T(8,128)(2,1)S(1)}, bf16[640,128]{1,0:T(8,128)(2,1)S(1)}, u32[]{:S(2)}, u32[]{:S(2)}) %collective-permute-start.1) | collective-permute-done | bytes 163872 | tf_op jit(solution)/shard_map/ppermute | solution.py:417
  19.6 1.7 %collective-permute-done.2 = bf16[640,128]{1,0:T(8,128)(2,1)S(1)} collective-permute-done((bf16[640,128]{1,0:T(8,128)(2,1)S(1)}, bf16[640,128]{1,0:T(8,128)(2,1)S(1)}, u32[]{:S(2)}, u32[]{:S(2)}) %collective-permute-start.2) | collective-permute-done | bytes 163872 | tf_op jit(solution)/shard_map/ppermute | solution.py:417
  21.3 0.9 %collective-permute-done.3 = bf16[640,128]{1,0:T(8,128)(2,1)S(1)} collective-permute-done((bf16[640,128]{1,0:T(8,128)(2,1)S(1)}, bf16[640,128]{1,0:T(8,128)(2,1)S(1)}, u32[]{:S(2)}, u32[]{:S(2)}) %collective-permute-start.3) | collective-permute-done | bytes 163872 | tf_op jit(solution)/shard_map/ppermute | solution.py:417
  22.4 1.5 %collective-permute-start.5 = (bf16[640,128]{1,0:T(8,128)(2,1)S(1)}, bf16[640,128]{1,0:T(8,128)(2,1)S(1)}, u32[]{:S(2)}, u32[]{:S(2)}) collective-permute-start(bf16[640,128]{1,0:T(8,128)(2,1)S(1)} %select_convert_fusion.own), channel_id=1, source_target_pairs={{0,8},{4,12},{8,0},{12,4},{16,20},{20,16},{24,28},{28,24},{1,9},{5... | collective-permute-start | bytes 491528 | tf_op jit(solution)/shard_map/ppermute | solution.py:417
  23.9 1.9 %collective-permute-start.4 = (bf16[640,128]{1,0:T(8,128)(2,1)S(1)}, bf16[640,128]{1,0:T(8,128)(2,1)S(1)}, u32[]{:S(2)}, u32[]{:S(2)}) collective-permute-start(bf16[640,128]{1,0:T(8,128)(2,1)S(1)} %select_convert_fusion.own), channel_id=1, source_target_pairs={{0,4},{4,0},{8,12},{12,8},{16,24},{20,28},{24,16},{28,20},{1,5},{5... | collective-permute-start | bytes 491528 | tf_op jit(solution)/shard_map/ppermute | solution.py:417
  25.9 2.4 %collective-permute-start.12 = (bf16[1280,128]{1,0:T(8,128)(2,1)S(1)}, bf16[1280,128]{1,0:T(8,128)(2,1)S(1)}, u32[]{:S(2)}, u32[]{:S(2)}) collective-permute-start(bf16[1280,128]{1,0:T(8,128)(2,1)S(1)} %fusion), channel_id=1, source_target_pairs={{0,4},{4,0},{8,12},{12,8},{16,24},{20,28},{24,16},{28,20},{1,5},{5... | collective-permute-start | bytes 983048 | tf_op jit(solution)/shard_map/ppermute | solution.py:417
  28.3 1.2 %collective-permute-done.5.after.rows_y = bf16[640,128]{1,0:T(8,128)(2,1)S(1)} collective-permute-done((bf16[640,128]{1,0:T(8,128)(2,1)S(1)}, bf16[640,128]{1,0:T(8,128)(2,1)S(1)}, u32[]{:S(2)}, u32[]{:S(2)}) %collective-permute-start.5) | collective-permute-done | bytes 163872 | tf_op jit(solution)/shard_map/ppermute | solution.py:417
  29.5 2.2 %collective-permute-start.6 = (bf16[640,128]{1,0:T(8,128)(2,1)S(1)}, bf16[640,128]{1,0:T(8,128)(2,1)S(1)}, u32[]{:S(2)}, u32[]{:S(2)}) collective-permute-start(bf16[640,128]{1,0:T(8,128)(2,1)S(1)} %collective-permute-done.5.after.rows_y), channel_id=1, source_target_pairs={{0,4},{4,0},{8,12},{12,8},{16,24},{20,28},{24,16},{28,20},{1,5},{5... | collective-permute-start | bytes 491528 | tf_op jit(solution)/shard_map/ppermute | solution.py:417
  31.7 0.8 %shard_map.71.panel_rows = bf16[2560,640]{1,0:T(8,128)(2,1)S(1)} custom-call(s32[3]{0:T(128)S(1)} %copy-done.1, s32[2,12]{1,0:T(2,128)S(1)} %copy-done, bf16[1536,640]{1,0:T(8,128)(2,1)S(1)} %copy-done.3, bf16[640,128]{1,0:T(8,128)(2,1)S(1)} %collective-permute-done.5.after.rows_y), custom_call_target="tpu_custom_call" | custom-call | flops 2000000000 | bytes 6553600 | tf_op jit(solution)/shard_map/pallas_call | solution.py:492
  32.5 0.8 %collective-permute-done.12 = bf16[1280,128]{1,0:T(8,128)(2,1)S(1)} collective-permute-done((bf16[1280,128]{1,0:T(8,128)(2,1)S(1)}, bf16[1280,128]{1,0:T(8,128)(2,1)S(1)}, u32[]{:S(2)}, u32[]{:S(2)}) %collective-permute-start.12) | collective-permute-done | bytes 327712 | tf_op jit(solution)/shard_map/ppermute | solution.py:417
  33.5 0.6 %shard_map.72 = (bf16[640,128]{1,0:T(8,128)(2,1)S(1)}, bf16[320,128]{1,0:T(8,128)(2,1)S(1)}) custom-call(bf16[1280,128]{1,0:T(8,128)(2,1)S(1)} %add_convert_fusion.y, bf16[3840,640]{1,0:T(8,128)(2,1)S(1)} %get-tuple-element.24.d_v), custom_call_target="tpu_custom_call" | custom-call | tf_op jit(solution)/shard_map/pallas_call | solution.py:505
  34.2 1.0 %collective-permute-done.6.rows_d = bf16[640,128]{1,0:T(8,128)(2,1)S(1)} collective-permute-done((bf16[640,128]{1,0:T(8,128)(2,1)S(1)}, bf16[640,128]{1,0:T(8,128)(2,1)S(1)}, u32[]{:S(2)}, u32[]{:S(2)}) %collective-permute-start.6) | collective-permute-done | bytes 163872 | tf_op jit(solution)/shard_map/ppermute | solution.py:417
  35.1 0.4 collective-permute-done.13
  35.6 0.7 %collective-permute-start.14 = (bf16[640,128]{1,0:T(8,128)(2,1)S(1)}, bf16[640,128]{1,0:T(8,128)(2,1)S(1)}, u32[]{:S(2)}, u32[]{:S(2)}) collective-permute-start(bf16[640,128]{1,0:T(8,128)(2,1)S(1)} %pad_maximum_fusion.root_rows), channel_id=1, source_target_pairs={{0,8},{4,12},{8,0},{12,4},{16,20},{20,16},{24,28},{28,24},{1,9},{5... | collective-permute-start | bytes 491528 | tf_op jit(solution)/shard_map/ppermute | solution.py:417
  36.4 2.8 %collective-permute-start.16 = (bf16[320,128]{1,0:T(8,128)(2,1)S(1)}, bf16[320,128]{1,0:T(8,128)(2,1)S(1)}, u32[]{:S(2)}, u32[]{:S(2)}) collective-permute-start(bf16[320,128]{1,0:T(8,128)(2,1)S(1)} %get-tuple-element.44), channel_id=1, source_target_pairs={{0,12},{4,8},{8,4},{12,0},{16,28},{20,24},{24,20},{28,16},{1,13},{... | collective-permute-start | bytes 245768 | tf_op jit(solution)/shard_map/ppermute | solution.py:417
  39.2 1.6 %shard_map.73 = (f32[128,640]{1,0:T(8,128)S(1)}, bf16[960,128]{1,0:T(8,128)(2,1)}) custom-call(bf16[640,128]{1,0:T(8,128)(2,1)S(1)} %select_convert_fusion.own, bf16[640,128]{1,0:T(8,128)(2,1)S(1)} %collective-permute-done.4.rows_x, bf16[640,128]{1,0:T(8,128)(2,1)S(1)} %collective-permute-done.5.after.rows_y, ...), custom_call_target="tpu_custom_call" | custom-call | flops 419430400 | bytes 3276800 | tf_op jit(solution)/shard_map/pallas_call | solution.py:521
  40.8 2.0 %collective-permute-done.14.mine = bf16[640,128]{1,0:T(8,128)(2,1)S(1)} collective-permute-done((bf16[640,128]{1,0:T(8,128)(2,1)S(1)}, bf16[640,128]{1,0:T(8,128)(2,1)S(1)}, u32[]{:S(2)}, u32[]{:S(2)}) %collective-permute-start.14) | collective-permute-done | bytes 163872 | tf_op jit(solution)/shard_map/ppermute | solution.py:417
  42.8 0.5 %collective-permute-start.17 = (bf16[320,128]{1,0:T(8,128)(2,1)S(1)}, bf16[320,128]{1,0:T(8,128)(2,1)S(1)}, u32[]{:S(2)}, u32[]{:S(2)}) collective-permute-start(bf16[320,128]{1,0:T(8,128)(2,1)S(1)} %collective-permute-done.16.mine_far), channel_id=1, source_target_pairs={{0,16},{16,0},{1,17},{17,1},{2,18},{18,2},{3,19},{19,3},{4,20},{20... | collective-permute-start | bytes 245768 | tf_op jit(solution)/shard_map/ppermute | solution.py:409
  43.3 1.0 %collective-permute-done.17.theirs_far = bf16[320,128]{1,0:T(8,128)(2,1)S(1)} collective-permute-done((bf16[320,128]{1,0:T(8,128)(2,1)S(1)}, bf16[320,128]{1,0:T(8,128)(2,1)S(1)}, u32[]{:S(2)}, u32[]{:S(2)}) %collective-permute-start.17) | collective-permute-done | bytes 81952 | tf_op jit(solution)/shard_map/ppermute | solution.py:409
  44.3 1.4 %shard_map.74 = bf16[960,128]{1,0:T(8,128)(2,1)} custom-call(bf16[640,128]{1,0:T(8,128)(2,1)S(1)} %collective-permute-done.14.mine, bf16[640,128]{1,0:T(8,128)(2,1)S(1)} %collective-permute-done.15.theirs, bf16[320,128]{1,0:T(8,128)(2,1)S(1)} %collective-permute-done.16.mine_far, bf16[320,128]{1,0:T(8,128)(2,1)S(1)} %collective-permute-done.17.theirs_far, ...), custom_call_target="tpu_custom_call" | custom-call | flops 209715200 | bytes 1638400 | tf_op jit(solution)/shard_map/pallas_call | solution.py:533
  (29 shorter events, 0.9 us)
Async XLA Ops:
  3.8 7.3 %copy-start.2 = (bf16[1536,640]{1,0:T(8,128)(2,1)}, bf16[1536,640]{1,0:T(8,128)(2,1)S(1)}, u32[]{:S(2)}) copy-start(bf16[1536,640]{1,0:T(8,128)(2,1)S(1)} %get-tuple-element.33.w_v) | copy-start | bytes 5898244
  3.9 1.8 %collective-permute-start = (bf16[1280,128]{1,0:T(8,128)(2,1)S(1)}, bf16[1280,128]{1,0:T(8,128)(2,1)S(1)}, u32[]{:S(2)}, u32[]{:S(2)}) collective-permute-start(bf16[1280,128]{1,0:T(8,128)(2,1)S(1)} %get-tuple-element.26), channel_id=1, source_target_pairs={{0,16},{16,0},{1,17},{17,1},{2,18},{18,2},{3,19},{19,3},{4,20},{20... | collective-permute-start | bytes 983048 | tf_op jit(solution)/shard_map/ppermute | solution.py:409
  5.7 9.0 %collective-permute-start.7 = (bf16[640,128]{1,0:T(8,128)(2,1)S(1)}, bf16[640,128]{1,0:T(8,128)(2,1)S(1)}, u32[]{:S(2)}, u32[]{:S(2)}) collective-permute-start(bf16[640,128]{1,0:T(8,128)(2,1)S(1)} %slice.47.after), channel_id=1, source_target_pairs={{0,4},{4,0},{8,12},{12,8},{16,24},{20,28},{24,16},{28,20},{1,5},{5... | collective-permute-start | bytes 491528 | tf_op jit(solution)/shard_map/ppermute | solution.py:417
  8.7 7.5 %collective-permute-start.8 = (bf16[320,128]{1,0:T(8,128)(2,1)S(1)}, bf16[320,128]{1,0:T(8,128)(2,1)S(1)}, u32[]{:S(2)}, u32[]{:S(2)}) collective-permute-start(bf16[320,128]{1,0:T(8,128)(2,1)S(1)} %slice.49), channel_id=1, source_target_pairs={{0,12},{4,8},{8,4},{12,0},{16,28},{20,24},{24,20},{28,16},{1,13},{... | collective-permute-start | bytes 245768 | tf_op jit(solution)/shard_map/ppermute | solution.py:417
  11.2 8.4 %collective-permute-start.1 = (bf16[640,128]{1,0:T(8,128)(2,1)S(1)}, bf16[640,128]{1,0:T(8,128)(2,1)S(1)}, u32[]{:S(2)}, u32[]{:S(2)}) collective-permute-start(bf16[640,128]{1,0:T(8,128)(2,1)S(1)} %get-tuple-element.28), channel_id=1, source_target_pairs={{0,12},{4,8},{8,4},{12,0},{16,28},{20,24},{24,20},{28,16},{1,13},{... | collective-permute-start | bytes 491528 | tf_op jit(solution)/shard_map/ppermute | solution.py:417
  12.7 8.6 %collective-permute-start.2 = (bf16[640,128]{1,0:T(8,128)(2,1)S(1)}, bf16[640,128]{1,0:T(8,128)(2,1)S(1)}, u32[]{:S(2)}, u32[]{:S(2)}) collective-permute-start(bf16[640,128]{1,0:T(8,128)(2,1)S(1)} %get-tuple-element.29), channel_id=1, source_target_pairs={{0,4},{4,0},{8,12},{12,8},{16,24},{20,28},{24,16},{28,20},{1,5},{5... | collective-permute-start | bytes 491528 | tf_op jit(solution)/shard_map/ppermute | solution.py:417
  12.8 9.4 %collective-permute-start.3 = (bf16[640,128]{1,0:T(8,128)(2,1)S(1)}, bf16[640,128]{1,0:T(8,128)(2,1)S(1)}, u32[]{:S(2)}, u32[]{:S(2)}) collective-permute-start(bf16[640,128]{1,0:T(8,128)(2,1)S(1)} %get-tuple-element.30), channel_id=1, source_target_pairs={{0,8},{4,12},{8,0},{12,4},{16,20},{20,16},{24,28},{28,24},{1,9},{5... | collective-permute-start | bytes 491528 | tf_op jit(solution)/shard_map/ppermute | solution.py:417
  14.8 1.6 %collective-permute-start.10 = (bf16[320,128]{1,0:T(8,128)(2,1)S(1)}, bf16[320,128]{1,0:T(8,128)(2,1)S(1)}, u32[]{:S(2)}, u32[]{:S(2)}) collective-permute-start(bf16[320,128]{1,0:T(8,128)(2,1)S(1)} %slice.42.yours), channel_id=1, source_target_pairs={{0,16},{16,0},{1,17},{17,1},{2,18},{18,2},{3,19},{19,3},{4,20},{20... | collective-permute-start | bytes 245768 | tf_op jit(solution)/shard_map/ppermute | solution.py:409
  16.2 15.5 %copy-start = (s32[2,12]{1,0:T(2,128)S(1)}, s32[2,12]{1,0:T(2,128)}, u32[]{:S(2)}) copy-start(s32[2,12]{1,0:T(2,128)} %pmap.3) | copy-start | bytes 292
  16.2 15.5 %copy-start.1 = (s32[3]{0:T(128)S(1)}, s32[3]{0:T(128)}, u32[]{:S(2)}) copy-start(s32[3]{0:T(128)} %live.3) | copy-start | bytes 40
  16.2 15.5 %copy-start.3 = (bf16[1536,640]{1,0:T(8,128)(2,1)S(1)}, bf16[1536,640]{1,0:T(8,128)(2,1)}, u32[]{:S(2)}) copy-start(bf16[1536,640]{1,0:T(8,128)(2,1)} %copy-done.2) | copy-start | bytes 5898244
  16.2 1.3 %collective-permute-start.9 = (bf16[320,128]{1,0:T(8,128)(2,1)S(1)}, bf16[320,128]{1,0:T(8,128)(2,1)S(1)}, u32[]{:S(2)}, u32[]{:S(2)}) collective-permute-start(bf16[320,128]{1,0:T(8,128)(2,1)S(1)} %fusion.3.mine), channel_id=1, source_target_pairs={{0,16},{16,0},{1,17},{17,1},{2,18},{18,2},{3,19},{19,3},{4,20},{20... | collective-permute-start | bytes 245768 | tf_op jit(solution)/shard_map/ppermute | solution.py:409
  18.2 7.6 %collective-permute-start.11 = (bf16[1280,128]{1,0:T(8,128)(2,1)S(1)}, bf16[1280,128]{1,0:T(8,128)(2,1)S(1)}, u32[]{:S(2)}, u32[]{:S(2)}) collective-permute-start(bf16[1280,128]{1,0:T(8,128)(2,1)S(1)} %shard_map.70), channel_id=1, source_target_pairs={{0,8},{4,12},{8,0},{12,4},{16,20},{20,16},{24,28},{28,24},{1,9},{5... | collective-permute-start | bytes 983048 | tf_op jit(solution)/shard_map/ppermute | solution.py:417
  22.4 7.1 %collective-permute-start.5 = (bf16[640,128]{1,0:T(8,128)(2,1)S(1)}, bf16[640,128]{1,0:T(8,128)(2,1)S(1)}, u32[]{:S(2)}, u32[]{:S(2)}) collective-permute-start(bf16[640,128]{1,0:T(8,128)(2,1)S(1)} %select_convert_fusion.own), channel_id=1, source_target_pairs={{0,8},{4,12},{8,0},{12,4},{16,20},{20,16},{24,28},{28,24},{1,9},{5... | collective-permute-start | bytes 491528 | tf_op jit(solution)/shard_map/ppermute | solution.py:417
  23.9 5.6 %collective-permute-start.4 = (bf16[640,128]{1,0:T(8,128)(2,1)S(1)}, bf16[640,128]{1,0:T(8,128)(2,1)S(1)}, u32[]{:S(2)}, u32[]{:S(2)}) collective-permute-start(bf16[640,128]{1,0:T(8,128)(2,1)S(1)} %select_convert_fusion.own), channel_id=1, source_target_pairs={{0,4},{4,0},{8,12},{12,8},{16,24},{20,28},{24,16},{28,20},{1,5},{5... | collective-permute-start | bytes 491528 | tf_op jit(solution)/shard_map/ppermute | solution.py:417
  25.9 7.5 %collective-permute-start.12 = (bf16[1280,128]{1,0:T(8,128)(2,1)S(1)}, bf16[1280,128]{1,0:T(8,128)(2,1)S(1)}, u32[]{:S(2)}, u32[]{:S(2)}) collective-permute-start(bf16[1280,128]{1,0:T(8,128)(2,1)S(1)} %fusion), channel_id=1, source_target_pairs={{0,4},{4,0},{8,12},{12,8},{16,24},{20,28},{24,16},{28,20},{1,5},{5... | collective-permute-start | bytes 983048 | tf_op jit(solution)/shard_map/ppermute | solution.py:417
  29.5 5.6 %collective-permute-start.6 = (bf16[640,128]{1,0:T(8,128)(2,1)S(1)}, bf16[640,128]{1,0:T(8,128)(2,1)S(1)}, u32[]{:S(2)}, u32[]{:S(2)}) collective-permute-start(bf16[640,128]{1,0:T(8,128)(2,1)S(1)} %collective-permute-done.5.after.rows_y), channel_id=1, source_target_pairs={{0,4},{4,0},{8,12},{12,8},{16,24},{20,28},{24,16},{28,20},{1,5},{5... | collective-permute-start | bytes 491528 | tf_op jit(solution)/shard_map/ppermute | solution.py:417
  34.1 1.5 %collective-permute-start.13 = (bf16[640,128]{1,0:T(8,128)(2,1)S(1)}, bf16[640,128]{1,0:T(8,128)(2,1)S(1)}, u32[]{:S(2)}, u32[]{:S(2)}) collective-permute-start(bf16[640,128]{1,0:T(8,128)(2,1)S(1)} %get-tuple-element.36), channel_id=1, source_target_pairs={{0,16},{16,0},{1,17},{17,1},{2,18},{18,2},{3,19},{19,3},{4,20},{20... | collective-permute-start | bytes 491528 | tf_op jit(solution)/shard_map/ppermute | solution.py:409
  35.6 7.1 %collective-permute-start.14 = (bf16[640,128]{1,0:T(8,128)(2,1)S(1)}, bf16[640,128]{1,0:T(8,128)(2,1)S(1)}, u32[]{:S(2)}, u32[]{:S(2)}) collective-permute-start(bf16[640,128]{1,0:T(8,128)(2,1)S(1)} %pad_maximum_fusion.root_rows), channel_id=1, source_target_pairs={{0,8},{4,12},{8,0},{12,4},{16,20},{20,16},{24,28},{28,24},{1,9},{5... | collective-permute-start | bytes 491528 | tf_op jit(solution)/shard_map/ppermute | solution.py:417
  36.4 6.4 %collective-permute-start.16 = (bf16[320,128]{1,0:T(8,128)(2,1)S(1)}, bf16[320,128]{1,0:T(8,128)(2,1)S(1)}, u32[]{:S(2)}, u32[]{:S(2)}) collective-permute-start(bf16[320,128]{1,0:T(8,128)(2,1)S(1)} %get-tuple-element.44), channel_id=1, source_target_pairs={{0,12},{4,8},{8,4},{12,0},{16,28},{20,24},{24,20},{28,16},{1,13},{... | collective-permute-start | bytes 245768 | tf_op jit(solution)/shard_map/ppermute | solution.py:417
  42.8 1.5 %collective-permute-start.15 = (bf16[640,128]{1,0:T(8,128)(2,1)S(1)}, bf16[640,128]{1,0:T(8,128)(2,1)S(1)}, u32[]{:S(2)}, u32[]{:S(2)}) collective-permute-start(bf16[640,128]{1,0:T(8,128)(2,1)S(1)} %collective-permute-done.14.mine), channel_id=1, source_target_pairs={{0,16},{16,0},{1,17},{17,1},{2,18},{18,2},{3,19},{19,3},{4,20},{20... | collective-permute-start | bytes 491528 | tf_op jit(solution)/shard_map/ppermute | solution.py:409
  42.8 1.5 %collective-permute-start.17 = (bf16[320,128]{1,0:T(8,128)(2,1)S(1)}, bf16[320,128]{1,0:T(8,128)(2,1)S(1)}, u32[]{:S(2)}, u32[]{:S(2)}) collective-permute-start(bf16[320,128]{1,0:T(8,128)(2,1)S(1)} %collective-permute-done.16.mine_far), channel_id=1, source_target_pairs={{0,16},{16,0},{1,17},{17,1},{2,18},{18,2},{3,19},{19,3},{4,20},{20... | collective-permute-start | bytes 245768 | tf_op jit(solution)/shard_map/ppermute | solution.py:409

commit v8 on v7

--- a/solution.py
+++ b/solution.py
@@ -250,14 +250,12 @@
     pmap,
     rhs,
     panel,
-    pivot,
     send,
     keep,
     b_v,
     masked,
     mask,
     w_v,
-    d_v,
     c_v,
     live_s,
     pmap_s,
@@ -275,7 +273,6 @@
     for i in range(parts):
         rows = pl.ds(i * step, step)
         gets.append(pltpu.make_async_copy(panel.at[rows], w_v.at[rows], sems.at[3 + i]))
-    gets.append(pltpu.make_async_copy(pivot, d_v, sems.at[3 + parts]))
     for get in gets:
         get.start()
     c_v[...] = jnp.zeros_like(c_v)
@@ -301,16 +298,25 @@
         out[pl.ds(half, half)] = c_v[rows_at(near + other, half)]
         out[pl.ds(quarter, half)] = c_v[rows_at((row_pos ^ 3) * quarter + mine, half)]
         out[pl.ds(quarter + half, half)] = c_v[rows_at(row_pos * quarter + mine, half)]
-    gets[3 + parts].wait()
-
-
-def leaf_pivot_kernel(sizes, masked, d_v, after, *outs):
-    quarter = sizes
+
+
+def load_kernel(rows, pivot, after, d_v, sem):
+    get = pltpu.make_async_copy(pivot.at[pl.ds(0, rows)], d_v, sem)
+    get.start()
+    get.wait()
+
+
+def leaf_pivot_kernel(sizes, masked, d_v, pivot, after, *outs_and_scratch):
+    quarter, base, rows = sizes
+    *outs, root_d, sem = outs_and_scratch
+    get = pltpu.make_async_copy(pivot.at[pl.ds(base, rows)], root_d, sem)
+    get.start()
     order = row_order(lax.axis_index("row"), lax.axis_index("leaf"))
     right = masked[...]
     for k in (3, 1, 2, 0):
         product = mm(d_v[rows_at(order[k] * quarter, quarter)], right)
         outs[k][...] = product.astype(BF)
+    get.wait()
 
 
 def scatter_kernel(sizes, live, pmap, w_v, after, out, live_s, pmap_s, sems):
@@ -339,20 +345,20 @@
 
 
 def root_pivot_kernel(sizes, mine, yours, other_mine, other_yours, d_v, out, q_v):
-    half, base = sizes
+    half = sizes
     leaf_pos = lax.axis_index("leaf")
     for own, other, at in ((mine, other_yours, leaf_pos), (yours, other_mine, 1 - leaf_pos)):
         value = own[...].astype(F32) + other[...].astype(F32)
         q_v[rows_at(at * half, half)] = (-value).astype(BF)
-    out[...] = mm(d_v[pl.ds(base, 4 * half)], q_v[...]).astype(BF)
+    out[...] = mm(d_v[pl.ds(0, 4 * half)], q_v[...]).astype(BF)
 
 
 def root_transposed_kernel(sizes, y, d_v, out, piece, s_v):
-    half, base = sizes
+    half = sizes
     leaf_pos = lax.axis_index("leaf")
     row_pos = lax.axis_index("row")
     piece[...] = y[rows_at(row_pos * half, half)]
-    s_v[...] = mm(y[...].T, d_v[pl.ds(base, 4 * half)]).T
+    s_v[...] = mm(y[...].T, d_v[pl.ds(0, 4 * half)]).T
     out[pl.ds(0, half)] = s_v[rows_at(leaf_pos * half, half)].astype(BF)
     out[pl.ds(half, half)] = s_v[rows_at((1 - leaf_pos) * half, half)].astype(BF)
 
@@ -431,7 +437,7 @@
     smem = [pltpu.SMEM(live.shape, jnp.int32), pltpu.SMEM(parent_map.shape, jnp.int32)]
 
     parts = 4 if updates % (4 * B) == 0 else 1
-    sent, keep, b_v, masked, mask, w_v, d_v = call(
+    sent, keep, b_v, masked, mask, w_v = call(
         functools.partial(panel_kernel, (quarter, half, parts, updates)),
         (
             kept(4 * half, columns),
@@ -440,31 +446,39 @@
             kept(quarter, columns),
             kept(quarter, columns),
             kept(updates, quarter),
-            kept(front + 4 * half, quarter),
         ),
-        [ANY] * 5,
-        [pltpu.VMEM((front, columns), BF), *smem, pltpu.SemaphoreType.DMA((4 + parts,))],
-        57_100_000,
+        [ANY] * 4,
+        [pltpu.VMEM((front, columns), BF), *smem, pltpu.SemaphoreType.DMA((3 + parts,))],
+        62_100_000,
         2 * updates * quarter * columns,
         2 * updates * quarter,
-    )(live, parent_map, rhs, panel, pivot_inverse)
-    got = leaf_swap(sent)
+    )(live, parent_map, rhs, panel)
+    d_v = call(
+        functools.partial(load_kernel, front),
+        kept(front, quarter),
+        [ANY, ANY],
+        [pltpu.SemaphoreType.DMA],
+        51_000_000,
+        0,
+        2 * front * quarter,
+    )(pivot_inverse, sent)
+    got = after(leaf_swap(sent), d_v)
     update = added(keep, got)
     away_far = update[quarter : quarter + half].astype(BF)
     away_near = update[:quarter].astype(BF)
     from_far = row_swap(away_far, 2)
     from_near = row_swap(away_near, 0)
 
-    pieces = call(
-        functools.partial(leaf_pivot_kernel, quarter),
-        (kept(quarter, columns),) * 4,
-        [VMEM, VMEM, ANY],
-        [],
-        16 * MIB,
+    *pieces, root_d = call(
+        functools.partial(leaf_pivot_kernel, (quarter, front, 4 * half)),
+        (*(kept(quarter, columns),) * 4, kept(4 * half, quarter)),
+        [VMEM, VMEM, ANY, ANY],
+        [pltpu.SemaphoreType.DMA],
+        49_500_000,
         2 * front * quarter * columns,
         2 * front * quarter,
-    )(masked, d_v, away_near)
-    from_near = after(from_near, pieces[0])
+    )(masked, d_v, pivot_inverse, away_near)
+    from_near = after(from_near, (pieces[0],))
     leaf_forward = pieces[0].astype(F32)
     for phase in (2, 0, 1):
         leaf_forward = leaf_forward + row_swap(pieces[1 + phase], phase).astype(F32)
@@ -472,23 +486,6 @@
     rows_y = row_swap(leaf_forward, 1)
     rows_x = row_swap(leaf_forward, 0)
     rows_d = row_swap(rows_y, 0)
-
-    term = update[quarter + half :] + from_far.astype(F32) - b_v[quarter:].astype(F32)
-    from_near = from_near.astype(F32)
-    negated_mine = (from_near[:half] + term).astype(BF)
-    negated_yours = from_near[half:].astype(BF)
-    other_yours = leaf_swap(negated_yours)
-    other_mine = leaf_swap(negated_mine)
-
-    partial = call(
-        functools.partial(root_pivot_kernel, (half, front)),
-        kept(4 * half, columns),
-        [VMEM] * 5,
-        [pltpu.VMEM((quarter, columns), BF)],
-        16 * MIB,
-        0,
-        0,
-    )(negated_mine, negated_yours, other_mine, other_yours, d_v)
     panel_rows = call(
         functools.partial(scatter_kernel, (quarter, updates)),
         kept(front, quarter),
@@ -498,20 +495,39 @@
         2000000000,
         4 * front * quarter,
     )(live, parent_map, w_v, after(rows_y, rows_x))
-    partial = added(partial, row_swap(partial, 1))
-    got = after(row_swap(partial.astype(BF), 0), panel_rows)
-    root_forward = (partial + got.astype(F32)).astype(BF)
+
+    term = update[quarter + half :] + from_far.astype(F32) - b_v[quarter:].astype(F32)
+    from_near = from_near.astype(F32)
+    negated_mine = (from_near[:half] + term).astype(BF)
+    negated_yours = from_near[half:].astype(BF)
+    other_yours = leaf_swap(negated_yours)
+    other_mine = leaf_swap(negated_mine)
+    other_mine = other_mine
+
+    partial = call(
+        functools.partial(root_pivot_kernel, half),
+        kept(4 * half, columns),
+        [VMEM] * 5,
+        [pltpu.VMEM((quarter, columns), BF)],
+        16 * MIB,
+        0,
+        front * quarter,
+    )(negated_mine, negated_yours, other_mine, other_yours, root_d)
+    got = row_swap(partial, 1)
+    partial = added(partial, got)
+    got = row_swap(partial.astype(BF), 0)
+    root_forward = added(partial, after(got, (panel_rows,))).astype(BF)
 
     part, root_piece = call(
-        functools.partial(root_transposed_kernel, (half, front)),
+        functools.partial(root_transposed_kernel, half),
         (kept(quarter, columns), kept(half, columns)),
-        [VMEM, VMEM],
+        [VMEM] * 2,
         [pltpu.VMEM((quarter, columns), F32)],
         16 * MIB,
         0,
-        0,
-    )(root_forward, d_v)
-    got = after(leaf_swap(part), rows_d)
+        front * quarter,
+    )(root_forward, root_d)
+    got = after(leaf_swap(part), (rows_d,))
     root_mine = added(part[:half], got[half:]).astype(BF)
     root_other = added(part[half:], got[:half]).astype(BF)
     root_rows = jnp.concatenate([root_mine, root_other], 0)
@@ -527,7 +543,7 @@
         2 * front * quarter * columns,
         2 * front * quarter,
     )(leaf_forward, rows_x, rows_y, rows_d, d_v, mask, root_rows, panel_rows, root_piece)
-    near = after(near, total)
+    near = after(near, (total, far))
     near_other = leaf_swap(near)
     far_other = leaf_swap(far)
     backward = call(

time: 45.9 us -> 46 us (level)
  starting transfers between devices: 21 us -> 17.2 us
  Pallas kernels: 9.31 us -> 11.8 us
  waiting for transfers between devices: 14 us -> 15.4 us
    ppermute x12, starting transfers between devices: 19.8 us -> 15.5 us  [row_swap(): return lax.ppermute(value, ('leaf', 'row'), route)]
    ppermute x12, waiting for transfers between devices: 10 us -> 13 us  [row_swap(): return lax.ppermute(value, ('leaf', 'row'), route)]
    pallas_call x3 -> x4, Pallas kernels: 2.24 us -> 5.2 us  [the longest x1 2.03 us: two_levels(): call(functools.partial(leaf_pivot_kernel, (quarter, front, 4 * half)), (*...]
    ppermute x6, waiting for transfers between devices: 3.94 us -> 2.36 us  [leaf_swap(): return lax.ppermute(value, 'leaf', [(0, 1), (1, 0)])]
    pallas_call x1, Pallas kernels: 3.21 us -> 2.71 us  [two_levels(): call(functools.partial(panel_kernel, (quarter, half, parts, updates)), (k...]
    ppermute x6, starting transfers between devices: 1.24 us -> 1.72 us  [leaf_swap(): return lax.ppermute(value, 'leaf', [(0, 1), (1, 0)])]
  transfers between devices with their start and end apart: 18 -> 18, of which waited for: 12 -> 13; matrix products, arithmetic and copies ran while one was open for 1% -> 1% of each run, Pallas kernels for 10% -> 17%
where the time goes in v8:
time: 46 us; the launch traced here: 45.7 us
  starting transfers between devices  17.2 us (37%)
  waiting for transfers between devices  15.4 us (33%)
  Pallas kernels  11.8 us (26%)
  between operations  0.78 us (2%)
  other arithmetic  0.54 us (1%)
    ppermute x12, starting transfers between devices, row_swap(): return lax.ppermute(value, ('leaf', 'row'), route)  15.5 us
    ppermute x12, waiting for transfers between devices, row_swap(): return lax.ppermute(value, ('leaf', 'row'), route)  13 us
    pallas_call x1, Pallas kernels, two_levels(): call(functools.partial(panel_kernel, (quarter, half, parts, updates)), (k...  2.71 us
    ppermute x6, waiting for transfers between devices, leaf_swap(): return lax.ppermute(value, 'leaf', [(0, 1), (1, 0)])  2.36 us
    pallas_call x1, Pallas kernels, two_levels(): call(functools.partial(leaf_pivot_kernel, (quarter, front, 4 * half)), (*...  2.03 us
    pallas_call x1, Pallas kernels, two_levels(): call(functools.partial(load_kernel, front), kept(front, quarter), [ANY, A...  1.93 us
    ppermute x6, starting transfers between devices, leaf_swap(): return lax.ppermute(value, 'leaf', [(0, 1), (1, 0)])  1.72 us
    pallas_call x1, Pallas kernels, two_levels(): call(functools.partial(leaf_transposed_kernel, (quarter, half)), (kept(co...  1.61 us
  transfers between devices with their start and end apart: 18, of which 13 were waited for; matrix products, arithmetic and copies ran while one was open for 1% of the time, Pallas kernels for 17%

profile of v8, /device:TPU:0, one launch (start us, length us, event | category | flops | bytes accessed | tf_op | source)
XLA Modules:
  0.0 45.7 jit_solution(14030953588726999658)
XLA Ops:
  0.6 2.7 %shard_map.68 = (bf16[1280,128]{1,0:T(8,128)(2,1)S(1)}, bf16[1280,128]{1,0:T(8,128)(2,1)S(1)}, bf16[960,128]{1,0:T(8,128)(2,1)S(1)}, bf16[640,128]{1,0:T(8,128)(...) custom-call(s32[3]{0:T(128)} %live.3, s32[2,12]{1,0:T(2,128)} %pmap.3, bf16[960,128]{1,0:T(8,128)(2,1)} %rhs.1, ...), custom_call_target="tpu_custom_call" | custom-call | flops 251658240 | bytes 1966080 | tf_op jit(solution)/shard_map/pallas_call | solution.py:440
  3.3 0.5 %collective-permute-start = (bf16[1280,128]{1,0:T(8,128)(2,1)S(1)}, bf16[1280,128]{1,0:T(8,128)(2,1)S(1)}, u32[]{:S(2)}, u32[]{:S(2)}) collective-permute-start(bf16[1280,128]{1,0:T(8,128)(2,1)S(1)} %get-tuple-element.25.after), channel_id=1, source_target_pairs={{0,16},{16,0},{1,17},{17,1},{2,18},{18,2},{3,19},{19,3},{4,20},{20... | collective-permute-start | bytes 983048 | tf_op jit(solution)/shard_map/ppermute | solution.py:415
  3.9 1.9 %shard_map.69.d_v = bf16[2560,640]{1,0:T(8,128)(2,1)S(1)} custom-call(bf16[3840,640]{1,0:T(8,128)(2,1)} %pivot.3, bf16[1280,128]{1,0:T(8,128)(2,1)S(1)} %get-tuple-element.25.after), custom_call_target="tpu_custom_call" | custom-call | bytes 3276800 | tf_op jit(solution)/shard_map/pallas_call | solution.py:456
  5.9 2.6 %collective-permute-start.7 = (bf16[640,128]{1,0:T(8,128)(2,1)S(1)}, bf16[640,128]{1,0:T(8,128)(2,1)S(1)}, u32[]{:S(2)}, u32[]{:S(2)}) collective-permute-start(bf16[640,128]{1,0:T(8,128)(2,1)S(1)} %slice.47.after), channel_id=1, source_target_pairs={{0,4},{4,0},{8,12},{12,8},{16,24},{20,28},{24,16},{28,20},{1,5},{5... | collective-permute-start | bytes 491528 | tf_op jit(solution)/shard_map/ppermute | solution.py:423
  8.5 1.5 %collective-permute-start.8 = (bf16[320,128]{1,0:T(8,128)(2,1)S(1)}, bf16[320,128]{1,0:T(8,128)(2,1)S(1)}, u32[]{:S(2)}, u32[]{:S(2)}) collective-permute-start(bf16[320,128]{1,0:T(8,128)(2,1)S(1)} %slice.49), channel_id=1, source_target_pairs={{0,12},{4,8},{8,4},{12,0},{16,28},{20,24},{24,20},{28,16},{1,13},{... | collective-permute-start | bytes 245768 | tf_op jit(solution)/shard_map/ppermute | solution.py:423
  10.0 2.0 %shard_map.70 = (bf16[640,128]{1,0:T(8,128)(2,1)S(1)}, bf16[640,128]{1,0:T(8,128)(2,1)S(1)}, bf16[640,128]{1,0:T(8,128)(2,1)S(1)}, bf16[640,128]{1,0:T(8,128)(2,1)S(1)}, bf16[1280,640]{1,0:T(8,128)(2,1)S(1)}) custom-call(bf16[640,128]{1,0:T(8,128)(2,1)S(1)} %get-tuple-element.24.masked, bf16[2560,640]{1,0:T(8,128)(2,1)S(1)} %shard_map.69.d_v, ...), custom_call_target="tpu_custom_call" | custom-call | flops 419430400 | bytes 3276800 | tf_op jit(solution)/shard_map/pallas_call | solution.py:472
  12.1 1.5 %collective-permute-start.1 = (bf16[640,128]{1,0:T(8,128)(2,1)S(1)}, bf16[640,128]{1,0:T(8,128)(2,1)S(1)}, u32[]{:S(2)}, u32[]{:S(2)}) collective-permute-start(bf16[640,128]{1,0:T(8,128)(2,1)S(1)} %get-tuple-element.29), channel_id=1, source_target_pairs={{0,12},{4,8},{8,4},{12,0},{16,28},{20,24},{24,20},{28,16},{1,13},{... | collective-permute-start | bytes 491528 | tf_op jit(solution)/shard_map/ppermute | solution.py:423
  13.7 1.9 %collective-permute-start.3 = (bf16[640,128]{1,0:T(8,128)(2,1)S(1)}, bf16[640,128]{1,0:T(8,128)(2,1)S(1)}, u32[]{:S(2)}, u32[]{:S(2)}) collective-permute-start(bf16[640,128]{1,0:T(8,128)(2,1)S(1)} %get-tuple-element.31), channel_id=1, source_target_pairs={{0,8},{4,12},{8,0},{12,4},{16,20},{20,16},{24,28},{28,24},{1,9},{5... | collective-permute-start | bytes 491528 | tf_op jit(solution)/shard_map/ppermute | solution.py:423
  15.8 0.6 %collective-permute-start.9 = (bf16[320,128]{1,0:T(8,128)(2,1)S(1)}, bf16[320,128]{1,0:T(8,128)(2,1)S(1)}, u32[]{:S(2)}, u32[]{:S(2)}) collective-permute-start(bf16[320,128]{1,0:T(8,128)(2,1)S(1)} %fusion.3.mine), channel_id=1, source_target_pairs={{0,16},{16,0},{1,17},{17,1},{2,18},{18,2},{3,19},{19,3},{4,20},{20... | collective-permute-start | bytes 245768 | tf_op jit(solution)/shard_map/ppermute | solution.py:415
  16.3 0.6 %collective-permute-done.10.other_yours = bf16[320,128]{1,0:T(8,128)(2,1)S(1)} collective-permute-done((bf16[320,128]{1,0:T(8,128)(2,1)S(1)}, bf16[320,128]{1,0:T(8,128)(2,1)S(1)}, u32[]{:S(2)}, u32[]{:S(2)}) %collective-permute-start.10) | collective-permute-done | bytes 81952 | tf_op jit(solution)/shard_map/ppermute | solution.py:415
  17.2 0.6 %shard_map.71 = bf16[1280,128]{1,0:T(8,128)(2,1)S(1)} custom-call(bf16[320,128]{1,0:T(8,128)(2,1)S(1)} %fusion.3.mine, bf16[320,128]{1,0:T(8,128)(2,1)S(1)} %slice.42.yours, bf16[320,128]{1,0:T(8,128)(2,1)S(1)} %collective-permute-done.9.other_mine, bf16[320,128]{1,0:T(8,128)(2,1)S(1)} %collective-permute-done.10.other_yours, ...), custom_call_target="tpu_custom_call" | custom-call | bytes 1638400 | tf_op jit(solution)/shard_map/pallas_call | solution.py:507
  17.9 0.5 %collective-permute-start.11 = (bf16[1280,128]{1,0:T(8,128)(2,1)S(1)}, bf16[1280,128]{1,0:T(8,128)(2,1)S(1)}, u32[]{:S(2)}, u32[]{:S(2)}) collective-permute-start(bf16[1280,128]{1,0:T(8,128)(2,1)S(1)} %shard_map.71), channel_id=1, source_target_pairs={{0,8},{4,12},{8,0},{12,4},{16,20},{20,16},{24,28},{28,24},{1,9},{5... | collective-permute-start | bytes 983048 | tf_op jit(solution)/shard_map/ppermute | solution.py:423
  18.4 1.8 %collective-permute-done.1 = bf16[640,128]{1,0:T(8,128)(2,1)S(1)} collective-permute-done((bf16[640,128]{1,0:T(8,128)(2,1)S(1)}, bf16[640,128]{1,0:T(8,128)(2,1)S(1)}, u32[]{:S(2)}, u32[]{:S(2)}) %collective-permute-start.1) | collective-permute-done | bytes 163872 | tf_op jit(solution)/shard_map/ppermute | solution.py:423
  20.1 1.8 %collective-permute-done.2 = bf16[640,128]{1,0:T(8,128)(2,1)S(1)} collective-permute-done((bf16[640,128]{1,0:T(8,128)(2,1)S(1)}, bf16[640,128]{1,0:T(8,128)(2,1)S(1)}, u32[]{:S(2)}, u32[]{:S(2)}) %collective-permute-start.2) | collective-permute-done | bytes 163872 | tf_op jit(solution)/shard_map/ppermute | solution.py:423
  21.9 0.6 %collective-permute-done.3 = bf16[640,128]{1,0:T(8,128)(2,1)S(1)} collective-permute-done((bf16[640,128]{1,0:T(8,128)(2,1)S(1)}, bf16[640,128]{1,0:T(8,128)(2,1)S(1)}, u32[]{:S(2)}, u32[]{:S(2)}) %collective-permute-start.3) | collective-permute-done | bytes 163872 | tf_op jit(solution)/shard_map/ppermute | solution.py:423
  22.7 1.7 %collective-permute-start.5 = (bf16[640,128]{1,0:T(8,128)(2,1)S(1)}, bf16[640,128]{1,0:T(8,128)(2,1)S(1)}, u32[]{:S(2)}, u32[]{:S(2)}) collective-permute-start(bf16[640,128]{1,0:T(8,128)(2,1)S(1)} %select_convert_fusion.own), channel_id=1, source_target_pairs={{0,8},{4,12},{8,0},{12,4},{16,20},{20,16},{24,28},{28,24},{1,9},{5... | collective-permute-start | bytes 491528 | tf_op jit(solution)/shard_map/ppermute | solution.py:423
  24.4 1.0 %collective-permute-start.4 = (bf16[640,128]{1,0:T(8,128)(2,1)S(1)}, bf16[640,128]{1,0:T(8,128)(2,1)S(1)}, u32[]{:S(2)}, u32[]{:S(2)}) collective-permute-start(bf16[640,128]{1,0:T(8,128)(2,1)S(1)} %select_convert_fusion.own), channel_id=1, source_target_pairs={{0,4},{4,0},{8,12},{12,8},{16,24},{20,28},{24,16},{28,20},{1,5},{5... | collective-permute-start | bytes 491528 | tf_op jit(solution)/shard_map/ppermute | solution.py:423
  25.4 0.7 %collective-permute-done.11 = bf16[1280,128]{1,0:T(8,128)(2,1)S(1)} collective-permute-done((bf16[1280,128]{1,0:T(8,128)(2,1)S(1)}, bf16[1280,128]{1,0:T(8,128)(2,1)S(1)}, u32[]{:S(2)}, u32[]{:S(2)}) %collective-permute-start.11) | collective-permute-done | bytes 327712 | tf_op jit(solution)/shard_map/ppermute | solution.py:423
  26.3 0.9 %collective-permute-start.12 = (bf16[1280,128]{1,0:T(8,128)(2,1)S(1)}, bf16[1280,128]{1,0:T(8,128)(2,1)S(1)}, u32[]{:S(2)}, u32[]{:S(2)}) collective-permute-start(bf16[1280,128]{1,0:T(8,128)(2,1)S(1)} %fusion), channel_id=1, source_target_pairs={{0,4},{4,0},{8,12},{12,8},{16,24},{20,28},{24,16},{28,20},{1,5},{5... | collective-permute-start | bytes 983048 | tf_op jit(solution)/shard_map/ppermute | solution.py:423
  27.2 2.6 %collective-permute-done.5.after.rows_y = bf16[640,128]{1,0:T(8,128)(2,1)S(1)} collective-permute-done((bf16[640,128]{1,0:T(8,128)(2,1)S(1)}, bf16[640,128]{1,0:T(8,128)(2,1)S(1)}, u32[]{:S(2)}, u32[]{:S(2)}) %collective-permute-start.5) | collective-permute-done | bytes 163872 | tf_op jit(solution)/shard_map/ppermute | solution.py:423
  29.8 1.3 %collective-permute-start.6 = (bf16[640,128]{1,0:T(8,128)(2,1)S(1)}, bf16[640,128]{1,0:T(8,128)(2,1)S(1)}, u32[]{:S(2)}, u32[]{:S(2)}) collective-permute-start(bf16[640,128]{1,0:T(8,128)(2,1)S(1)} %collective-permute-done.5.after.rows_y), channel_id=1, source_target_pairs={{0,4},{4,0},{8,12},{12,8},{16,24},{20,28},{24,16},{28,20},{1,5},{5... | collective-permute-start | bytes 491528 | tf_op jit(solution)/shard_map/ppermute | solution.py:423
  31.1 0.8 %shard_map.72.panel_rows = bf16[2560,640]{1,0:T(8,128)(2,1)S(1)} custom-call(s32[3]{0:T(128)S(1)} %copy-done.1, s32[2,12]{1,0:T(2,128)S(1)} %copy-done, bf16[1536,640]{1,0:T(8,128)(2,1)S(1)} %get-tuple-element.35.w_v, bf16[640,128]{1,0:T(8,128)(2,1)S(1)} %collective-permute-done.5.after.rows_y), custom_call_target="tpu_custom_call" | custom-call | flops 2000000000 | bytes 6553600 | tf_op jit(solution)/shard_map/pallas_call | solution.py:489
  32.0 1.5 %collective-permute-done.12 = bf16[1280,128]{1,0:T(8,128)(2,1)S(1)} collective-permute-done((bf16[1280,128]{1,0:T(8,128)(2,1)S(1)}, bf16[1280,128]{1,0:T(8,128)(2,1)S(1)}, u32[]{:S(2)}, u32[]{:S(2)}) %collective-permute-start.12) | collective-permute-done | bytes 327712 | tf_op jit(solution)/shard_map/ppermute | solution.py:423
  33.5 0.6 %shard_map.73 = (bf16[640,128]{1,0:T(8,128)(2,1)S(1)}, bf16[320,128]{1,0:T(8,128)(2,1)S(1)}) custom-call(bf16[1280,128]{1,0:T(8,128)(2,1)S(1)} %add_convert_fusion.y, bf16[1280,640]{1,0:T(8,128)(2,1)S(1)} %get-tuple-element.34.d_v), custom_call_target="tpu_custom_call" | custom-call | bytes 1638400 | tf_op jit(solution)/shard_map/pallas_call | solution.py:521
  34.2 0.9 %collective-permute-done.6.rows_d = bf16[640,128]{1,0:T(8,128)(2,1)S(1)} collective-permute-done((bf16[640,128]{1,0:T(8,128)(2,1)S(1)}, bf16[640,128]{1,0:T(8,128)(2,1)S(1)}, u32[]{:S(2)}, u32[]{:S(2)}) %collective-permute-start.6) | collective-permute-done | bytes 163872 | tf_op jit(solution)/shard_map/ppermute | solution.py:423
  35.7 1.0 %collective-permute-start.14 = (bf16[640,128]{1,0:T(8,128)(2,1)S(1)}, bf16[640,128]{1,0:T(8,128)(2,1)S(1)}, u32[]{:S(2)}, u32[]{:S(2)}) collective-permute-start(bf16[640,128]{1,0:T(8,128)(2,1)S(1)} %pad_maximum_fusion.root_rows), channel_id=1, source_target_pairs={{0,8},{4,12},{8,0},{12,4},{16,20},{20,16},{24,28},{28,24},{1,9},{5... | collective-permute-start | bytes 491528 | tf_op jit(solution)/shard_map/ppermute | solution.py:423
  36.7 1.4 %collective-permute-start.15 = (bf16[320,128]{1,0:T(8,128)(2,1)S(1)}, bf16[320,128]{1,0:T(8,128)(2,1)S(1)}, u32[]{:S(2)}, u32[]{:S(2)}) collective-permute-start(bf16[320,128]{1,0:T(8,128)(2,1)S(1)} %get-tuple-element.46), channel_id=1, source_target_pairs={{0,12},{4,8},{8,4},{12,0},{16,28},{20,24},{24,20},{28,16},{1,13},{... | collective-permute-start | bytes 245768 | tf_op jit(solution)/shard_map/ppermute | solution.py:423
  38.1 1.6 %shard_map.74 = (f32[128,640]{1,0:T(8,128)S(1)}, bf16[960,128]{1,0:T(8,128)(2,1)}) custom-call(bf16[640,128]{1,0:T(8,128)(2,1)S(1)} %select_convert_fusion.own, bf16[640,128]{1,0:T(8,128)(2,1)S(1)} %collective-permute-done.4.rows_x, bf16[640,128]{1,0:T(8,128)(2,1)S(1)} %collective-permute-done.5.after.rows_y, ...), custom_call_target="tpu_custom_call" | custom-call | flops 419430400 | bytes 3276800 | tf_op jit(solution)/shard_map/pallas_call | solution.py:537
  39.7 2.7 %collective-permute-done.15.mine_far = bf16[320,128]{1,0:T(8,128)(2,1)S(1)} collective-permute-done((bf16[320,128]{1,0:T(8,128)(2,1)S(1)}, bf16[320,128]{1,0:T(8,128)(2,1)S(1)}, u32[]{:S(2)}, u32[]{:S(2)}) %collective-permute-start.15) | collective-permute-done | bytes 81952 | tf_op jit(solution)/shard_map/ppermute | solution.py:423
  42.8 0.5 %collective-permute-start.17 = (bf16[320,128]{1,0:T(8,128)(2,1)S(1)}, bf16[320,128]{1,0:T(8,128)(2,1)S(1)}, u32[]{:S(2)}, u32[]{:S(2)}) collective-permute-start(bf16[320,128]{1,0:T(8,128)(2,1)S(1)} %collective-permute-done.15.mine_far), channel_id=1, source_target_pairs={{0,16},{16,0},{1,17},{17,1},{2,18},{18,2},{3,19},{19,3},{4,20},{20... | collective-permute-start | bytes 245768 | tf_op jit(solution)/shard_map/ppermute | solution.py:415
  43.3 1.0 %collective-permute-done.17.theirs_far = bf16[320,128]{1,0:T(8,128)(2,1)S(1)} collective-permute-done((bf16[320,128]{1,0:T(8,128)(2,1)S(1)}, bf16[320,128]{1,0:T(8,128)(2,1)S(1)}, u32[]{:S(2)}, u32[]{:S(2)}) %collective-permute-start.17) | collective-permute-done | bytes 81952 | tf_op jit(solution)/shard_map/ppermute | solution.py:415
  44.3 1.4 %shard_map.75 = bf16[960,128]{1,0:T(8,128)(2,1)} custom-call(bf16[640,128]{1,0:T(8,128)(2,1)S(1)} %collective-permute-done.14.mine, bf16[640,128]{1,0:T(8,128)(2,1)S(1)} %collective-permute-done.16.theirs, bf16[320,128]{1,0:T(8,128)(2,1)S(1)} %collective-permute-done.15.mine_far, bf16[320,128]{1,0:T(8,128)(2,1)S(1)} %collective-permute-done.17.theirs_far, ...), custom_call_target="tpu_custom_call" | custom-call | flops 209715200 | bytes 1638400 | tf_op jit(solution)/shard_map/pallas_call | solution.py:549
  (26 shorter events, 2.0 us)
Async XLA Ops:
  3.3 2.5 %collective-permute-start = (bf16[1280,128]{1,0:T(8,128)(2,1)S(1)}, bf16[1280,128]{1,0:T(8,128)(2,1)S(1)}, u32[]{:S(2)}, u32[]{:S(2)}) collective-permute-start(bf16[1280,128]{1,0:T(8,128)(2,1)S(1)} %get-tuple-element.25.after), channel_id=1, source_target_pairs={{0,16},{16,0},{1,17},{17,1},{2,18},{18,2},{3,19},{19,3},{4,20},{20... | collective-permute-start | bytes 983048 | tf_op jit(solution)/shard_map/ppermute | solution.py:415
  5.9 9.7 %collective-permute-start.7 = (bf16[640,128]{1,0:T(8,128)(2,1)S(1)}, bf16[640,128]{1,0:T(8,128)(2,1)S(1)}, u32[]{:S(2)}, u32[]{:S(2)}) collective-permute-start(bf16[640,128]{1,0:T(8,128)(2,1)S(1)} %slice.47.after), channel_id=1, source_target_pairs={{0,4},{4,0},{8,12},{12,8},{16,24},{20,28},{24,16},{28,20},{1,5},{5... | collective-permute-start | bytes 491528 | tf_op jit(solution)/shard_map/ppermute | solution.py:423
  8.5 7.2 %collective-permute-start.8 = (bf16[320,128]{1,0:T(8,128)(2,1)S(1)}, bf16[320,128]{1,0:T(8,128)(2,1)S(1)}, u32[]{:S(2)}, u32[]{:S(2)}) collective-permute-start(bf16[320,128]{1,0:T(8,128)(2,1)S(1)} %slice.49), channel_id=1, source_target_pairs={{0,12},{4,8},{8,4},{12,0},{16,28},{20,24},{24,20},{28,16},{1,13},{... | collective-permute-start | bytes 245768 | tf_op jit(solution)/shard_map/ppermute | solution.py:423
  12.0 19.1 %copy-start = (s32[2,12]{1,0:T(2,128)S(1)}, s32[2,12]{1,0:T(2,128)}, u32[]{:S(2)}) copy-start(s32[2,12]{1,0:T(2,128)} %pmap.3) | copy-start | bytes 292
  12.1 19.1 %copy-start.1 = (s32[3]{0:T(128)S(1)}, s32[3]{0:T(128)}, u32[]{:S(2)}) copy-start(s32[3]{0:T(128)} %live.3) | copy-start | bytes 40
  12.1 8.1 %collective-permute-start.1 = (bf16[640,128]{1,0:T(8,128)(2,1)S(1)}, bf16[640,128]{1,0:T(8,128)(2,1)S(1)}, u32[]{:S(2)}, u32[]{:S(2)}) collective-permute-start(bf16[640,128]{1,0:T(8,128)(2,1)S(1)} %get-tuple-element.29), channel_id=1, source_target_pairs={{0,12},{4,8},{8,4},{12,0},{16,28},{20,24},{24,20},{28,16},{1,13},{... | collective-permute-start | bytes 491528 | tf_op jit(solution)/shard_map/ppermute | solution.py:423
  13.6 8.4 %collective-permute-start.2 = (bf16[640,128]{1,0:T(8,128)(2,1)S(1)}, bf16[640,128]{1,0:T(8,128)(2,1)S(1)}, u32[]{:S(2)}, u32[]{:S(2)}) collective-permute-start(bf16[640,128]{1,0:T(8,128)(2,1)S(1)} %get-tuple-element.30), channel_id=1, source_target_pairs={{0,4},{4,0},{8,12},{12,8},{16,24},{20,28},{24,16},{28,20},{1,5},{5... | collective-permute-start | bytes 491528 | tf_op jit(solution)/shard_map/ppermute | solution.py:423
  13.7 8.8 %collective-permute-start.3 = (bf16[640,128]{1,0:T(8,128)(2,1)S(1)}, bf16[640,128]{1,0:T(8,128)(2,1)S(1)}, u32[]{:S(2)}, u32[]{:S(2)}) collective-permute-start(bf16[640,128]{1,0:T(8,128)(2,1)S(1)} %get-tuple-element.31), channel_id=1, source_target_pairs={{0,8},{4,12},{8,0},{12,4},{16,20},{20,16},{24,28},{28,24},{1,9},{5... | collective-permute-start | bytes 491528 | tf_op jit(solution)/shard_map/ppermute | solution.py:423
  15.6 1.3 %collective-permute-start.10 = (bf16[320,128]{1,0:T(8,128)(2,1)S(1)}, bf16[320,128]{1,0:T(8,128)(2,1)S(1)}, u32[]{:S(2)}, u32[]{:S(2)}) collective-permute-start(bf16[320,128]{1,0:T(8,128)(2,1)S(1)} %slice.42.yours), channel_id=1, source_target_pairs={{0,16},{16,0},{1,17},{17,1},{2,18},{18,2},{3,19},{19,3},{4,20},{20... | collective-permute-start | bytes 245768 | tf_op jit(solution)/shard_map/ppermute | solution.py:415
  15.8 1.5 %collective-permute-start.9 = (bf16[320,128]{1,0:T(8,128)(2,1)S(1)}, bf16[320,128]{1,0:T(8,128)(2,1)S(1)}, u32[]{:S(2)}, u32[]{:S(2)}) collective-permute-start(bf16[320,128]{1,0:T(8,128)(2,1)S(1)} %fusion.3.mine), channel_id=1, source_target_pairs={{0,16},{16,0},{1,17},{17,1},{2,18},{18,2},{3,19},{19,3},{4,20},{20... | collective-permute-start | bytes 245768 | tf_op jit(solution)/shard_map/ppermute | solution.py:415
  17.9 8.3 %collective-permute-start.11 = (bf16[1280,128]{1,0:T(8,128)(2,1)S(1)}, bf16[1280,128]{1,0:T(8,128)(2,1)S(1)}, u32[]{:S(2)}, u32[]{:S(2)}) collective-permute-start(bf16[1280,128]{1,0:T(8,128)(2,1)S(1)} %shard_map.71), channel_id=1, source_target_pairs={{0,8},{4,12},{8,0},{12,4},{16,20},{20,16},{24,28},{28,24},{1,9},{5... | collective-permute-start | bytes 983048 | tf_op jit(solution)/shard_map/ppermute | solution.py:423
  22.7 7.1 %collective-permute-start.5 = (bf16[640,128]{1,0:T(8,128)(2,1)S(1)}, bf16[640,128]{1,0:T(8,128)(2,1)S(1)}, u32[]{:S(2)}, u32[]{:S(2)}) collective-permute-start(bf16[640,128]{1,0:T(8,128)(2,1)S(1)} %select_convert_fusion.own), channel_id=1, source_target_pairs={{0,8},{4,12},{8,0},{12,4},{16,20},{20,16},{24,28},{28,24},{1,9},{5... | collective-permute-start | bytes 491528 | tf_op jit(solution)/shard_map/ppermute | solution.py:423
  24.4 5.4 %collective-permute-start.4 = (bf16[640,128]{1,0:T(8,128)(2,1)S(1)}, bf16[640,128]{1,0:T(8,128)(2,1)S(1)}, u32[]{:S(2)}, u32[]{:S(2)}) collective-permute-start(bf16[640,128]{1,0:T(8,128)(2,1)S(1)} %select_convert_fusion.own), channel_id=1, source_target_pairs={{0,4},{4,0},{8,12},{12,8},{16,24},{20,28},{24,16},{28,20},{1,5},{5... | collective-permute-start | bytes 491528 | tf_op jit(solution)/shard_map/ppermute | solution.py:423
  26.3 7.1 %collective-permute-start.12 = (bf16[1280,128]{1,0:T(8,128)(2,1)S(1)}, bf16[1280,128]{1,0:T(8,128)(2,1)S(1)}, u32[]{:S(2)}, u32[]{:S(2)}) collective-permute-start(bf16[1280,128]{1,0:T(8,128)(2,1)S(1)} %fusion), channel_id=1, source_target_pairs={{0,4},{4,0},{8,12},{12,8},{16,24},{20,28},{24,16},{28,20},{1,5},{5... | collective-permute-start | bytes 983048 | tf_op jit(solution)/shard_map/ppermute | solution.py:423
  29.8 5.4 %collective-permute-start.6 = (bf16[640,128]{1,0:T(8,128)(2,1)S(1)}, bf16[640,128]{1,0:T(8,128)(2,1)S(1)}, u32[]{:S(2)}, u32[]{:S(2)}) collective-permute-start(bf16[640,128]{1,0:T(8,128)(2,1)S(1)} %collective-permute-done.5.after.rows_y), channel_id=1, source_target_pairs={{0,4},{4,0},{8,12},{12,8},{16,24},{20,28},{24,16},{28,20},{1,5},{5... | collective-permute-start | bytes 491528 | tf_op jit(solution)/shard_map/ppermute | solution.py:423
  34.1 1.5 %collective-permute-start.13 = (bf16[640,128]{1,0:T(8,128)(2,1)S(1)}, bf16[640,128]{1,0:T(8,128)(2,1)S(1)}, u32[]{:S(2)}, u32[]{:S(2)}) collective-permute-start(bf16[640,128]{1,0:T(8,128)(2,1)S(1)} %get-tuple-element.38), channel_id=1, source_target_pairs={{0,16},{16,0},{1,17},{17,1},{2,18},{18,2},{3,19},{19,3},{4,20},{20... | collective-permute-start | bytes 491528 | tf_op jit(solution)/shard_map/ppermute | solution.py:415
  35.7 7.1 %collective-permute-start.14 = (bf16[640,128]{1,0:T(8,128)(2,1)S(1)}, bf16[640,128]{1,0:T(8,128)(2,1)S(1)}, u32[]{:S(2)}, u32[]{:S(2)}) collective-permute-start(bf16[640,128]{1,0:T(8,128)(2,1)S(1)} %pad_maximum_fusion.root_rows), channel_id=1, source_target_pairs={{0,8},{4,12},{8,0},{12,4},{16,20},{20,16},{24,28},{28,24},{1,9},{5... | collective-permute-start | bytes 491528 | tf_op jit(solution)/shard_map/ppermute | solution.py:423
  36.7 5.7 %collective-permute-start.15 = (bf16[320,128]{1,0:T(8,128)(2,1)S(1)}, bf16[320,128]{1,0:T(8,128)(2,1)S(1)}, u32[]{:S(2)}, u32[]{:S(2)}) collective-permute-start(bf16[320,128]{1,0:T(8,128)(2,1)S(1)} %get-tuple-element.46), channel_id=1, source_target_pairs={{0,12},{4,8},{8,4},{12,0},{16,28},{20,24},{24,20},{28,16},{1,13},{... | collective-permute-start | bytes 245768 | tf_op jit(solution)/shard_map/ppermute | solution.py:423
  42.8 1.5 %collective-permute-start.16 = (bf16[640,128]{1,0:T(8,128)(2,1)S(1)}, bf16[640,128]{1,0:T(8,128)(2,1)S(1)}, u32[]{:S(2)}, u32[]{:S(2)}) collective-permute-start(bf16[640,128]{1,0:T(8,128)(2,1)S(1)} %collective-permute-done.14.mine), channel_id=1, source_target_pairs={{0,16},{16,0},{1,17},{17,1},{2,18},{18,2},{3,19},{19,3},{4,20},{20... | collective-permute-start | bytes 491528 | tf_op jit(solution)/shard_map/ppermute | solution.py:415
  42.8 1.5 %collective-permute-start.17 = (bf16[320,128]{1,0:T(8,128)(2,1)S(1)}, bf16[320,128]{1,0:T(8,128)(2,1)S(1)}, u32[]{:S(2)}, u32[]{:S(2)}) collective-permute-start(bf16[320,128]{1,0:T(8,128)(2,1)S(1)} %collective-permute-done.15.mine_far), channel_id=1, source_target_pairs={{0,16},{16,0},{1,17},{17,1},{2,18},{18,2},{3,19},{19,3},{4,20},{20... | collective-permute-start | bytes 245768 | tf_op jit(solution)/shard_map/ppermute | solution.py:415

commit v9 on v7

--- a/solution.py
+++ b/solution.py
@@ -251,8 +251,10 @@
     rhs,
     panel,
     pivot,
-    send,
-    keep,
+    send_near,
+    send_rest,
+    keep_near,
+    keep_rest,
     b_v,
     masked,
     mask,
@@ -275,7 +277,8 @@
     for i in range(parts):
         rows = pl.ds(i * step, step)
         gets.append(pltpu.make_async_copy(panel.at[rows], w_v.at[rows], sems.at[3 + i]))
-    gets.append(pltpu.make_async_copy(pivot, d_v, sems.at[3 + parts]))
+    get = pltpu.make_async_copy(pivot.at[pl.ds(0, 4 * quarter)], d_v, sems.at[3 + parts])
+    gets.append(get)
     for get in gets:
         get.start()
     c_v[...] = jnp.zeros_like(c_v)
@@ -294,23 +297,30 @@
         for e in range(step // B):
             block = pmap_s[leaf_pos, i * (step // B) + e]
             c_v[pl.ds(pl.multiple_of(block * B, B), B)] = product[e * B : (e + 1) * B]
-    for out, side in ((keep, leaf_pos), (send, 1 - leaf_pos)):
+    for near_out, rest, side in (
+        (send_near, send_rest, 1 - leaf_pos),
+        (keep_near, keep_rest, leaf_pos),
+    ):
         near = (row_pos ^ (1 + side)) * quarter
         mine, other = side * half, (1 - side) * half
-        out[pl.ds(0, half)] = c_v[rows_at(near + mine, half)]
-        out[pl.ds(half, half)] = c_v[rows_at(near + other, half)]
-        out[pl.ds(quarter, half)] = c_v[rows_at((row_pos ^ 3) * quarter + mine, half)]
-        out[pl.ds(quarter + half, half)] = c_v[rows_at(row_pos * quarter + mine, half)]
+        near_out[pl.ds(0, half)] = c_v[rows_at(near + mine, half)]
+        near_out[pl.ds(half, half)] = c_v[rows_at(near + other, half)]
+        rest[pl.ds(0, half)] = c_v[rows_at((row_pos ^ 3) * quarter + mine, half)]
+        rest[pl.ds(half, half)] = c_v[rows_at(row_pos * quarter + mine, half)]
     gets[3 + parts].wait()
 
 
-def leaf_pivot_kernel(sizes, masked, d_v, after, *outs):
-    quarter = sizes
+def leaf_pivot_kernel(sizes, masked, d_v, pivot, after, *outs_and_scratch):
+    quarter, rows = sizes
+    *outs, root_d, sem = outs_and_scratch
+    get = pltpu.make_async_copy(pivot.at[pl.ds(4 * quarter, rows)], root_d, sem)
+    get.start()
     order = row_order(lax.axis_index("row"), lax.axis_index("leaf"))
     right = masked[...]
     for k in (3, 1, 2, 0):
         product = mm(d_v[rows_at(order[k] * quarter, quarter)], right)
         outs[k][...] = product.astype(BF)
+    get.wait()
 
 
 def scatter_kernel(sizes, live, pmap, w_v, after, out, live_s, pmap_s, sems):
@@ -339,20 +349,20 @@
 
 
 def root_pivot_kernel(sizes, mine, yours, other_mine, other_yours, d_v, out, q_v):
-    half, base = sizes
+    half = sizes
     leaf_pos = lax.axis_index("leaf")
     for own, other, at in ((mine, other_yours, leaf_pos), (yours, other_mine, 1 - leaf_pos)):
         value = own[...].astype(F32) + other[...].astype(F32)
         q_v[rows_at(at * half, half)] = (-value).astype(BF)
-    out[...] = mm(d_v[pl.ds(base, 4 * half)], q_v[...]).astype(BF)
+    out[...] = mm(d_v[pl.ds(0, 4 * half)], q_v[...]).astype(BF)
 
 
 def root_transposed_kernel(sizes, y, d_v, out, piece, s_v):
-    half, base = sizes
+    half = sizes
     leaf_pos = lax.axis_index("leaf")
     row_pos = lax.axis_index("row")
     piece[...] = y[rows_at(row_pos * half, half)]
-    s_v[...] = mm(y[...].T, d_v[pl.ds(base, 4 * half)]).T
+    s_v[...] = mm(y[...].T, d_v[pl.ds(0, 4 * half)]).T
     out[pl.ds(0, half)] = s_v[rows_at(leaf_pos * half, half)].astype(BF)
     out[pl.ds(half, half)] = s_v[rows_at((1 - leaf_pos) * half, half)].astype(BF)
 
@@ -393,14 +403,22 @@
     total[...] = value - mm(s_v[...].T, panel_rows[pl.ds(0, quarter)])
 
 
-def last_kernel(sizes, mine, theirs, mine_far, theirs_far, total, panel_rows, root_rows, out, s_v):
+def own_kernel(sizes, near, far, total, panel_rows, out, s_v):
     quarter, half = sizes
     leaf_pos = lax.axis_index("leaf")
-    put(s_v, 1, half, mine, (leaf_pos, 1 - leaf_pos))
-    put(s_v, 0, half, theirs, (1 - leaf_pos, leaf_pos))
-    put(s_v, 2, half, mine_far, (leaf_pos,))
-    put(s_v, 2, half, theirs_far, (1 - leaf_pos,))
-    value = total[...] - mm(s_v[...].T, panel_rows[pl.ds(quarter, 3 * quarter)])
+    put(s_v, 0, half, near, (leaf_pos, 1 - leaf_pos))
+    value = total[...] - mm(s_v[...].T, panel_rows[pl.ds(2 * quarter, quarter)])
+    rows = rows_at(3 * quarter + leaf_pos * half, half)
+    out[...] = value - mm(far[...].T, panel_rows[rows])
+
+
+def last_kernel(sizes, near, far, total, panel_rows, root_rows, out, s_v):
+    quarter, half = sizes
+    leaf_pos = lax.axis_index("leaf")
+    put(s_v, 0, half, near, (1 - leaf_pos, leaf_pos))
+    value = total[...] - mm(s_v[...].T, panel_rows[pl.ds(quarter, quarter)])
+    rows = rows_at(3 * quarter + (1 - leaf_pos) * half, half)
+    value = value - mm(far[...].T, panel_rows[rows])
     out[pl.ds(0, quarter)] = value.T.astype(BF)
     out[pl.ds(quarter, half)] = root_rows[pl.ds(0, half)]
 
@@ -431,39 +449,40 @@
     smem = [pltpu.SMEM(live.shape, jnp.int32), pltpu.SMEM(parent_map.shape, jnp.int32)]
 
     parts = 4 if updates % (4 * B) == 0 else 1
-    sent, keep, b_v, masked, mask, w_v, d_v = call(
+    send_near, send_rest, keep_near, keep_rest, b_v, masked, mask, w_v, d_v = call(
         functools.partial(panel_kernel, (quarter, half, parts, updates)),
         (
-            kept(4 * half, columns),
-            kept(4 * half, columns),
+            kept(quarter, columns),
+            kept(quarter, columns),
+            kept(quarter, columns),
+            kept(quarter, columns),
             kept(quarter + half, columns),
             kept(quarter, columns),
             kept(quarter, columns),
             kept(updates, quarter),
-            kept(front + 4 * half, quarter),
+            kept(front, quarter),
         ),
         [ANY] * 5,
         [pltpu.VMEM((front, columns), BF), *smem, pltpu.SemaphoreType.DMA((4 + parts,))],
-        57_100_000,
+        58_700_000,
         2 * updates * quarter * columns,
         2 * updates * quarter,
     )(live, parent_map, rhs, panel, pivot_inverse)
-    got = leaf_swap(sent)
-    update = added(keep, got)
-    away_far = update[quarter : quarter + half].astype(BF)
-    away_near = update[:quarter].astype(BF)
+    away_near = added(keep_near, leaf_swap(send_near)).astype(BF)
+    rest = added(keep_rest, leaf_swap(send_rest))
+    away_far = rest[:half].astype(BF)
     from_far = row_swap(away_far, 2)
     from_near = row_swap(away_near, 0)
 
-    pieces = call(
-        functools.partial(leaf_pivot_kernel, quarter),
-        (kept(quarter, columns),) * 4,
-        [VMEM, VMEM, ANY],
-        [],
-        16 * MIB,
+    *pieces, root_d = call(
+        functools.partial(leaf_pivot_kernel, (quarter, 4 * half)),
+        (*(kept(quarter, columns),) * 4, kept(4 * half, quarter)),
+        [VMEM, VMEM, ANY, ANY],
+        [pltpu.SemaphoreType.DMA],
+        49_500_000,
         2 * front * quarter * columns,
         2 * front * quarter,
-    )(masked, d_v, away_near)
+    )(masked, d_v, pivot_inverse, away_near)
     from_near = after(from_near, pieces[0])
     leaf_forward = pieces[0].astype(F32)
     for phase in (2, 0, 1):
@@ -473,7 +492,7 @@
     rows_x = row_swap(leaf_forward, 0)
     rows_d = row_swap(rows_y, 0)
 
-    term = update[quarter + half :] + from_far.astype(F32) - b_v[quarter:].astype(F32)
+    term = rest[half:] + from_far.astype(F32) - b_v[quarter:].astype(F32)
     from_near = from_near.astype(F32)
     negated_mine = (from_near[:half] + term).astype(BF)
     negated_yours = from_near[half:].astype(BF)
@@ -481,14 +500,14 @@
     other_mine = leaf_swap(negated_mine)
 
     partial = call(
-        functools.partial(root_pivot_kernel, (half, front)),
+        functools.partial(root_pivot_kernel, half),
         kept(4 * half, columns),
         [VMEM] * 5,
         [pltpu.VMEM((quarter, columns), BF)],
         16 * MIB,
         0,
         0,
-    )(negated_mine, negated_yours, other_mine, other_yours, d_v)
+    )(negated_mine, negated_yours, other_mine, other_yours, root_d)
     panel_rows = call(
         functools.partial(scatter_kernel, (quarter, updates)),
         kept(front, quarter),
@@ -503,14 +522,14 @@
     root_forward = (partial + got.astype(F32)).astype(BF)
 
     part, root_piece = call(
-        functools.partial(root_transposed_kernel, (half, front)),
+        functools.partial(root_transposed_kernel, half),
         (kept(quarter, columns), kept(half, columns)),
         [VMEM, VMEM],
         [pltpu.VMEM((quarter, columns), F32)],
         16 * MIB,
         0,
         0,
-    )(root_forward, d_v)
+    )(root_forward, root_d)
     got = after(leaf_swap(part), rows_d)
     root_mine = added(part[:half], got[half:]).astype(BF)
     root_other = added(part[half:], got[:half]).astype(BF)
@@ -530,15 +549,24 @@
     near = after(near, total)
     near_other = leaf_swap(near)
     far_other = leaf_swap(far)
+    total = call(
+        functools.partial(own_kernel, (quarter, half)),
+        kept(columns, quarter, F32),
+        [VMEM] * 4,
+        [pltpu.VMEM((quarter, columns), BF)],
+        16 * MIB,
+        0,
+        0,
+    )(near, far, total, panel_rows)
     backward = call(
         functools.partial(last_kernel, (quarter, half)),
         stored(quarter + half, columns),
-        [VMEM] * 7,
-        [pltpu.VMEM((3 * quarter, columns), BF)],
+        [VMEM] * 5,
+        [pltpu.VMEM((quarter, columns), BF)],
         16 * MIB,
         front * quarter * columns,
         front * quarter,
-    )(near, near_other, far, far_other, total, panel_rows, root_rows)
+    )(near_other, far_other, total, panel_rows, root_rows)
     return forward, backward
 
 

time: 45.9 us -> 45.1 us (0.983)
  starting transfers between devices: 21 us -> 19.4 us
  Pallas kernels: 9.31 us -> 10.1 us
    ppermute x12, starting transfers between devices: 19.8 us -> 18.2 us  [row_swap(): return lax.ppermute(value, ('leaf', 'row'), route)]
    pallas_call x3 -> x4, Pallas kernels: 2.24 us -> 3.71 us  [the longest x1 2.02 us: two_levels(): call(functools.partial(leaf_pivot_kernel, (quarter, 4 * half)), (*(kept(q...]
    ppermute x12, waiting for transfers between devices: 10 us -> 10.9 us  [row_swap(): return lax.ppermute(value, ('leaf', 'row'), route)]
    ppermute x6 -> x7, waiting for transfers between devices: 3.94 us -> 3.11 us  [leaf_swap(): return lax.ppermute(value, 'leaf', [(0, 1), (1, 0)])]
    pallas_call x1, Pallas kernels: 3.21 us -> 2.74 us  [two_levels(): call(functools.partial(panel_kernel, (quarter, half, parts, updates)), (k...]
    ppermute x6 -> x7, starting transfers between devices: 1.24 us -> 1.24 us  [leaf_swap(): return lax.ppermute(value, 'leaf', [(0, 1), (1, 0)])]
  transfers between devices with their start and end apart: 18 -> 19, of which waited for: 12 -> 14; matrix products, arithmetic and copies ran while one was open for 1% -> 1% of each run, Pallas kernels for 10% -> 14%
where the time goes in v9:
time: 45.1 us; the launch traced here: 44.9 us
  starting transfers between devices  19.4 us (43%)
  waiting for transfers between devices  14 us (31%)
  Pallas kernels  10.1 us (22%)
  between operations  0.77 us (2%)
  other arithmetic  0.55 us (1%)
    ppermute x12, starting transfers between devices, row_swap(): return lax.ppermute(value, ('leaf', 'row'), route)  18.2 us
    ppermute x12, waiting for transfers between devices, row_swap(): return lax.ppermute(value, ('leaf', 'row'), route)  10.9 us
    ppermute x7, waiting for transfers between devices, leaf_swap(): return lax.ppermute(value, 'leaf', [(0, 1), (1, 0)])  3.11 us
    pallas_call x1, Pallas kernels, two_levels(): call(functools.partial(panel_kernel, (quarter, half, parts, updates)), (k...  2.74 us
    pallas_call x1, Pallas kernels, two_levels(): call(functools.partial(leaf_pivot_kernel, (quarter, 4 * half)), (*(kept(q...  2.02 us
    pallas_call x1, Pallas kernels, two_levels(): call(functools.partial(leaf_transposed_kernel, (quarter, half)), (kept(co...  1.57 us
    pallas_call x1, Pallas kernels, two_levels(): call(functools.partial(last_kernel, (quarter, half)), stored(quarter + ha...  1.26 us
    ppermute x7, starting transfers between devices, leaf_swap(): return lax.ppermute(value, 'leaf', [(0, 1), (1, 0)])  1.24 us
  transfers between devices with their start and end apart: 19, of which 14 were waited for; matrix products, arithmetic and copies ran while one was open for 1% of the time, Pallas kernels for 14%

profile of v9, /device:TPU:0, one launch (start us, length us, event | category | flops | bytes accessed | tf_op | source)
XLA Modules:
  0.0 44.9 jit_solution(6501952792789884462)
XLA Ops:
  0.6 2.7 %shard_map.68 = (bf16[640,128]{1,0:T(8,128)(2,1)S(1)}, bf16[640,128]{1,0:T(8,128)(2,1)S(1)}, bf16[640,128]{1,0:T(8,128)(2,1)S(1)}, bf16[640,128]{1,0:T(8,128)(2,...) custom-call(s32[3]{0:T(128)} %live.3, ...), custom_call_target="tpu_custom_call" | custom-call | flops 251658240 | bytes 1966080 | tf_op jit(solution)/shard_map/pallas_call | solution.py:452
  3.4 0.5 %collective-permute-start = (bf16[640,128]{1,0:T(8,128)(2,1)S(1)}, bf16[640,128]{1,0:T(8,128)(2,1)S(1)}, u32[]{:S(2)}, u32[]{:S(2)}) collective-permute-start(bf16[640,128]{1,0:T(8,128)(2,1)S(1)} %get-tuple-element.29), channel_id=1, source_target_pairs={{0,16},{16,0},{1,17},{17,1},{2,18},{18,2},{3,19},{19,3},{4,20},{20... | collective-permute-start | bytes 491528 | tf_op jit(solution)/shard_map/ppermute | solution.py:427
  4.0 0.9 %collective-permute-done = bf16[640,128]{1,0:T(8,128)(2,1)S(1)} collective-permute-done((bf16[640,128]{1,0:T(8,128)(2,1)S(1)}, bf16[640,128]{1,0:T(8,128)(2,1)S(1)}, u32[]{:S(2)}, u32[]{:S(2)}) %collective-permute-start) | collective-permute-done | bytes 163872 | tf_op jit(solution)/shard_map/ppermute | solution.py:427
  5.0 2.9 %collective-permute-start.7 = (bf16[640,128]{1,0:T(8,128)(2,1)S(1)}, bf16[640,128]{1,0:T(8,128)(2,1)S(1)}, u32[]{:S(2)}, u32[]{:S(2)}) collective-permute-start(bf16[640,128]{1,0:T(8,128)(2,1)S(1)} %add_convert_fusion.1.after), channel_id=1, source_target_pairs={{0,4},{4,0},{8,12},{12,8},{16,24},{20,28},{24,16},{28,20},{1,5},{5... | collective-permute-start | bytes 491528 | tf_op jit(solution)/shard_map/ppermute | solution.py:435
  8.0 1.6 %collective-permute-start.9 = (bf16[320,128]{1,0:T(8,128)(2,1)S(1)}, bf16[320,128]{1,0:T(8,128)(2,1)S(1)}, u32[]{:S(2)}, u32[]{:S(2)}) collective-permute-start(bf16[320,128]{1,0:T(8,128)(2,1)S(1)} %slice.59), channel_id=1, source_target_pairs={{0,12},{4,8},{8,4},{12,0},{16,28},{20,24},{24,20},{28,16},{1,13},{... | collective-permute-start | bytes 245768 | tf_op jit(solution)/shard_map/ppermute | solution.py:435
  9.5 2.0 %shard_map.69 = (bf16[640,128]{1,0:T(8,128)(2,1)S(1)}, bf16[640,128]{1,0:T(8,128)(2,1)S(1)}, bf16[640,128]{1,0:T(8,128)(2,1)S(1)}, bf16[640,128]{1,0:T(8,128)(2,1)S(1)}, bf16[1280,640]{1,0:T(8,128)(2,1)S(1)}) custom-call(bf16[640,128]{1,0:T(8,128)(2,1)S(1)} %get-tuple-element.26.masked, bf16[2560,640]{1,0:T(8,128)(2,1)S(1)} %get-tuple-element.27.d_v, ...), custom_call_target="tpu_custom_call" | custom-call | flops 419430400 | bytes 3276800 | tf_op jit(solution)/shard_map/pallas_call | solution.py:477
  11.6 1.5 %collective-permute-start.1 = (bf16[640,128]{1,0:T(8,128)(2,1)S(1)}, bf16[640,128]{1,0:T(8,128)(2,1)S(1)}, u32[]{:S(2)}, u32[]{:S(2)}) collective-permute-start(bf16[640,128]{1,0:T(8,128)(2,1)S(1)} %get-tuple-element.31), channel_id=1, source_target_pairs={{0,12},{4,8},{8,4},{12,0},{16,28},{20,24},{24,20},{28,16},{1,13},{... | collective-permute-start | bytes 491528 | tf_op jit(solution)/shard_map/ppermute | solution.py:435
  13.2 1.9 %collective-permute-start.3 = (bf16[640,128]{1,0:T(8,128)(2,1)S(1)}, bf16[640,128]{1,0:T(8,128)(2,1)S(1)}, u32[]{:S(2)}, u32[]{:S(2)}) collective-permute-start(bf16[640,128]{1,0:T(8,128)(2,1)S(1)} %get-tuple-element.33), channel_id=1, source_target_pairs={{0,8},{4,12},{8,0},{12,4},{16,20},{20,16},{24,28},{28,24},{1,9},{5... | collective-permute-start | bytes 491528 | tf_op jit(solution)/shard_map/ppermute | solution.py:435
  15.3 0.5 %collective-permute-start.11 = (bf16[320,128]{1,0:T(8,128)(2,1)S(1)}, bf16[320,128]{1,0:T(8,128)(2,1)S(1)}, u32[]{:S(2)}, u32[]{:S(2)}) collective-permute-start(bf16[320,128]{1,0:T(8,128)(2,1)S(1)} %slice.37.yours), channel_id=1, source_target_pairs={{0,16},{16,0},{1,17},{17,1},{2,18},{18,2},{3,19},{19,3},{4,20},{20... | collective-permute-start | bytes 245768 | tf_op jit(solution)/shard_map/ppermute | solution.py:427
  15.8 0.8 %collective-permute-done.10.other_mine = bf16[320,128]{1,0:T(8,128)(2,1)S(1)} collective-permute-done((bf16[320,128]{1,0:T(8,128)(2,1)S(1)}, bf16[320,128]{1,0:T(8,128)(2,1)S(1)}, u32[]{:S(2)}, u32[]{:S(2)}) %collective-permute-start.10) | collective-permute-done | bytes 81952 | tf_op jit(solution)/shard_map/ppermute | solution.py:427
  16.7 0.6 %shard_map.70 = bf16[1280,128]{1,0:T(8,128)(2,1)S(1)} custom-call(bf16[320,128]{1,0:T(8,128)(2,1)S(1)} %fusion.3.mine, bf16[320,128]{1,0:T(8,128)(2,1)S(1)} %slice.37.yours, bf16[320,128]{1,0:T(8,128)(2,1)S(1)} %collective-permute-done.10.other_mine, bf16[320,128]{1,0:T(8,128)(2,1)S(1)} %collective-permute-done.11.other_yours, ...), custom_call_target="tpu_custom_call" | custom-call | tf_op jit(solution)/shard_map/pallas_call | solution.py:502
  17.5 2.2 %collective-permute-done.1 = bf16[640,128]{1,0:T(8,128)(2,1)S(1)} collective-permute-done((bf16[640,128]{1,0:T(8,128)(2,1)S(1)}, bf16[640,128]{1,0:T(8,128)(2,1)S(1)}, u32[]{:S(2)}, u32[]{:S(2)}) %collective-permute-start.1) | collective-permute-done | bytes 163872 | tf_op jit(solution)/shard_map/ppermute | solution.py:435
  19.7 2.1 %collective-permute-done.2 = bf16[640,128]{1,0:T(8,128)(2,1)S(1)} collective-permute-done((bf16[640,128]{1,0:T(8,128)(2,1)S(1)}, bf16[640,128]{1,0:T(8,128)(2,1)S(1)}, u32[]{:S(2)}, u32[]{:S(2)}) %collective-permute-start.2) | collective-permute-done | bytes 163872 | tf_op jit(solution)/shard_map/ppermute | solution.py:435
  21.9 1.2 %collective-permute-start.4 = (bf16[640,128]{1,0:T(8,128)(2,1)S(1)}, bf16[640,128]{1,0:T(8,128)(2,1)S(1)}, u32[]{:S(2)}, u32[]{:S(2)}) collective-permute-start(bf16[640,128]{1,0:T(8,128)(2,1)S(1)} %select_convert_fusion.own), channel_id=1, source_target_pairs={{0,4},{4,0},{8,12},{12,8},{16,24},{20,28},{24,16},{28,20},{1,5},{5... | collective-permute-start | bytes 491528 | tf_op jit(solution)/shard_map/ppermute | solution.py:435
  23.1 1.6 %collective-permute-start.5 = (bf16[640,128]{1,0:T(8,128)(2,1)S(1)}, bf16[640,128]{1,0:T(8,128)(2,1)S(1)}, u32[]{:S(2)}, u32[]{:S(2)}) collective-permute-start(bf16[640,128]{1,0:T(8,128)(2,1)S(1)} %select_convert_fusion.own), channel_id=1, source_target_pairs={{0,8},{4,12},{8,0},{12,4},{16,20},{20,16},{24,28},{28,24},{1,9},{5... | collective-permute-start | bytes 491528 | tf_op jit(solution)/shard_map/ppermute | solution.py:435
  24.8 0.9 %collective-permute-done.12 = bf16[1280,128]{1,0:T(8,128)(2,1)S(1)} collective-permute-done((bf16[1280,128]{1,0:T(8,128)(2,1)S(1)}, bf16[1280,128]{1,0:T(8,128)(2,1)S(1)}, u32[]{:S(2)}, u32[]{:S(2)}) %collective-permute-start.12) | collective-permute-done | bytes 327712 | tf_op jit(solution)/shard_map/ppermute | solution.py:435
  25.8 1.9 %collective-permute-start.13 = (bf16[1280,128]{1,0:T(8,128)(2,1)S(1)}, bf16[1280,128]{1,0:T(8,128)(2,1)S(1)}, u32[]{:S(2)}, u32[]{:S(2)}) collective-permute-start(bf16[1280,128]{1,0:T(8,128)(2,1)S(1)} %fusion), channel_id=1, source_target_pairs={{0,4},{4,0},{8,12},{12,8},{16,24},{20,28},{24,16},{28,20},{1,5},{5... | collective-permute-start | bytes 983048 | tf_op jit(solution)/shard_map/ppermute | solution.py:435
  27.7 1.1 %collective-permute-done.4.rows_x = bf16[640,128]{1,0:T(8,128)(2,1)S(1)} collective-permute-done((bf16[640,128]{1,0:T(8,128)(2,1)S(1)}, bf16[640,128]{1,0:T(8,128)(2,1)S(1)}, u32[]{:S(2)}, u32[]{:S(2)}) %collective-permute-start.4) | collective-permute-done | bytes 163872 | tf_op jit(solution)/shard_map/ppermute | solution.py:435
  28.8 0.5 %collective-permute-done.5.after.rows_y = bf16[640,128]{1,0:T(8,128)(2,1)S(1)} collective-permute-done((bf16[640,128]{1,0:T(8,128)(2,1)S(1)}, bf16[640,128]{1,0:T(8,128)(2,1)S(1)}, u32[]{:S(2)}, u32[]{:S(2)}) %collective-permute-start.5) | collective-permute-done | bytes 163872 | tf_op jit(solution)/shard_map/ppermute | solution.py:435
  29.3 1.9 %collective-permute-start.6 = (bf16[640,128]{1,0:T(8,128)(2,1)S(1)}, bf16[640,128]{1,0:T(8,128)(2,1)S(1)}, u32[]{:S(2)}, u32[]{:S(2)}) collective-permute-start(bf16[640,128]{1,0:T(8,128)(2,1)S(1)} %collective-permute-done.5.after.rows_y), channel_id=1, source_target_pairs={{0,4},{4,0},{8,12},{12,8},{16,24},{20,28},{24,16},{28,20},{1,5},{5... | collective-permute-start | bytes 491528 | tf_op jit(solution)/shard_map/ppermute | solution.py:435
  31.1 0.8 %shard_map.71.panel_rows = bf16[2560,640]{1,0:T(8,128)(2,1)S(1)} custom-call(s32[3]{0:T(128)S(1)} %copy-done.1, s32[2,12]{1,0:T(2,128)S(1)} %copy-done, bf16[1536,640]{1,0:T(8,128)(2,1)S(1)} %get-tuple-element.39.w_v, bf16[640,128]{1,0:T(8,128)(2,1)S(1)} %collective-permute-done.5.after.rows_y), custom_call_target="tpu_custom_call" | custom-call | flops 2000000000 | bytes 6553600 | tf_op jit(solution)/shard_map/pallas_call | solution.py:511
  32.0 0.9 %collective-permute-done.13 = bf16[1280,128]{1,0:T(8,128)(2,1)S(1)} collective-permute-done((bf16[1280,128]{1,0:T(8,128)(2,1)S(1)}, bf16[1280,128]{1,0:T(8,128)(2,1)S(1)}, u32[]{:S(2)}, u32[]{:S(2)}) %collective-permute-start.13) | collective-permute-done | bytes 327712 | tf_op jit(solution)/shard_map/ppermute | solution.py:435
  33.1 0.6 %shard_map.72 = (bf16[640,128]{1,0:T(8,128)(2,1)S(1)}, bf16[320,128]{1,0:T(8,128)(2,1)S(1)}) custom-call(bf16[1280,128]{1,0:T(8,128)(2,1)S(1)} %add_convert_fusion.y, bf16[1280,640]{1,0:T(8,128)(2,1)S(1)} %get-tuple-element.38.d_v), custom_call_target="tpu_custom_call" | custom-call | tf_op jit(solution)/shard_map/pallas_call | solution.py:524
  33.7 1.0 %collective-permute-done.6.rows_d = bf16[640,128]{1,0:T(8,128)(2,1)S(1)} collective-permute-done((bf16[640,128]{1,0:T(8,128)(2,1)S(1)}, bf16[640,128]{1,0:T(8,128)(2,1)S(1)}, u32[]{:S(2)}, u32[]{:S(2)}) %collective-permute-start.6) | collective-permute-done | bytes 163872 | tf_op jit(solution)/shard_map/ppermute | solution.py:435
  35.2 1.9 %collective-permute-start.15 = (bf16[640,128]{1,0:T(8,128)(2,1)S(1)}, bf16[640,128]{1,0:T(8,128)(2,1)S(1)}, u32[]{:S(2)}, u32[]{:S(2)}) collective-permute-start(bf16[640,128]{1,0:T(8,128)(2,1)S(1)} %pad_maximum_fusion.root_rows), channel_id=1, source_target_pairs={{0,8},{4,12},{8,0},{12,4},{16,20},{20,16},{24,28},{28,24},{1,9},{5... | collective-permute-start | bytes 491528 | tf_op jit(solution)/shard_map/ppermute | solution.py:435
  37.1 1.5 %collective-permute-start.17 = (bf16[320,128]{1,0:T(8,128)(2,1)S(1)}, bf16[320,128]{1,0:T(8,128)(2,1)S(1)}, u32[]{:S(2)}, u32[]{:S(2)}) collective-permute-start(bf16[320,128]{1,0:T(8,128)(2,1)S(1)} %get-tuple-element.48), channel_id=1, source_target_pairs={{0,12},{4,8},{8,4},{12,0},{16,28},{20,24},{24,20},{28,16},{1,13},{... | collective-permute-start | bytes 245768 | tf_op jit(solution)/shard_map/ppermute | solution.py:435
  38.6 1.6 %shard_map.73 = (f32[128,640]{1,0:T(8,128)S(1)}, bf16[960,128]{1,0:T(8,128)(2,1)}) custom-call(bf16[640,128]{1,0:T(8,128)(2,1)S(1)} %select_convert_fusion.own, bf16[640,128]{1,0:T(8,128)(2,1)S(1)} %collective-permute-done.4.rows_x, bf16[640,128]{1,0:T(8,128)(2,1)S(1)} %collective-permute-done.5.after.rows_y, ...), custom_call_target="tpu_custom_call" | custom-call | flops 419430400 | bytes 3276800 | tf_op jit(solution)/shard_map/pallas_call | solution.py:540
  40.1 1.5 %collective-permute-done.15.near = bf16[640,128]{1,0:T(8,128)(2,1)S(1)} collective-permute-done((bf16[640,128]{1,0:T(8,128)(2,1)S(1)}, bf16[640,128]{1,0:T(8,128)(2,1)S(1)}, u32[]{:S(2)}, u32[]{:S(2)}) %collective-permute-start.15) | collective-permute-done | bytes 163872 | tf_op jit(solution)/shard_map/ppermute | solution.py:435
  41.7 0.7 %collective-permute-done.17.far = bf16[320,128]{1,0:T(8,128)(2,1)S(1)} collective-permute-done((bf16[320,128]{1,0:T(8,128)(2,1)S(1)}, bf16[320,128]{1,0:T(8,128)(2,1)S(1)}, u32[]{:S(2)}, u32[]{:S(2)}) %collective-permute-start.17) | collective-permute-done | bytes 81952 | tf_op jit(solution)/shard_map/ppermute | solution.py:435
  42.4 0.5 %shard_map.74.total = f32[128,640]{1,0:T(8,128)S(1)} custom-call(bf16[640,128]{1,0:T(8,128)(2,1)S(1)} %collective-permute-done.15.near, bf16[320,128]{1,0:T(8,128)(2,1)S(1)} %collective-permute-done.17.far, f32[128,640]{1,0:T(8,128)S(1)} %get-tuple-element.46.total, bf16[2560,640]{1,0:T(8,128)(2,1)S(1)} %shard_map.71.panel_rows), custom_call_target="tpu_custom_call" | custom-call | tf_op jit(solution)/shard_map/pallas_call | solution.py:552
  42.9 0.8 %collective-permute-done.18.far = bf16[320,128]{1,0:T(8,128)(2,1)S(1)} collective-permute-done((bf16[320,128]{1,0:T(8,128)(2,1)S(1)}, bf16[320,128]{1,0:T(8,128)(2,1)S(1)}, u32[]{:S(2)}, u32[]{:S(2)}) %collective-permute-start.18) | collective-permute-done | bytes 81952 | tf_op jit(solution)/shard_map/ppermute | solution.py:427
  43.7 1.3 %shard_map.75 = bf16[960,128]{1,0:T(8,128)(2,1)} custom-call(bf16[640,128]{1,0:T(8,128)(2,1)S(1)} %collective-permute-done.16.near, bf16[320,128]{1,0:T(8,128)(2,1)S(1)} %collective-permute-done.18.far, f32[128,640]{1,0:T(8,128)S(1)} %shard_map.74.total, bf16[2560,640]{1,0:T(8,128)(2,1)S(1)} %shard_map.71.panel_rows, ...), custom_call_target="tpu_custom_call" | custom-call | flops 209715200 | bytes 1638400 | tf_op jit(solution)/shard_map/pallas_call | solution.py:561
  (28 shorter events, 1.7 us)
Async XLA Ops:
  3.4 1.5 %collective-permute-start = (bf16[640,128]{1,0:T(8,128)(2,1)S(1)}, bf16[640,128]{1,0:T(8,128)(2,1)S(1)}, u32[]{:S(2)}, u32[]{:S(2)}) collective-permute-start(bf16[640,128]{1,0:T(8,128)(2,1)S(1)} %get-tuple-element.29), channel_id=1, source_target_pairs={{0,16},{16,0},{1,17},{17,1},{2,18},{18,2},{3,19},{19,3},{4,20},{20... | collective-permute-start | bytes 491528 | tf_op jit(solution)/shard_map/ppermute | solution.py:427
  3.9 4.0 %collective-permute-start.8 = (bf16[640,128]{1,0:T(8,128)(2,1)S(1)}, bf16[640,128]{1,0:T(8,128)(2,1)S(1)}, u32[]{:S(2)}, u32[]{:S(2)}) collective-permute-start(bf16[640,128]{1,0:T(8,128)(2,1)S(1)} %get-tuple-element.36), channel_id=1, source_target_pairs={{0,16},{16,0},{1,17},{17,1},{2,18},{18,2},{3,19},{19,3},{4,20},{20... | collective-permute-start | bytes 491528 | tf_op jit(solution)/shard_map/ppermute | solution.py:427
  5.0 10.2 %collective-permute-start.7 = (bf16[640,128]{1,0:T(8,128)(2,1)S(1)}, bf16[640,128]{1,0:T(8,128)(2,1)S(1)}, u32[]{:S(2)}, u32[]{:S(2)}) collective-permute-start(bf16[640,128]{1,0:T(8,128)(2,1)S(1)} %add_convert_fusion.1.after), channel_id=1, source_target_pairs={{0,4},{4,0},{8,12},{12,8},{16,24},{20,28},{24,16},{28,20},{1,5},{5... | collective-permute-start | bytes 491528 | tf_op jit(solution)/shard_map/ppermute | solution.py:435
  8.0 7.2 %collective-permute-start.9 = (bf16[320,128]{1,0:T(8,128)(2,1)S(1)}, bf16[320,128]{1,0:T(8,128)(2,1)S(1)}, u32[]{:S(2)}, u32[]{:S(2)}) collective-permute-start(bf16[320,128]{1,0:T(8,128)(2,1)S(1)} %slice.59), channel_id=1, source_target_pairs={{0,12},{4,8},{8,4},{12,0},{16,28},{20,24},{24,20},{28,16},{1,13},{... | collective-permute-start | bytes 245768 | tf_op jit(solution)/shard_map/ppermute | solution.py:435
  11.5 19.6 %copy-start = (s32[2,12]{1,0:T(2,128)S(1)}, s32[2,12]{1,0:T(2,128)}, u32[]{:S(2)}) copy-start(s32[2,12]{1,0:T(2,128)} %pmap.3) | copy-start | bytes 292
  11.6 19.6 %copy-start.1 = (s32[3]{0:T(128)S(1)}, s32[3]{0:T(128)}, u32[]{:S(2)}) copy-start(s32[3]{0:T(128)} %live.3) | copy-start | bytes 40
  11.6 8.1 %collective-permute-start.1 = (bf16[640,128]{1,0:T(8,128)(2,1)S(1)}, bf16[640,128]{1,0:T(8,128)(2,1)S(1)}, u32[]{:S(2)}, u32[]{:S(2)}) collective-permute-start(bf16[640,128]{1,0:T(8,128)(2,1)S(1)} %get-tuple-element.31), channel_id=1, source_target_pairs={{0,12},{4,8},{8,4},{12,0},{16,28},{20,24},{24,20},{28,16},{1,13},{... | collective-permute-start | bytes 491528 | tf_op jit(solution)/shard_map/ppermute | solution.py:435
  13.1 8.7 %collective-permute-start.2 = (bf16[640,128]{1,0:T(8,128)(2,1)S(1)}, bf16[640,128]{1,0:T(8,128)(2,1)S(1)}, u32[]{:S(2)}, u32[]{:S(2)}) collective-permute-start(bf16[640,128]{1,0:T(8,128)(2,1)S(1)} %get-tuple-element.32), channel_id=1, source_target_pairs={{0,4},{4,0},{8,12},{12,8},{16,24},{20,28},{24,16},{28,20},{1,5},{5... | collective-permute-start | bytes 491528 | tf_op jit(solution)/shard_map/ppermute | solution.py:435
  13.2 8.6 %collective-permute-start.3 = (bf16[640,128]{1,0:T(8,128)(2,1)S(1)}, bf16[640,128]{1,0:T(8,128)(2,1)S(1)}, u32[]{:S(2)}, u32[]{:S(2)}) collective-permute-start(bf16[640,128]{1,0:T(8,128)(2,1)S(1)} %get-tuple-element.33), channel_id=1, source_target_pairs={{0,8},{4,12},{8,0},{12,4},{16,20},{20,16},{24,28},{28,24},{1,9},{5... | collective-permute-start | bytes 491528 | tf_op jit(solution)/shard_map/ppermute | solution.py:435
  15.2 1.3 %collective-permute-start.10 = (bf16[320,128]{1,0:T(8,128)(2,1)S(1)}, bf16[320,128]{1,0:T(8,128)(2,1)S(1)}, u32[]{:S(2)}, u32[]{:S(2)}) collective-permute-start(bf16[320,128]{1,0:T(8,128)(2,1)S(1)} %fusion.3.mine), channel_id=1, source_target_pairs={{0,16},{16,0},{1,17},{17,1},{2,18},{18,2},{3,19},{19,3},{4,20},{20... | collective-permute-start | bytes 245768 | tf_op jit(solution)/shard_map/ppermute | solution.py:427
  15.3 1.4 %collective-permute-start.11 = (bf16[320,128]{1,0:T(8,128)(2,1)S(1)}, bf16[320,128]{1,0:T(8,128)(2,1)S(1)}, u32[]{:S(2)}, u32[]{:S(2)}) collective-permute-start(bf16[320,128]{1,0:T(8,128)(2,1)S(1)} %slice.37.yours), channel_id=1, source_target_pairs={{0,16},{16,0},{1,17},{17,1},{2,18},{18,2},{3,19},{19,3},{4,20},{20... | collective-permute-start | bytes 245768 | tf_op jit(solution)/shard_map/ppermute | solution.py:427
  17.4 8.4 %collective-permute-start.12 = (bf16[1280,128]{1,0:T(8,128)(2,1)S(1)}, bf16[1280,128]{1,0:T(8,128)(2,1)S(1)}, u32[]{:S(2)}, u32[]{:S(2)}) collective-permute-start(bf16[1280,128]{1,0:T(8,128)(2,1)S(1)} %shard_map.70), channel_id=1, source_target_pairs={{0,8},{4,12},{8,0},{12,4},{16,20},{20,16},{24,28},{28,24},{1,9},{5... | collective-permute-start | bytes 983048 | tf_op jit(solution)/shard_map/ppermute | solution.py:435
  21.9 6.9 %collective-permute-start.4 = (bf16[640,128]{1,0:T(8,128)(2,1)S(1)}, bf16[640,128]{1,0:T(8,128)(2,1)S(1)}, u32[]{:S(2)}, u32[]{:S(2)}) collective-permute-start(bf16[640,128]{1,0:T(8,128)(2,1)S(1)} %select_convert_fusion.own), channel_id=1, source_target_pairs={{0,4},{4,0},{8,12},{12,8},{16,24},{20,28},{24,16},{28,20},{1,5},{5... | collective-permute-start | bytes 491528 | tf_op jit(solution)/shard_map/ppermute | solution.py:435
  23.1 6.1 %collective-permute-start.5 = (bf16[640,128]{1,0:T(8,128)(2,1)S(1)}, bf16[640,128]{1,0:T(8,128)(2,1)S(1)}, u32[]{:S(2)}, u32[]{:S(2)}) collective-permute-start(bf16[640,128]{1,0:T(8,128)(2,1)S(1)} %select_convert_fusion.own), channel_id=1, source_target_pairs={{0,8},{4,12},{8,0},{12,4},{16,20},{20,16},{24,28},{28,24},{1,9},{5... | collective-permute-start | bytes 491528 | tf_op jit(solution)/shard_map/ppermute | solution.py:435
  25.8 7.1 %collective-permute-start.13 = (bf16[1280,128]{1,0:T(8,128)(2,1)S(1)}, bf16[1280,128]{1,0:T(8,128)(2,1)S(1)}, u32[]{:S(2)}, u32[]{:S(2)}) collective-permute-start(bf16[1280,128]{1,0:T(8,128)(2,1)S(1)} %fusion), channel_id=1, source_target_pairs={{0,4},{4,0},{8,12},{12,8},{16,24},{20,28},{24,16},{28,20},{1,5},{5... | collective-permute-start | bytes 983048 | tf_op jit(solution)/shard_map/ppermute | solution.py:435
  29.3 5.4 %collective-permute-start.6 = (bf16[640,128]{1,0:T(8,128)(2,1)S(1)}, bf16[640,128]{1,0:T(8,128)(2,1)S(1)}, u32[]{:S(2)}, u32[]{:S(2)}) collective-permute-start(bf16[640,128]{1,0:T(8,128)(2,1)S(1)} %collective-permute-done.5.after.rows_y), channel_id=1, source_target_pairs={{0,4},{4,0},{8,12},{12,8},{16,24},{20,28},{24,16},{28,20},{1,5},{5... | collective-permute-start | bytes 491528 | tf_op jit(solution)/shard_map/ppermute | solution.py:435
  33.7 1.5 %collective-permute-start.14 = (bf16[640,128]{1,0:T(8,128)(2,1)S(1)}, bf16[640,128]{1,0:T(8,128)(2,1)S(1)}, u32[]{:S(2)}, u32[]{:S(2)}) collective-permute-start(bf16[640,128]{1,0:T(8,128)(2,1)S(1)} %get-tuple-element.42), channel_id=1, source_target_pairs={{0,16},{16,0},{1,17},{17,1},{2,18},{18,2},{3,19},{19,3},{4,20},{20... | collective-permute-start | bytes 491528 | tf_op jit(solution)/shard_map/ppermute | solution.py:427
  35.2 6.5 %collective-permute-start.15 = (bf16[640,128]{1,0:T(8,128)(2,1)S(1)}, bf16[640,128]{1,0:T(8,128)(2,1)S(1)}, u32[]{:S(2)}, u32[]{:S(2)}) collective-permute-start(bf16[640,128]{1,0:T(8,128)(2,1)S(1)} %pad_maximum_fusion.root_rows), channel_id=1, source_target_pairs={{0,8},{4,12},{8,0},{12,4},{16,20},{20,16},{24,28},{28,24},{1,9},{5... | collective-permute-start | bytes 491528 | tf_op jit(solution)/shard_map/ppermute | solution.py:435
  37.1 5.3 %collective-permute-start.17 = (bf16[320,128]{1,0:T(8,128)(2,1)S(1)}, bf16[320,128]{1,0:T(8,128)(2,1)S(1)}, u32[]{:S(2)}, u32[]{:S(2)}) collective-permute-start(bf16[320,128]{1,0:T(8,128)(2,1)S(1)} %get-tuple-element.48), channel_id=1, source_target_pairs={{0,12},{4,8},{8,4},{12,0},{16,28},{20,24},{24,20},{28,16},{1,13},{... | collective-permute-start | bytes 245768 | tf_op jit(solution)/shard_map/ppermute | solution.py:435
  41.7 2.0 %collective-permute-start.16 = (bf16[640,128]{1,0:T(8,128)(2,1)S(1)}, bf16[640,128]{1,0:T(8,128)(2,1)S(1)}, u32[]{:S(2)}, u32[]{:S(2)}) collective-permute-start(bf16[640,128]{1,0:T(8,128)(2,1)S(1)} %collective-permute-done.15.near), channel_id=1, source_target_pairs={{0,16},{16,0},{1,17},{17,1},{2,18},{18,2},{3,19},{19,3},{4,20},{20... | collective-permute-start | bytes 491528 | tf_op jit(solution)/shard_map/ppermute | solution.py:427
  42.4 1.3 %collective-permute-start.18 = (bf16[320,128]{1,0:T(8,128)(2,1)S(1)}, bf16[320,128]{1,0:T(8,128)(2,1)S(1)}, u32[]{:S(2)}, u32[]{:S(2)}) collective-permute-start(bf16[320,128]{1,0:T(8,128)(2,1)S(1)} %collective-permute-done.17.far), channel_id=1, source_target_pairs={{0,16},{16,0},{1,17},{17,1},{2,18},{18,2},{3,19},{19,3},{4,20},{20... | collective-permute-start | bytes 245768 | tf_op jit(solution)/shard_map/ppermute | solution.py:427

commit v10 on v9

--- a/solution.py
+++ b/solution.py
@@ -240,6 +240,18 @@
     return jnp.dot(left, right, preferred_element_type=F32)
 
 
+def copies(source, first_row, target, rows, parts, sems, first_sem):
+    step = rows // parts
+    return [
+        pltpu.make_async_copy(
+            source.at[pl.ds(first_row + i * step, step)],
+            target.at[pl.ds(i * step, step)],
+            sems.at[first_sem + i],
+        )
+        for i in range(parts)
+    ]
+
+
 def row_order(row_pos, leaf_pos):
     return (row_pos, row_pos ^ (1 + leaf_pos), row_pos ^ (2 - leaf_pos), row_pos ^ 3)
 
@@ -277,8 +289,7 @@
     for i in range(parts):
         rows = pl.ds(i * step, step)
         gets.append(pltpu.make_async_copy(panel.at[rows], w_v.at[rows], sems.at[3 + i]))
-    get = pltpu.make_async_copy(pivot.at[pl.ds(0, 4 * quarter)], d_v, sems.at[3 + parts])
-    gets.append(get)
+    gets += copies(pivot, 0, d_v, 4 * quarter, 8, sems, 3 + parts)
     for get in gets:
         get.start()
     c_v[...] = jnp.zeros_like(c_v)
@@ -307,20 +318,23 @@
         near_out[pl.ds(half, half)] = c_v[rows_at(near + other, half)]
         rest[pl.ds(0, half)] = c_v[rows_at((row_pos ^ 3) * quarter + mine, half)]
         rest[pl.ds(half, half)] = c_v[rows_at(row_pos * quarter + mine, half)]
-    gets[3 + parts].wait()
+    for get in gets[3 + parts :]:
+        get.wait()
 
 
 def leaf_pivot_kernel(sizes, masked, d_v, pivot, after, *outs_and_scratch):
     quarter, rows = sizes
-    *outs, root_d, sem = outs_and_scratch
-    get = pltpu.make_async_copy(pivot.at[pl.ds(4 * quarter, rows)], root_d, sem)
-    get.start()
+    *outs, root_d, sems = outs_and_scratch
+    gets = copies(pivot, 4 * quarter, root_d, rows, 4, sems, 0)
+    for get in gets:
+        get.start()
     order = row_order(lax.axis_index("row"), lax.axis_index("leaf"))
     right = masked[...]
     for k in (3, 1, 2, 0):
         product = mm(d_v[rows_at(order[k] * quarter, quarter)], right)
         outs[k][...] = product.astype(BF)
-    get.wait()
+    for get in gets:
+        get.wait()
 
 
 def scatter_kernel(sizes, live, pmap, w_v, after, out, live_s, pmap_s, sems):
@@ -463,7 +477,7 @@
             kept(front, quarter),
         ),
         [ANY] * 5,
-        [pltpu.VMEM((front, columns), BF), *smem, pltpu.SemaphoreType.DMA((4 + parts,))],
+        [pltpu.VMEM((front, columns), BF), *smem, pltpu.SemaphoreType.DMA((11 + parts,))],
         58_700_000,
         2 * updates * quarter * columns,
         2 * updates * quarter,
@@ -478,7 +492,7 @@
         functools.partial(leaf_pivot_kernel, (quarter, 4 * half)),
         (*(kept(quarter, columns),) * 4, kept(4 * half, quarter)),
         [VMEM, VMEM, ANY, ANY],
-        [pltpu.SemaphoreType.DMA],
+        [pltpu.SemaphoreType.DMA((4,))],
         49_500_000,
         2 * front * quarter * columns,
         2 * front * quarter,

time: 45.1 us -> 45.4 us (level)
    ppermute x12, waiting for transfers between devices: 10.9 us -> 11.4 us  [row_swap(): return lax.ppermute(value, ('leaf', 'row'), route)]
  transfers between devices with their start and end apart: 19 -> 19, of which waited for: 14 -> 14; matrix products, arithmetic and copies ran while one was open for 1% -> 1% of each run, Pallas kernels for 14% -> 13%
where the time goes in v10:
time: 45.4 us; the launch traced here: 45.2 us
  starting transfers between devices  19.4 us (43%)
  waiting for transfers between devices  14.4 us (32%)
  Pallas kernels  10 us (22%)
  between operations  0.77 us (2%)
  other arithmetic  0.55 us (1%)
    ppermute x12, starting transfers between devices, row_swap(): return lax.ppermute(value, ('leaf', 'row'), route)  18.2 us
    ppermute x12, waiting for transfers between devices, row_swap(): return lax.ppermute(value, ('leaf', 'row'), route)  11.4 us
    ppermute x7, waiting for transfers between devices, leaf_swap(): return lax.ppermute(value, 'leaf', [(0, 1), (1, 0)])  2.99 us
    pallas_call x1, Pallas kernels, two_levels(): call(functools.partial(panel_kernel, (quarter, half, parts, updates)), (k...  2.78 us
    pallas_call x1, Pallas kernels, two_levels(): call(functools.partial(leaf_pivot_kernel, (quarter, 4 * half)), (*(kept(q...  1.9 us
    pallas_call x1, Pallas kernels, two_levels(): call(functools.partial(leaf_transposed_kernel, (quarter, half)), (kept(co...  1.57 us
    pallas_call x1, Pallas kernels, two_levels(): call(functools.partial(last_kernel, (quarter, half)), stored(quarter + ha...  1.26 us
    ppermute x7, starting transfers between devices, leaf_swap(): return lax.ppermute(value, 'leaf', [(0, 1), (1, 0)])  1.24 us
  transfers between devices with their start and end apart: 19, of which 14 were waited for; matrix products, arithmetic and copies ran while one was open for 1% of the time, Pallas kernels for 13%

profile of v10, /device:TPU:0, one launch (start us, length us, event | category | flops | bytes accessed | tf_op | source)
XLA Modules:
  0.0 45.2 jit_solution(9582725959989409142)
XLA Ops:
  0.6 2.8 %shard_map.68 = (bf16[640,128]{1,0:T(8,128)(2,1)S(1)}, bf16[640,128]{1,0:T(8,128)(2,1)S(1)}, bf16[640,128]{1,0:T(8,128)(2,1)S(1)}, bf16[640,128]{1,0:T(8,128)(2,...) custom-call(s32[3]{0:T(128)} %live.3, ...), custom_call_target="tpu_custom_call" | custom-call | flops 251658240 | bytes 1966080 | tf_op jit(solution)/shard_map/pallas_call | solution.py:466
  3.4 0.5 %collective-permute-start = (bf16[640,128]{1,0:T(8,128)(2,1)S(1)}, bf16[640,128]{1,0:T(8,128)(2,1)S(1)}, u32[]{:S(2)}, u32[]{:S(2)}) collective-permute-start(bf16[640,128]{1,0:T(8,128)(2,1)S(1)} %get-tuple-element.29), channel_id=1, source_target_pairs={{0,16},{16,0},{1,17},{17,1},{2,18},{18,2},{3,19},{19,3},{4,20},{20... | collective-permute-start | bytes 491528 | tf_op jit(solution)/shard_map/ppermute | solution.py:441
  4.0 0.9 %collective-permute-done = bf16[640,128]{1,0:T(8,128)(2,1)S(1)} collective-permute-done((bf16[640,128]{1,0:T(8,128)(2,1)S(1)}, bf16[640,128]{1,0:T(8,128)(2,1)S(1)}, u32[]{:S(2)}, u32[]{:S(2)}) %collective-permute-start) | collective-permute-done | bytes 163872 | tf_op jit(solution)/shard_map/ppermute | solution.py:441
  5.0 2.9 %collective-permute-start.7 = (bf16[640,128]{1,0:T(8,128)(2,1)S(1)}, bf16[640,128]{1,0:T(8,128)(2,1)S(1)}, u32[]{:S(2)}, u32[]{:S(2)}) collective-permute-start(bf16[640,128]{1,0:T(8,128)(2,1)S(1)} %add_convert_fusion.1.after), channel_id=1, source_target_pairs={{0,4},{4,0},{8,12},{12,8},{16,24},{20,28},{24,16},{28,20},{1,5},{5... | collective-permute-start | bytes 491528 | tf_op jit(solution)/shard_map/ppermute | solution.py:449
  8.0 1.6 %collective-permute-start.9 = (bf16[320,128]{1,0:T(8,128)(2,1)S(1)}, bf16[320,128]{1,0:T(8,128)(2,1)S(1)}, u32[]{:S(2)}, u32[]{:S(2)}) collective-permute-start(bf16[320,128]{1,0:T(8,128)(2,1)S(1)} %slice.59), channel_id=1, source_target_pairs={{0,12},{4,8},{8,4},{12,0},{16,28},{20,24},{24,20},{28,16},{1,13},{... | collective-permute-start | bytes 245768 | tf_op jit(solution)/shard_map/ppermute | solution.py:449
  9.6 1.9 %shard_map.69 = (bf16[640,128]{1,0:T(8,128)(2,1)S(1)}, bf16[640,128]{1,0:T(8,128)(2,1)S(1)}, bf16[640,128]{1,0:T(8,128)(2,1)S(1)}, bf16[640,128]{1,0:T(8,128)(2,1)S(1)}, bf16[1280,640]{1,0:T(8,128)(2,1)S(1)}) custom-call(bf16[640,128]{1,0:T(8,128)(2,1)S(1)} %get-tuple-element.26.masked, bf16[2560,640]{1,0:T(8,128)(2,1)S(1)} %get-tuple-element.27.d_v, ...), custom_call_target="tpu_custom_call" | custom-call | flops 419430400 | bytes 3276800 | tf_op jit(solution)/shard_map/pallas_call | solution.py:491
  11.5 1.5 %collective-permute-start.1 = (bf16[640,128]{1,0:T(8,128)(2,1)S(1)}, bf16[640,128]{1,0:T(8,128)(2,1)S(1)}, u32[]{:S(2)}, u32[]{:S(2)}) collective-permute-start(bf16[640,128]{1,0:T(8,128)(2,1)S(1)} %get-tuple-element.31), channel_id=1, source_target_pairs={{0,12},{4,8},{8,4},{12,0},{16,28},{20,24},{24,20},{28,16},{1,13},{... | collective-permute-start | bytes 491528 | tf_op jit(solution)/shard_map/ppermute | solution.py:449
  13.1 1.9 %collective-permute-start.3 = (bf16[640,128]{1,0:T(8,128)(2,1)S(1)}, bf16[640,128]{1,0:T(8,128)(2,1)S(1)}, u32[]{:S(2)}, u32[]{:S(2)}) collective-permute-start(bf16[640,128]{1,0:T(8,128)(2,1)S(1)} %get-tuple-element.33), channel_id=1, source_target_pairs={{0,8},{4,12},{8,0},{12,4},{16,20},{20,16},{24,28},{28,24},{1,9},{5... | collective-permute-start | bytes 491528 | tf_op jit(solution)/shard_map/ppermute | solution.py:449
  15.2 0.5 %collective-permute-start.11 = (bf16[320,128]{1,0:T(8,128)(2,1)S(1)}, bf16[320,128]{1,0:T(8,128)(2,1)S(1)}, u32[]{:S(2)}, u32[]{:S(2)}) collective-permute-start(bf16[320,128]{1,0:T(8,128)(2,1)S(1)} %slice.37.yours), channel_id=1, source_target_pairs={{0,16},{16,0},{1,17},{17,1},{2,18},{18,2},{3,19},{19,3},{4,20},{20... | collective-permute-start | bytes 245768 | tf_op jit(solution)/shard_map/ppermute | solution.py:441
  15.7 0.8 %collective-permute-done.10.other_mine = bf16[320,128]{1,0:T(8,128)(2,1)S(1)} collective-permute-done((bf16[320,128]{1,0:T(8,128)(2,1)S(1)}, bf16[320,128]{1,0:T(8,128)(2,1)S(1)}, u32[]{:S(2)}, u32[]{:S(2)}) %collective-permute-start.10) | collective-permute-done | bytes 81952 | tf_op jit(solution)/shard_map/ppermute | solution.py:441
  16.6 0.7 %shard_map.70 = bf16[1280,128]{1,0:T(8,128)(2,1)S(1)} custom-call(bf16[320,128]{1,0:T(8,128)(2,1)S(1)} %fusion.3.mine, bf16[320,128]{1,0:T(8,128)(2,1)S(1)} %slice.37.yours, bf16[320,128]{1,0:T(8,128)(2,1)S(1)} %collective-permute-done.10.other_mine, bf16[320,128]{1,0:T(8,128)(2,1)S(1)} %collective-permute-done.11.other_yours, ...), custom_call_target="tpu_custom_call" | custom-call | tf_op jit(solution)/shard_map/pallas_call | solution.py:516
  17.4 2.2 %collective-permute-done.1 = bf16[640,128]{1,0:T(8,128)(2,1)S(1)} collective-permute-done((bf16[640,128]{1,0:T(8,128)(2,1)S(1)}, bf16[640,128]{1,0:T(8,128)(2,1)S(1)}, u32[]{:S(2)}, u32[]{:S(2)}) %collective-permute-start.1) | collective-permute-done | bytes 163872 | tf_op jit(solution)/shard_map/ppermute | solution.py:449
  19.6 2.1 %collective-permute-done.2 = bf16[640,128]{1,0:T(8,128)(2,1)S(1)} collective-permute-done((bf16[640,128]{1,0:T(8,128)(2,1)S(1)}, bf16[640,128]{1,0:T(8,128)(2,1)S(1)}, u32[]{:S(2)}, u32[]{:S(2)}) %collective-permute-start.2) | collective-permute-done | bytes 163872 | tf_op jit(solution)/shard_map/ppermute | solution.py:449
  21.8 1.4 %collective-permute-start.4 = (bf16[640,128]{1,0:T(8,128)(2,1)S(1)}, bf16[640,128]{1,0:T(8,128)(2,1)S(1)}, u32[]{:S(2)}, u32[]{:S(2)}) collective-permute-start(bf16[640,128]{1,0:T(8,128)(2,1)S(1)} %select_convert_fusion.own), channel_id=1, source_target_pairs={{0,4},{4,0},{8,12},{12,8},{16,24},{20,28},{24,16},{28,20},{1,5},{5... | collective-permute-start | bytes 491528 | tf_op jit(solution)/shard_map/ppermute | solution.py:449
  23.2 1.8 %collective-permute-start.5 = (bf16[640,128]{1,0:T(8,128)(2,1)S(1)}, bf16[640,128]{1,0:T(8,128)(2,1)S(1)}, u32[]{:S(2)}, u32[]{:S(2)}) collective-permute-start(bf16[640,128]{1,0:T(8,128)(2,1)S(1)} %select_convert_fusion.own), channel_id=1, source_target_pairs={{0,8},{4,12},{8,0},{12,4},{16,20},{20,16},{24,28},{28,24},{1,9},{5... | collective-permute-start | bytes 491528 | tf_op jit(solution)/shard_map/ppermute | solution.py:449
  24.9 0.7 %collective-permute-done.12 = bf16[1280,128]{1,0:T(8,128)(2,1)S(1)} collective-permute-done((bf16[1280,128]{1,0:T(8,128)(2,1)S(1)}, bf16[1280,128]{1,0:T(8,128)(2,1)S(1)}, u32[]{:S(2)}, u32[]{:S(2)}) %collective-permute-start.12) | collective-permute-done | bytes 327712 | tf_op jit(solution)/shard_map/ppermute | solution.py:449
  25.7 1.9 %collective-permute-start.13 = (bf16[1280,128]{1,0:T(8,128)(2,1)S(1)}, bf16[1280,128]{1,0:T(8,128)(2,1)S(1)}, u32[]{:S(2)}, u32[]{:S(2)}) collective-permute-start(bf16[1280,128]{1,0:T(8,128)(2,1)S(1)} %fusion), channel_id=1, source_target_pairs={{0,4},{4,0},{8,12},{12,8},{16,24},{20,28},{24,16},{28,20},{1,5},{5... | collective-permute-start | bytes 983048 | tf_op jit(solution)/shard_map/ppermute | solution.py:449
  27.6 1.1 %collective-permute-done.4.rows_x = bf16[640,128]{1,0:T(8,128)(2,1)S(1)} collective-permute-done((bf16[640,128]{1,0:T(8,128)(2,1)S(1)}, bf16[640,128]{1,0:T(8,128)(2,1)S(1)}, u32[]{:S(2)}, u32[]{:S(2)}) %collective-permute-start.4) | collective-permute-done | bytes 163872 | tf_op jit(solution)/shard_map/ppermute | solution.py:449
  28.7 0.7 %collective-permute-done.5.after.rows_y = bf16[640,128]{1,0:T(8,128)(2,1)S(1)} collective-permute-done((bf16[640,128]{1,0:T(8,128)(2,1)S(1)}, bf16[640,128]{1,0:T(8,128)(2,1)S(1)}, u32[]{:S(2)}, u32[]{:S(2)}) %collective-permute-start.5) | collective-permute-done | bytes 163872 | tf_op jit(solution)/shard_map/ppermute | solution.py:449
  29.4 1.6 %collective-permute-start.6 = (bf16[640,128]{1,0:T(8,128)(2,1)S(1)}, bf16[640,128]{1,0:T(8,128)(2,1)S(1)}, u32[]{:S(2)}, u32[]{:S(2)}) collective-permute-start(bf16[640,128]{1,0:T(8,128)(2,1)S(1)} %collective-permute-done.5.after.rows_y), channel_id=1, source_target_pairs={{0,4},{4,0},{8,12},{12,8},{16,24},{20,28},{24,16},{28,20},{1,5},{5... | collective-permute-start | bytes 491528 | tf_op jit(solution)/shard_map/ppermute | solution.py:449
  31.1 0.8 %shard_map.71.panel_rows = bf16[2560,640]{1,0:T(8,128)(2,1)S(1)} custom-call(s32[3]{0:T(128)S(1)} %copy-done.1, s32[2,12]{1,0:T(2,128)S(1)} %copy-done, bf16[1536,640]{1,0:T(8,128)(2,1)S(1)} %get-tuple-element.39.w_v, bf16[640,128]{1,0:T(8,128)(2,1)S(1)} %collective-permute-done.5.after.rows_y), custom_call_target="tpu_custom_call" | custom-call | flops 2000000000 | bytes 6553600 | tf_op jit(solution)/shard_map/pallas_call | solution.py:525
  31.9 1.0 %collective-permute-done.13 = bf16[1280,128]{1,0:T(8,128)(2,1)S(1)} collective-permute-done((bf16[1280,128]{1,0:T(8,128)(2,1)S(1)}, bf16[1280,128]{1,0:T(8,128)(2,1)S(1)}, u32[]{:S(2)}, u32[]{:S(2)}) %collective-permute-start.13) | collective-permute-done | bytes 327712 | tf_op jit(solution)/shard_map/ppermute | solution.py:449
  33.0 0.6 %shard_map.72 = (bf16[640,128]{1,0:T(8,128)(2,1)S(1)}, bf16[320,128]{1,0:T(8,128)(2,1)S(1)}) custom-call(bf16[1280,128]{1,0:T(8,128)(2,1)S(1)} %add_convert_fusion.y, bf16[1280,640]{1,0:T(8,128)(2,1)S(1)} %get-tuple-element.38.d_v), custom_call_target="tpu_custom_call" | custom-call | tf_op jit(solution)/shard_map/pallas_call | solution.py:538
  33.7 1.1 %collective-permute-done.6.rows_d = bf16[640,128]{1,0:T(8,128)(2,1)S(1)} collective-permute-done((bf16[640,128]{1,0:T(8,128)(2,1)S(1)}, bf16[640,128]{1,0:T(8,128)(2,1)S(1)}, u32[]{:S(2)}, u32[]{:S(2)}) %collective-permute-start.6) | collective-permute-done | bytes 163872 | tf_op jit(solution)/shard_map/ppermute | solution.py:449
  35.1 2.2 %collective-permute-start.15 = (bf16[640,128]{1,0:T(8,128)(2,1)S(1)}, bf16[640,128]{1,0:T(8,128)(2,1)S(1)}, u32[]{:S(2)}, u32[]{:S(2)}) collective-permute-start(bf16[640,128]{1,0:T(8,128)(2,1)S(1)} %pad_maximum_fusion.root_rows), channel_id=1, source_target_pairs={{0,8},{4,12},{8,0},{12,4},{16,20},{20,16},{24,28},{28,24},{1,9},{5... | collective-permute-start | bytes 491528 | tf_op jit(solution)/shard_map/ppermute | solution.py:449
  37.4 1.1 %collective-permute-start.17 = (bf16[320,128]{1,0:T(8,128)(2,1)S(1)}, bf16[320,128]{1,0:T(8,128)(2,1)S(1)}, u32[]{:S(2)}, u32[]{:S(2)}) collective-permute-start(bf16[320,128]{1,0:T(8,128)(2,1)S(1)} %get-tuple-element.48), channel_id=1, source_target_pairs={{0,12},{4,8},{8,4},{12,0},{16,28},{20,24},{24,20},{28,16},{1,13},{... | collective-permute-start | bytes 245768 | tf_op jit(solution)/shard_map/ppermute | solution.py:449
  38.5 1.6 %shard_map.73 = (f32[128,640]{1,0:T(8,128)S(1)}, bf16[960,128]{1,0:T(8,128)(2,1)}) custom-call(bf16[640,128]{1,0:T(8,128)(2,1)S(1)} %select_convert_fusion.own, bf16[640,128]{1,0:T(8,128)(2,1)S(1)} %collective-permute-done.4.rows_x, bf16[640,128]{1,0:T(8,128)(2,1)S(1)} %collective-permute-done.5.after.rows_y, ...), custom_call_target="tpu_custom_call" | custom-call | flops 419430400 | bytes 3276800 | tf_op jit(solution)/shard_map/pallas_call | solution.py:554
  40.0 1.9 %collective-permute-done.15.near = bf16[640,128]{1,0:T(8,128)(2,1)S(1)} collective-permute-done((bf16[640,128]{1,0:T(8,128)(2,1)S(1)}, bf16[640,128]{1,0:T(8,128)(2,1)S(1)}, u32[]{:S(2)}, u32[]{:S(2)}) %collective-permute-start.15) | collective-permute-done | bytes 163872 | tf_op jit(solution)/shard_map/ppermute | solution.py:449
  42.0 0.7 %collective-permute-done.17.far = bf16[320,128]{1,0:T(8,128)(2,1)S(1)} collective-permute-done((bf16[320,128]{1,0:T(8,128)(2,1)S(1)}, bf16[320,128]{1,0:T(8,128)(2,1)S(1)}, u32[]{:S(2)}, u32[]{:S(2)}) %collective-permute-start.17) | collective-permute-done | bytes 81952 | tf_op jit(solution)/shard_map/ppermute | solution.py:449
  42.7 0.5 %shard_map.74.total = f32[128,640]{1,0:T(8,128)S(1)} custom-call(bf16[640,128]{1,0:T(8,128)(2,1)S(1)} %collective-permute-done.15.near, bf16[320,128]{1,0:T(8,128)(2,1)S(1)} %collective-permute-done.17.far, f32[128,640]{1,0:T(8,128)S(1)} %get-tuple-element.46.total, bf16[2560,640]{1,0:T(8,128)(2,1)S(1)} %shard_map.71.panel_rows), custom_call_target="tpu_custom_call" | custom-call | tf_op jit(solution)/shard_map/pallas_call | solution.py:566
  43.2 0.8 %collective-permute-done.18.far = bf16[320,128]{1,0:T(8,128)(2,1)S(1)} collective-permute-done((bf16[320,128]{1,0:T(8,128)(2,1)S(1)}, bf16[320,128]{1,0:T(8,128)(2,1)S(1)}, u32[]{:S(2)}, u32[]{:S(2)}) %collective-permute-start.18) | collective-permute-done | bytes 81952 | tf_op jit(solution)/shard_map/ppermute | solution.py:441
  44.0 1.3 %shard_map.75 = bf16[960,128]{1,0:T(8,128)(2,1)} custom-call(bf16[640,128]{1,0:T(8,128)(2,1)S(1)} %collective-permute-done.16.near, bf16[320,128]{1,0:T(8,128)(2,1)S(1)} %collective-permute-done.18.far, f32[128,640]{1,0:T(8,128)S(1)} %shard_map.74.total, bf16[2560,640]{1,0:T(8,128)(2,1)S(1)} %shard_map.71.panel_rows, ...), custom_call_target="tpu_custom_call" | custom-call | flops 209715200 | bytes 1638400 | tf_op jit(solution)/shard_map/pallas_call | solution.py:575
  (28 shorter events, 1.6 us)
Async XLA Ops:
  3.4 1.5 %collective-permute-start = (bf16[640,128]{1,0:T(8,128)(2,1)S(1)}, bf16[640,128]{1,0:T(8,128)(2,1)S(1)}, u32[]{:S(2)}, u32[]{:S(2)}) collective-permute-start(bf16[640,128]{1,0:T(8,128)(2,1)S(1)} %get-tuple-element.29), channel_id=1, source_target_pairs={{0,16},{16,0},{1,17},{17,1},{2,18},{18,2},{3,19},{19,3},{4,20},{20... | collective-permute-start | bytes 491528 | tf_op jit(solution)/shard_map/ppermute | solution.py:441
  3.9 4.0 %collective-permute-start.8 = (bf16[640,128]{1,0:T(8,128)(2,1)S(1)}, bf16[640,128]{1,0:T(8,128)(2,1)S(1)}, u32[]{:S(2)}, u32[]{:S(2)}) collective-permute-start(bf16[640,128]{1,0:T(8,128)(2,1)S(1)} %get-tuple-element.36), channel_id=1, source_target_pairs={{0,16},{16,0},{1,17},{17,1},{2,18},{18,2},{3,19},{19,3},{4,20},{20... | collective-permute-start | bytes 491528 | tf_op jit(solution)/shard_map/ppermute | solution.py:441
  5.0 10.0 %collective-permute-start.7 = (bf16[640,128]{1,0:T(8,128)(2,1)S(1)}, bf16[640,128]{1,0:T(8,128)(2,1)S(1)}, u32[]{:S(2)}, u32[]{:S(2)}) collective-permute-start(bf16[640,128]{1,0:T(8,128)(2,1)S(1)} %add_convert_fusion.1.after), channel_id=1, source_target_pairs={{0,4},{4,0},{8,12},{12,8},{16,24},{20,28},{24,16},{28,20},{1,5},{5... | collective-permute-start | bytes 491528 | tf_op jit(solution)/shard_map/ppermute | solution.py:449
  8.0 7.1 %collective-permute-start.9 = (bf16[320,128]{1,0:T(8,128)(2,1)S(1)}, bf16[320,128]{1,0:T(8,128)(2,1)S(1)}, u32[]{:S(2)}, u32[]{:S(2)}) collective-permute-start(bf16[320,128]{1,0:T(8,128)(2,1)S(1)} %slice.59), channel_id=1, source_target_pairs={{0,12},{4,8},{8,4},{12,0},{16,28},{20,24},{24,20},{28,16},{1,13},{... | collective-permute-start | bytes 245768 | tf_op jit(solution)/shard_map/ppermute | solution.py:449
  11.5 19.6 %copy-start = (s32[2,12]{1,0:T(2,128)S(1)}, s32[2,12]{1,0:T(2,128)}, u32[]{:S(2)}) copy-start(s32[2,12]{1,0:T(2,128)} %pmap.3) | copy-start | bytes 292
  11.5 19.6 %copy-start.1 = (s32[3]{0:T(128)S(1)}, s32[3]{0:T(128)}, u32[]{:S(2)}) copy-start(s32[3]{0:T(128)} %live.3) | copy-start | bytes 40
  11.5 8.1 %collective-permute-start.1 = (bf16[640,128]{1,0:T(8,128)(2,1)S(1)}, bf16[640,128]{1,0:T(8,128)(2,1)S(1)}, u32[]{:S(2)}, u32[]{:S(2)}) collective-permute-start(bf16[640,128]{1,0:T(8,128)(2,1)S(1)} %get-tuple-element.31), channel_id=1, source_target_pairs={{0,12},{4,8},{8,4},{12,0},{16,28},{20,24},{24,20},{28,16},{1,13},{... | collective-permute-start | bytes 491528 | tf_op jit(solution)/shard_map/ppermute | solution.py:449
  13.0 8.7 %collective-permute-start.2 = (bf16[640,128]{1,0:T(8,128)(2,1)S(1)}, bf16[640,128]{1,0:T(8,128)(2,1)S(1)}, u32[]{:S(2)}, u32[]{:S(2)}) collective-permute-start(bf16[640,128]{1,0:T(8,128)(2,1)S(1)} %get-tuple-element.32), channel_id=1, source_target_pairs={{0,4},{4,0},{8,12},{12,8},{16,24},{20,28},{24,16},{28,20},{1,5},{5... | collective-permute-start | bytes 491528 | tf_op jit(solution)/shard_map/ppermute | solution.py:449
  13.1 8.6 %collective-permute-start.3 = (bf16[640,128]{1,0:T(8,128)(2,1)S(1)}, bf16[640,128]{1,0:T(8,128)(2,1)S(1)}, u32[]{:S(2)}, u32[]{:S(2)}) collective-permute-start(bf16[640,128]{1,0:T(8,128)(2,1)S(1)} %get-tuple-element.33), channel_id=1, source_target_pairs={{0,8},{4,12},{8,0},{12,4},{16,20},{20,16},{24,28},{28,24},{1,9},{5... | collective-permute-start | bytes 491528 | tf_op jit(solution)/shard_map/ppermute | solution.py:449
  15.1 1.3 %collective-permute-start.10 = (bf16[320,128]{1,0:T(8,128)(2,1)S(1)}, bf16[320,128]{1,0:T(8,128)(2,1)S(1)}, u32[]{:S(2)}, u32[]{:S(2)}) collective-permute-start(bf16[320,128]{1,0:T(8,128)(2,1)S(1)} %fusion.3.mine), channel_id=1, source_target_pairs={{0,16},{16,0},{1,17},{17,1},{2,18},{18,2},{3,19},{19,3},{4,20},{20... | collective-permute-start | bytes 245768 | tf_op jit(solution)/shard_map/ppermute | solution.py:441
  15.2 1.4 %collective-permute-start.11 = (bf16[320,128]{1,0:T(8,128)(2,1)S(1)}, bf16[320,128]{1,0:T(8,128)(2,1)S(1)}, u32[]{:S(2)}, u32[]{:S(2)}) collective-permute-start(bf16[320,128]{1,0:T(8,128)(2,1)S(1)} %slice.37.yours), channel_id=1, source_target_pairs={{0,16},{16,0},{1,17},{17,1},{2,18},{18,2},{3,19},{19,3},{4,20},{20... | collective-permute-start | bytes 245768 | tf_op jit(solution)/shard_map/ppermute | solution.py:441
  17.3 8.4 %collective-permute-start.12 = (bf16[1280,128]{1,0:T(8,128)(2,1)S(1)}, bf16[1280,128]{1,0:T(8,128)(2,1)S(1)}, u32[]{:S(2)}, u32[]{:S(2)}) collective-permute-start(bf16[1280,128]{1,0:T(8,128)(2,1)S(1)} %shard_map.70), channel_id=1, source_target_pairs={{0,8},{4,12},{8,0},{12,4},{16,20},{20,16},{24,28},{28,24},{1,9},{5... | collective-permute-start | bytes 983048 | tf_op jit(solution)/shard_map/ppermute | solution.py:449
  21.8 6.9 %collective-permute-start.4 = (bf16[640,128]{1,0:T(8,128)(2,1)S(1)}, bf16[640,128]{1,0:T(8,128)(2,1)S(1)}, u32[]{:S(2)}, u32[]{:S(2)}) collective-permute-start(bf16[640,128]{1,0:T(8,128)(2,1)S(1)} %select_convert_fusion.own), channel_id=1, source_target_pairs={{0,4},{4,0},{8,12},{12,8},{16,24},{20,28},{24,16},{28,20},{1,5},{5... | collective-permute-start | bytes 491528 | tf_op jit(solution)/shard_map/ppermute | solution.py:449
  23.2 6.2 %collective-permute-start.5 = (bf16[640,128]{1,0:T(8,128)(2,1)S(1)}, bf16[640,128]{1,0:T(8,128)(2,1)S(1)}, u32[]{:S(2)}, u32[]{:S(2)}) collective-permute-start(bf16[640,128]{1,0:T(8,128)(2,1)S(1)} %select_convert_fusion.own), channel_id=1, source_target_pairs={{0,8},{4,12},{8,0},{12,4},{16,20},{20,16},{24,28},{28,24},{1,9},{5... | collective-permute-start | bytes 491528 | tf_op jit(solution)/shard_map/ppermute | solution.py:449
  25.7 7.1 %collective-permute-start.13 = (bf16[1280,128]{1,0:T(8,128)(2,1)S(1)}, bf16[1280,128]{1,0:T(8,128)(2,1)S(1)}, u32[]{:S(2)}, u32[]{:S(2)}) collective-permute-start(bf16[1280,128]{1,0:T(8,128)(2,1)S(1)} %fusion), channel_id=1, source_target_pairs={{0,4},{4,0},{8,12},{12,8},{16,24},{20,28},{24,16},{28,20},{1,5},{5... | collective-permute-start | bytes 983048 | tf_op jit(solution)/shard_map/ppermute | solution.py:449
  29.4 5.3 %collective-permute-start.6 = (bf16[640,128]{1,0:T(8,128)(2,1)S(1)}, bf16[640,128]{1,0:T(8,128)(2,1)S(1)}, u32[]{:S(2)}, u32[]{:S(2)}) collective-permute-start(bf16[640,128]{1,0:T(8,128)(2,1)S(1)} %collective-permute-done.5.after.rows_y), channel_id=1, source_target_pairs={{0,4},{4,0},{8,12},{12,8},{16,24},{20,28},{24,16},{28,20},{1,5},{5... | collective-permute-start | bytes 491528 | tf_op jit(solution)/shard_map/ppermute | solution.py:449
  33.6 1.5 %collective-permute-start.14 = (bf16[640,128]{1,0:T(8,128)(2,1)S(1)}, bf16[640,128]{1,0:T(8,128)(2,1)S(1)}, u32[]{:S(2)}, u32[]{:S(2)}) collective-permute-start(bf16[640,128]{1,0:T(8,128)(2,1)S(1)} %get-tuple-element.42), channel_id=1, source_target_pairs={{0,16},{16,0},{1,17},{17,1},{2,18},{18,2},{3,19},{19,3},{4,20},{20... | collective-permute-start | bytes 491528 | tf_op jit(solution)/shard_map/ppermute | solution.py:441
  35.1 6.8 %collective-permute-start.15 = (bf16[640,128]{1,0:T(8,128)(2,1)S(1)}, bf16[640,128]{1,0:T(8,128)(2,1)S(1)}, u32[]{:S(2)}, u32[]{:S(2)}) collective-permute-start(bf16[640,128]{1,0:T(8,128)(2,1)S(1)} %pad_maximum_fusion.root_rows), channel_id=1, source_target_pairs={{0,8},{4,12},{8,0},{12,4},{16,20},{20,16},{24,28},{28,24},{1,9},{5... | collective-permute-start | bytes 491528 | tf_op jit(solution)/shard_map/ppermute | solution.py:449
  37.4 5.3 %collective-permute-start.17 = (bf16[320,128]{1,0:T(8,128)(2,1)S(1)}, bf16[320,128]{1,0:T(8,128)(2,1)S(1)}, u32[]{:S(2)}, u32[]{:S(2)}) collective-permute-start(bf16[320,128]{1,0:T(8,128)(2,1)S(1)} %get-tuple-element.48), channel_id=1, source_target_pairs={{0,12},{4,8},{8,4},{12,0},{16,28},{20,24},{24,20},{28,16},{1,13},{... | collective-permute-start | bytes 245768 | tf_op jit(solution)/shard_map/ppermute | solution.py:449
  42.0 2.0 %collective-permute-start.16 = (bf16[640,128]{1,0:T(8,128)(2,1)S(1)}, bf16[640,128]{1,0:T(8,128)(2,1)S(1)}, u32[]{:S(2)}, u32[]{:S(2)}) collective-permute-start(bf16[640,128]{1,0:T(8,128)(2,1)S(1)} %collective-permute-done.15.near), channel_id=1, source_target_pairs={{0,16},{16,0},{1,17},{17,1},{2,18},{18,2},{3,19},{19,3},{4,20},{20... | collective-permute-start | bytes 491528 | tf_op jit(solution)/shard_map/ppermute | solution.py:441
  42.7 1.3 %collective-permute-start.18 = (bf16[320,128]{1,0:T(8,128)(2,1)S(1)}, bf16[320,128]{1,0:T(8,128)(2,1)S(1)}, u32[]{:S(2)}, u32[]{:S(2)}) collective-permute-start(bf16[320,128]{1,0:T(8,128)(2,1)S(1)} %collective-permute-done.17.far), channel_id=1, source_target_pairs={{0,16},{16,0},{1,17},{17,1},{2,18},{18,2},{3,19},{19,3},{4,20},{20... | collective-permute-start | bytes 245768 | tf_op jit(solution)/shard_map/ppermute | solution.py:441

commit v11 on v9

--- a/solution.py
+++ b/solution.py
@@ -255,6 +255,7 @@
     send_rest,
     keep_near,
     keep_rest,
+    first,
     b_v,
     masked,
     mask,
@@ -277,8 +278,11 @@
     for i in range(parts):
         rows = pl.ds(i * step, step)
         gets.append(pltpu.make_async_copy(panel.at[rows], w_v.at[rows], sems.at[3 + i]))
-    get = pltpu.make_async_copy(pivot.at[pl.ds(0, 4 * quarter)], d_v, sems.at[3 + parts])
-    gets.append(get)
+    order = row_order(row_pos, leaf_pos)
+    for k in (1, 0, 2, 3):
+        rows = rows_at(order[k] * quarter, quarter)
+        get = pltpu.make_async_copy(pivot.at[rows], d_v.at[rows], sems.at[3 + parts + k])
+        gets.append(get)
     for get in gets:
         get.start()
     c_v[...] = jnp.zeros_like(c_v)
@@ -308,6 +312,9 @@
         rest[pl.ds(0, half)] = c_v[rows_at((row_pos ^ 3) * quarter + mine, half)]
         rest[pl.ds(half, half)] = c_v[rows_at(row_pos * quarter + mine, half)]
     gets[3 + parts].wait()
+    first[...] = mm(d_v[rows_at(order[1] * quarter, quarter)], right).astype(BF)
+    for get in gets[4 + parts :]:
+        get.wait()
 
 
 def leaf_pivot_kernel(sizes, masked, d_v, pivot, after, *outs_and_scratch):
@@ -317,9 +324,9 @@
     get.start()
     order = row_order(lax.axis_index("row"), lax.axis_index("leaf"))
     right = masked[...]
-    for k in (3, 1, 2, 0):
+    for k, out in zip((3, 2, 0), outs):
         product = mm(d_v[rows_at(order[k] * quarter, quarter)], right)
-        outs[k][...] = product.astype(BF)
+        out[...] = product.astype(BF)
     get.wait()
 
 
@@ -449,9 +456,21 @@
     smem = [pltpu.SMEM(live.shape, jnp.int32), pltpu.SMEM(parent_map.shape, jnp.int32)]
 
     parts = 4 if updates % (4 * B) == 0 else 1
-    send_near, send_rest, keep_near, keep_rest, b_v, masked, mask, w_v, d_v = call(
+    (
+        send_near,
+        send_rest,
+        keep_near,
+        keep_rest,
+        first,
+        b_v,
+        masked,
+        mask,
+        w_v,
+        d_v,
+    ) = call(
         functools.partial(panel_kernel, (quarter, half, parts, updates)),
         (
+            kept(quarter, columns),
             kept(quarter, columns),
             kept(quarter, columns),
             kept(quarter, columns),
@@ -463,7 +482,7 @@
             kept(front, quarter),
         ),
         [ANY] * 5,
-        [pltpu.VMEM((front, columns), BF), *smem, pltpu.SemaphoreType.DMA((4 + parts,))],
+        [pltpu.VMEM((front, columns), BF), *smem, pltpu.SemaphoreType.DMA((7 + parts,))],
         58_700_000,
         2 * updates * quarter * columns,
         2 * updates * quarter,
@@ -474,19 +493,20 @@
     from_far = row_swap(away_far, 2)
     from_near = row_swap(away_near, 0)
 
+    got_first = row_swap(first, 0)
     *pieces, root_d = call(
         functools.partial(leaf_pivot_kernel, (quarter, 4 * half)),
-        (*(kept(quarter, columns),) * 4, kept(4 * half, quarter)),
+        (*(kept(quarter, columns),) * 3, kept(4 * half, quarter)),
         [VMEM, VMEM, ANY, ANY],
         [pltpu.SemaphoreType.DMA],
         49_500_000,
         2 * front * quarter * columns,
         2 * front * quarter,
-    )(masked, d_v, pivot_inverse, away_near)
+    )(masked, d_v, pivot_inverse, after(got_first,(away_near,away_far)))
     from_near = after(from_near, pieces[0])
-    leaf_forward = pieces[0].astype(F32)
-    for phase in (2, 0, 1):
-        leaf_forward = leaf_forward + row_swap(pieces[1 + phase], phase).astype(F32)
+    leaf_forward = added(pieces[2], got_first)
+    leaf_forward = leaf_forward + row_swap(pieces[0], 2).astype(F32)
+    leaf_forward = leaf_forward + row_swap(pieces[1], 1).astype(F32)
     leaf_forward = jnp.where(mask > 0, leaf_forward, 0.0).astype(BF)
     rows_y = row_swap(leaf_forward, 1)
     rows_x = row_swap(leaf_forward, 0)

time: 45.1 us -> 46.7 us (1.035)
  waiting for transfers between devices: 14 us -> 16.1 us
  starting transfers between devices: 19.4 us -> 18.8 us
    ppermute x12, waiting for transfers between devices: 10.9 us -> 13.9 us  [row_swap(): return lax.ppermute(value, ('leaf', 'row'), route)]
    ppermute x7, waiting for transfers between devices: 3.11 us -> 2.17 us  [leaf_swap(): return lax.ppermute(value, 'leaf', [(0, 1), (1, 0)])]
    ppermute x12, starting transfers between devices: 18.2 us -> 17.6 us  [row_swap(): return lax.ppermute(value, ('leaf', 'row'), route)]
  transfers between devices with their start and end apart: 19 -> 19, of which waited for: 14 -> 14; matrix products, arithmetic and copies ran while one was open for 1% -> 1% of each run, Pallas kernels for 14% -> 13%
where the time goes in v11:
time: 46.7 us; the launch traced here: 46.6 us
  starting transfers between devices  18.8 us (40%)
  waiting for transfers between devices  16.1 us (34%)
  Pallas kernels  10.3 us (22%)
  between operations  0.77 us (2%)
  other arithmetic  0.54 us (1%)
    ppermute x12, starting transfers between devices, row_swap(): return lax.ppermute(value, ('leaf', 'row'), route)  17.6 us
    ppermute x12, waiting for transfers between devices, row_swap(): return lax.ppermute(value, ('leaf', 'row'), route)  13.9 us
    pallas_call x1, Pallas kernels, two_levels(): call(functools.partial(panel_kernel, (quarter, half, parts, updates)), (k...  3.12 us
    ppermute x7, waiting for transfers between devices, leaf_swap(): return lax.ppermute(value, 'leaf', [(0, 1), (1, 0)])  2.17 us
    pallas_call x1, Pallas kernels, two_levels(): call(functools.partial(leaf_pivot_kernel, (quarter, 4 * half)), (*(kept(q...  1.82 us
    pallas_call x1, Pallas kernels, two_levels(): call(functools.partial(leaf_transposed_kernel, (quarter, half)), (kept(co...  1.57 us
    pallas_call x1, Pallas kernels, two_levels(): call(functools.partial(last_kernel, (quarter, half)), stored(quarter + ha...  1.26 us
    ppermute x7, starting transfers between devices, leaf_swap(): return lax.ppermute(value, 'leaf', [(0, 1), (1, 0)])  1.24 us
  transfers between devices with their start and end apart: 19, of which 14 were waited for; matrix products, arithmetic and copies ran while one was open for 1% of the time, Pallas kernels for 13%

profile of v11, /device:TPU:0, one launch (start us, length us, event | category | flops | bytes accessed | tf_op | source)
XLA Modules:
  0.0 46.6 jit_solution(8607481936291322470)
XLA Ops:
  0.6 3.1 %shard_map.68 = (bf16[640,128]{1,0:T(8,128)(2,1)S(1)}, bf16[640,128]{1,0:T(8,128)(2,1)S(1)}, bf16[640,128]{1,0:T(8,128)(2,1)S(1)}, bf16[640,128]{1,0:T(8,128)(2,...) custom-call(s32[3]{0:T(128)} %live.3, ...), custom_call_target="tpu_custom_call" | custom-call | flops 251658240 | bytes 1966080 | tf_op jit(solution)/shard_map/pallas_call | solution.py:470
  3.8 0.5 %collective-permute-start.1 = (bf16[640,128]{1,0:T(8,128)(2,1)S(1)}, bf16[640,128]{1,0:T(8,128)(2,1)S(1)}, u32[]{:S(2)}, u32[]{:S(2)}) collective-permute-start(bf16[640,128]{1,0:T(8,128)(2,1)S(1)} %get-tuple-element.31), channel_id=1, source_target_pairs={{0,16},{16,0},{1,17},{17,1},{2,18},{18,2},{3,19},{19,3},{4,20},{20... | collective-permute-start | bytes 491528 | tf_op jit(solution)/shard_map/ppermute | solution.py:434
  4.4 2.9 %collective-permute-start = (bf16[640,128]{1,0:T(8,128)(2,1)S(1)}, bf16[640,128]{1,0:T(8,128)(2,1)S(1)}, u32[]{:S(2)}, u32[]{:S(2)}) collective-permute-start(bf16[640,128]{1,0:T(8,128)(2,1)S(1)} %get-tuple-element.29), channel_id=1, source_target_pairs={{0,4},{4,0},{8,12},{12,8},{16,24},{20,28},{24,16},{28,20},{1,5},{5... | collective-permute-start | bytes 491528 | tf_op jit(solution)/shard_map/ppermute | solution.py:442
  7.3 0.9 %collective-permute-start.8 = (bf16[640,128]{1,0:T(8,128)(2,1)S(1)}, bf16[640,128]{1,0:T(8,128)(2,1)S(1)}, u32[]{:S(2)}, u32[]{:S(2)}) collective-permute-start(bf16[640,128]{1,0:T(8,128)(2,1)S(1)} %add_convert_fusion.1), channel_id=1, source_target_pairs={{0,4},{4,0},{8,12},{12,8},{16,24},{20,28},{24,16},{28,20},{1,5},{5... | collective-permute-start | bytes 491528 | tf_op jit(solution)/shard_map/ppermute | solution.py:442
  8.3 2.2 %collective-permute-start.9 = (bf16[320,128]{1,0:T(8,128)(2,1)S(1)}, bf16[320,128]{1,0:T(8,128)(2,1)S(1)}, u32[]{:S(2)}, u32[]{:S(2)}) collective-permute-start(bf16[320,128]{1,0:T(8,128)(2,1)S(1)} %slice.59), channel_id=1, source_target_pairs={{0,12},{4,8},{8,4},{12,0},{16,28},{20,24},{24,20},{28,16},{1,13},{... | collective-permute-start | bytes 245768 | tf_op jit(solution)/shard_map/ppermute | solution.py:442
  10.6 1.8 %shard_map.69 = (bf16[640,128]{1,0:T(8,128)(2,1)S(1)}, bf16[640,128]{1,0:T(8,128)(2,1)S(1)}, bf16[640,128]{1,0:T(8,128)(2,1)S(1)}, bf16[1280,640]{1,0:T(8,128)(2,1)S(1)}) custom-call(bf16[640,128]{1,0:T(8,128)(2,1)S(1)} %get-tuple-element.27.masked, bf16[2560,640]{1,0:T(8,128)(2,1)S(1)} %get-tuple-element.28.d_v, bf16[3840,640]{1,0:T(8,128)(2,1)} %pivot.3, ...), custom_call_target="tpu_custom_call" | custom-call | flops 419430400 | bytes 3276800 | tf_op jit(solution)/shard_map/pallas_call | solution.py:497
  12.4 3.2 %collective-permute-start.3 = (bf16[640,128]{1,0:T(8,128)(2,1)S(1)}, bf16[640,128]{1,0:T(8,128)(2,1)S(1)}, u32[]{:S(2)}, u32[]{:S(2)}) collective-permute-start(bf16[640,128]{1,0:T(8,128)(2,1)S(1)} %get-tuple-element.36), channel_id=1, source_target_pairs={{0,12},{4,8},{8,4},{12,0},{16,28},{20,24},{24,20},{28,16},{1,13},{... | collective-permute-start | bytes 491528 | tf_op jit(solution)/shard_map/ppermute | solution.py:442
  16.1 0.5 %collective-permute-start.11 = (bf16[320,128]{1,0:T(8,128)(2,1)S(1)}, bf16[320,128]{1,0:T(8,128)(2,1)S(1)}, u32[]{:S(2)}, u32[]{:S(2)}) collective-permute-start(bf16[320,128]{1,0:T(8,128)(2,1)S(1)} %slice.37.yours), channel_id=1, source_target_pairs={{0,16},{16,0},{1,17},{17,1},{2,18},{18,2},{3,19},{19,3},{4,20},{20... | collective-permute-start | bytes 245768 | tf_op jit(solution)/shard_map/ppermute | solution.py:434
  16.6 0.8 %collective-permute-done.10.other_mine = bf16[320,128]{1,0:T(8,128)(2,1)S(1)} collective-permute-done((bf16[320,128]{1,0:T(8,128)(2,1)S(1)}, bf16[320,128]{1,0:T(8,128)(2,1)S(1)}, u32[]{:S(2)}, u32[]{:S(2)}) %collective-permute-start.10) | collective-permute-done | bytes 81952 | tf_op jit(solution)/shard_map/ppermute | solution.py:434
  17.5 0.7 %shard_map.70 = bf16[1280,128]{1,0:T(8,128)(2,1)S(1)} custom-call(bf16[320,128]{1,0:T(8,128)(2,1)S(1)} %fusion.3.mine, bf16[320,128]{1,0:T(8,128)(2,1)S(1)} %slice.37.yours, bf16[320,128]{1,0:T(8,128)(2,1)S(1)} %collective-permute-done.10.other_mine, bf16[320,128]{1,0:T(8,128)(2,1)S(1)} %collective-permute-done.11.other_yours, ...), custom_call_target="tpu_custom_call" | custom-call | tf_op jit(solution)/shard_map/pallas_call | solution.py:522
  18.2 1.8 %collective-permute-start.12 = (bf16[1280,128]{1,0:T(8,128)(2,1)S(1)}, bf16[1280,128]{1,0:T(8,128)(2,1)S(1)}, u32[]{:S(2)}, u32[]{:S(2)}) collective-permute-start(bf16[1280,128]{1,0:T(8,128)(2,1)S(1)} %shard_map.70), channel_id=1, source_target_pairs={{0,8},{4,12},{8,0},{12,4},{16,20},{20,16},{24,28},{28,24},{1,9},{5... | collective-permute-start | bytes 983048 | tf_op jit(solution)/shard_map/ppermute | solution.py:442
  20.0 0.8 %collective-permute-done.3 = bf16[640,128]{1,0:T(8,128)(2,1)S(1)} collective-permute-done((bf16[640,128]{1,0:T(8,128)(2,1)S(1)}, bf16[640,128]{1,0:T(8,128)(2,1)S(1)}, u32[]{:S(2)}, u32[]{:S(2)}) %collective-permute-start.3) | collective-permute-done | bytes 163872 | tf_op jit(solution)/shard_map/ppermute | solution.py:442
  20.8 1.0 %collective-permute-done.4 = bf16[640,128]{1,0:T(8,128)(2,1)S(1)} collective-permute-done((bf16[640,128]{1,0:T(8,128)(2,1)S(1)}, bf16[640,128]{1,0:T(8,128)(2,1)S(1)}, u32[]{:S(2)}, u32[]{:S(2)}) %collective-permute-start.4) | collective-permute-done | bytes 163872 | tf_op jit(solution)/shard_map/ppermute | solution.py:442
  21.9 1.2 %collective-permute-start.5 = (bf16[640,128]{1,0:T(8,128)(2,1)S(1)}, bf16[640,128]{1,0:T(8,128)(2,1)S(1)}, u32[]{:S(2)}, u32[]{:S(2)}) collective-permute-start(bf16[640,128]{1,0:T(8,128)(2,1)S(1)} %select_convert_fusion.own), channel_id=1, source_target_pairs={{0,4},{4,0},{8,12},{12,8},{16,24},{20,28},{24,16},{28,20},{1,5},{5... | collective-permute-start | bytes 491528 | tf_op jit(solution)/shard_map/ppermute | solution.py:442
  23.1 1.3 %collective-permute-start.6 = (bf16[640,128]{1,0:T(8,128)(2,1)S(1)}, bf16[640,128]{1,0:T(8,128)(2,1)S(1)}, u32[]{:S(2)}, u32[]{:S(2)}) collective-permute-start(bf16[640,128]{1,0:T(8,128)(2,1)S(1)} %select_convert_fusion.own), channel_id=1, source_target_pairs={{0,8},{4,12},{8,0},{12,4},{16,20},{20,16},{24,28},{28,24},{1,9},{5... | collective-permute-start | bytes 491528 | tf_op jit(solution)/shard_map/ppermute | solution.py:442
  24.4 2.5 %collective-permute-done.12 = bf16[1280,128]{1,0:T(8,128)(2,1)S(1)} collective-permute-done((bf16[1280,128]{1,0:T(8,128)(2,1)S(1)}, bf16[1280,128]{1,0:T(8,128)(2,1)S(1)}, u32[]{:S(2)}, u32[]{:S(2)}) %collective-permute-start.12) | collective-permute-done | bytes 327712 | tf_op jit(solution)/shard_map/ppermute | solution.py:442
  27.0 0.7 %collective-permute-start.13 = (bf16[1280,128]{1,0:T(8,128)(2,1)S(1)}, bf16[1280,128]{1,0:T(8,128)(2,1)S(1)}, u32[]{:S(2)}, u32[]{:S(2)}) collective-permute-start(bf16[1280,128]{1,0:T(8,128)(2,1)S(1)} %fusion), channel_id=1, source_target_pairs={{0,4},{4,0},{8,12},{12,8},{16,24},{20,28},{24,16},{28,20},{1,5},{5... | collective-permute-start | bytes 983048 | tf_op jit(solution)/shard_map/ppermute | solution.py:442
  27.7 0.5 %collective-permute-done.5.rows_x = bf16[640,128]{1,0:T(8,128)(2,1)S(1)} collective-permute-done((bf16[640,128]{1,0:T(8,128)(2,1)S(1)}, bf16[640,128]{1,0:T(8,128)(2,1)S(1)}, u32[]{:S(2)}, u32[]{:S(2)}) %collective-permute-start.5) | collective-permute-done | bytes 163872 | tf_op jit(solution)/shard_map/ppermute | solution.py:442
  28.2 1.8 %collective-permute-done.6.after.rows_y = bf16[640,128]{1,0:T(8,128)(2,1)S(1)} collective-permute-done((bf16[640,128]{1,0:T(8,128)(2,1)S(1)}, bf16[640,128]{1,0:T(8,128)(2,1)S(1)}, u32[]{:S(2)}, u32[]{:S(2)}) %collective-permute-start.6) | collective-permute-done | bytes 163872 | tf_op jit(solution)/shard_map/ppermute | solution.py:442
  30.1 0.8 %collective-permute-start.7 = (bf16[640,128]{1,0:T(8,128)(2,1)S(1)}, bf16[640,128]{1,0:T(8,128)(2,1)S(1)}, u32[]{:S(2)}, u32[]{:S(2)}) collective-permute-start(bf16[640,128]{1,0:T(8,128)(2,1)S(1)} %collective-permute-done.6.after.rows_y), channel_id=1, source_target_pairs={{0,4},{4,0},{8,12},{12,8},{16,24},{20,28},{24,16},{28,20},{1,5},{5... | collective-permute-start | bytes 491528 | tf_op jit(solution)/shard_map/ppermute | solution.py:442
  30.9 0.8 %shard_map.71.panel_rows = bf16[2560,640]{1,0:T(8,128)(2,1)S(1)} custom-call(s32[3]{0:T(128)S(1)} %copy-done.1, s32[2,12]{1,0:T(2,128)S(1)} %copy-done, bf16[1536,640]{1,0:T(8,128)(2,1)S(1)} %get-tuple-element.41.w_v, bf16[640,128]{1,0:T(8,128)(2,1)S(1)} %collective-permute-done.6.after.rows_y), custom_call_target="tpu_custom_call" | custom-call | flops 2000000000 | bytes 6553600 | tf_op jit(solution)/shard_map/pallas_call | solution.py:531
  31.7 2.4 %collective-permute-done.13 = bf16[1280,128]{1,0:T(8,128)(2,1)S(1)} collective-permute-done((bf16[1280,128]{1,0:T(8,128)(2,1)S(1)}, bf16[1280,128]{1,0:T(8,128)(2,1)S(1)}, u32[]{:S(2)}, u32[]{:S(2)}) %collective-permute-start.13) | collective-permute-done | bytes 327712 | tf_op jit(solution)/shard_map/ppermute | solution.py:442
  34.3 0.6 %shard_map.72 = (bf16[640,128]{1,0:T(8,128)(2,1)S(1)}, bf16[320,128]{1,0:T(8,128)(2,1)S(1)}) custom-call(bf16[1280,128]{1,0:T(8,128)(2,1)S(1)} %add_convert_fusion.y, bf16[1280,640]{1,0:T(8,128)(2,1)S(1)} %get-tuple-element.40.d_v), custom_call_target="tpu_custom_call" | custom-call | tf_op jit(solution)/shard_map/pallas_call | solution.py:544
  35.0 0.9 %collective-permute-done.7.rows_d = bf16[640,128]{1,0:T(8,128)(2,1)S(1)} collective-permute-done((bf16[640,128]{1,0:T(8,128)(2,1)S(1)}, bf16[640,128]{1,0:T(8,128)(2,1)S(1)}, u32[]{:S(2)}, u32[]{:S(2)}) %collective-permute-start.7) | collective-permute-done | bytes 163872 | tf_op jit(solution)/shard_map/ppermute | solution.py:442
  35.9 0.4 collective-permute-done.14
  36.4 1.9 %collective-permute-start.15 = (bf16[640,128]{1,0:T(8,128)(2,1)S(1)}, bf16[640,128]{1,0:T(8,128)(2,1)S(1)}, u32[]{:S(2)}, u32[]{:S(2)}) collective-permute-start(bf16[640,128]{1,0:T(8,128)(2,1)S(1)} %pad_maximum_fusion.root_rows), channel_id=1, source_target_pairs={{0,8},{4,12},{8,0},{12,4},{16,20},{20,16},{24,28},{28,24},{1,9},{5... | collective-permute-start | bytes 491528 | tf_op jit(solution)/shard_map/ppermute | solution.py:442
  38.6 1.6 %shard_map.73 = (f32[128,640]{1,0:T(8,128)S(1)}, bf16[960,128]{1,0:T(8,128)(2,1)}) custom-call(bf16[640,128]{1,0:T(8,128)(2,1)S(1)} %select_convert_fusion.own, bf16[640,128]{1,0:T(8,128)(2,1)S(1)} %collective-permute-done.5.rows_x, bf16[640,128]{1,0:T(8,128)(2,1)S(1)} %collective-permute-done.6.after.rows_y, ...), custom_call_target="tpu_custom_call" | custom-call | flops 419430400 | bytes 3276800 | tf_op jit(solution)/shard_map/pallas_call | solution.py:560
  40.2 2.8 %collective-permute-done.15.near = bf16[640,128]{1,0:T(8,128)(2,1)S(1)} collective-permute-done((bf16[640,128]{1,0:T(8,128)(2,1)S(1)}, bf16[640,128]{1,0:T(8,128)(2,1)S(1)}, u32[]{:S(2)}, u32[]{:S(2)}) %collective-permute-start.15) | collective-permute-done | bytes 163872 | tf_op jit(solution)/shard_map/ppermute | solution.py:442
  43.0 1.1 %collective-permute-done.17.far = bf16[320,128]{1,0:T(8,128)(2,1)S(1)} collective-permute-done((bf16[320,128]{1,0:T(8,128)(2,1)S(1)}, bf16[320,128]{1,0:T(8,128)(2,1)S(1)}, u32[]{:S(2)}, u32[]{:S(2)}) %collective-permute-start.17) | collective-permute-done | bytes 81952 | tf_op jit(solution)/shard_map/ppermute | solution.py:442
  44.0 0.5 shard_map.74.total
  44.5 0.8 %collective-permute-done.18.far = bf16[320,128]{1,0:T(8,128)(2,1)S(1)} collective-permute-done((bf16[320,128]{1,0:T(8,128)(2,1)S(1)}, bf16[320,128]{1,0:T(8,128)(2,1)S(1)}, u32[]{:S(2)}, u32[]{:S(2)}) %collective-permute-start.18) | collective-permute-done | bytes 81952 | tf_op jit(solution)/shard_map/ppermute | solution.py:434
  45.3 1.3 %shard_map.75 = bf16[960,128]{1,0:T(8,128)(2,1)} custom-call(bf16[640,128]{1,0:T(8,128)(2,1)S(1)} %collective-permute-done.16.near, bf16[320,128]{1,0:T(8,128)(2,1)S(1)} %collective-permute-done.18.far, f32[128,640]{1,0:T(8,128)S(1)} %shard_map.74.total, bf16[2560,640]{1,0:T(8,128)(2,1)S(1)} %shard_map.71.panel_rows, ...), custom_call_target="tpu_custom_call" | custom-call | flops 209715200 | bytes 1638400 | tf_op jit(solution)/shard_map/pallas_call | solution.py:581
  (28 shorter events, 1.6 us)
Async XLA Ops:
  3.8 3.5 %collective-permute-start.1 = (bf16[640,128]{1,0:T(8,128)(2,1)S(1)}, bf16[640,128]{1,0:T(8,128)(2,1)S(1)}, u32[]{:S(2)}, u32[]{:S(2)}) collective-permute-start(bf16[640,128]{1,0:T(8,128)(2,1)S(1)} %get-tuple-element.31), channel_id=1, source_target_pairs={{0,16},{16,0},{1,17},{17,1},{2,18},{18,2},{3,19},{19,3},{4,20},{20... | collective-permute-start | bytes 491528 | tf_op jit(solution)/shard_map/ppermute | solution.py:434
  4.3 4.0 %collective-permute-start.2 = (bf16[640,128]{1,0:T(8,128)(2,1)S(1)}, bf16[640,128]{1,0:T(8,128)(2,1)S(1)}, u32[]{:S(2)}, u32[]{:S(2)}) collective-permute-start(bf16[640,128]{1,0:T(8,128)(2,1)S(1)} %get-tuple-element.33), channel_id=1, source_target_pairs={{0,16},{16,0},{1,17},{17,1},{2,18},{18,2},{3,19},{19,3},{4,20},{20... | collective-permute-start | bytes 491528 | tf_op jit(solution)/shard_map/ppermute | solution.py:434
  4.4 6.2 %collective-permute-start = (bf16[640,128]{1,0:T(8,128)(2,1)S(1)}, bf16[640,128]{1,0:T(8,128)(2,1)S(1)}, u32[]{:S(2)}, u32[]{:S(2)}) collective-permute-start(bf16[640,128]{1,0:T(8,128)(2,1)S(1)} %get-tuple-element.29), channel_id=1, source_target_pairs={{0,4},{4,0},{8,12},{12,8},{16,24},{20,28},{24,16},{28,20},{1,5},{5... | collective-permute-start | bytes 491528 | tf_op jit(solution)/shard_map/ppermute | solution.py:442
  7.3 8.6 %collective-permute-start.8 = (bf16[640,128]{1,0:T(8,128)(2,1)S(1)}, bf16[640,128]{1,0:T(8,128)(2,1)S(1)}, u32[]{:S(2)}, u32[]{:S(2)}) collective-permute-start(bf16[640,128]{1,0:T(8,128)(2,1)S(1)} %add_convert_fusion.1), channel_id=1, source_target_pairs={{0,4},{4,0},{8,12},{12,8},{16,24},{20,28},{24,16},{28,20},{1,5},{5... | collective-permute-start | bytes 491528 | tf_op jit(solution)/shard_map/ppermute | solution.py:442
  8.3 7.6 %collective-permute-start.9 = (bf16[320,128]{1,0:T(8,128)(2,1)S(1)}, bf16[320,128]{1,0:T(8,128)(2,1)S(1)}, u32[]{:S(2)}, u32[]{:S(2)}) collective-permute-start(bf16[320,128]{1,0:T(8,128)(2,1)S(1)} %slice.59), channel_id=1, source_target_pairs={{0,12},{4,8},{8,4},{12,0},{16,28},{20,24},{24,20},{28,16},{1,13},{... | collective-permute-start | bytes 245768 | tf_op jit(solution)/shard_map/ppermute | solution.py:442
  12.4 18.5 %copy-start = (s32[2,12]{1,0:T(2,128)S(1)}, s32[2,12]{1,0:T(2,128)}, u32[]{:S(2)}) copy-start(s32[2,12]{1,0:T(2,128)} %pmap.3) | copy-start | bytes 292
  12.4 18.5 %copy-start.1 = (s32[3]{0:T(128)S(1)}, s32[3]{0:T(128)}, u32[]{:S(2)}) copy-start(s32[3]{0:T(128)} %live.3) | copy-start | bytes 40
  12.4 8.4 %collective-permute-start.3 = (bf16[640,128]{1,0:T(8,128)(2,1)S(1)}, bf16[640,128]{1,0:T(8,128)(2,1)S(1)}, u32[]{:S(2)}, u32[]{:S(2)}) collective-permute-start(bf16[640,128]{1,0:T(8,128)(2,1)S(1)} %get-tuple-element.36), channel_id=1, source_target_pairs={{0,12},{4,8},{8,4},{12,0},{16,28},{20,24},{24,20},{28,16},{1,13},{... | collective-permute-start | bytes 491528 | tf_op jit(solution)/shard_map/ppermute | solution.py:442
  15.7 6.1 %collective-permute-start.4 = (bf16[640,128]{1,0:T(8,128)(2,1)S(1)}, bf16[640,128]{1,0:T(8,128)(2,1)S(1)}, u32[]{:S(2)}, u32[]{:S(2)}) collective-permute-start(bf16[640,128]{1,0:T(8,128)(2,1)S(1)} %get-tuple-element.37), channel_id=1, source_target_pairs={{0,8},{4,12},{8,0},{12,4},{16,20},{20,16},{24,28},{28,24},{1,9},{5... | collective-permute-start | bytes 491528 | tf_op jit(solution)/shard_map/ppermute | solution.py:442
  16.0 1.3 %collective-permute-start.10 = (bf16[320,128]{1,0:T(8,128)(2,1)S(1)}, bf16[320,128]{1,0:T(8,128)(2,1)S(1)}, u32[]{:S(2)}, u32[]{:S(2)}) collective-permute-start(bf16[320,128]{1,0:T(8,128)(2,1)S(1)} %fusion.3.mine), channel_id=1, source_target_pairs={{0,16},{16,0},{1,17},{17,1},{2,18},{18,2},{3,19},{19,3},{4,20},{20... | collective-permute-start | bytes 245768 | tf_op jit(solution)/shard_map/ppermute | solution.py:434
  16.1 1.4 %collective-permute-start.11 = (bf16[320,128]{1,0:T(8,128)(2,1)S(1)}, bf16[320,128]{1,0:T(8,128)(2,1)S(1)}, u32[]{:S(2)}, u32[]{:S(2)}) collective-permute-start(bf16[320,128]{1,0:T(8,128)(2,1)S(1)} %slice.37.yours), channel_id=1, source_target_pairs={{0,16},{16,0},{1,17},{17,1},{2,18},{18,2},{3,19},{19,3},{4,20},{20... | collective-permute-start | bytes 245768 | tf_op jit(solution)/shard_map/ppermute | solution.py:434
  18.2 8.7 %collective-permute-start.12 = (bf16[1280,128]{1,0:T(8,128)(2,1)S(1)}, bf16[1280,128]{1,0:T(8,128)(2,1)S(1)}, u32[]{:S(2)}, u32[]{:S(2)}) collective-permute-start(bf16[1280,128]{1,0:T(8,128)(2,1)S(1)} %shard_map.70), channel_id=1, source_target_pairs={{0,8},{4,12},{8,0},{12,4},{16,20},{20,16},{24,28},{28,24},{1,9},{5... | collective-permute-start | bytes 983048 | tf_op jit(solution)/shard_map/ppermute | solution.py:442
  21.9 6.3 %collective-permute-start.5 = (bf16[640,128]{1,0:T(8,128)(2,1)S(1)}, bf16[640,128]{1,0:T(8,128)(2,1)S(1)}, u32[]{:S(2)}, u32[]{:S(2)}) collective-permute-start(bf16[640,128]{1,0:T(8,128)(2,1)S(1)} %select_convert_fusion.own), channel_id=1, source_target_pairs={{0,4},{4,0},{8,12},{12,8},{16,24},{20,28},{24,16},{28,20},{1,5},{5... | collective-permute-start | bytes 491528 | tf_op jit(solution)/shard_map/ppermute | solution.py:442
  23.1 7.0 %collective-permute-start.6 = (bf16[640,128]{1,0:T(8,128)(2,1)S(1)}, bf16[640,128]{1,0:T(8,128)(2,1)S(1)}, u32[]{:S(2)}, u32[]{:S(2)}) collective-permute-start(bf16[640,128]{1,0:T(8,128)(2,1)S(1)} %select_convert_fusion.own), channel_id=1, source_target_pairs={{0,8},{4,12},{8,0},{12,4},{16,20},{20,16},{24,28},{28,24},{1,9},{5... | collective-permute-start | bytes 491528 | tf_op jit(solution)/shard_map/ppermute | solution.py:442
  27.0 7.1 %collective-permute-start.13 = (bf16[1280,128]{1,0:T(8,128)(2,1)S(1)}, bf16[1280,128]{1,0:T(8,128)(2,1)S(1)}, u32[]{:S(2)}, u32[]{:S(2)}) collective-permute-start(bf16[1280,128]{1,0:T(8,128)(2,1)S(1)} %fusion), channel_id=1, source_target_pairs={{0,4},{4,0},{8,12},{12,8},{16,24},{20,28},{24,16},{28,20},{1,5},{5... | collective-permute-start | bytes 983048 | tf_op jit(solution)/shard_map/ppermute | solution.py:442
  30.1 5.8 %collective-permute-start.7 = (bf16[640,128]{1,0:T(8,128)(2,1)S(1)}, bf16[640,128]{1,0:T(8,128)(2,1)S(1)}, u32[]{:S(2)}, u32[]{:S(2)}) collective-permute-start(bf16[640,128]{1,0:T(8,128)(2,1)S(1)} %collective-permute-done.6.after.rows_y), channel_id=1, source_target_pairs={{0,4},{4,0},{8,12},{12,8},{16,24},{20,28},{24,16},{28,20},{1,5},{5... | collective-permute-start | bytes 491528 | tf_op jit(solution)/shard_map/ppermute | solution.py:442
  34.9 1.5 %collective-permute-start.14 = (bf16[640,128]{1,0:T(8,128)(2,1)S(1)}, bf16[640,128]{1,0:T(8,128)(2,1)S(1)}, u32[]{:S(2)}, u32[]{:S(2)}) collective-permute-start(bf16[640,128]{1,0:T(8,128)(2,1)S(1)} %get-tuple-element.44), channel_id=1, source_target_pairs={{0,16},{16,0},{1,17},{17,1},{2,18},{18,2},{3,19},{19,3},{4,20},{20... | collective-permute-start | bytes 491528 | tf_op jit(solution)/shard_map/ppermute | solution.py:434
  36.4 6.5 %collective-permute-start.15 = (bf16[640,128]{1,0:T(8,128)(2,1)S(1)}, bf16[640,128]{1,0:T(8,128)(2,1)S(1)}, u32[]{:S(2)}, u32[]{:S(2)}) collective-permute-start(bf16[640,128]{1,0:T(8,128)(2,1)S(1)} %pad_maximum_fusion.root_rows), channel_id=1, source_target_pairs={{0,8},{4,12},{8,0},{12,4},{16,20},{20,16},{24,28},{28,24},{1,9},{5... | collective-permute-start | bytes 491528 | tf_op jit(solution)/shard_map/ppermute | solution.py:442
  38.4 5.7 %collective-permute-start.17 = (bf16[320,128]{1,0:T(8,128)(2,1)S(1)}, bf16[320,128]{1,0:T(8,128)(2,1)S(1)}, u32[]{:S(2)}, u32[]{:S(2)}) collective-permute-start(bf16[320,128]{1,0:T(8,128)(2,1)S(1)} %get-tuple-element.50), channel_id=1, source_target_pairs={{0,12},{4,8},{8,4},{12,0},{16,28},{20,24},{24,20},{28,16},{1,13},{... | collective-permute-start | bytes 245768 | tf_op jit(solution)/shard_map/ppermute | solution.py:442
  42.9 2.4 %collective-permute-start.16 = (bf16[640,128]{1,0:T(8,128)(2,1)S(1)}, bf16[640,128]{1,0:T(8,128)(2,1)S(1)}, u32[]{:S(2)}, u32[]{:S(2)}) collective-permute-start(bf16[640,128]{1,0:T(8,128)(2,1)S(1)} %collective-permute-done.15.near), channel_id=1, source_target_pairs={{0,16},{16,0},{1,17},{17,1},{2,18},{18,2},{3,19},{19,3},{4,20},{20... | collective-permute-start | bytes 491528 | tf_op jit(solution)/shard_map/ppermute | solution.py:434
  44.0 1.3 %collective-permute-start.18 = (bf16[320,128]{1,0:T(8,128)(2,1)S(1)}, bf16[320,128]{1,0:T(8,128)(2,1)S(1)}, u32[]{:S(2)}, u32[]{:S(2)}) collective-permute-start(bf16[320,128]{1,0:T(8,128)(2,1)S(1)} %collective-permute-done.17.far), channel_id=1, source_target_pairs={{0,16},{16,0},{1,17},{17,1},{2,18},{18,2},{3,19},{19,3},{4,20},{20... | collective-permute-start | bytes 245768 | tf_op jit(solution)/shard_map/ppermute | solution.py:434

commit v12 on v11

--- a/solution.py
+++ b/solution.py
@@ -502,11 +502,12 @@
         49_500_000,
         2 * front * quarter * columns,
         2 * front * quarter,
-    )(masked, d_v, pivot_inverse, after(got_first,(away_near,away_far)))
+    )(masked, d_v, pivot_inverse, after(away_near,away_far))
     from_near = after(from_near, pieces[0])
     leaf_forward = added(pieces[2], got_first)
     leaf_forward = leaf_forward + row_swap(pieces[0], 2).astype(F32)
-    leaf_forward = leaf_forward + row_swap(pieces[1], 1).astype(F32)
+    second = row_swap(after(pieces[1], got_first), 1)
+    leaf_forward = leaf_forward + second.astype(F32)
     leaf_forward = jnp.where(mask > 0, leaf_forward, 0.0).astype(BF)
     rows_y = row_swap(leaf_forward, 1)
     rows_x = row_swap(leaf_forward, 0)

time: 46.7 us -> 47.2 us (1.011)
  starting transfers between devices: 18.8 us -> 21.5 us
  waiting for transfers between devices: 16.1 us -> 14 us
    ppermute x12, starting transfers between devices: 17.6 us -> 19.7 us  [row_swap(): return lax.ppermute(value, ('leaf', 'row'), route)]
    ppermute x12, waiting for transfers between devices: 13.9 us -> 12.1 us  [row_swap(): return lax.ppermute(value, ('leaf', 'row'), route)]
    ppermute x7, starting transfers between devices: 1.24 us -> 1.75 us  [leaf_swap(): return lax.ppermute(value, 'leaf', [(0, 1), (1, 0)])]
  transfers between devices with their start and end apart: 19 -> 19, of which waited for: 14 -> 10; matrix products, arithmetic and copies ran while one was open for 1% -> 1% of each run, Pallas kernels for 13% -> 13%
where the time goes in v12:
time: 47.2 us; the launch traced here: 47.1 us
  starting transfers between devices  21.5 us (46%)
  waiting for transfers between devices  14 us (30%)
  Pallas kernels  10.3 us (22%)
  between operations  0.78 us (2%)
  other arithmetic  0.54 us (1%)
    ppermute x12, starting transfers between devices, row_swap(): return lax.ppermute(value, ('leaf', 'row'), route)  19.7 us
    ppermute x12, waiting for transfers between devices, row_swap(): return lax.ppermute(value, ('leaf', 'row'), route)  12.1 us
    pallas_call x1, Pallas kernels, two_levels(): call(functools.partial(panel_kernel, (quarter, half, parts, updates)), (k...  3.12 us
    ppermute x7, waiting for transfers between devices, leaf_swap(): return lax.ppermute(value, 'leaf', [(0, 1), (1, 0)])  1.89 us
    pallas_call x1, Pallas kernels, two_levels(): call(functools.partial(leaf_pivot_kernel, (quarter, 4 * half)), (*(kept(q...  1.82 us
    ppermute x7, starting transfers between devices, leaf_swap(): return lax.ppermute(value, 'leaf', [(0, 1), (1, 0)])  1.75 us
    pallas_call x1, Pallas kernels, two_levels(): call(functools.partial(leaf_transposed_kernel, (quarter, half)), (kept(co...  1.57 us
    pallas_call x1, Pallas kernels, two_levels(): call(functools.partial(last_kernel, (quarter, half)), stored(quarter + ha...  1.26 us
  transfers between devices with their start and end apart: 19, of which 10 were waited for; matrix products, arithmetic and copies ran while one was open for 1% of the time, Pallas kernels for 13%

profile of v12, /device:TPU:0, one launch (start us, length us, event | category | flops | bytes accessed | tf_op | source)
XLA Modules:
  0.0 47.1 jit_solution(14550202331996049841)
XLA Ops:
  0.6 3.1 %shard_map.68 = (bf16[640,128]{1,0:T(8,128)(2,1)S(1)}, bf16[640,128]{1,0:T(8,128)(2,1)S(1)}, bf16[640,128]{1,0:T(8,128)(2,1)S(1)}, bf16[640,128]{1,0:T(8,128)(2,...) custom-call(s32[3]{0:T(128)} %live.3, ...), custom_call_target="tpu_custom_call" | custom-call | flops 251658240 | bytes 1966080 | tf_op jit(solution)/shard_map/pallas_call | solution.py:470
  3.8 0.5 %collective-permute-start = (bf16[640,128]{1,0:T(8,128)(2,1)S(1)}, bf16[640,128]{1,0:T(8,128)(2,1)S(1)}, u32[]{:S(2)}, u32[]{:S(2)}) collective-permute-start(bf16[640,128]{1,0:T(8,128)(2,1)S(1)} %get-tuple-element.31), channel_id=1, source_target_pairs={{0,16},{16,0},{1,17},{17,1},{2,18},{18,2},{3,19},{19,3},{4,20},{20... | collective-permute-start | bytes 491528 | tf_op jit(solution)/shard_map/ppermute | solution.py:434
  4.4 2.9 %collective-permute-start.2 = (bf16[640,128]{1,0:T(8,128)(2,1)S(1)}, bf16[640,128]{1,0:T(8,128)(2,1)S(1)}, u32[]{:S(2)}, u32[]{:S(2)}) collective-permute-start(bf16[640,128]{1,0:T(8,128)(2,1)S(1)} %get-tuple-element.36), channel_id=1, source_target_pairs={{0,4},{4,0},{8,12},{12,8},{16,24},{20,28},{24,16},{28,20},{1,5},{5... | collective-permute-start | bytes 491528 | tf_op jit(solution)/shard_map/ppermute | solution.py:442
  7.3 0.9 %collective-permute-start.8 = (bf16[640,128]{1,0:T(8,128)(2,1)S(1)}, bf16[640,128]{1,0:T(8,128)(2,1)S(1)}, u32[]{:S(2)}, u32[]{:S(2)}) collective-permute-start(bf16[640,128]{1,0:T(8,128)(2,1)S(1)} %add_convert_fusion.1.after), channel_id=1, source_target_pairs={{0,4},{4,0},{8,12},{12,8},{16,24},{20,28},{24,16},{28,20},{1,5},{5... | collective-permute-start | bytes 491528 | tf_op jit(solution)/shard_map/ppermute | solution.py:442
  8.3 2.2 %collective-permute-start.9 = (bf16[320,128]{1,0:T(8,128)(2,1)S(1)}, bf16[320,128]{1,0:T(8,128)(2,1)S(1)}, u32[]{:S(2)}, u32[]{:S(2)}) collective-permute-start(bf16[320,128]{1,0:T(8,128)(2,1)S(1)} %slice.59), channel_id=1, source_target_pairs={{0,12},{4,8},{8,4},{12,0},{16,28},{20,24},{24,20},{28,16},{1,13},{... | collective-permute-start | bytes 245768 | tf_op jit(solution)/shard_map/ppermute | solution.py:442
  10.5 1.8 %shard_map.69 = (bf16[640,128]{1,0:T(8,128)(2,1)S(1)}, bf16[640,128]{1,0:T(8,128)(2,1)S(1)}, bf16[640,128]{1,0:T(8,128)(2,1)S(1)}, bf16[1280,640]{1,0:T(8,128)(2,1)S(1)}) custom-call(bf16[640,128]{1,0:T(8,128)(2,1)S(1)} %get-tuple-element.28.masked, bf16[2560,640]{1,0:T(8,128)(2,1)S(1)} %get-tuple-element.29.d_v, bf16[3840,640]{1,0:T(8,128)(2,1)} %pivot.3, ...), custom_call_target="tpu_custom_call" | custom-call | flops 419430400 | bytes 3276800 | tf_op jit(solution)/shard_map/pallas_call | solution.py:497
  12.4 0.6 %collective-permute-start.4 = (bf16[640,128]{1,0:T(8,128)(2,1)S(1)}, bf16[640,128]{1,0:T(8,128)(2,1)S(1)}, u32[]{:S(2)}, u32[]{:S(2)}) collective-permute-start(bf16[640,128]{1,0:T(8,128)(2,1)S(1)} %get-tuple-element.39), channel_id=1, source_target_pairs={{0,8},{4,12},{8,0},{12,4},{16,20},{20,16},{24,28},{28,24},{1,9},{5... | collective-permute-start | bytes 491528 | tf_op jit(solution)/shard_map/ppermute | solution.py:442
  12.9 1.8 %collective-permute-start.3 = (bf16[640,128]{1,0:T(8,128)(2,1)S(1)}, bf16[640,128]{1,0:T(8,128)(2,1)S(1)}, u32[]{:S(2)}, u32[]{:S(2)}) collective-permute-start(bf16[640,128]{1,0:T(8,128)(2,1)S(1)} %get-tuple-element.37), channel_id=1, source_target_pairs={{0,12},{4,8},{8,4},{12,0},{16,28},{20,24},{24,20},{28,16},{1,13},{... | collective-permute-start | bytes 491528 | tf_op jit(solution)/shard_map/ppermute | solution.py:442
  14.8 1.4 %collective-permute-done.9 = bf16[320,128]{1,0:T(8,128)(2,1)S(1)} collective-permute-done((bf16[320,128]{1,0:T(8,128)(2,1)S(1)}, bf16[320,128]{1,0:T(8,128)(2,1)S(1)}, u32[]{:S(2)}, u32[]{:S(2)}) %collective-permute-start.9) | collective-permute-done | bytes 81952 | tf_op jit(solution)/shard_map/ppermute | solution.py:442
  16.3 0.5 %collective-permute-start.11 = (bf16[320,128]{1,0:T(8,128)(2,1)S(1)}, bf16[320,128]{1,0:T(8,128)(2,1)S(1)}, u32[]{:S(2)}, u32[]{:S(2)}) collective-permute-start(bf16[320,128]{1,0:T(8,128)(2,1)S(1)} %slice.37.yours), channel_id=1, source_target_pairs={{0,16},{16,0},{1,17},{17,1},{2,18},{18,2},{3,19},{19,3},{4,20},{20... | collective-permute-start | bytes 245768 | tf_op jit(solution)/shard_map/ppermute | solution.py:434
  16.8 0.8 %collective-permute-done.10.other_mine = bf16[320,128]{1,0:T(8,128)(2,1)S(1)} collective-permute-done((bf16[320,128]{1,0:T(8,128)(2,1)S(1)}, bf16[320,128]{1,0:T(8,128)(2,1)S(1)}, u32[]{:S(2)}, u32[]{:S(2)}) %collective-permute-start.10) | collective-permute-done | bytes 81952 | tf_op jit(solution)/shard_map/ppermute | solution.py:434
  17.7 0.7 %shard_map.70 = bf16[1280,128]{1,0:T(8,128)(2,1)S(1)} custom-call(bf16[320,128]{1,0:T(8,128)(2,1)S(1)} %fusion.3.mine, bf16[320,128]{1,0:T(8,128)(2,1)S(1)} %slice.37.yours, bf16[320,128]{1,0:T(8,128)(2,1)S(1)} %collective-permute-done.10.other_mine, bf16[320,128]{1,0:T(8,128)(2,1)S(1)} %collective-permute-done.11.other_yours, ...), custom_call_target="tpu_custom_call" | custom-call | tf_op jit(solution)/shard_map/pallas_call | solution.py:523
  18.4 0.6 %collective-permute-start.12 = (bf16[1280,128]{1,0:T(8,128)(2,1)S(1)}, bf16[1280,128]{1,0:T(8,128)(2,1)S(1)}, u32[]{:S(2)}, u32[]{:S(2)}) collective-permute-start(bf16[1280,128]{1,0:T(8,128)(2,1)S(1)} %shard_map.70), channel_id=1, source_target_pairs={{0,8},{4,12},{8,0},{12,4},{16,20},{20,16},{24,28},{28,24},{1,9},{5... | collective-permute-start | bytes 983048 | tf_op jit(solution)/shard_map/ppermute | solution.py:442
  18.9 2.4 %collective-permute-done.4 = bf16[640,128]{1,0:T(8,128)(2,1)S(1)} collective-permute-done((bf16[640,128]{1,0:T(8,128)(2,1)S(1)}, bf16[640,128]{1,0:T(8,128)(2,1)S(1)}, u32[]{:S(2)}, u32[]{:S(2)}) %collective-permute-start.4) | collective-permute-done | bytes 163872 | tf_op jit(solution)/shard_map/ppermute | solution.py:442
  21.5 1.7 %collective-permute-start.5 = (bf16[640,128]{1,0:T(8,128)(2,1)S(1)}, bf16[640,128]{1,0:T(8,128)(2,1)S(1)}, u32[]{:S(2)}, u32[]{:S(2)}) collective-permute-start(bf16[640,128]{1,0:T(8,128)(2,1)S(1)} %select_convert_fusion.own), channel_id=1, source_target_pairs={{0,4},{4,0},{8,12},{12,8},{16,24},{20,28},{24,16},{28,20},{1,5},{5... | collective-permute-start | bytes 491528 | tf_op jit(solution)/shard_map/ppermute | solution.py:442
  23.2 0.6 %collective-permute-start.6 = (bf16[640,128]{1,0:T(8,128)(2,1)S(1)}, bf16[640,128]{1,0:T(8,128)(2,1)S(1)}, u32[]{:S(2)}, u32[]{:S(2)}) collective-permute-start(bf16[640,128]{1,0:T(8,128)(2,1)S(1)} %select_convert_fusion.own), channel_id=1, source_target_pairs={{0,8},{4,12},{8,0},{12,4},{16,20},{20,16},{24,28},{28,24},{1,9},{5... | collective-permute-start | bytes 491528 | tf_op jit(solution)/shard_map/ppermute | solution.py:442
  23.8 3.4 %collective-permute-done.12 = bf16[1280,128]{1,0:T(8,128)(2,1)S(1)} collective-permute-done((bf16[1280,128]{1,0:T(8,128)(2,1)S(1)}, bf16[1280,128]{1,0:T(8,128)(2,1)S(1)}, u32[]{:S(2)}, u32[]{:S(2)}) %collective-permute-start.12) | collective-permute-done | bytes 327712 | tf_op jit(solution)/shard_map/ppermute | solution.py:442
  27.3 2.6 %collective-permute-start.13 = (bf16[1280,128]{1,0:T(8,128)(2,1)S(1)}, bf16[1280,128]{1,0:T(8,128)(2,1)S(1)}, u32[]{:S(2)}, u32[]{:S(2)}) collective-permute-start(bf16[1280,128]{1,0:T(8,128)(2,1)S(1)} %fusion), channel_id=1, source_target_pairs={{0,4},{4,0},{8,12},{12,8},{16,24},{20,28},{24,16},{28,20},{1,5},{5... | collective-permute-start | bytes 983048 | tf_op jit(solution)/shard_map/ppermute | solution.py:442
  29.9 2.3 %collective-permute-start.7 = (bf16[640,128]{1,0:T(8,128)(2,1)S(1)}, bf16[640,128]{1,0:T(8,128)(2,1)S(1)}, u32[]{:S(2)}, u32[]{:S(2)}) collective-permute-start(bf16[640,128]{1,0:T(8,128)(2,1)S(1)} %collective-permute-done.6.after.rows_y), channel_id=1, source_target_pairs={{0,4},{4,0},{8,12},{12,8},{16,24},{20,28},{24,16},{28,20},{1,5},{5... | collective-permute-start | bytes 491528 | tf_op jit(solution)/shard_map/ppermute | solution.py:442
  32.1 0.8 %shard_map.71.panel_rows = bf16[2560,640]{1,0:T(8,128)(2,1)S(1)} custom-call(s32[3]{0:T(128)S(1)} %copy-done.1, s32[2,12]{1,0:T(2,128)S(1)} %copy-done, bf16[1536,640]{1,0:T(8,128)(2,1)S(1)} %get-tuple-element.43.w_v, bf16[640,128]{1,0:T(8,128)(2,1)S(1)} %collective-permute-done.6.after.rows_y), custom_call_target="tpu_custom_call" | custom-call | flops 2000000000 | bytes 6553600 | tf_op jit(solution)/shard_map/pallas_call | solution.py:532
  33.0 1.9 %collective-permute-done.13 = bf16[1280,128]{1,0:T(8,128)(2,1)S(1)} collective-permute-done((bf16[1280,128]{1,0:T(8,128)(2,1)S(1)}, bf16[1280,128]{1,0:T(8,128)(2,1)S(1)}, u32[]{:S(2)}, u32[]{:S(2)}) %collective-permute-start.13) | collective-permute-done | bytes 327712 | tf_op jit(solution)/shard_map/ppermute | solution.py:442
  35.0 0.6 %shard_map.72 = (bf16[640,128]{1,0:T(8,128)(2,1)S(1)}, bf16[320,128]{1,0:T(8,128)(2,1)S(1)}) custom-call(bf16[1280,128]{1,0:T(8,128)(2,1)S(1)} %add_convert_fusion.y, bf16[1280,640]{1,0:T(8,128)(2,1)S(1)} %get-tuple-element.42.d_v), custom_call_target="tpu_custom_call" | custom-call | tf_op jit(solution)/shard_map/pallas_call | solution.py:545
  35.7 1.0 %collective-permute-done.7.rows_d = bf16[640,128]{1,0:T(8,128)(2,1)S(1)} collective-permute-done((bf16[640,128]{1,0:T(8,128)(2,1)S(1)}, bf16[640,128]{1,0:T(8,128)(2,1)S(1)}, u32[]{:S(2)}, u32[]{:S(2)}) %collective-permute-start.7) | collective-permute-done | bytes 163872 | tf_op jit(solution)/shard_map/ppermute | solution.py:442
  36.7 0.4 collective-permute-done.14
  37.2 0.3 collective-permute-start.15
  37.4 3.3 %collective-permute-start.17 = (bf16[320,128]{1,0:T(8,128)(2,1)S(1)}, bf16[320,128]{1,0:T(8,128)(2,1)S(1)}, u32[]{:S(2)}, u32[]{:S(2)}) collective-permute-start(bf16[320,128]{1,0:T(8,128)(2,1)S(1)} %get-tuple-element.52), channel_id=1, source_target_pairs={{0,12},{4,8},{8,4},{12,0},{16,28},{20,24},{24,20},{28,16},{1,13},{... | collective-permute-start | bytes 245768 | tf_op jit(solution)/shard_map/ppermute | solution.py:442
  40.7 1.6 %shard_map.73 = (f32[128,640]{1,0:T(8,128)S(1)}, bf16[960,128]{1,0:T(8,128)(2,1)}) custom-call(bf16[640,128]{1,0:T(8,128)(2,1)S(1)} %select_convert_fusion.own, bf16[640,128]{1,0:T(8,128)(2,1)S(1)} %collective-permute-done.5.rows_x, bf16[640,128]{1,0:T(8,128)(2,1)S(1)} %collective-permute-done.6.after.rows_y, ...), custom_call_target="tpu_custom_call" | custom-call | flops 419430400 | bytes 3276800 | tf_op jit(solution)/shard_map/pallas_call | solution.py:561
  42.3 2.0 %collective-permute-done.15.near = bf16[640,128]{1,0:T(8,128)(2,1)S(1)} collective-permute-done((bf16[640,128]{1,0:T(8,128)(2,1)S(1)}, bf16[640,128]{1,0:T(8,128)(2,1)S(1)}, u32[]{:S(2)}, u32[]{:S(2)}) %collective-permute-start.15) | collective-permute-done | bytes 163872 | tf_op jit(solution)/shard_map/ppermute | solution.py:442
  44.3 0.5 %collective-permute-start.18 = (bf16[320,128]{1,0:T(8,128)(2,1)S(1)}, bf16[320,128]{1,0:T(8,128)(2,1)S(1)}, u32[]{:S(2)}, u32[]{:S(2)}) collective-permute-start(bf16[320,128]{1,0:T(8,128)(2,1)S(1)} %collective-permute-done.17.far), channel_id=1, source_target_pairs={{0,16},{16,0},{1,17},{17,1},{2,18},{18,2},{3,19},{19,3},{4,20},{20... | collective-permute-start | bytes 245768 | tf_op jit(solution)/shard_map/ppermute | solution.py:434
  44.8 0.5 shard_map.74.total
  45.3 0.5 %collective-permute-done.18.far = bf16[320,128]{1,0:T(8,128)(2,1)S(1)} collective-permute-done((bf16[320,128]{1,0:T(8,128)(2,1)S(1)}, bf16[320,128]{1,0:T(8,128)(2,1)S(1)}, u32[]{:S(2)}, u32[]{:S(2)}) %collective-permute-start.18) | collective-permute-done | bytes 81952 | tf_op jit(solution)/shard_map/ppermute | solution.py:434
  45.8 1.3 %shard_map.75 = bf16[960,128]{1,0:T(8,128)(2,1)} custom-call(bf16[640,128]{1,0:T(8,128)(2,1)S(1)} %collective-permute-done.16.near, bf16[320,128]{1,0:T(8,128)(2,1)S(1)} %collective-permute-done.18.far, f32[128,640]{1,0:T(8,128)S(1)} %shard_map.74.total, bf16[2560,640]{1,0:T(8,128)(2,1)S(1)} %shard_map.71.panel_rows, ...), custom_call_target="tpu_custom_call" | custom-call | flops 209715200 | bytes 1638400 | tf_op jit(solution)/shard_map/pallas_call | solution.py:582
  (28 shorter events, 1.0 us)
Async XLA Ops:
  3.8 3.5 %collective-permute-start = (bf16[640,128]{1,0:T(8,128)(2,1)S(1)}, bf16[640,128]{1,0:T(8,128)(2,1)S(1)}, u32[]{:S(2)}, u32[]{:S(2)}) collective-permute-start(bf16[640,128]{1,0:T(8,128)(2,1)S(1)} %get-tuple-element.31), channel_id=1, source_target_pairs={{0,16},{16,0},{1,17},{17,1},{2,18},{18,2},{3,19},{19,3},{4,20},{20... | collective-permute-start | bytes 491528 | tf_op jit(solution)/shard_map/ppermute | solution.py:434
  4.3 4.0 %collective-permute-start.1 = (bf16[640,128]{1,0:T(8,128)(2,1)S(1)}, bf16[640,128]{1,0:T(8,128)(2,1)S(1)}, u32[]{:S(2)}, u32[]{:S(2)}) collective-permute-start(bf16[640,128]{1,0:T(8,128)(2,1)S(1)} %get-tuple-element.33), channel_id=1, source_target_pairs={{0,16},{16,0},{1,17},{17,1},{2,18},{18,2},{3,19},{19,3},{4,20},{20... | collective-permute-start | bytes 491528 | tf_op jit(solution)/shard_map/ppermute | solution.py:434
  4.4 8.0 %collective-permute-start.2 = (bf16[640,128]{1,0:T(8,128)(2,1)S(1)}, bf16[640,128]{1,0:T(8,128)(2,1)S(1)}, u32[]{:S(2)}, u32[]{:S(2)}) collective-permute-start(bf16[640,128]{1,0:T(8,128)(2,1)S(1)} %get-tuple-element.36), channel_id=1, source_target_pairs={{0,4},{4,0},{8,12},{12,8},{16,24},{20,28},{24,16},{28,20},{1,5},{5... | collective-permute-start | bytes 491528 | tf_op jit(solution)/shard_map/ppermute | solution.py:442
  7.3 7.5 %collective-permute-start.8 = (bf16[640,128]{1,0:T(8,128)(2,1)S(1)}, bf16[640,128]{1,0:T(8,128)(2,1)S(1)}, u32[]{:S(2)}, u32[]{:S(2)}) collective-permute-start(bf16[640,128]{1,0:T(8,128)(2,1)S(1)} %add_convert_fusion.1.after), channel_id=1, source_target_pairs={{0,4},{4,0},{8,12},{12,8},{16,24},{20,28},{24,16},{28,20},{1,5},{5... | collective-permute-start | bytes 491528 | tf_op jit(solution)/shard_map/ppermute | solution.py:442
  8.3 7.8 %collective-permute-start.9 = (bf16[320,128]{1,0:T(8,128)(2,1)S(1)}, bf16[320,128]{1,0:T(8,128)(2,1)S(1)}, u32[]{:S(2)}, u32[]{:S(2)}) collective-permute-start(bf16[320,128]{1,0:T(8,128)(2,1)S(1)} %slice.59), channel_id=1, source_target_pairs={{0,12},{4,8},{8,4},{12,0},{16,28},{20,24},{24,20},{28,16},{1,13},{... | collective-permute-start | bytes 245768 | tf_op jit(solution)/shard_map/ppermute | solution.py:442
  12.3 19.8 %copy-start = (s32[2,12]{1,0:T(2,128)S(1)}, s32[2,12]{1,0:T(2,128)}, u32[]{:S(2)}) copy-start(s32[2,12]{1,0:T(2,128)} %pmap.3) | copy-start | bytes 292
  12.3 19.8 %copy-start.1 = (s32[3]{0:T(128)S(1)}, s32[3]{0:T(128)}, u32[]{:S(2)}) copy-start(s32[3]{0:T(128)} %live.3) | copy-start | bytes 40
  12.4 9.0 %collective-permute-start.4 = (bf16[640,128]{1,0:T(8,128)(2,1)S(1)}, bf16[640,128]{1,0:T(8,128)(2,1)S(1)}, u32[]{:S(2)}, u32[]{:S(2)}) collective-permute-start(bf16[640,128]{1,0:T(8,128)(2,1)S(1)} %get-tuple-element.39), channel_id=1, source_target_pairs={{0,8},{4,12},{8,0},{12,4},{16,20},{20,16},{24,28},{28,24},{1,9},{5... | collective-permute-start | bytes 491528 | tf_op jit(solution)/shard_map/ppermute | solution.py:442
  12.9 8.4 %collective-permute-start.3 = (bf16[640,128]{1,0:T(8,128)(2,1)S(1)}, bf16[640,128]{1,0:T(8,128)(2,1)S(1)}, u32[]{:S(2)}, u32[]{:S(2)}) collective-permute-start(bf16[640,128]{1,0:T(8,128)(2,1)S(1)} %get-tuple-element.37), channel_id=1, source_target_pairs={{0,12},{4,8},{8,4},{12,0},{16,28},{20,24},{24,20},{28,16},{1,13},{... | collective-permute-start | bytes 491528 | tf_op jit(solution)/shard_map/ppermute | solution.py:442
  16.2 1.3 %collective-permute-start.10 = (bf16[320,128]{1,0:T(8,128)(2,1)S(1)}, bf16[320,128]{1,0:T(8,128)(2,1)S(1)}, u32[]{:S(2)}, u32[]{:S(2)}) collective-permute-start(bf16[320,128]{1,0:T(8,128)(2,1)S(1)} %fusion.3.mine), channel_id=1, source_target_pairs={{0,16},{16,0},{1,17},{17,1},{2,18},{18,2},{3,19},{19,3},{4,20},{20... | collective-permute-start | bytes 245768 | tf_op jit(solution)/shard_map/ppermute | solution.py:434
  16.3 1.4 %collective-permute-start.11 = (bf16[320,128]{1,0:T(8,128)(2,1)S(1)}, bf16[320,128]{1,0:T(8,128)(2,1)S(1)}, u32[]{:S(2)}, u32[]{:S(2)}) collective-permute-start(bf16[320,128]{1,0:T(8,128)(2,1)S(1)} %slice.37.yours), channel_id=1, source_target_pairs={{0,16},{16,0},{1,17},{17,1},{2,18},{18,2},{3,19},{19,3},{4,20},{20... | collective-permute-start | bytes 245768 | tf_op jit(solution)/shard_map/ppermute | solution.py:434
  18.4 8.8 %collective-permute-start.12 = (bf16[1280,128]{1,0:T(8,128)(2,1)S(1)}, bf16[1280,128]{1,0:T(8,128)(2,1)S(1)}, u32[]{:S(2)}, u32[]{:S(2)}) collective-permute-start(bf16[1280,128]{1,0:T(8,128)(2,1)S(1)} %shard_map.70), channel_id=1, source_target_pairs={{0,8},{4,12},{8,0},{12,4},{16,20},{20,16},{24,28},{28,24},{1,9},{5... | collective-permute-start | bytes 983048 | tf_op jit(solution)/shard_map/ppermute | solution.py:442
  21.5 8.4 %collective-permute-start.5 = (bf16[640,128]{1,0:T(8,128)(2,1)S(1)}, bf16[640,128]{1,0:T(8,128)(2,1)S(1)}, u32[]{:S(2)}, u32[]{:S(2)}) collective-permute-start(bf16[640,128]{1,0:T(8,128)(2,1)S(1)} %select_convert_fusion.own), channel_id=1, source_target_pairs={{0,4},{4,0},{8,12},{12,8},{16,24},{20,28},{24,16},{28,20},{1,5},{5... | collective-permute-start | bytes 491528 | tf_op jit(solution)/shard_map/ppermute | solution.py:442
  23.2 6.7 %collective-permute-start.6 = (bf16[640,128]{1,0:T(8,128)(2,1)S(1)}, bf16[640,128]{1,0:T(8,128)(2,1)S(1)}, u32[]{:S(2)}, u32[]{:S(2)}) collective-permute-start(bf16[640,128]{1,0:T(8,128)(2,1)S(1)} %select_convert_fusion.own), channel_id=1, source_target_pairs={{0,8},{4,12},{8,0},{12,4},{16,20},{20,16},{24,28},{28,24},{1,9},{5... | collective-permute-start | bytes 491528 | tf_op jit(solution)/shard_map/ppermute | solution.py:442
  27.3 7.6 %collective-permute-start.13 = (bf16[1280,128]{1,0:T(8,128)(2,1)S(1)}, bf16[1280,128]{1,0:T(8,128)(2,1)S(1)}, u32[]{:S(2)}, u32[]{:S(2)}) collective-permute-start(bf16[1280,128]{1,0:T(8,128)(2,1)S(1)} %fusion), channel_id=1, source_target_pairs={{0,4},{4,0},{8,12},{12,8},{16,24},{20,28},{24,16},{28,20},{1,5},{5... | collective-permute-start | bytes 983048 | tf_op jit(solution)/shard_map/ppermute | solution.py:442
  29.9 6.8 %collective-permute-start.7 = (bf16[640,128]{1,0:T(8,128)(2,1)S(1)}, bf16[640,128]{1,0:T(8,128)(2,1)S(1)}, u32[]{:S(2)}, u32[]{:S(2)}) collective-permute-start(bf16[640,128]{1,0:T(8,128)(2,1)S(1)} %collective-permute-done.6.after.rows_y), channel_id=1, source_target_pairs={{0,4},{4,0},{8,12},{12,8},{16,24},{20,28},{24,16},{28,20},{1,5},{5... | collective-permute-start | bytes 491528 | tf_op jit(solution)/shard_map/ppermute | solution.py:442
  35.6 1.5 %collective-permute-start.14 = (bf16[640,128]{1,0:T(8,128)(2,1)S(1)}, bf16[640,128]{1,0:T(8,128)(2,1)S(1)}, u32[]{:S(2)}, u32[]{:S(2)}) collective-permute-start(bf16[640,128]{1,0:T(8,128)(2,1)S(1)} %get-tuple-element.46), channel_id=1, source_target_pairs={{0,16},{16,0},{1,17},{17,1},{2,18},{18,2},{3,19},{19,3},{4,20},{20... | collective-permute-start | bytes 491528 | tf_op jit(solution)/shard_map/ppermute | solution.py:434
  37.2 7.1 %collective-permute-start.15 = (bf16[640,128]{1,0:T(8,128)(2,1)S(1)}, bf16[640,128]{1,0:T(8,128)(2,1)S(1)}, u32[]{:S(2)}, u32[]{:S(2)}) collective-permute-start(bf16[640,128]{1,0:T(8,128)(2,1)S(1)} %pad_maximum_fusion.root_rows), channel_id=1, source_target_pairs={{0,8},{4,12},{8,0},{12,4},{16,20},{20,16},{24,28},{28,24},{1,9},{5... | collective-permute-start | bytes 491528 | tf_op jit(solution)/shard_map/ppermute | solution.py:442
  37.4 6.9 %collective-permute-start.17 = (bf16[320,128]{1,0:T(8,128)(2,1)S(1)}, bf16[320,128]{1,0:T(8,128)(2,1)S(1)}, u32[]{:S(2)}, u32[]{:S(2)}) collective-permute-start(bf16[320,128]{1,0:T(8,128)(2,1)S(1)} %get-tuple-element.52), channel_id=1, source_target_pairs={{0,12},{4,8},{8,4},{12,0},{16,28},{20,24},{24,20},{28,16},{1,13},{... | collective-permute-start | bytes 245768 | tf_op jit(solution)/shard_map/ppermute | solution.py:442
  44.3 1.5 %collective-permute-start.16 = (bf16[640,128]{1,0:T(8,128)(2,1)S(1)}, bf16[640,128]{1,0:T(8,128)(2,1)S(1)}, u32[]{:S(2)}, u32[]{:S(2)}) collective-permute-start(bf16[640,128]{1,0:T(8,128)(2,1)S(1)} %collective-permute-done.15.near), channel_id=1, source_target_pairs={{0,16},{16,0},{1,17},{17,1},{2,18},{18,2},{3,19},{19,3},{4,20},{20... | collective-permute-start | bytes 491528 | tf_op jit(solution)/shard_map/ppermute | solution.py:434
  44.3 1.5 %collective-permute-start.18 = (bf16[320,128]{1,0:T(8,128)(2,1)S(1)}, bf16[320,128]{1,0:T(8,128)(2,1)S(1)}, u32[]{:S(2)}, u32[]{:S(2)}) collective-permute-start(bf16[320,128]{1,0:T(8,128)(2,1)S(1)} %collective-permute-done.17.far), channel_id=1, source_target_pairs={{0,16},{16,0},{1,17},{17,1},{2,18},{18,2},{3,19},{19,3},{4,20},{20... | collective-permute-start | bytes 245768 | tf_op jit(solution)/shard_map/ppermute | solution.py:434

commit v13 on v9

--- a/solution.py
+++ b/solution.py
@@ -376,8 +376,8 @@
 def leaf_transposed_kernel(
     sizes,
     own,
+    rows_y,
     rows_x,
-    rows_y,
     rows_d,
     d_v,
     mask,
@@ -545,7 +545,7 @@
         16 * MIB,
         2 * front * quarter * columns,
         2 * front * quarter,
-    )(leaf_forward, rows_x, rows_y, rows_d, d_v, mask, root_rows, panel_rows, root_piece)
+    )(leaf_forward, rows_y, rows_x, rows_d, d_v, mask, root_rows, panel_rows, root_piece)
     near = after(near, total)
     near_other = leaf_swap(near)
     far_other = leaf_swap(far)

time: 45.1 us -> 45.1 us (level)
  waiting for transfers between devices: 14 us -> 16.2 us
  starting transfers between devices: 19.4 us -> 17.3 us
    ppermute x12, starting transfers between devices: 18.2 us -> 15.6 us  [row_swap(): return lax.ppermute(value, ('leaf', 'row'), route)]
    ppermute x12, waiting for transfers between devices: 10.9 us -> 13.4 us  [row_swap(): return lax.ppermute(value, ('leaf', 'row'), route)]
    ppermute x7, starting transfers between devices: 1.24 us -> 1.75 us  [leaf_swap(): return lax.ppermute(value, 'leaf', [(0, 1), (1, 0)])]
  transfers between devices with their start and end apart: 19 -> 19, of which waited for: 14 -> 13; matrix products, arithmetic and copies ran while one was open for 1% -> 1% of each run, Pallas kernels for 14% -> 14%
where the time goes in v13:
time: 45.1 us; the launch traced here: 45 us
  starting transfers between devices  17.3 us (38%)
  waiting for transfers between devices  16.2 us (36%)
  Pallas kernels  10.1 us (22%)
  between operations  0.77 us (2%)
  other arithmetic  0.55 us (1%)
    ppermute x12, starting transfers between devices, row_swap(): return lax.ppermute(value, ('leaf', 'row'), route)  15.6 us
    ppermute x12, waiting for transfers between devices, row_swap(): return lax.ppermute(value, ('leaf', 'row'), route)  13.4 us
    ppermute x7, waiting for transfers between devices, leaf_swap(): return lax.ppermute(value, 'leaf', [(0, 1), (1, 0)])  2.78 us
    pallas_call x1, Pallas kernels, two_levels(): call(functools.partial(panel_kernel, (quarter, half, parts, updates)), (k...  2.74 us
    pallas_call x1, Pallas kernels, two_levels(): call(functools.partial(leaf_pivot_kernel, (quarter, 4 * half)), (*(kept(q...  2.02 us
    ppermute x7, starting transfers between devices, leaf_swap(): return lax.ppermute(value, 'leaf', [(0, 1), (1, 0)])  1.75 us
    pallas_call x1, Pallas kernels, two_levels(): call(functools.partial(leaf_transposed_kernel, (quarter, half)), (kept(co...  1.57 us
    pallas_call x1, Pallas kernels, two_levels(): call(functools.partial(last_kernel, (quarter, half)), stored(quarter + ha...  1.26 us
  transfers between devices with their start and end apart: 19, of which 13 were waited for; matrix products, arithmetic and copies ran while one was open for 1% of the time, Pallas kernels for 14%

profile of v13, /device:TPU:0, one launch (start us, length us, event | category | flops | bytes accessed | tf_op | source)
XLA Modules:
  0.0 45.0 jit_solution(5181872031353438862)
XLA Ops:
  0.6 2.7 %shard_map.68 = (bf16[640,128]{1,0:T(8,128)(2,1)S(1)}, bf16[640,128]{1,0:T(8,128)(2,1)S(1)}, bf16[640,128]{1,0:T(8,128)(2,1)S(1)}, bf16[640,128]{1,0:T(8,128)(2,...) custom-call(s32[3]{0:T(128)} %live.3, ...), custom_call_target="tpu_custom_call" | custom-call | flops 251658240 | bytes 1966080 | tf_op jit(solution)/shard_map/pallas_call | solution.py:452
  3.4 0.5 %collective-permute-start = (bf16[640,128]{1,0:T(8,128)(2,1)S(1)}, bf16[640,128]{1,0:T(8,128)(2,1)S(1)}, u32[]{:S(2)}, u32[]{:S(2)}) collective-permute-start(bf16[640,128]{1,0:T(8,128)(2,1)S(1)} %get-tuple-element.29), channel_id=1, source_target_pairs={{0,16},{16,0},{1,17},{17,1},{2,18},{18,2},{3,19},{19,3},{4,20},{20... | collective-permute-start | bytes 491528 | tf_op jit(solution)/shard_map/ppermute | solution.py:427
  4.0 0.9 %collective-permute-done = bf16[640,128]{1,0:T(8,128)(2,1)S(1)} collective-permute-done((bf16[640,128]{1,0:T(8,128)(2,1)S(1)}, bf16[640,128]{1,0:T(8,128)(2,1)S(1)}, u32[]{:S(2)}, u32[]{:S(2)}) %collective-permute-start) | collective-permute-done | bytes 163872 | tf_op jit(solution)/shard_map/ppermute | solution.py:427
  5.0 2.9 %collective-permute-start.7 = (bf16[640,128]{1,0:T(8,128)(2,1)S(1)}, bf16[640,128]{1,0:T(8,128)(2,1)S(1)}, u32[]{:S(2)}, u32[]{:S(2)}) collective-permute-start(bf16[640,128]{1,0:T(8,128)(2,1)S(1)} %add_convert_fusion.1.after), channel_id=1, source_target_pairs={{0,4},{4,0},{8,12},{12,8},{16,24},{20,28},{24,16},{28,20},{1,5},{5... | collective-permute-start | bytes 491528 | tf_op jit(solution)/shard_map/ppermute | solution.py:435
  8.0 1.6 %collective-permute-start.9 = (bf16[320,128]{1,0:T(8,128)(2,1)S(1)}, bf16[320,128]{1,0:T(8,128)(2,1)S(1)}, u32[]{:S(2)}, u32[]{:S(2)}) collective-permute-start(bf16[320,128]{1,0:T(8,128)(2,1)S(1)} %slice.59), channel_id=1, source_target_pairs={{0,12},{4,8},{8,4},{12,0},{16,28},{20,24},{24,20},{28,16},{1,13},{... | collective-permute-start | bytes 245768 | tf_op jit(solution)/shard_map/ppermute | solution.py:435
  9.5 2.0 %shard_map.69 = (bf16[640,128]{1,0:T(8,128)(2,1)S(1)}, bf16[640,128]{1,0:T(8,128)(2,1)S(1)}, bf16[640,128]{1,0:T(8,128)(2,1)S(1)}, bf16[640,128]{1,0:T(8,128)(2,1)S(1)}, bf16[1280,640]{1,0:T(8,128)(2,1)S(1)}) custom-call(bf16[640,128]{1,0:T(8,128)(2,1)S(1)} %get-tuple-element.26.masked, bf16[2560,640]{1,0:T(8,128)(2,1)S(1)} %get-tuple-element.27.d_v, ...), custom_call_target="tpu_custom_call" | custom-call | flops 419430400 | bytes 3276800 | tf_op jit(solution)/shard_map/pallas_call | solution.py:477
  11.6 1.5 %collective-permute-start.1 = (bf16[640,128]{1,0:T(8,128)(2,1)S(1)}, bf16[640,128]{1,0:T(8,128)(2,1)S(1)}, u32[]{:S(2)}, u32[]{:S(2)}) collective-permute-start(bf16[640,128]{1,0:T(8,128)(2,1)S(1)} %get-tuple-element.31), channel_id=1, source_target_pairs={{0,12},{4,8},{8,4},{12,0},{16,28},{20,24},{24,20},{28,16},{1,13},{... | collective-permute-start | bytes 491528 | tf_op jit(solution)/shard_map/ppermute | solution.py:435
  13.2 1.9 %collective-permute-start.3 = (bf16[640,128]{1,0:T(8,128)(2,1)S(1)}, bf16[640,128]{1,0:T(8,128)(2,1)S(1)}, u32[]{:S(2)}, u32[]{:S(2)}) collective-permute-start(bf16[640,128]{1,0:T(8,128)(2,1)S(1)} %get-tuple-element.33), channel_id=1, source_target_pairs={{0,8},{4,12},{8,0},{12,4},{16,20},{20,16},{24,28},{28,24},{1,9},{5... | collective-permute-start | bytes 491528 | tf_op jit(solution)/shard_map/ppermute | solution.py:435
  15.3 0.5 %collective-permute-start.11 = (bf16[320,128]{1,0:T(8,128)(2,1)S(1)}, bf16[320,128]{1,0:T(8,128)(2,1)S(1)}, u32[]{:S(2)}, u32[]{:S(2)}) collective-permute-start(bf16[320,128]{1,0:T(8,128)(2,1)S(1)} %slice.37.yours), channel_id=1, source_target_pairs={{0,16},{16,0},{1,17},{17,1},{2,18},{18,2},{3,19},{19,3},{4,20},{20... | collective-permute-start | bytes 245768 | tf_op jit(solution)/shard_map/ppermute | solution.py:427
  15.8 0.8 %collective-permute-done.10.other_mine = bf16[320,128]{1,0:T(8,128)(2,1)S(1)} collective-permute-done((bf16[320,128]{1,0:T(8,128)(2,1)S(1)}, bf16[320,128]{1,0:T(8,128)(2,1)S(1)}, u32[]{:S(2)}, u32[]{:S(2)}) %collective-permute-start.10) | collective-permute-done | bytes 81952 | tf_op jit(solution)/shard_map/ppermute | solution.py:427
  16.7 0.6 %shard_map.70 = bf16[1280,128]{1,0:T(8,128)(2,1)S(1)} custom-call(bf16[320,128]{1,0:T(8,128)(2,1)S(1)} %fusion.3.mine, bf16[320,128]{1,0:T(8,128)(2,1)S(1)} %slice.37.yours, bf16[320,128]{1,0:T(8,128)(2,1)S(1)} %collective-permute-done.10.other_mine, bf16[320,128]{1,0:T(8,128)(2,1)S(1)} %collective-permute-done.11.other_yours, ...), custom_call_target="tpu_custom_call" | custom-call | tf_op jit(solution)/shard_map/pallas_call | solution.py:502
  17.5 2.2 %collective-permute-done.1 = bf16[640,128]{1,0:T(8,128)(2,1)S(1)} collective-permute-done((bf16[640,128]{1,0:T(8,128)(2,1)S(1)}, bf16[640,128]{1,0:T(8,128)(2,1)S(1)}, u32[]{:S(2)}, u32[]{:S(2)}) %collective-permute-start.1) | collective-permute-done | bytes 163872 | tf_op jit(solution)/shard_map/ppermute | solution.py:435
  19.7 2.1 %collective-permute-done.2 = bf16[640,128]{1,0:T(8,128)(2,1)S(1)} collective-permute-done((bf16[640,128]{1,0:T(8,128)(2,1)S(1)}, bf16[640,128]{1,0:T(8,128)(2,1)S(1)}, u32[]{:S(2)}, u32[]{:S(2)}) %collective-permute-start.2) | collective-permute-done | bytes 163872 | tf_op jit(solution)/shard_map/ppermute | solution.py:435
  21.9 2.1 %collective-permute-start.4 = (bf16[640,128]{1,0:T(8,128)(2,1)S(1)}, bf16[640,128]{1,0:T(8,128)(2,1)S(1)}, u32[]{:S(2)}, u32[]{:S(2)}) collective-permute-start(bf16[640,128]{1,0:T(8,128)(2,1)S(1)} %select_convert_fusion.own), channel_id=1, source_target_pairs={{0,8},{4,12},{8,0},{12,4},{16,20},{20,16},{24,28},{28,24},{1,9},{5... | collective-permute-start | bytes 491528 | tf_op jit(solution)/shard_map/ppermute | solution.py:435
  24.0 0.8 %collective-permute-start.5 = (bf16[640,128]{1,0:T(8,128)(2,1)S(1)}, bf16[640,128]{1,0:T(8,128)(2,1)S(1)}, u32[]{:S(2)}, u32[]{:S(2)}) collective-permute-start(bf16[640,128]{1,0:T(8,128)(2,1)S(1)} %select_convert_fusion.own), channel_id=1, source_target_pairs={{0,4},{4,0},{8,12},{12,8},{16,24},{20,28},{24,16},{28,20},{1,5},{5... | collective-permute-start | bytes 491528 | tf_op jit(solution)/shard_map/ppermute | solution.py:435
  24.8 0.6 %collective-permute-done.12 = bf16[1280,128]{1,0:T(8,128)(2,1)S(1)} collective-permute-done((bf16[1280,128]{1,0:T(8,128)(2,1)S(1)}, bf16[1280,128]{1,0:T(8,128)(2,1)S(1)}, u32[]{:S(2)}, u32[]{:S(2)}) %collective-permute-start.12) | collective-permute-done | bytes 327712 | tf_op jit(solution)/shard_map/ppermute | solution.py:435
  25.5 1.1 %collective-permute-start.13 = (bf16[1280,128]{1,0:T(8,128)(2,1)S(1)}, bf16[1280,128]{1,0:T(8,128)(2,1)S(1)}, u32[]{:S(2)}, u32[]{:S(2)}) collective-permute-start(bf16[1280,128]{1,0:T(8,128)(2,1)S(1)} %fusion), channel_id=1, source_target_pairs={{0,4},{4,0},{8,12},{12,8},{16,24},{20,28},{24,16},{28,20},{1,5},{5... | collective-permute-start | bytes 983048 | tf_op jit(solution)/shard_map/ppermute | solution.py:435
  26.6 2.4 %collective-permute-done.4.after.rows_y = bf16[640,128]{1,0:T(8,128)(2,1)S(1)} collective-permute-done((bf16[640,128]{1,0:T(8,128)(2,1)S(1)}, bf16[640,128]{1,0:T(8,128)(2,1)S(1)}, u32[]{:S(2)}, u32[]{:S(2)}) %collective-permute-start.4) | collective-permute-done | bytes 163872 | tf_op jit(solution)/shard_map/ppermute | solution.py:435
  29.3 0.9 %collective-permute-start.6 = (bf16[640,128]{1,0:T(8,128)(2,1)S(1)}, bf16[640,128]{1,0:T(8,128)(2,1)S(1)}, u32[]{:S(2)}, u32[]{:S(2)}) collective-permute-start(bf16[640,128]{1,0:T(8,128)(2,1)S(1)} %collective-permute-done.4.after.rows_y), channel_id=1, source_target_pairs={{0,4},{4,0},{8,12},{12,8},{16,24},{20,28},{24,16},{28,20},{1,5},{5... | collective-permute-start | bytes 491528 | tf_op jit(solution)/shard_map/ppermute | solution.py:435
  30.2 0.8 %shard_map.71.panel_rows = bf16[2560,640]{1,0:T(8,128)(2,1)S(1)} custom-call(s32[3]{0:T(128)S(1)} %copy-done.1, s32[2,12]{1,0:T(2,128)S(1)} %copy-done, bf16[1536,640]{1,0:T(8,128)(2,1)S(1)} %get-tuple-element.39.w_v, bf16[640,128]{1,0:T(8,128)(2,1)S(1)} %collective-permute-done.4.after.rows_y), custom_call_target="tpu_custom_call" | custom-call | flops 2000000000 | bytes 6553600 | tf_op jit(solution)/shard_map/pallas_call | solution.py:511
  31.1 1.7 %collective-permute-done.13 = bf16[1280,128]{1,0:T(8,128)(2,1)S(1)} collective-permute-done((bf16[1280,128]{1,0:T(8,128)(2,1)S(1)}, bf16[1280,128]{1,0:T(8,128)(2,1)S(1)}, u32[]{:S(2)}, u32[]{:S(2)}) %collective-permute-start.13) | collective-permute-done | bytes 327712 | tf_op jit(solution)/shard_map/ppermute | solution.py:435
  32.9 0.6 %shard_map.72 = (bf16[640,128]{1,0:T(8,128)(2,1)S(1)}, bf16[320,128]{1,0:T(8,128)(2,1)S(1)}) custom-call(bf16[1280,128]{1,0:T(8,128)(2,1)S(1)} %add_convert_fusion.y, bf16[1280,640]{1,0:T(8,128)(2,1)S(1)} %get-tuple-element.38.d_v), custom_call_target="tpu_custom_call" | custom-call | tf_op jit(solution)/shard_map/pallas_call | solution.py:524
  33.6 1.0 %collective-permute-done.6.rows_d = bf16[640,128]{1,0:T(8,128)(2,1)S(1)} collective-permute-done((bf16[640,128]{1,0:T(8,128)(2,1)S(1)}, bf16[640,128]{1,0:T(8,128)(2,1)S(1)}, u32[]{:S(2)}, u32[]{:S(2)}) %collective-permute-start.6) | collective-permute-done | bytes 163872 | tf_op jit(solution)/shard_map/ppermute | solution.py:435
  34.6 0.4 collective-permute-done.14
  35.1 0.9 %collective-permute-start.15 = (bf16[640,128]{1,0:T(8,128)(2,1)S(1)}, bf16[640,128]{1,0:T(8,128)(2,1)S(1)}, u32[]{:S(2)}, u32[]{:S(2)}) collective-permute-start(bf16[640,128]{1,0:T(8,128)(2,1)S(1)} %pad_maximum_fusion.root_rows), channel_id=1, source_target_pairs={{0,8},{4,12},{8,0},{12,4},{16,20},{20,16},{24,28},{28,24},{1,9},{5... | collective-permute-start | bytes 491528 | tf_op jit(solution)/shard_map/ppermute | solution.py:435
  35.9 1.5 %collective-permute-start.17 = (bf16[320,128]{1,0:T(8,128)(2,1)S(1)}, bf16[320,128]{1,0:T(8,128)(2,1)S(1)}, u32[]{:S(2)}, u32[]{:S(2)}) collective-permute-start(bf16[320,128]{1,0:T(8,128)(2,1)S(1)} %get-tuple-element.48), channel_id=1, source_target_pairs={{0,12},{4,8},{8,4},{12,0},{16,28},{20,24},{24,20},{28,16},{1,13},{... | collective-permute-start | bytes 245768 | tf_op jit(solution)/shard_map/ppermute | solution.py:435
  37.5 1.6 %shard_map.73 = (f32[128,640]{1,0:T(8,128)S(1)}, bf16[960,128]{1,0:T(8,128)(2,1)}) custom-call(bf16[640,128]{1,0:T(8,128)(2,1)S(1)} %select_convert_fusion.own, bf16[640,128]{1,0:T(8,128)(2,1)S(1)} %collective-permute-done.4.after.rows_y, bf16[640,128]{1,0:T(8,128)(2,1)S(1)} %collective-permute-done.5.rows_x, ...), custom_call_target="tpu_custom_call" | custom-call | flops 419430400 | bytes 3276800 | tf_op jit(solution)/shard_map/pallas_call | solution.py:540
  39.0 3.2 %collective-permute-done.15.near = bf16[640,128]{1,0:T(8,128)(2,1)S(1)} collective-permute-done((bf16[640,128]{1,0:T(8,128)(2,1)S(1)}, bf16[640,128]{1,0:T(8,128)(2,1)S(1)}, u32[]{:S(2)}, u32[]{:S(2)}) %collective-permute-start.15) | collective-permute-done | bytes 163872 | tf_op jit(solution)/shard_map/ppermute | solution.py:435
  42.2 0.5 %collective-permute-start.18 = (bf16[320,128]{1,0:T(8,128)(2,1)S(1)}, bf16[320,128]{1,0:T(8,128)(2,1)S(1)}, u32[]{:S(2)}, u32[]{:S(2)}) collective-permute-start(bf16[320,128]{1,0:T(8,128)(2,1)S(1)} %collective-permute-done.17.far), channel_id=1, source_target_pairs={{0,16},{16,0},{1,17},{17,1},{2,18},{18,2},{3,19},{19,3},{4,20},{20... | collective-permute-start | bytes 245768 | tf_op jit(solution)/shard_map/ppermute | solution.py:427
  42.7 0.5 %shard_map.74.total = f32[128,640]{1,0:T(8,128)S(1)} custom-call(bf16[640,128]{1,0:T(8,128)(2,1)S(1)} %collective-permute-done.15.near, bf16[320,128]{1,0:T(8,128)(2,1)S(1)} %collective-permute-done.17.far, f32[128,640]{1,0:T(8,128)S(1)} %get-tuple-element.46.total, bf16[2560,640]{1,0:T(8,128)(2,1)S(1)} %shard_map.71.panel_rows), custom_call_target="tpu_custom_call" | custom-call | tf_op jit(solution)/shard_map/pallas_call | solution.py:552
  43.2 0.5 %collective-permute-done.18.far = bf16[320,128]{1,0:T(8,128)(2,1)S(1)} collective-permute-done((bf16[320,128]{1,0:T(8,128)(2,1)S(1)}, bf16[320,128]{1,0:T(8,128)(2,1)S(1)}, u32[]{:S(2)}, u32[]{:S(2)}) %collective-permute-start.18) | collective-permute-done | bytes 81952 | tf_op jit(solution)/shard_map/ppermute | solution.py:427
  43.7 1.3 %shard_map.75 = bf16[960,128]{1,0:T(8,128)(2,1)} custom-call(bf16[640,128]{1,0:T(8,128)(2,1)S(1)} %collective-permute-done.16.near, bf16[320,128]{1,0:T(8,128)(2,1)S(1)} %collective-permute-done.18.far, f32[128,640]{1,0:T(8,128)S(1)} %shard_map.74.total, bf16[2560,640]{1,0:T(8,128)(2,1)S(1)} %shard_map.71.panel_rows, ...), custom_call_target="tpu_custom_call" | custom-call | flops 209715200 | bytes 1638400 | tf_op jit(solution)/shard_map/pallas_call | solution.py:561
  (28 shorter events, 1.5 us)
Async XLA Ops:
  3.4 1.5 %collective-permute-start = (bf16[640,128]{1,0:T(8,128)(2,1)S(1)}, bf16[640,128]{1,0:T(8,128)(2,1)S(1)}, u32[]{:S(2)}, u32[]{:S(2)}) collective-permute-start(bf16[640,128]{1,0:T(8,128)(2,1)S(1)} %get-tuple-element.29), channel_id=1, source_target_pairs={{0,16},{16,0},{1,17},{17,1},{2,18},{18,2},{3,19},{19,3},{4,20},{20... | collective-permute-start | bytes 491528 | tf_op jit(solution)/shard_map/ppermute | solution.py:427
  3.9 4.0 %collective-permute-start.8 = (bf16[640,128]{1,0:T(8,128)(2,1)S(1)}, bf16[640,128]{1,0:T(8,128)(2,1)S(1)}, u32[]{:S(2)}, u32[]{:S(2)}) collective-permute-start(bf16[640,128]{1,0:T(8,128)(2,1)S(1)} %get-tuple-element.36), channel_id=1, source_target_pairs={{0,16},{16,0},{1,17},{17,1},{2,18},{18,2},{3,19},{19,3},{4,20},{20... | collective-permute-start | bytes 491528 | tf_op jit(solution)/shard_map/ppermute | solution.py:427
  5.0 10.2 %collective-permute-start.7 = (bf16[640,128]{1,0:T(8,128)(2,1)S(1)}, bf16[640,128]{1,0:T(8,128)(2,1)S(1)}, u32[]{:S(2)}, u32[]{:S(2)}) collective-permute-start(bf16[640,128]{1,0:T(8,128)(2,1)S(1)} %add_convert_fusion.1.after), channel_id=1, source_target_pairs={{0,4},{4,0},{8,12},{12,8},{16,24},{20,28},{24,16},{28,20},{1,5},{5... | collective-permute-start | bytes 491528 | tf_op jit(solution)/shard_map/ppermute | solution.py:435
  8.0 7.2 %collective-permute-start.9 = (bf16[320,128]{1,0:T(8,128)(2,1)S(1)}, bf16[320,128]{1,0:T(8,128)(2,1)S(1)}, u32[]{:S(2)}, u32[]{:S(2)}) collective-permute-start(bf16[320,128]{1,0:T(8,128)(2,1)S(1)} %slice.59), channel_id=1, source_target_pairs={{0,12},{4,8},{8,4},{12,0},{16,28},{20,24},{24,20},{28,16},{1,13},{... | collective-permute-start | bytes 245768 | tf_op jit(solution)/shard_map/ppermute | solution.py:435
  11.5 18.7 %copy-start = (s32[2,12]{1,0:T(2,128)S(1)}, s32[2,12]{1,0:T(2,128)}, u32[]{:S(2)}) copy-start(s32[2,12]{1,0:T(2,128)} %pmap.3) | copy-start | bytes 292
  11.6 18.7 %copy-start.1 = (s32[3]{0:T(128)S(1)}, s32[3]{0:T(128)}, u32[]{:S(2)}) copy-start(s32[3]{0:T(128)} %live.3) | copy-start | bytes 40
  11.6 8.1 %collective-permute-start.1 = (bf16[640,128]{1,0:T(8,128)(2,1)S(1)}, bf16[640,128]{1,0:T(8,128)(2,1)S(1)}, u32[]{:S(2)}, u32[]{:S(2)}) collective-permute-start(bf16[640,128]{1,0:T(8,128)(2,1)S(1)} %get-tuple-element.31), channel_id=1, source_target_pairs={{0,12},{4,8},{8,4},{12,0},{16,28},{20,24},{24,20},{28,16},{1,13},{... | collective-permute-start | bytes 491528 | tf_op jit(solution)/shard_map/ppermute | solution.py:435
  13.1 8.7 %collective-permute-start.2 = (bf16[640,128]{1,0:T(8,128)(2,1)S(1)}, bf16[640,128]{1,0:T(8,128)(2,1)S(1)}, u32[]{:S(2)}, u32[]{:S(2)}) collective-permute-start(bf16[640,128]{1,0:T(8,128)(2,1)S(1)} %get-tuple-element.32), channel_id=1, source_target_pairs={{0,4},{4,0},{8,12},{12,8},{16,24},{20,28},{24,16},{28,20},{1,5},{5... | collective-permute-start | bytes 491528 | tf_op jit(solution)/shard_map/ppermute | solution.py:435
  13.2 8.6 %collective-permute-start.3 = (bf16[640,128]{1,0:T(8,128)(2,1)S(1)}, bf16[640,128]{1,0:T(8,128)(2,1)S(1)}, u32[]{:S(2)}, u32[]{:S(2)}) collective-permute-start(bf16[640,128]{1,0:T(8,128)(2,1)S(1)} %get-tuple-element.33), channel_id=1, source_target_pairs={{0,8},{4,12},{8,0},{12,4},{16,20},{20,16},{24,28},{28,24},{1,9},{5... | collective-permute-start | bytes 491528 | tf_op jit(solution)/shard_map/ppermute | solution.py:435
  15.2 1.3 %collective-permute-start.10 = (bf16[320,128]{1,0:T(8,128)(2,1)S(1)}, bf16[320,128]{1,0:T(8,128)(2,1)S(1)}, u32[]{:S(2)}, u32[]{:S(2)}) collective-permute-start(bf16[320,128]{1,0:T(8,128)(2,1)S(1)} %fusion.3.mine), channel_id=1, source_target_pairs={{0,16},{16,0},{1,17},{17,1},{2,18},{18,2},{3,19},{19,3},{4,20},{20... | collective-permute-start | bytes 245768 | tf_op jit(solution)/shard_map/ppermute | solution.py:427
  15.3 1.4 %collective-permute-start.11 = (bf16[320,128]{1,0:T(8,128)(2,1)S(1)}, bf16[320,128]{1,0:T(8,128)(2,1)S(1)}, u32[]{:S(2)}, u32[]{:S(2)}) collective-permute-start(bf16[320,128]{1,0:T(8,128)(2,1)S(1)} %slice.37.yours), channel_id=1, source_target_pairs={{0,16},{16,0},{1,17},{17,1},{2,18},{18,2},{3,19},{19,3},{4,20},{20... | collective-permute-start | bytes 245768 | tf_op jit(solution)/shard_map/ppermute | solution.py:427
  17.4 8.0 %collective-permute-start.12 = (bf16[1280,128]{1,0:T(8,128)(2,1)S(1)}, bf16[1280,128]{1,0:T(8,128)(2,1)S(1)}, u32[]{:S(2)}, u32[]{:S(2)}) collective-permute-start(bf16[1280,128]{1,0:T(8,128)(2,1)S(1)} %shard_map.70), channel_id=1, source_target_pairs={{0,8},{4,12},{8,0},{12,4},{16,20},{20,16},{24,28},{28,24},{1,9},{5... | collective-permute-start | bytes 983048 | tf_op jit(solution)/shard_map/ppermute | solution.py:435
  21.9 7.1 %collective-permute-start.4 = (bf16[640,128]{1,0:T(8,128)(2,1)S(1)}, bf16[640,128]{1,0:T(8,128)(2,1)S(1)}, u32[]{:S(2)}, u32[]{:S(2)}) collective-permute-start(bf16[640,128]{1,0:T(8,128)(2,1)S(1)} %select_convert_fusion.own), channel_id=1, source_target_pairs={{0,8},{4,12},{8,0},{12,4},{16,20},{20,16},{24,28},{28,24},{1,9},{5... | collective-permute-start | bytes 491528 | tf_op jit(solution)/shard_map/ppermute | solution.py:435
  24.0 5.3 %collective-permute-start.5 = (bf16[640,128]{1,0:T(8,128)(2,1)S(1)}, bf16[640,128]{1,0:T(8,128)(2,1)S(1)}, u32[]{:S(2)}, u32[]{:S(2)}) collective-permute-start(bf16[640,128]{1,0:T(8,128)(2,1)S(1)} %select_convert_fusion.own), channel_id=1, source_target_pairs={{0,4},{4,0},{8,12},{12,8},{16,24},{20,28},{24,16},{28,20},{1,5},{5... | collective-permute-start | bytes 491528 | tf_op jit(solution)/shard_map/ppermute | solution.py:435
  25.5 7.3 %collective-permute-start.13 = (bf16[1280,128]{1,0:T(8,128)(2,1)S(1)}, bf16[1280,128]{1,0:T(8,128)(2,1)S(1)}, u32[]{:S(2)}, u32[]{:S(2)}) collective-permute-start(bf16[1280,128]{1,0:T(8,128)(2,1)S(1)} %fusion), channel_id=1, source_target_pairs={{0,4},{4,0},{8,12},{12,8},{16,24},{20,28},{24,16},{28,20},{1,5},{5... | collective-permute-start | bytes 983048 | tf_op jit(solution)/shard_map/ppermute | solution.py:435
  29.3 5.3 %collective-permute-start.6 = (bf16[640,128]{1,0:T(8,128)(2,1)S(1)}, bf16[640,128]{1,0:T(8,128)(2,1)S(1)}, u32[]{:S(2)}, u32[]{:S(2)}) collective-permute-start(bf16[640,128]{1,0:T(8,128)(2,1)S(1)} %collective-permute-done.4.after.rows_y), channel_id=1, source_target_pairs={{0,4},{4,0},{8,12},{12,8},{16,24},{20,28},{24,16},{28,20},{1,5},{5... | collective-permute-start | bytes 491528 | tf_op jit(solution)/shard_map/ppermute | solution.py:435
  33.5 1.5 %collective-permute-start.14 = (bf16[640,128]{1,0:T(8,128)(2,1)S(1)}, bf16[640,128]{1,0:T(8,128)(2,1)S(1)}, u32[]{:S(2)}, u32[]{:S(2)}) collective-permute-start(bf16[640,128]{1,0:T(8,128)(2,1)S(1)} %get-tuple-element.42), channel_id=1, source_target_pairs={{0,16},{16,0},{1,17},{17,1},{2,18},{18,2},{3,19},{19,3},{4,20},{20... | collective-permute-start | bytes 491528 | tf_op jit(solution)/shard_map/ppermute | solution.py:427
  35.1 7.1 %collective-permute-start.15 = (bf16[640,128]{1,0:T(8,128)(2,1)S(1)}, bf16[640,128]{1,0:T(8,128)(2,1)S(1)}, u32[]{:S(2)}, u32[]{:S(2)}) collective-permute-start(bf16[640,128]{1,0:T(8,128)(2,1)S(1)} %pad_maximum_fusion.root_rows), channel_id=1, source_target_pairs={{0,8},{4,12},{8,0},{12,4},{16,20},{20,16},{24,28},{28,24},{1,9},{5... | collective-permute-start | bytes 491528 | tf_op jit(solution)/shard_map/ppermute | solution.py:435
  35.9 6.3 %collective-permute-start.17 = (bf16[320,128]{1,0:T(8,128)(2,1)S(1)}, bf16[320,128]{1,0:T(8,128)(2,1)S(1)}, u32[]{:S(2)}, u32[]{:S(2)}) collective-permute-start(bf16[320,128]{1,0:T(8,128)(2,1)S(1)} %get-tuple-element.48), channel_id=1, source_target_pairs={{0,12},{4,8},{8,4},{12,0},{16,28},{20,24},{24,20},{28,16},{1,13},{... | collective-permute-start | bytes 245768 | tf_op jit(solution)/shard_map/ppermute | solution.py:435
  42.2 1.5 %collective-permute-start.16 = (bf16[640,128]{1,0:T(8,128)(2,1)S(1)}, bf16[640,128]{1,0:T(8,128)(2,1)S(1)}, u32[]{:S(2)}, u32[]{:S(2)}) collective-permute-start(bf16[640,128]{1,0:T(8,128)(2,1)S(1)} %collective-permute-done.15.near), channel_id=1, source_target_pairs={{0,16},{16,0},{1,17},{17,1},{2,18},{18,2},{3,19},{19,3},{4,20},{20... | collective-permute-start | bytes 491528 | tf_op jit(solution)/shard_map/ppermute | solution.py:427
  42.2 1.5 %collective-permute-start.18 = (bf16[320,128]{1,0:T(8,128)(2,1)S(1)}, bf16[320,128]{1,0:T(8,128)(2,1)S(1)}, u32[]{:S(2)}, u32[]{:S(2)}) collective-permute-start(bf16[320,128]{1,0:T(8,128)(2,1)S(1)} %collective-permute-done.17.far), channel_id=1, source_target_pairs={{0,16},{16,0},{1,17},{17,1},{2,18},{18,2},{3,19},{19,3},{4,20},{20... | collective-permute-start | bytes 245768 | tf_op jit(solution)/shard_map/ppermute | solution.py:427

commit v14 on v13

--- a/solution.py
+++ b/solution.py
@@ -310,17 +310,28 @@
     gets[3 + parts].wait()
 
 
-def leaf_pivot_kernel(sizes, masked, d_v, pivot, after, *outs_and_scratch):
-    quarter, rows = sizes
-    *outs, root_d, sem = outs_and_scratch
-    get = pltpu.make_async_copy(pivot.at[pl.ds(4 * quarter, rows)], root_d, sem)
-    get.start()
+def load_kernel(sizes, pivot, after, root_d, sems):
+    first, rows = sizes
+    step = rows // 4
+    gets = [
+        pltpu.make_async_copy(
+            pivot.at[pl.ds(first + i * step, step)], root_d.at[pl.ds(i * step, step)], sems.at[i]
+        )
+        for i in range(4)
+    ]
+    for get in gets:
+        get.start()
+    for get in gets:
+        get.wait()
+
+
+def leaf_pivot_kernel(sizes, masked, d_v, after, *outs):
+    quarter = sizes
     order = row_order(lax.axis_index("row"), lax.axis_index("leaf"))
     right = masked[...]
     for k in (3, 1, 2, 0):
         product = mm(d_v[rows_at(order[k] * quarter, quarter)], right)
         outs[k][...] = product.astype(BF)
-    get.wait()
 
 
 def scatter_kernel(sizes, live, pmap, w_v, after, out, live_s, pmap_s, sems):
@@ -474,15 +485,15 @@
     from_far = row_swap(away_far, 2)
     from_near = row_swap(away_near, 0)
 
-    *pieces, root_d = call(
-        functools.partial(leaf_pivot_kernel, (quarter, 4 * half)),
-        (*(kept(quarter, columns),) * 4, kept(4 * half, quarter)),
-        [VMEM, VMEM, ANY, ANY],
-        [pltpu.SemaphoreType.DMA],
-        49_500_000,
+    pieces = call(
+        functools.partial(leaf_pivot_kernel, quarter),
+        (kept(quarter, columns),) * 4,
+        [VMEM, VMEM, ANY],
+        [],
+        16 * MIB,
         2 * front * quarter * columns,
         2 * front * quarter,
-    )(masked, d_v, pivot_inverse, away_near)
+    )(masked, d_v, away_near)
     from_near = after(from_near, pieces[0])
     leaf_forward = pieces[0].astype(F32)
     for phase in (2, 0, 1):
@@ -499,6 +510,15 @@
     other_yours = leaf_swap(negated_yours)
     other_mine = leaf_swap(negated_mine)
 
+    root_d = call(
+        functools.partial(load_kernel, (front, 4 * half)),
+        kept(4 * half, quarter),
+        [ANY, ANY],
+        [pltpu.SemaphoreType.DMA((4,))],
+        51_500_000,
+        0,
+        0,
+    )(pivot_inverse, negated_mine)
     partial = call(
         functools.partial(root_pivot_kernel, half),
         kept(4 * half, columns),

time: 45.1 us -> 47.3 us (1.049)
  starting transfers between devices: 17.3 us -> 23.2 us
  waiting for transfers between devices: 16.2 us -> 10.7 us
  local copies, waits for them, and re-layouts: 0.03 us -> 1.33 us
    ppermute x12, starting transfers between devices: 15.6 us -> 21.5 us  [row_swap(): return lax.ppermute(value, ('leaf', 'row'), route)]
    ppermute x12, waiting for transfers between devices: 13.4 us -> 8.8 us  [row_swap(): return lax.ppermute(value, ('leaf', 'row'), route)]
    unnamed x4 -> x8, local copies, waits for them, and re-layouts: 0.01 us -> 1.31 us
    ppermute x7, waiting for transfers between devices: 2.78 us -> 1.94 us  [leaf_swap(): return lax.ppermute(value, 'leaf', [(0, 1), (1, 0)])]
    pallas_call x1 -> x2, Pallas kernels: 2.02 us -> 2.41 us  [the longest x1 1.41 us: two_levels(): call(functools.partial(load_kernel, (front, 4 * half)), kept(4 * half, qu...]
  transfers between devices with their start and end apart: 19 -> 19, of which waited for: 13 -> 11; matrix products, arithmetic and copies ran while one was open for 1% -> 1% of each run, Pallas kernels for 14% -> 14%
where the time goes in v14:
time: 47.3 us; the launch traced here: 47.1 us
  starting transfers between devices  23.2 us (49%)
  waiting for transfers between devices  10.7 us (23%)
  Pallas kernels  10.5 us (22%)
  local copies, waits for them, and re-layouts  1.33 us (3%)
  between operations  0.81 us (2%)
  other arithmetic  0.52 us (1%)
    ppermute x12, starting transfers between devices, row_swap(): return lax.ppermute(value, ('leaf', 'row'), route)  21.5 us
    ppermute x12, waiting for transfers between devices, row_swap(): return lax.ppermute(value, ('leaf', 'row'), route)  8.8 us
    pallas_call x1, Pallas kernels, two_levels(): call(functools.partial(panel_kernel, (quarter, half, parts, updates)), (k...  2.74 us
    ppermute x7, waiting for transfers between devices, leaf_swap(): return lax.ppermute(value, 'leaf', [(0, 1), (1, 0)])  1.94 us
    ppermute x7, starting transfers between devices, leaf_swap(): return lax.ppermute(value, 'leaf', [(0, 1), (1, 0)])  1.66 us
    pallas_call x1, Pallas kernels, two_levels(): call(functools.partial(leaf_transposed_kernel, (quarter, half)), (kept(co...  1.57 us
    pallas_call x1, Pallas kernels, two_levels(): call(functools.partial(load_kernel, (front, 4 * half)), kept(4 * half, qu...  1.41 us
    unnamed x8, local copies, waits for them, and re-layouts  1.31 us
  transfers between devices with their start and end apart: 19, of which 11 were waited for; matrix products, arithmetic and copies ran while one was open for 1% of the time, Pallas kernels for 14%

profile of v14, /device:TPU:0, one launch (start us, length us, event | category | flops | bytes accessed | tf_op | source)
XLA Modules:
  0.0 47.1 jit_solution(9653592414642692961)
XLA Ops:
  0.6 2.7 %shard_map.68 = (bf16[640,128]{1,0:T(8,128)(2,1)S(1)}, bf16[640,128]{1,0:T(8,128)(2,1)S(1)}, bf16[640,128]{1,0:T(8,128)(2,1)S(1)}, bf16[640,128]{1,0:T(8,128)(2,...) custom-call(s32[3]{0:T(128)} %live.3, ...), custom_call_target="tpu_custom_call" | custom-call | flops 251658240 | bytes 1966080 | tf_op jit(solution)/shard_map/pallas_call | solution.py:463
  3.4 1.3 %copy-done.2 = bf16[1536,640]{1,0:T(8,128)(2,1)} copy-done((bf16[1536,640]{1,0:T(8,128)(2,1)}, bf16[1536,640]{1,0:T(8,128)(2,1)S(1)}, u32[]{:S(2)}) %copy-start.2) | copy-done | bytes 1966104
  4.7 0.5 collective-permute-start
  5.2 1.0 %collective-permute-done = bf16[640,128]{1,0:T(8,128)(2,1)S(1)} collective-permute-done((bf16[640,128]{1,0:T(8,128)(2,1)S(1)}, bf16[640,128]{1,0:T(8,128)(2,1)S(1)}, u32[]{:S(2)}, u32[]{:S(2)}) %collective-permute-start) | collective-permute-done | bytes 163872 | tf_op jit(solution)/shard_map/ppermute | solution.py:438
  6.2 2.9 %collective-permute-start.7 = (bf16[640,128]{1,0:T(8,128)(2,1)S(1)}, bf16[640,128]{1,0:T(8,128)(2,1)S(1)}, u32[]{:S(2)}, u32[]{:S(2)}) collective-permute-start(bf16[640,128]{1,0:T(8,128)(2,1)S(1)} %add_convert_fusion.1.after), channel_id=1, source_target_pairs={{0,4},{4,0},{8,12},{12,8},{16,24},{20,28},{24,16},{28,20},{1,5},{5... | collective-permute-start | bytes 491528 | tf_op jit(solution)/shard_map/ppermute | solution.py:446
  9.2 1.6 %collective-permute-start.9 = (bf16[320,128]{1,0:T(8,128)(2,1)S(1)}, bf16[320,128]{1,0:T(8,128)(2,1)S(1)}, u32[]{:S(2)}, u32[]{:S(2)}) collective-permute-start(bf16[320,128]{1,0:T(8,128)(2,1)S(1)} %slice.59), channel_id=1, source_target_pairs={{0,12},{4,8},{8,4},{12,0},{16,28},{20,24},{24,20},{28,16},{1,13},{... | collective-permute-start | bytes 245768 | tf_op jit(solution)/shard_map/ppermute | solution.py:446
  10.7 1.0 %shard_map.69 = (bf16[640,128]{1,0:T(8,128)(2,1)S(1)}, bf16[640,128]{1,0:T(8,128)(2,1)S(1)}, bf16[640,128]{1,0:T(8,128)(2,1)S(1)}, bf16[640,128]{1,0:T(8,128)(2,1)S(1)}) custom-call(bf16[640,128]{1,0:T(8,128)(2,1)S(1)} %get-tuple-element.25.masked, bf16[2560,640]{1,0:T(8,128)(2,1)S(1)} %get-tuple-element.26.d_v, bf16[640,128]{1,0:T(8,128)(2,1)S(1)} %add_convert_fusion.1.after), custom_call_target="tpu_custom_call" | custom-call | flops 419430400 | bytes 3276800 | tf_op jit(solution)/shard_map/pallas_call | solution.py:488
  11.8 1.5 %collective-permute-start.1 = (bf16[640,128]{1,0:T(8,128)(2,1)S(1)}, bf16[640,128]{1,0:T(8,128)(2,1)S(1)}, u32[]{:S(2)}, u32[]{:S(2)}) collective-permute-start(bf16[640,128]{1,0:T(8,128)(2,1)S(1)} %get-tuple-element.30), channel_id=1, source_target_pairs={{0,12},{4,8},{8,4},{12,0},{16,28},{20,24},{24,20},{28,16},{1,13},{... | collective-permute-start | bytes 491528 | tf_op jit(solution)/shard_map/ppermute | solution.py:446
  13.4 1.9 %collective-permute-start.3 = (bf16[640,128]{1,0:T(8,128)(2,1)S(1)}, bf16[640,128]{1,0:T(8,128)(2,1)S(1)}, u32[]{:S(2)}, u32[]{:S(2)}) collective-permute-start(bf16[640,128]{1,0:T(8,128)(2,1)S(1)} %get-tuple-element.32), channel_id=1, source_target_pairs={{0,8},{4,12},{8,0},{12,4},{16,20},{20,16},{24,28},{28,24},{1,9},{5... | collective-permute-start | bytes 491528 | tf_op jit(solution)/shard_map/ppermute | solution.py:446
  15.3 1.2 %collective-permute-done.9 = bf16[320,128]{1,0:T(8,128)(2,1)S(1)} collective-permute-done((bf16[320,128]{1,0:T(8,128)(2,1)S(1)}, bf16[320,128]{1,0:T(8,128)(2,1)S(1)}, u32[]{:S(2)}, u32[]{:S(2)}) %collective-permute-start.9) | collective-permute-done | bytes 81952 | tf_op jit(solution)/shard_map/ppermute | solution.py:446
  16.6 0.5 %collective-permute-start.11 = (bf16[320,128]{1,0:T(8,128)(2,1)S(1)}, bf16[320,128]{1,0:T(8,128)(2,1)S(1)}, u32[]{:S(2)}, u32[]{:S(2)}) collective-permute-start(bf16[320,128]{1,0:T(8,128)(2,1)S(1)} %slice.37.yours), channel_id=1, source_target_pairs={{0,16},{16,0},{1,17},{17,1},{2,18},{18,2},{3,19},{19,3},{4,20},{20... | collective-permute-start | bytes 245768 | tf_op jit(solution)/shard_map/ppermute | solution.py:438
  17.1 1.4 %shard_map.70.d_v = bf16[1280,640]{1,0:T(8,128)(2,1)S(1)} custom-call(bf16[3840,640]{1,0:T(8,128)(2,1)} %pivot.3, bf16[320,128]{1,0:T(8,128)(2,1)S(1)} %fusion.3.after.mine), custom_call_target="tpu_custom_call" | custom-call | tf_op jit(solution)/shard_map/pallas_call | solution.py:513
  18.6 0.6 %shard_map.71 = bf16[1280,128]{1,0:T(8,128)(2,1)S(1)} custom-call(bf16[320,128]{1,0:T(8,128)(2,1)S(1)} %fusion.3.after.mine, bf16[320,128]{1,0:T(8,128)(2,1)S(1)} %slice.37.yours, bf16[320,128]{1,0:T(8,128)(2,1)S(1)} %collective-permute-done.10.other_mine, bf16[320,128]{1,0:T(8,128)(2,1)S(1)} %collective-permute-done.11.other_yours, ...), custom_call_target="tpu_custom_call" | custom-call | tf_op jit(solution)/shard_map/pallas_call | solution.py:522
  19.5 0.5 collective-permute-done.1
  19.9 2.0 %collective-permute-done.2 = bf16[640,128]{1,0:T(8,128)(2,1)S(1)} collective-permute-done((bf16[640,128]{1,0:T(8,128)(2,1)S(1)}, bf16[640,128]{1,0:T(8,128)(2,1)S(1)}, u32[]{:S(2)}, u32[]{:S(2)}) %collective-permute-start.2) | collective-permute-done | bytes 163872 | tf_op jit(solution)/shard_map/ppermute | solution.py:446
  21.9 0.8 %collective-permute-done.3 = bf16[640,128]{1,0:T(8,128)(2,1)S(1)} collective-permute-done((bf16[640,128]{1,0:T(8,128)(2,1)S(1)}, bf16[640,128]{1,0:T(8,128)(2,1)S(1)}, u32[]{:S(2)}, u32[]{:S(2)}) %collective-permute-start.3) | collective-permute-done | bytes 163872 | tf_op jit(solution)/shard_map/ppermute | solution.py:446
  22.8 1.4 %collective-permute-start.4 = (bf16[640,128]{1,0:T(8,128)(2,1)S(1)}, bf16[640,128]{1,0:T(8,128)(2,1)S(1)}, u32[]{:S(2)}, u32[]{:S(2)}) collective-permute-start(bf16[640,128]{1,0:T(8,128)(2,1)S(1)} %select_convert_fusion.own), channel_id=1, source_target_pairs={{0,8},{4,12},{8,0},{12,4},{16,20},{20,16},{24,28},{28,24},{1,9},{5... | collective-permute-start | bytes 491528 | tf_op jit(solution)/shard_map/ppermute | solution.py:446
  24.2 1.6 %collective-permute-start.5 = (bf16[640,128]{1,0:T(8,128)(2,1)S(1)}, bf16[640,128]{1,0:T(8,128)(2,1)S(1)}, u32[]{:S(2)}, u32[]{:S(2)}) collective-permute-start(bf16[640,128]{1,0:T(8,128)(2,1)S(1)} %select_convert_fusion.own), channel_id=1, source_target_pairs={{0,4},{4,0},{8,12},{12,8},{16,24},{20,28},{24,16},{28,20},{1,5},{5... | collective-permute-start | bytes 491528 | tf_op jit(solution)/shard_map/ppermute | solution.py:446
  25.8 0.6 %collective-permute-done.12 = bf16[1280,128]{1,0:T(8,128)(2,1)S(1)} collective-permute-done((bf16[1280,128]{1,0:T(8,128)(2,1)S(1)}, bf16[1280,128]{1,0:T(8,128)(2,1)S(1)}, u32[]{:S(2)}, u32[]{:S(2)}) %collective-permute-start.12) | collective-permute-done | bytes 327712 | tf_op jit(solution)/shard_map/ppermute | solution.py:446
  26.5 3.4 %collective-permute-start.13 = (bf16[1280,128]{1,0:T(8,128)(2,1)S(1)}, bf16[1280,128]{1,0:T(8,128)(2,1)S(1)}, u32[]{:S(2)}, u32[]{:S(2)}) collective-permute-start(bf16[1280,128]{1,0:T(8,128)(2,1)S(1)} %fusion), channel_id=1, source_target_pairs={{0,4},{4,0},{8,12},{12,8},{16,24},{20,28},{24,16},{28,20},{1,5},{5... | collective-permute-start | bytes 983048 | tf_op jit(solution)/shard_map/ppermute | solution.py:446
  29.9 3.4 %collective-permute-start.6 = (bf16[640,128]{1,0:T(8,128)(2,1)S(1)}, bf16[640,128]{1,0:T(8,128)(2,1)S(1)}, u32[]{:S(2)}, u32[]{:S(2)}) collective-permute-start(bf16[640,128]{1,0:T(8,128)(2,1)S(1)} %collective-permute-done.4.after.rows_y), channel_id=1, source_target_pairs={{0,4},{4,0},{8,12},{12,8},{16,24},{20,28},{24,16},{28,20},{1,5},{5... | collective-permute-start | bytes 491528 | tf_op jit(solution)/shard_map/ppermute | solution.py:446
  33.2 0.8 %shard_map.72.panel_rows = bf16[2560,640]{1,0:T(8,128)(2,1)S(1)} custom-call(s32[3]{0:T(128)S(1)} %copy-done.1, s32[2,12]{1,0:T(2,128)S(1)} %copy-done, bf16[1536,640]{1,0:T(8,128)(2,1)S(1)} %copy-done.3, bf16[640,128]{1,0:T(8,128)(2,1)S(1)} %collective-permute-done.4.after.rows_y), custom_call_target="tpu_custom_call" | custom-call | flops 2000000000 | bytes 6553600 | tf_op jit(solution)/shard_map/pallas_call | solution.py:531
  34.1 0.8 %collective-permute-done.13 = bf16[1280,128]{1,0:T(8,128)(2,1)S(1)} collective-permute-done((bf16[1280,128]{1,0:T(8,128)(2,1)S(1)}, bf16[1280,128]{1,0:T(8,128)(2,1)S(1)}, u32[]{:S(2)}, u32[]{:S(2)}) %collective-permute-start.13) | collective-permute-done | bytes 327712 | tf_op jit(solution)/shard_map/ppermute | solution.py:446
  35.1 0.6 %shard_map.73 = (bf16[640,128]{1,0:T(8,128)(2,1)S(1)}, bf16[320,128]{1,0:T(8,128)(2,1)S(1)}) custom-call(bf16[1280,128]{1,0:T(8,128)(2,1)S(1)} %add_convert_fusion.y, bf16[1280,640]{1,0:T(8,128)(2,1)S(1)} %shard_map.70.d_v), custom_call_target="tpu_custom_call" | custom-call | tf_op jit(solution)/shard_map/pallas_call | solution.py:544
  35.7 1.0 %collective-permute-done.6.rows_d = bf16[640,128]{1,0:T(8,128)(2,1)S(1)} collective-permute-done((bf16[640,128]{1,0:T(8,128)(2,1)S(1)}, bf16[640,128]{1,0:T(8,128)(2,1)S(1)}, u32[]{:S(2)}, u32[]{:S(2)}) %collective-permute-start.6) | collective-permute-done | bytes 163872 | tf_op jit(solution)/shard_map/ppermute | solution.py:446
  37.3 3.5 %collective-permute-start.17 = (bf16[320,128]{1,0:T(8,128)(2,1)S(1)}, bf16[320,128]{1,0:T(8,128)(2,1)S(1)}, u32[]{:S(2)}, u32[]{:S(2)}) collective-permute-start(bf16[320,128]{1,0:T(8,128)(2,1)S(1)} %get-tuple-element.46), channel_id=1, source_target_pairs={{0,12},{4,8},{8,4},{12,0},{16,28},{20,24},{24,20},{28,16},{1,13},{... | collective-permute-start | bytes 245768 | tf_op jit(solution)/shard_map/ppermute | solution.py:446
  40.7 1.6 %shard_map.74 = (f32[128,640]{1,0:T(8,128)S(1)}, bf16[960,128]{1,0:T(8,128)(2,1)}) custom-call(bf16[640,128]{1,0:T(8,128)(2,1)S(1)} %select_convert_fusion.own, bf16[640,128]{1,0:T(8,128)(2,1)S(1)} %collective-permute-done.4.after.rows_y, bf16[640,128]{1,0:T(8,128)(2,1)S(1)} %collective-permute-done.5.rows_x, ...), custom_call_target="tpu_custom_call" | custom-call | flops 419430400 | bytes 3276800 | tf_op jit(solution)/shard_map/pallas_call | solution.py:560
  42.3 2.0 %collective-permute-done.15.near = bf16[640,128]{1,0:T(8,128)(2,1)S(1)} collective-permute-done((bf16[640,128]{1,0:T(8,128)(2,1)S(1)}, bf16[640,128]{1,0:T(8,128)(2,1)S(1)}, u32[]{:S(2)}, u32[]{:S(2)}) %collective-permute-start.15) | collective-permute-done | bytes 163872 | tf_op jit(solution)/shard_map/ppermute | solution.py:446
  44.3 0.5 %collective-permute-start.18 = (bf16[320,128]{1,0:T(8,128)(2,1)S(1)}, bf16[320,128]{1,0:T(8,128)(2,1)S(1)}, u32[]{:S(2)}, u32[]{:S(2)}) collective-permute-start(bf16[320,128]{1,0:T(8,128)(2,1)S(1)} %collective-permute-done.17.far), channel_id=1, source_target_pairs={{0,16},{16,0},{1,17},{17,1},{2,18},{18,2},{3,19},{19,3},{4,20},{20... | collective-permute-start | bytes 245768 | tf_op jit(solution)/shard_map/ppermute | solution.py:438
  44.8 0.5 shard_map.75.total
  45.3 0.5 %collective-permute-done.18.far = bf16[320,128]{1,0:T(8,128)(2,1)S(1)} collective-permute-done((bf16[320,128]{1,0:T(8,128)(2,1)S(1)}, bf16[320,128]{1,0:T(8,128)(2,1)S(1)}, u32[]{:S(2)}, u32[]{:S(2)}) %collective-permute-start.18) | collective-permute-done | bytes 81952 | tf_op jit(solution)/shard_map/ppermute | solution.py:438
  45.8 1.3 %shard_map.76 = bf16[960,128]{1,0:T(8,128)(2,1)} custom-call(bf16[640,128]{1,0:T(8,128)(2,1)S(1)} %collective-permute-done.16.near, bf16[320,128]{1,0:T(8,128)(2,1)S(1)} %collective-permute-done.18.far, f32[128,640]{1,0:T(8,128)S(1)} %shard_map.75.total, bf16[2560,640]{1,0:T(8,128)(2,1)S(1)} %shard_map.72.panel_rows, ...), custom_call_target="tpu_custom_call" | custom-call | flops 209715200 | bytes 1638400 | tf_op jit(solution)/shard_map/pallas_call | solution.py:581
  (33 shorter events, 1.6 us)
Async XLA Ops:
  3.4 1.3 %copy-start.2 = (bf16[1536,640]{1,0:T(8,128)(2,1)}, bf16[1536,640]{1,0:T(8,128)(2,1)S(1)}, u32[]{:S(2)}) copy-start(bf16[1536,640]{1,0:T(8,128)(2,1)S(1)} %get-tuple-element.37.w_v) | copy-start | bytes 5898244
  4.7 1.5 %collective-permute-start = (bf16[640,128]{1,0:T(8,128)(2,1)S(1)}, bf16[640,128]{1,0:T(8,128)(2,1)S(1)}, u32[]{:S(2)}, u32[]{:S(2)}) collective-permute-start(bf16[640,128]{1,0:T(8,128)(2,1)S(1)} %get-tuple-element.28), channel_id=1, source_target_pairs={{0,16},{16,0},{1,17},{17,1},{2,18},{18,2},{3,19},{19,3},{4,20},{20... | collective-permute-start | bytes 491528 | tf_op jit(solution)/shard_map/ppermute | solution.py:438
  5.1 4.0 %collective-permute-start.8 = (bf16[640,128]{1,0:T(8,128)(2,1)S(1)}, bf16[640,128]{1,0:T(8,128)(2,1)S(1)}, u32[]{:S(2)}, u32[]{:S(2)}) collective-permute-start(bf16[640,128]{1,0:T(8,128)(2,1)S(1)} %get-tuple-element.35), channel_id=1, source_target_pairs={{0,16},{16,0},{1,17},{17,1},{2,18},{18,2},{3,19},{19,3},{4,20},{20... | collective-permute-start | bytes 491528 | tf_op jit(solution)/shard_map/ppermute | solution.py:438
  6.2 9.1 %collective-permute-start.7 = (bf16[640,128]{1,0:T(8,128)(2,1)S(1)}, bf16[640,128]{1,0:T(8,128)(2,1)S(1)}, u32[]{:S(2)}, u32[]{:S(2)}) collective-permute-start(bf16[640,128]{1,0:T(8,128)(2,1)S(1)} %add_convert_fusion.1.after), channel_id=1, source_target_pairs={{0,4},{4,0},{8,12},{12,8},{16,24},{20,28},{24,16},{28,20},{1,5},{5... | collective-permute-start | bytes 491528 | tf_op jit(solution)/shard_map/ppermute | solution.py:446
  9.2 7.3 %collective-permute-start.9 = (bf16[320,128]{1,0:T(8,128)(2,1)S(1)}, bf16[320,128]{1,0:T(8,128)(2,1)S(1)}, u32[]{:S(2)}, u32[]{:S(2)}) collective-permute-start(bf16[320,128]{1,0:T(8,128)(2,1)S(1)} %slice.59), channel_id=1, source_target_pairs={{0,12},{4,8},{8,4},{12,0},{16,28},{20,24},{24,20},{28,16},{1,13},{... | collective-permute-start | bytes 245768 | tf_op jit(solution)/shard_map/ppermute | solution.py:446
  11.8 8.2 %collective-permute-start.1 = (bf16[640,128]{1,0:T(8,128)(2,1)S(1)}, bf16[640,128]{1,0:T(8,128)(2,1)S(1)}, u32[]{:S(2)}, u32[]{:S(2)}) collective-permute-start(bf16[640,128]{1,0:T(8,128)(2,1)S(1)} %get-tuple-element.30), channel_id=1, source_target_pairs={{0,12},{4,8},{8,4},{12,0},{16,28},{20,24},{24,20},{28,16},{1,13},{... | collective-permute-start | bytes 491528 | tf_op jit(solution)/shard_map/ppermute | solution.py:446
  13.3 8.7 %collective-permute-start.2 = (bf16[640,128]{1,0:T(8,128)(2,1)S(1)}, bf16[640,128]{1,0:T(8,128)(2,1)S(1)}, u32[]{:S(2)}, u32[]{:S(2)}) collective-permute-start(bf16[640,128]{1,0:T(8,128)(2,1)S(1)} %get-tuple-element.31), channel_id=1, source_target_pairs={{0,4},{4,0},{8,12},{12,8},{16,24},{20,28},{24,16},{28,20},{1,5},{5... | collective-permute-start | bytes 491528 | tf_op jit(solution)/shard_map/ppermute | solution.py:446
  13.4 9.3 %collective-permute-start.3 = (bf16[640,128]{1,0:T(8,128)(2,1)S(1)}, bf16[640,128]{1,0:T(8,128)(2,1)S(1)}, u32[]{:S(2)}, u32[]{:S(2)}) collective-permute-start(bf16[640,128]{1,0:T(8,128)(2,1)S(1)} %get-tuple-element.32), channel_id=1, source_target_pairs={{0,8},{4,12},{8,0},{12,4},{16,20},{20,16},{24,28},{28,24},{1,9},{5... | collective-permute-start | bytes 491528 | tf_op jit(solution)/shard_map/ppermute | solution.py:446
  16.5 2.0 %collective-permute-start.10 = (bf16[320,128]{1,0:T(8,128)(2,1)S(1)}, bf16[320,128]{1,0:T(8,128)(2,1)S(1)}, u32[]{:S(2)}, u32[]{:S(2)}) collective-permute-start(bf16[320,128]{1,0:T(8,128)(2,1)S(1)} %fusion.3.after.mine), channel_id=1, source_target_pairs={{0,16},{16,0},{1,17},{17,1},{2,18},{18,2},{3,19},{19,3},{4,20},{20... | collective-permute-start | bytes 245768 | tf_op jit(solution)/shard_map/ppermute | solution.py:438
  16.6 2.0 %collective-permute-start.11 = (bf16[320,128]{1,0:T(8,128)(2,1)S(1)}, bf16[320,128]{1,0:T(8,128)(2,1)S(1)}, u32[]{:S(2)}, u32[]{:S(2)}) collective-permute-start(bf16[320,128]{1,0:T(8,128)(2,1)S(1)} %slice.37.yours), channel_id=1, source_target_pairs={{0,16},{16,0},{1,17},{17,1},{2,18},{18,2},{3,19},{19,3},{4,20},{20... | collective-permute-start | bytes 245768 | tf_op jit(solution)/shard_map/ppermute | solution.py:438
  18.5 14.7 %copy-start = (s32[2,12]{1,0:T(2,128)S(1)}, s32[2,12]{1,0:T(2,128)}, u32[]{:S(2)}) copy-start(s32[2,12]{1,0:T(2,128)} %pmap.3) | copy-start | bytes 292
  18.5 14.7 %copy-start.1 = (s32[3]{0:T(128)S(1)}, s32[3]{0:T(128)}, u32[]{:S(2)}) copy-start(s32[3]{0:T(128)} %live.3) | copy-start | bytes 40
  18.6 14.7 %copy-start.3 = (bf16[1536,640]{1,0:T(8,128)(2,1)S(1)}, bf16[1536,640]{1,0:T(8,128)(2,1)}, u32[]{:S(2)}) copy-start(bf16[1536,640]{1,0:T(8,128)(2,1)} %copy-done.2) | copy-start | bytes 5898244
  19.2 7.1 %collective-permute-start.12 = (bf16[1280,128]{1,0:T(8,128)(2,1)S(1)}, bf16[1280,128]{1,0:T(8,128)(2,1)S(1)}, u32[]{:S(2)}, u32[]{:S(2)}) collective-permute-start(bf16[1280,128]{1,0:T(8,128)(2,1)S(1)} %shard_map.71), channel_id=1, source_target_pairs={{0,8},{4,12},{8,0},{12,4},{16,20},{20,16},{24,28},{28,24},{1,9},{5... | collective-permute-start | bytes 983048 | tf_op jit(solution)/shard_map/ppermute | solution.py:446
  22.8 7.1 %collective-permute-start.4 = (bf16[640,128]{1,0:T(8,128)(2,1)S(1)}, bf16[640,128]{1,0:T(8,128)(2,1)S(1)}, u32[]{:S(2)}, u32[]{:S(2)}) collective-permute-start(bf16[640,128]{1,0:T(8,128)(2,1)S(1)} %select_convert_fusion.own), channel_id=1, source_target_pairs={{0,8},{4,12},{8,0},{12,4},{16,20},{20,16},{24,28},{28,24},{1,9},{5... | collective-permute-start | bytes 491528 | tf_op jit(solution)/shard_map/ppermute | solution.py:446
  24.2 5.7 %collective-permute-start.5 = (bf16[640,128]{1,0:T(8,128)(2,1)S(1)}, bf16[640,128]{1,0:T(8,128)(2,1)S(1)}, u32[]{:S(2)}, u32[]{:S(2)}) collective-permute-start(bf16[640,128]{1,0:T(8,128)(2,1)S(1)} %select_convert_fusion.own), channel_id=1, source_target_pairs={{0,4},{4,0},{8,12},{12,8},{16,24},{20,28},{24,16},{28,20},{1,5},{5... | collective-permute-start | bytes 491528 | tf_op jit(solution)/shard_map/ppermute | solution.py:446
  26.5 8.5 %collective-permute-start.13 = (bf16[1280,128]{1,0:T(8,128)(2,1)S(1)}, bf16[1280,128]{1,0:T(8,128)(2,1)S(1)}, u32[]{:S(2)}, u32[]{:S(2)}) collective-permute-start(bf16[1280,128]{1,0:T(8,128)(2,1)S(1)} %fusion), channel_id=1, source_target_pairs={{0,4},{4,0},{8,12},{12,8},{16,24},{20,28},{24,16},{28,20},{1,5},{5... | collective-permute-start | bytes 983048 | tf_op jit(solution)/shard_map/ppermute | solution.py:446
  29.9 6.8 %collective-permute-start.6 = (bf16[640,128]{1,0:T(8,128)(2,1)S(1)}, bf16[640,128]{1,0:T(8,128)(2,1)S(1)}, u32[]{:S(2)}, u32[]{:S(2)}) collective-permute-start(bf16[640,128]{1,0:T(8,128)(2,1)S(1)} %collective-permute-done.4.after.rows_y), channel_id=1, source_target_pairs={{0,4},{4,0},{8,12},{12,8},{16,24},{20,28},{24,16},{28,20},{1,5},{5... | collective-permute-start | bytes 491528 | tf_op jit(solution)/shard_map/ppermute | solution.py:446
  35.6 1.5 %collective-permute-start.14 = (bf16[640,128]{1,0:T(8,128)(2,1)S(1)}, bf16[640,128]{1,0:T(8,128)(2,1)S(1)}, u32[]{:S(2)}, u32[]{:S(2)}) collective-permute-start(bf16[640,128]{1,0:T(8,128)(2,1)S(1)} %get-tuple-element.40), channel_id=1, source_target_pairs={{0,16},{16,0},{1,17},{17,1},{2,18},{18,2},{3,19},{19,3},{4,20},{20... | collective-permute-start | bytes 491528 | tf_op jit(solution)/shard_map/ppermute | solution.py:438
  37.2 7.1 %collective-permute-start.15 = (bf16[640,128]{1,0:T(8,128)(2,1)S(1)}, bf16[640,128]{1,0:T(8,128)(2,1)S(1)}, u32[]{:S(2)}, u32[]{:S(2)}) collective-permute-start(bf16[640,128]{1,0:T(8,128)(2,1)S(1)} %pad_maximum_fusion.root_rows), channel_id=1, source_target_pairs={{0,8},{4,12},{8,0},{12,4},{16,20},{20,16},{24,28},{28,24},{1,9},{5... | collective-permute-start | bytes 491528 | tf_op jit(solution)/shard_map/ppermute | solution.py:446
  37.3 7.1 %collective-permute-start.17 = (bf16[320,128]{1,0:T(8,128)(2,1)S(1)}, bf16[320,128]{1,0:T(8,128)(2,1)S(1)}, u32[]{:S(2)}, u32[]{:S(2)}) collective-permute-start(bf16[320,128]{1,0:T(8,128)(2,1)S(1)} %get-tuple-element.46), channel_id=1, source_target_pairs={{0,12},{4,8},{8,4},{12,0},{16,28},{20,24},{24,20},{28,16},{1,13},{... | collective-permute-start | bytes 245768 | tf_op jit(solution)/shard_map/ppermute | solution.py:446
  44.3 1.5 %collective-permute-start.16 = (bf16[640,128]{1,0:T(8,128)(2,1)S(1)}, bf16[640,128]{1,0:T(8,128)(2,1)S(1)}, u32[]{:S(2)}, u32[]{:S(2)}) collective-permute-start(bf16[640,128]{1,0:T(8,128)(2,1)S(1)} %collective-permute-done.15.near), channel_id=1, source_target_pairs={{0,16},{16,0},{1,17},{17,1},{2,18},{18,2},{3,19},{19,3},{4,20},{20... | collective-permute-start | bytes 491528 | tf_op jit(solution)/shard_map/ppermute | solution.py:438
  44.3 1.5 %collective-permute-start.18 = (bf16[320,128]{1,0:T(8,128)(2,1)S(1)}, bf16[320,128]{1,0:T(8,128)(2,1)S(1)}, u32[]{:S(2)}, u32[]{:S(2)}) collective-permute-start(bf16[320,128]{1,0:T(8,128)(2,1)S(1)} %collective-permute-done.17.far), channel_id=1, source_target_pairs={{0,16},{16,0},{1,17},{17,1},{2,18},{18,2},{3,19},{19,3},{4,20},{20... | collective-permute-start | bytes 245768 | tf_op jit(solution)/shard_map/ppermute | solution.py:438

commit v15 on v13

--- a/solution.py
+++ b/solution.py
@@ -485,7 +485,7 @@
     )(masked, d_v, pivot_inverse, away_near)
     from_near = after(from_near, pieces[0])
     leaf_forward = pieces[0].astype(F32)
-    for phase in (2, 0, 1):
+    for phase in (0, 2, 1):
         leaf_forward = leaf_forward + row_swap(pieces[1 + phase], phase).astype(F32)
     leaf_forward = jnp.where(mask > 0, leaf_forward, 0.0).astype(BF)
     rows_y = row_swap(leaf_forward, 1)

time: 45.1 us -> 45.1 us (level)
  waiting for transfers between devices: 16.2 us -> 14.4 us
  starting transfers between devices: 17.3 us -> 19 us
    ppermute x12, waiting for transfers between devices: 13.4 us -> 11.6 us  [row_swap(): return lax.ppermute(value, ('leaf', 'row'), route)]
    ppermute x12, starting transfers between devices: 15.6 us -> 17.3 us  [row_swap(): return lax.ppermute(value, ('leaf', 'row'), route)]
  transfers between devices with their start and end apart: 19 -> 19, of which waited for: 13 -> 14; matrix products, arithmetic and copies ran while one was open for 1% -> 1% of each run, Pallas kernels for 14% -> 14%
where the time goes in v15:
time: 45.1 us; the launch traced here: 44.9 us
  starting transfers between devices  19 us (42%)
  waiting for transfers between devices  14.4 us (32%)
  Pallas kernels  10.1 us (22%)
  between operations  0.77 us (2%)
  other arithmetic  0.55 us (1%)
    ppermute x12, starting transfers between devices, row_swap(): return lax.ppermute(value, ('leaf', 'row'), route)  17.3 us
    ppermute x12, waiting for transfers between devices, row_swap(): return lax.ppermute(value, ('leaf', 'row'), route)  11.6 us
    ppermute x7, waiting for transfers between devices, leaf_swap(): return lax.ppermute(value, 'leaf', [(0, 1), (1, 0)])  2.78 us
    pallas_call x1, Pallas kernels, two_levels(): call(functools.partial(panel_kernel, (quarter, half, parts, updates)), (k...  2.74 us
    pallas_call x1, Pallas kernels, two_levels(): call(functools.partial(leaf_pivot_kernel, (quarter, 4 * half)), (*(kept(q...  2.02 us
    ppermute x7, starting transfers between devices, leaf_swap(): return lax.ppermute(value, 'leaf', [(0, 1), (1, 0)])  1.75 us
    pallas_call x1, Pallas kernels, two_levels(): call(functools.partial(leaf_transposed_kernel, (quarter, half)), (kept(co...  1.57 us
    pallas_call x1, Pallas kernels, two_levels(): call(functools.partial(last_kernel, (quarter, half)), stored(quarter + ha...  1.26 us
  transfers between devices with their start and end apart: 19, of which 14 were waited for; matrix products, arithmetic and copies ran while one was open for 1% of the time, Pallas kernels for 14%

profile of v15, /device:TPU:0, one launch (start us, length us, event | category | flops | bytes accessed | tf_op | source)
XLA Modules:
  0.0 44.9 jit_solution(7434729239331465793)
XLA Ops:
  0.6 2.7 %shard_map.68 = (bf16[640,128]{1,0:T(8,128)(2,1)S(1)}, bf16[640,128]{1,0:T(8,128)(2,1)S(1)}, bf16[640,128]{1,0:T(8,128)(2,1)S(1)}, bf16[640,128]{1,0:T(8,128)(2,...) custom-call(s32[3]{0:T(128)} %live.3, ...), custom_call_target="tpu_custom_call" | custom-call | flops 251658240 | bytes 1966080 | tf_op jit(solution)/shard_map/pallas_call | solution.py:452
  3.4 0.5 %collective-permute-start = (bf16[640,128]{1,0:T(8,128)(2,1)S(1)}, bf16[640,128]{1,0:T(8,128)(2,1)S(1)}, u32[]{:S(2)}, u32[]{:S(2)}) collective-permute-start(bf16[640,128]{1,0:T(8,128)(2,1)S(1)} %get-tuple-element.29), channel_id=1, source_target_pairs={{0,16},{16,0},{1,17},{17,1},{2,18},{18,2},{3,19},{19,3},{4,20},{20... | collective-permute-start | bytes 491528 | tf_op jit(solution)/shard_map/ppermute | solution.py:427
  4.0 0.9 %collective-permute-done = bf16[640,128]{1,0:T(8,128)(2,1)S(1)} collective-permute-done((bf16[640,128]{1,0:T(8,128)(2,1)S(1)}, bf16[640,128]{1,0:T(8,128)(2,1)S(1)}, u32[]{:S(2)}, u32[]{:S(2)}) %collective-permute-start) | collective-permute-done | bytes 163872 | tf_op jit(solution)/shard_map/ppermute | solution.py:427
  5.0 2.9 %collective-permute-start.7 = (bf16[640,128]{1,0:T(8,128)(2,1)S(1)}, bf16[640,128]{1,0:T(8,128)(2,1)S(1)}, u32[]{:S(2)}, u32[]{:S(2)}) collective-permute-start(bf16[640,128]{1,0:T(8,128)(2,1)S(1)} %add_convert_fusion.1.after), channel_id=1, source_target_pairs={{0,4},{4,0},{8,12},{12,8},{16,24},{20,28},{24,16},{28,20},{1,5},{5... | collective-permute-start | bytes 491528 | tf_op jit(solution)/shard_map/ppermute | solution.py:435
  8.0 1.6 %collective-permute-start.9 = (bf16[320,128]{1,0:T(8,128)(2,1)S(1)}, bf16[320,128]{1,0:T(8,128)(2,1)S(1)}, u32[]{:S(2)}, u32[]{:S(2)}) collective-permute-start(bf16[320,128]{1,0:T(8,128)(2,1)S(1)} %slice.59), channel_id=1, source_target_pairs={{0,12},{4,8},{8,4},{12,0},{16,28},{20,24},{24,20},{28,16},{1,13},{... | collective-permute-start | bytes 245768 | tf_op jit(solution)/shard_map/ppermute | solution.py:435
  9.5 2.0 %shard_map.69 = (bf16[640,128]{1,0:T(8,128)(2,1)S(1)}, bf16[640,128]{1,0:T(8,128)(2,1)S(1)}, bf16[640,128]{1,0:T(8,128)(2,1)S(1)}, bf16[640,128]{1,0:T(8,128)(2,1)S(1)}, bf16[1280,640]{1,0:T(8,128)(2,1)S(1)}) custom-call(bf16[640,128]{1,0:T(8,128)(2,1)S(1)} %get-tuple-element.26.masked, bf16[2560,640]{1,0:T(8,128)(2,1)S(1)} %get-tuple-element.27.d_v, ...), custom_call_target="tpu_custom_call" | custom-call | flops 419430400 | bytes 3276800 | tf_op jit(solution)/shard_map/pallas_call | solution.py:477
  11.6 1.6 %collective-permute-start.1 = (bf16[640,128]{1,0:T(8,128)(2,1)S(1)}, bf16[640,128]{1,0:T(8,128)(2,1)S(1)}, u32[]{:S(2)}, u32[]{:S(2)}) collective-permute-start(bf16[640,128]{1,0:T(8,128)(2,1)S(1)} %get-tuple-element.31), channel_id=1, source_target_pairs={{0,4},{4,0},{8,12},{12,8},{16,24},{20,28},{24,16},{28,20},{1,5},{5... | collective-permute-start | bytes 491528 | tf_op jit(solution)/shard_map/ppermute | solution.py:435
  13.2 1.9 %collective-permute-start.3 = (bf16[640,128]{1,0:T(8,128)(2,1)S(1)}, bf16[640,128]{1,0:T(8,128)(2,1)S(1)}, u32[]{:S(2)}, u32[]{:S(2)}) collective-permute-start(bf16[640,128]{1,0:T(8,128)(2,1)S(1)} %get-tuple-element.33), channel_id=1, source_target_pairs={{0,8},{4,12},{8,0},{12,4},{16,20},{20,16},{24,28},{28,24},{1,9},{5... | collective-permute-start | bytes 491528 | tf_op jit(solution)/shard_map/ppermute | solution.py:435
  15.3 0.5 %collective-permute-start.11 = (bf16[320,128]{1,0:T(8,128)(2,1)S(1)}, bf16[320,128]{1,0:T(8,128)(2,1)S(1)}, u32[]{:S(2)}, u32[]{:S(2)}) collective-permute-start(bf16[320,128]{1,0:T(8,128)(2,1)S(1)} %slice.37.yours), channel_id=1, source_target_pairs={{0,16},{16,0},{1,17},{17,1},{2,18},{18,2},{3,19},{19,3},{4,20},{20... | collective-permute-start | bytes 245768 | tf_op jit(solution)/shard_map/ppermute | solution.py:427
  15.8 0.8 %collective-permute-done.10.other_mine = bf16[320,128]{1,0:T(8,128)(2,1)S(1)} collective-permute-done((bf16[320,128]{1,0:T(8,128)(2,1)S(1)}, bf16[320,128]{1,0:T(8,128)(2,1)S(1)}, u32[]{:S(2)}, u32[]{:S(2)}) %collective-permute-start.10) | collective-permute-done | bytes 81952 | tf_op jit(solution)/shard_map/ppermute | solution.py:427
  16.7 0.6 %shard_map.70 = bf16[1280,128]{1,0:T(8,128)(2,1)S(1)} custom-call(bf16[320,128]{1,0:T(8,128)(2,1)S(1)} %fusion.3.mine, bf16[320,128]{1,0:T(8,128)(2,1)S(1)} %slice.37.yours, bf16[320,128]{1,0:T(8,128)(2,1)S(1)} %collective-permute-done.10.other_mine, bf16[320,128]{1,0:T(8,128)(2,1)S(1)} %collective-permute-done.11.other_yours, ...), custom_call_target="tpu_custom_call" | custom-call | tf_op jit(solution)/shard_map/pallas_call | solution.py:502
  17.5 1.2 %collective-permute-done.1 = bf16[640,128]{1,0:T(8,128)(2,1)S(1)} collective-permute-done((bf16[640,128]{1,0:T(8,128)(2,1)S(1)}, bf16[640,128]{1,0:T(8,128)(2,1)S(1)}, u32[]{:S(2)}, u32[]{:S(2)}) %collective-permute-start.1) | collective-permute-done | bytes 163872 | tf_op jit(solution)/shard_map/ppermute | solution.py:435
  18.7 2.5 %collective-permute-done.2 = bf16[640,128]{1,0:T(8,128)(2,1)S(1)} collective-permute-done((bf16[640,128]{1,0:T(8,128)(2,1)S(1)}, bf16[640,128]{1,0:T(8,128)(2,1)S(1)}, u32[]{:S(2)}, u32[]{:S(2)}) %collective-permute-start.2) | collective-permute-done | bytes 163872 | tf_op jit(solution)/shard_map/ppermute | solution.py:435
  21.2 0.4 collective-permute-done.3
  21.8 2.1 %collective-permute-start.4 = (bf16[640,128]{1,0:T(8,128)(2,1)S(1)}, bf16[640,128]{1,0:T(8,128)(2,1)S(1)}, u32[]{:S(2)}, u32[]{:S(2)}) collective-permute-start(bf16[640,128]{1,0:T(8,128)(2,1)S(1)} %select_convert_fusion.own), channel_id=1, source_target_pairs={{0,8},{4,12},{8,0},{12,4},{16,20},{20,16},{24,28},{28,24},{1,9},{5... | collective-permute-start | bytes 491528 | tf_op jit(solution)/shard_map/ppermute | solution.py:435
  23.9 1.0 %collective-permute-start.5 = (bf16[640,128]{1,0:T(8,128)(2,1)S(1)}, bf16[640,128]{1,0:T(8,128)(2,1)S(1)}, u32[]{:S(2)}, u32[]{:S(2)}) collective-permute-start(bf16[640,128]{1,0:T(8,128)(2,1)S(1)} %select_convert_fusion.own), channel_id=1, source_target_pairs={{0,4},{4,0},{8,12},{12,8},{16,24},{20,28},{24,16},{28,20},{1,5},{5... | collective-permute-start | bytes 491528 | tf_op jit(solution)/shard_map/ppermute | solution.py:435
  24.9 0.5 %collective-permute-done.12 = bf16[1280,128]{1,0:T(8,128)(2,1)S(1)} collective-permute-done((bf16[1280,128]{1,0:T(8,128)(2,1)S(1)}, bf16[1280,128]{1,0:T(8,128)(2,1)S(1)}, u32[]{:S(2)}, u32[]{:S(2)}) %collective-permute-start.12) | collective-permute-done | bytes 327712 | tf_op jit(solution)/shard_map/ppermute | solution.py:435
  25.5 1.3 %collective-permute-start.13 = (bf16[1280,128]{1,0:T(8,128)(2,1)S(1)}, bf16[1280,128]{1,0:T(8,128)(2,1)S(1)}, u32[]{:S(2)}, u32[]{:S(2)}) collective-permute-start(bf16[1280,128]{1,0:T(8,128)(2,1)S(1)} %fusion), channel_id=1, source_target_pairs={{0,4},{4,0},{8,12},{12,8},{16,24},{20,28},{24,16},{28,20},{1,5},{5... | collective-permute-start | bytes 983048 | tf_op jit(solution)/shard_map/ppermute | solution.py:435
  26.8 2.0 %collective-permute-done.4.after.rows_y = bf16[640,128]{1,0:T(8,128)(2,1)S(1)} collective-permute-done((bf16[640,128]{1,0:T(8,128)(2,1)S(1)}, bf16[640,128]{1,0:T(8,128)(2,1)S(1)}, u32[]{:S(2)}, u32[]{:S(2)}) %collective-permute-start.4) | collective-permute-done | bytes 163872 | tf_op jit(solution)/shard_map/ppermute | solution.py:435
  29.2 1.7 %collective-permute-start.6 = (bf16[640,128]{1,0:T(8,128)(2,1)S(1)}, bf16[640,128]{1,0:T(8,128)(2,1)S(1)}, u32[]{:S(2)}, u32[]{:S(2)}) collective-permute-start(bf16[640,128]{1,0:T(8,128)(2,1)S(1)} %collective-permute-done.4.after.rows_y), channel_id=1, source_target_pairs={{0,4},{4,0},{8,12},{12,8},{16,24},{20,28},{24,16},{28,20},{1,5},{5... | collective-permute-start | bytes 491528 | tf_op jit(solution)/shard_map/ppermute | solution.py:435
  30.9 0.8 %shard_map.71.panel_rows = bf16[2560,640]{1,0:T(8,128)(2,1)S(1)} custom-call(s32[3]{0:T(128)S(1)} %copy-done.1, s32[2,12]{1,0:T(2,128)S(1)} %copy-done, bf16[1536,640]{1,0:T(8,128)(2,1)S(1)} %get-tuple-element.39.w_v, bf16[640,128]{1,0:T(8,128)(2,1)S(1)} %collective-permute-done.4.after.rows_y), custom_call_target="tpu_custom_call" | custom-call | flops 2000000000 | bytes 6553600 | tf_op jit(solution)/shard_map/pallas_call | solution.py:511
  31.8 0.9 %collective-permute-done.13 = bf16[1280,128]{1,0:T(8,128)(2,1)S(1)} collective-permute-done((bf16[1280,128]{1,0:T(8,128)(2,1)S(1)}, bf16[1280,128]{1,0:T(8,128)(2,1)S(1)}, u32[]{:S(2)}, u32[]{:S(2)}) %collective-permute-start.13) | collective-permute-done | bytes 327712 | tf_op jit(solution)/shard_map/ppermute | solution.py:435
  32.9 0.6 %shard_map.72 = (bf16[640,128]{1,0:T(8,128)(2,1)S(1)}, bf16[320,128]{1,0:T(8,128)(2,1)S(1)}) custom-call(bf16[1280,128]{1,0:T(8,128)(2,1)S(1)} %add_convert_fusion.y, bf16[1280,640]{1,0:T(8,128)(2,1)S(1)} %get-tuple-element.38.d_v), custom_call_target="tpu_custom_call" | custom-call | tf_op jit(solution)/shard_map/pallas_call | solution.py:524
  33.5 1.0 %collective-permute-done.6.rows_d = bf16[640,128]{1,0:T(8,128)(2,1)S(1)} collective-permute-done((bf16[640,128]{1,0:T(8,128)(2,1)S(1)}, bf16[640,128]{1,0:T(8,128)(2,1)S(1)}, u32[]{:S(2)}, u32[]{:S(2)}) %collective-permute-start.6) | collective-permute-done | bytes 163872 | tf_op jit(solution)/shard_map/ppermute | solution.py:435
  35.0 1.4 %collective-permute-start.15 = (bf16[640,128]{1,0:T(8,128)(2,1)S(1)}, bf16[640,128]{1,0:T(8,128)(2,1)S(1)}, u32[]{:S(2)}, u32[]{:S(2)}) collective-permute-start(bf16[640,128]{1,0:T(8,128)(2,1)S(1)} %pad_maximum_fusion.root_rows), channel_id=1, source_target_pairs={{0,8},{4,12},{8,0},{12,4},{16,20},{20,16},{24,28},{28,24},{1,9},{5... | collective-permute-start | bytes 491528 | tf_op jit(solution)/shard_map/ppermute | solution.py:435
  36.4 1.4 %collective-permute-start.17 = (bf16[320,128]{1,0:T(8,128)(2,1)S(1)}, bf16[320,128]{1,0:T(8,128)(2,1)S(1)}, u32[]{:S(2)}, u32[]{:S(2)}) collective-permute-start(bf16[320,128]{1,0:T(8,128)(2,1)S(1)} %get-tuple-element.48), channel_id=1, source_target_pairs={{0,12},{4,8},{8,4},{12,0},{16,28},{20,24},{24,20},{28,16},{1,13},{... | collective-permute-start | bytes 245768 | tf_op jit(solution)/shard_map/ppermute | solution.py:435
  37.9 1.6 %shard_map.73 = (f32[128,640]{1,0:T(8,128)S(1)}, bf16[960,128]{1,0:T(8,128)(2,1)}) custom-call(bf16[640,128]{1,0:T(8,128)(2,1)S(1)} %select_convert_fusion.own, bf16[640,128]{1,0:T(8,128)(2,1)S(1)} %collective-permute-done.4.after.rows_y, bf16[640,128]{1,0:T(8,128)(2,1)S(1)} %collective-permute-done.5.rows_x, ...), custom_call_target="tpu_custom_call" | custom-call | flops 419430400 | bytes 3276800 | tf_op jit(solution)/shard_map/pallas_call | solution.py:540
  39.4 2.7 %collective-permute-done.15.near = bf16[640,128]{1,0:T(8,128)(2,1)S(1)} collective-permute-done((bf16[640,128]{1,0:T(8,128)(2,1)S(1)}, bf16[640,128]{1,0:T(8,128)(2,1)S(1)}, u32[]{:S(2)}, u32[]{:S(2)}) %collective-permute-start.15) | collective-permute-done | bytes 163872 | tf_op jit(solution)/shard_map/ppermute | solution.py:435
  42.1 0.5 %collective-permute-start.18 = (bf16[320,128]{1,0:T(8,128)(2,1)S(1)}, bf16[320,128]{1,0:T(8,128)(2,1)S(1)}, u32[]{:S(2)}, u32[]{:S(2)}) collective-permute-start(bf16[320,128]{1,0:T(8,128)(2,1)S(1)} %collective-permute-done.17.far), channel_id=1, source_target_pairs={{0,16},{16,0},{1,17},{17,1},{2,18},{18,2},{3,19},{19,3},{4,20},{20... | collective-permute-start | bytes 245768 | tf_op jit(solution)/shard_map/ppermute | solution.py:427
  42.6 0.5 %shard_map.74.total = f32[128,640]{1,0:T(8,128)S(1)} custom-call(bf16[640,128]{1,0:T(8,128)(2,1)S(1)} %collective-permute-done.15.near, bf16[320,128]{1,0:T(8,128)(2,1)S(1)} %collective-permute-done.17.far, f32[128,640]{1,0:T(8,128)S(1)} %get-tuple-element.46.total, bf16[2560,640]{1,0:T(8,128)(2,1)S(1)} %shard_map.71.panel_rows), custom_call_target="tpu_custom_call" | custom-call | tf_op jit(solution)/shard_map/pallas_call | solution.py:552
  43.1 0.5 %collective-permute-done.18.far = bf16[320,128]{1,0:T(8,128)(2,1)S(1)} collective-permute-done((bf16[320,128]{1,0:T(8,128)(2,1)S(1)}, bf16[320,128]{1,0:T(8,128)(2,1)S(1)}, u32[]{:S(2)}, u32[]{:S(2)}) %collective-permute-start.18) | collective-permute-done | bytes 81952 | tf_op jit(solution)/shard_map/ppermute | solution.py:427
  43.6 1.3 %shard_map.75 = bf16[960,128]{1,0:T(8,128)(2,1)} custom-call(bf16[640,128]{1,0:T(8,128)(2,1)S(1)} %collective-permute-done.16.near, bf16[320,128]{1,0:T(8,128)(2,1)S(1)} %collective-permute-done.18.far, f32[128,640]{1,0:T(8,128)S(1)} %shard_map.74.total, bf16[2560,640]{1,0:T(8,128)(2,1)S(1)} %shard_map.71.panel_rows, ...), custom_call_target="tpu_custom_call" | custom-call | flops 209715200 | bytes 1638400 | tf_op jit(solution)/shard_map/pallas_call | solution.py:561
  (28 shorter events, 1.9 us)
Async XLA Ops:
  3.4 1.5 %collective-permute-start = (bf16[640,128]{1,0:T(8,128)(2,1)S(1)}, bf16[640,128]{1,0:T(8,128)(2,1)S(1)}, u32[]{:S(2)}, u32[]{:S(2)}) collective-permute-start(bf16[640,128]{1,0:T(8,128)(2,1)S(1)} %get-tuple-element.29), channel_id=1, source_target_pairs={{0,16},{16,0},{1,17},{17,1},{2,18},{18,2},{3,19},{19,3},{4,20},{20... | collective-permute-start | bytes 491528 | tf_op jit(solution)/shard_map/ppermute | solution.py:427
  3.9 4.0 %collective-permute-start.8 = (bf16[640,128]{1,0:T(8,128)(2,1)S(1)}, bf16[640,128]{1,0:T(8,128)(2,1)S(1)}, u32[]{:S(2)}, u32[]{:S(2)}) collective-permute-start(bf16[640,128]{1,0:T(8,128)(2,1)S(1)} %get-tuple-element.36), channel_id=1, source_target_pairs={{0,16},{16,0},{1,17},{17,1},{2,18},{18,2},{3,19},{19,3},{4,20},{20... | collective-permute-start | bytes 491528 | tf_op jit(solution)/shard_map/ppermute | solution.py:427
  5.0 10.2 %collective-permute-start.7 = (bf16[640,128]{1,0:T(8,128)(2,1)S(1)}, bf16[640,128]{1,0:T(8,128)(2,1)S(1)}, u32[]{:S(2)}, u32[]{:S(2)}) collective-permute-start(bf16[640,128]{1,0:T(8,128)(2,1)S(1)} %add_convert_fusion.1.after), channel_id=1, source_target_pairs={{0,4},{4,0},{8,12},{12,8},{16,24},{20,28},{24,16},{28,20},{1,5},{5... | collective-permute-start | bytes 491528 | tf_op jit(solution)/shard_map/ppermute | solution.py:435
  8.0 7.2 %collective-permute-start.9 = (bf16[320,128]{1,0:T(8,128)(2,1)S(1)}, bf16[320,128]{1,0:T(8,128)(2,1)S(1)}, u32[]{:S(2)}, u32[]{:S(2)}) collective-permute-start(bf16[320,128]{1,0:T(8,128)(2,1)S(1)} %slice.59), channel_id=1, source_target_pairs={{0,12},{4,8},{8,4},{12,0},{16,28},{20,24},{24,20},{28,16},{1,13},{... | collective-permute-start | bytes 245768 | tf_op jit(solution)/shard_map/ppermute | solution.py:435
  11.5 19.4 %copy-start = (s32[2,12]{1,0:T(2,128)S(1)}, s32[2,12]{1,0:T(2,128)}, u32[]{:S(2)}) copy-start(s32[2,12]{1,0:T(2,128)} %pmap.3) | copy-start | bytes 292
  11.6 19.4 %copy-start.1 = (s32[3]{0:T(128)S(1)}, s32[3]{0:T(128)}, u32[]{:S(2)}) copy-start(s32[3]{0:T(128)} %live.3) | copy-start | bytes 40
  11.6 7.1 %collective-permute-start.1 = (bf16[640,128]{1,0:T(8,128)(2,1)S(1)}, bf16[640,128]{1,0:T(8,128)(2,1)S(1)}, u32[]{:S(2)}, u32[]{:S(2)}) collective-permute-start(bf16[640,128]{1,0:T(8,128)(2,1)S(1)} %get-tuple-element.31), channel_id=1, source_target_pairs={{0,4},{4,0},{8,12},{12,8},{16,24},{20,28},{24,16},{28,20},{1,5},{5... | collective-permute-start | bytes 491528 | tf_op jit(solution)/shard_map/ppermute | solution.py:435
  13.1 8.1 %collective-permute-start.2 = (bf16[640,128]{1,0:T(8,128)(2,1)S(1)}, bf16[640,128]{1,0:T(8,128)(2,1)S(1)}, u32[]{:S(2)}, u32[]{:S(2)}) collective-permute-start(bf16[640,128]{1,0:T(8,128)(2,1)S(1)} %get-tuple-element.32), channel_id=1, source_target_pairs={{0,12},{4,8},{8,4},{12,0},{16,28},{20,24},{24,20},{28,16},{1,13},{... | collective-permute-start | bytes 491528 | tf_op jit(solution)/shard_map/ppermute | solution.py:435
  13.2 8.4 %collective-permute-start.3 = (bf16[640,128]{1,0:T(8,128)(2,1)S(1)}, bf16[640,128]{1,0:T(8,128)(2,1)S(1)}, u32[]{:S(2)}, u32[]{:S(2)}) collective-permute-start(bf16[640,128]{1,0:T(8,128)(2,1)S(1)} %get-tuple-element.33), channel_id=1, source_target_pairs={{0,8},{4,12},{8,0},{12,4},{16,20},{20,16},{24,28},{28,24},{1,9},{5... | collective-permute-start | bytes 491528 | tf_op jit(solution)/shard_map/ppermute | solution.py:435
  15.2 1.3 %collective-permute-start.10 = (bf16[320,128]{1,0:T(8,128)(2,1)S(1)}, bf16[320,128]{1,0:T(8,128)(2,1)S(1)}, u32[]{:S(2)}, u32[]{:S(2)}) collective-permute-start(bf16[320,128]{1,0:T(8,128)(2,1)S(1)} %fusion.3.mine), channel_id=1, source_target_pairs={{0,16},{16,0},{1,17},{17,1},{2,18},{18,2},{3,19},{19,3},{4,20},{20... | collective-permute-start | bytes 245768 | tf_op jit(solution)/shard_map/ppermute | solution.py:427
  15.3 1.4 %collective-permute-start.11 = (bf16[320,128]{1,0:T(8,128)(2,1)S(1)}, bf16[320,128]{1,0:T(8,128)(2,1)S(1)}, u32[]{:S(2)}, u32[]{:S(2)}) collective-permute-start(bf16[320,128]{1,0:T(8,128)(2,1)S(1)} %slice.37.yours), channel_id=1, source_target_pairs={{0,16},{16,0},{1,17},{17,1},{2,18},{18,2},{3,19},{19,3},{4,20},{20... | collective-permute-start | bytes 245768 | tf_op jit(solution)/shard_map/ppermute | solution.py:427
  17.4 8.1 %collective-permute-start.12 = (bf16[1280,128]{1,0:T(8,128)(2,1)S(1)}, bf16[1280,128]{1,0:T(8,128)(2,1)S(1)}, u32[]{:S(2)}, u32[]{:S(2)}) collective-permute-start(bf16[1280,128]{1,0:T(8,128)(2,1)S(1)} %shard_map.70), channel_id=1, source_target_pairs={{0,8},{4,12},{8,0},{12,4},{16,20},{20,16},{24,28},{28,24},{1,9},{5... | collective-permute-start | bytes 983048 | tf_op jit(solution)/shard_map/ppermute | solution.py:435
  21.8 7.1 %collective-permute-start.4 = (bf16[640,128]{1,0:T(8,128)(2,1)S(1)}, bf16[640,128]{1,0:T(8,128)(2,1)S(1)}, u32[]{:S(2)}, u32[]{:S(2)}) collective-permute-start(bf16[640,128]{1,0:T(8,128)(2,1)S(1)} %select_convert_fusion.own), channel_id=1, source_target_pairs={{0,8},{4,12},{8,0},{12,4},{16,20},{20,16},{24,28},{28,24},{1,9},{5... | collective-permute-start | bytes 491528 | tf_op jit(solution)/shard_map/ppermute | solution.py:435
  23.9 5.3 %collective-permute-start.5 = (bf16[640,128]{1,0:T(8,128)(2,1)S(1)}, bf16[640,128]{1,0:T(8,128)(2,1)S(1)}, u32[]{:S(2)}, u32[]{:S(2)}) collective-permute-start(bf16[640,128]{1,0:T(8,128)(2,1)S(1)} %select_convert_fusion.own), channel_id=1, source_target_pairs={{0,4},{4,0},{8,12},{12,8},{16,24},{20,28},{24,16},{28,20},{1,5},{5... | collective-permute-start | bytes 491528 | tf_op jit(solution)/shard_map/ppermute | solution.py:435
  25.5 7.2 %collective-permute-start.13 = (bf16[1280,128]{1,0:T(8,128)(2,1)S(1)}, bf16[1280,128]{1,0:T(8,128)(2,1)S(1)}, u32[]{:S(2)}, u32[]{:S(2)}) collective-permute-start(bf16[1280,128]{1,0:T(8,128)(2,1)S(1)} %fusion), channel_id=1, source_target_pairs={{0,4},{4,0},{8,12},{12,8},{16,24},{20,28},{24,16},{28,20},{1,5},{5... | collective-permute-start | bytes 983048 | tf_op jit(solution)/shard_map/ppermute | solution.py:435
  29.2 5.3 %collective-permute-start.6 = (bf16[640,128]{1,0:T(8,128)(2,1)S(1)}, bf16[640,128]{1,0:T(8,128)(2,1)S(1)}, u32[]{:S(2)}, u32[]{:S(2)}) collective-permute-start(bf16[640,128]{1,0:T(8,128)(2,1)S(1)} %collective-permute-done.4.after.rows_y), channel_id=1, source_target_pairs={{0,4},{4,0},{8,12},{12,8},{16,24},{20,28},{24,16},{28,20},{1,5},{5... | collective-permute-start | bytes 491528 | tf_op jit(solution)/shard_map/ppermute | solution.py:435
  33.4 1.5 %collective-permute-start.14 = (bf16[640,128]{1,0:T(8,128)(2,1)S(1)}, bf16[640,128]{1,0:T(8,128)(2,1)S(1)}, u32[]{:S(2)}, u32[]{:S(2)}) collective-permute-start(bf16[640,128]{1,0:T(8,128)(2,1)S(1)} %get-tuple-element.42), channel_id=1, source_target_pairs={{0,16},{16,0},{1,17},{17,1},{2,18},{18,2},{3,19},{19,3},{4,20},{20... | collective-permute-start | bytes 491528 | tf_op jit(solution)/shard_map/ppermute | solution.py:427
  35.0 7.1 %collective-permute-start.15 = (bf16[640,128]{1,0:T(8,128)(2,1)S(1)}, bf16[640,128]{1,0:T(8,128)(2,1)S(1)}, u32[]{:S(2)}, u32[]{:S(2)}) collective-permute-start(bf16[640,128]{1,0:T(8,128)(2,1)S(1)} %pad_maximum_fusion.root_rows), channel_id=1, source_target_pairs={{0,8},{4,12},{8,0},{12,4},{16,20},{20,16},{24,28},{28,24},{1,9},{5... | collective-permute-start | bytes 491528 | tf_op jit(solution)/shard_map/ppermute | solution.py:435
  36.4 5.7 %collective-permute-start.17 = (bf16[320,128]{1,0:T(8,128)(2,1)S(1)}, bf16[320,128]{1,0:T(8,128)(2,1)S(1)}, u32[]{:S(2)}, u32[]{:S(2)}) collective-permute-start(bf16[320,128]{1,0:T(8,128)(2,1)S(1)} %get-tuple-element.48), channel_id=1, source_target_pairs={{0,12},{4,8},{8,4},{12,0},{16,28},{20,24},{24,20},{28,16},{1,13},{... | collective-permute-start | bytes 245768 | tf_op jit(solution)/shard_map/ppermute | solution.py:435
  42.1 1.5 %collective-permute-start.16 = (bf16[640,128]{1,0:T(8,128)(2,1)S(1)}, bf16[640,128]{1,0:T(8,128)(2,1)S(1)}, u32[]{:S(2)}, u32[]{:S(2)}) collective-permute-start(bf16[640,128]{1,0:T(8,128)(2,1)S(1)} %collective-permute-done.15.near), channel_id=1, source_target_pairs={{0,16},{16,0},{1,17},{17,1},{2,18},{18,2},{3,19},{19,3},{4,20},{20... | collective-permute-start | bytes 491528 | tf_op jit(solution)/shard_map/ppermute | solution.py:427
  42.1 1.5 %collective-permute-start.18 = (bf16[320,128]{1,0:T(8,128)(2,1)S(1)}, bf16[320,128]{1,0:T(8,128)(2,1)S(1)}, u32[]{:S(2)}, u32[]{:S(2)}) collective-permute-start(bf16[320,128]{1,0:T(8,128)(2,1)S(1)} %collective-permute-done.17.far), channel_id=1, source_target_pairs={{0,16},{16,0},{1,17},{17,1},{2,18},{18,2},{3,19},{19,3},{4,20},{20... | collective-permute-start | bytes 245768 | tf_op jit(solution)/shard_map/ppermute | solution.py:427
